TPU v7x, 32 devices: a whole 2x2x4 slice. The times are simulated.
32 devices in a mesh: pipe: 4 (over y, x), ctx: 4 (over z), head: 2 (over core).
Axes of the slice: x: 2, y: 2, z: 4, core: 2. Of those that a mesh axis runs over, the one named last changes fastest.
Arguments:
- queries: bfloat16 [4, 512, 64, 128], P('pipe', 'ctx', 'head'), may hold values from -160 to 160
- key_heads: bfloat16 [4, 512, 8, 128], P('pipe', 'ctx', 'head'), may hold values from -6 to 6
- value_heads: bfloat16 [4, 512, 8, 128], P('pipe', 'ctx', 'head'), may hold values from -6 to 6
- forward_out: bfloat16 [4, 512, 64, 128], P('pipe', 'ctx', 'head'), may hold values from -4 to 4
- output_grad: bfloat16 [4, 512, 64, 128], P('pipe', 'ctx', 'head'), may hold values from -6 to 6
- block_order: int32 [8], replicated, may hold values from 0 to 7, each once
Outputs:
- key_grad: bfloat16 [4, 512, 8, 128], P('pipe', 'ctx', 'head')
- value_grad: bfloat16 [4, 512, 8, 128], P('pipe', 'ctx', 'head')
- handed: bfloat16 [4, 512, 64, 128], P('pipe', 'ctx', 'head')
Inputs may be any that keep to these rules, and one draw needn't show every extreme that they name: `block_order`: every half-block number appears exactly once.
All inputs are finite; a program needn't handle non-finite values.
Results may differ from a plain program's by a relative error of at most 0.012.
The roundings to bfloat16 on the way count: a program that leaves them out, or rounds other values in their place, can miss the bound.
Values may be sent and summed in bfloat16 or wider, within the bound.
No kernel may reach another device: no remote copies, remote signals or barrier semaphores. Data moves between devices by JAX's collectives and lax.ppermute only.
A program may use at most 64 MiB of HBM per device.

v0:
```python
import math

import jax
import jax.numpy as jnp
from jax import lax
from jax.sharding import PartitionSpec as P

NEG = -1e30


def passed_along(value, axis, steps):
    count = lax.axis_size(axis)
    pairs = [(source, (source + steps) % count) for source in range(count)]
    return lax.ppermute(value, axis, pairs)


def shifted(value, axis, steps):
    count = lax.axis_size(axis)
    first, last = (max(0, -steps), min(count, count - steps))
    return lax.ppermute(value, axis, [(source, source + steps) for source in range(first, last)])


def hadamard(size_in):
    indices = jnp.arange(size_in, dtype=jnp.int32)
    parity = jnp.zeros((size_in, size_in), jnp.int32)
    for bit_place in range(size_in.bit_length() - 1):
        digit = indices // 2**bit_place % 2
        parity = parity + digit[:, None] * digit[None, :]
    parity = parity % 2
    return (1.0 - 2.0 * parity.astype(jnp.float32)) / math.sqrt(size_in)


def rotate(values, rotation):
    return jnp.dot(values.astype(jnp.float32), rotation, precision=lax.Precision.HIGHEST).astype(
        jnp.bfloat16
    )


def half_starts(block_order, source):
    return lax.dynamic_slice_in_dim(block_order, source * 2, 2)


def stat_update(running, q_rows, q_pos, k_rows, k_pos, score_scale):
    row_top, row_total = running
    scores = (
        jnp.einsum("iagd,jad->agij", q_rows, k_rows, preferred_element_type=jnp.float32)
        * score_scale
    )
    visible = k_pos[None, :] <= q_pos[:, None]
    scores = jnp.where(visible, scores, NEG)
    new_top = jnp.maximum(row_top, jnp.max(scores, -1))
    weight = jnp.where(visible, jnp.exp(scores - new_top[..., None]), 0.0)
    row_total = row_total * jnp.exp(row_top - new_top) + jnp.sum(weight, -1)
    return (new_top, row_total)


def pair_grads(q_rows, g_rows, lse_rows, delta_rows, q_pos, k_rows, v_rows, k_pos, score_scale):
    scores = (
        jnp.einsum("iagd,jad->agij", q_rows, k_rows, preferred_element_type=jnp.float32)
        * score_scale
    )
    visible = k_pos[None, :] <= q_pos[:, None]
    scores = jnp.where(visible, scores, NEG)
    weights = jnp.exp(scores - lse_rows[..., None])
    weight_grad = jnp.einsum("iagd,jad->agij", g_rows, v_rows, preferred_element_type=jnp.float32)
    dscore = (weights * (weight_grad - delta_rows[..., None])).astype(jnp.bfloat16)
    weights_low = weights.astype(jnp.bfloat16)
    dq_part = jnp.einsum("agij,jad->iagd", dscore, k_rows, preferred_element_type=jnp.float32)
    dk_part = jnp.einsum("agij,iagd->jad", dscore, q_rows, preferred_element_type=jnp.float32)
    dv_part = jnp.einsum("agij,iagd->jad", weights_low, g_rows, preferred_element_type=jnp.float32)
    return (dq_part, dk_part, dv_part)


def keep_sums(sums):
    return sums


def shards(queries, key_heads, value_heads, forward_out, output_grad, block_order):
    head_size = queries.shape[-1]
    tok_rows = queries.shape[1]
    half_rows = tok_rows // 2
    kv_groups = key_heads.shape[2]
    q_heads = queries.shape[2]
    per_group = q_heads // kv_groups
    rotation = hadamard(head_size)
    score_scale = 1.0 / math.sqrt(head_size)
    cycle_size = lax.axis_size("ctx")
    cycle_place = lax.axis_index("ctx")
    q_rot = rotate(queries[0], rotation).reshape(tok_rows, kv_groups, per_group, head_size)
    k_rot = rotate(key_heads[0], rotation)
    v_heads = value_heads[0]
    grad_out = output_grad[0].reshape(tok_rows, kv_groups, per_group, head_size)
    saved_out = forward_out[0].reshape(tok_rows, kv_groups, per_group, head_size)
    row_delta = jnp.transpose(
        jnp.sum(grad_out.astype(jnp.float32) * saved_out.astype(jnp.float32), -1), (1, 2, 0)
    )
    offsets = jnp.arange(half_rows, dtype=jnp.int32)
    q_starts = half_starts(block_order, cycle_place)
    q_pos = (q_starts[:, None] * half_rows + offsets[None, :]).reshape(tok_rows)
    top_init = jnp.full((kv_groups, per_group, tok_rows), NEG, jnp.float32)
    total_init = jnp.zeros((kv_groups, per_group, tok_rows), jnp.float32)

    def absorb_stats(running, k_block, source):
        k_starts = half_starts(block_order, source)
        for k_half in range(2):
            k_pos = k_starts[k_half] * half_rows + offsets
            k_piece = k_block[k_half * half_rows : (k_half + 1) * half_rows]

            def apply_stats(carried, k_piece=k_piece, k_pos=k_pos):
                return stat_update(carried, q_rot, q_pos, k_piece, k_pos, score_scale)

            running = lax.cond(
                k_starts[k_half] <= jnp.max(q_starts), apply_stats, keep_sums, running
            )
        return running

    row_stats = absorb_stats((top_init, total_init), k_rot, cycle_place)

    def stat_step(hop_index, loop_state):
        running, k_block = loop_state
        k_block = passed_along(k_block, "ctx", 1)
        running = absorb_stats(running, k_block, (cycle_place - hop_index) % cycle_size)
        return (running, k_block)

    row_stats, last_block = lax.fori_loop(1, cycle_size, stat_step, (row_stats, k_rot))
    row_lse = row_stats[0] + jnp.log(row_stats[1])

    def absorb_grads(dq_sum, kv_block, sum_block, first_group, source):
        k_block, v_block = kv_block
        dk_sum, dv_sum = sum_block
        width = k_block.shape[1]
        last_group = first_group + width
        k_starts = half_starts(block_order, source)
        sums = (dq_sum, dk_sum, dv_sum)
        for q_half in range(2):
            for k_half in range(2):

                def apply_pair(carried, q_half=q_half, k_half=k_half):
                    dq_acc, dk_acc, dv_acc = carried
                    q_lo = q_half * half_rows
                    k_lo = k_half * half_rows
                    k_pos = k_starts[k_half] * half_rows + offsets
                    parts = pair_grads(
                        q_rot[q_lo : q_lo + half_rows, first_group:last_group],
                        grad_out[q_lo : q_lo + half_rows, first_group:last_group],
                        row_lse[first_group:last_group, :, q_lo : q_lo + half_rows],
                        row_delta[first_group:last_group, :, q_lo : q_lo + half_rows],
                        q_pos[q_lo : q_lo + half_rows],
                        k_block[k_lo : k_lo + half_rows],
                        v_block[k_lo : k_lo + half_rows],
                        k_pos,
                        score_scale,
                    )
                    dq_acc = dq_acc.at[q_lo : q_lo + half_rows, first_group:last_group].add(
                        parts[0]
                    )
                    dk_acc = dk_acc.at[k_lo : k_lo + half_rows].add(parts[1])
                    dv_acc = dv_acc.at[k_lo : k_lo + half_rows].add(parts[2])
                    return (dq_acc, dk_acc, dv_acc)

                sums = lax.cond(k_starts[k_half] <= q_starts[q_half], apply_pair, keep_sums, sums)
        return (sums[0], (sums[1], sums[2]))

    dq_init = jnp.zeros((tok_rows, kv_groups, per_group, head_size), jnp.float32)
    acc_zero = jnp.zeros((tok_rows, kv_groups, head_size), jnp.float32)

    def cycle_step(hop_index, loop_state):
        dq_sum, kv_block, sum_block = loop_state
        dq_sum, sum_block = absorb_grads(
            dq_sum, kv_block, sum_block, 0, (cycle_place - hop_index) % cycle_size
        )
        kv_block = passed_along((kv_block[0], kv_block[1]), "ctx", 1)
        sum_block = passed_along((sum_block[0], sum_block[1]), "ctx", 1)
        return (dq_sum, kv_block, sum_block)

    dq_sum, kv_block, sum_block = lax.fori_loop(
        0, cycle_size, cycle_step, (dq_init, (k_rot, v_heads), (acc_zero, acc_zero))
    )
    dk_sum, dv_sum = sum_block
    dq_full = jnp.dot(
        (dq_sum * score_scale).reshape(-1, head_size), rotation.T, precision=lax.Precision.HIGHEST
    )
    dk_full = jnp.dot(
        (dk_sum * score_scale).reshape(-1, head_size), rotation.T, precision=lax.Precision.HIGHEST
    )
    key_grad = dk_full.reshape(1, tok_rows, kv_groups, head_size).astype(jnp.bfloat16)
    value_grad = dv_sum.reshape(1, tok_rows, kv_groups, head_size).astype(jnp.bfloat16)
    handed_local = (grad_out.astype(jnp.float32).reshape(-1, head_size) + dq_full).astype(
        jnp.bfloat16
    )
    handed_local = handed_local.reshape(1, tok_rows, q_heads, head_size)
    handed = shifted(handed_local, "pipe", -1)
    return (key_grad, value_grad, handed)


def solution(mesh):
    placed = (
        P("pipe", "ctx", "head", None),
        P("pipe", "ctx", "head", None),
        P("pipe", "ctx", "head", None),
        P("pipe", "ctx", "head", None),
        P("pipe", "ctx", "head", None),
        P(),
    )
    return jax.shard_map(
        shards,
        mesh=mesh,
        in_specs=placed,
        out_specs=(
            P("pipe", "ctx", "head", None),
            P("pipe", "ctx", "head", None),
            P("pipe", "ctx", "head", None),
        ),
        check_vma=False,
    )
```

profile of v0, /device:TPU:0, one launch (start us, length us, event | category | flops | bytes accessed | tf_op | source)
XLA Modules:
  0.0 344.3 jit_solution(6517602067687427658)
XLA Ops:
  1.3 2.0 fusion.119
  5.1 1.3 broadcast_multiply_fusion
  6.4 1.3 fusion.174
  7.7 1.4 reduce_max.58
  9.1 1.3 iota_add_fusion.3
  14.1 1.7 copy.68
  17.3 3.0 convolution_convert_fusion
  20.3 1.6 copy.70
  21.9 3.3 conditional.8
  22.1 1.5 fusion.167
  25.2 4.7 %conditional.9 = ((f32[4,8,128]{2,1,0:T(8,128)}, f32[4,8,128]{2,1,0:T(8,128)S(1)})) conditional(s32[]{:T(128)} %convert_element_type.160, (f32[4,8,128]{2,1,0:T(8,128)}, f32[4,8,128]{2,1,0:T(8,128)S(1)}) %conditional.8, (s32[]{:T(128)}, s32[64]{0:T(128)S(1)}, s32[2,64]{1,0:T(2,128)S(1)}, bf16[128,4,128]{2,0,1:T(8,128)(2,1)}, ...), branch_computations={%region_5.6_spmd, %region_6.9_spmd} | conditional | flops 68698176 | bytes 3451176 | solution.py:112
  26.0 1.6 fusion.168
  29.9 32.5 %while.58 = (s32[]{:T(128)}, f32[4,8,128]{2,1,0:T(8,128)}, f32[4,8,128]{2,1,0:T(8,128)S(1)}, bf16[128,4,128]{2,0,1:T(8,128)(2,1)S(1)}, s32[]{:T(128)}, /*index=5...) while((s32[]{:T(128)}, f32[4,8,128]{2,1,0:T(8,128)}, ...), condition=%wide.region_18.19_spmd.clone.clone, body=%wide.region_9.18_spmd.clone.clone.sunk | while | flops 137396512 | bytes 7820916 | solution.py:125
  29.9 3.0 collective-permute-start
  38.5 7.9 %collective-permute-start = (bf16[128,4,128]{2,0,1:T(8,128)(2,1)S(1)}, bf16[128,4,128]{2,0,1:T(8,128)(2,1)S(1)}, u32[]{:S(2)}, u32[]{:S(2)}) collective-permute-start(bf16[128,4,128]{2,0,1:T(8,128)(2,1)S(1)} %get-tuple-element.1673), channel_id=1, source_target_pairs={{0,2},{2,4},{4,6},{6,0},{1,3},{3,5},{5,7},{7,1},{8,10},{10,12},{12... | collective-permute-start | bytes 393224 | tf_op jit(solution)/shard_map/while/body/eval_jaxpr/ppermute | solution.py:14
  51.8 5.2 %collective-permute-start = (bf16[128,4,128]{2,0,1:T(8,128)(2,1)S(1)}, bf16[128,4,128]{2,0,1:T(8,128)(2,1)S(1)}, u32[]{:S(2)}, u32[]{:S(2)}) collective-permute-start(bf16[128,4,128]{2,0,1:T(8,128)(2,1)S(1)} %get-tuple-element.1673), channel_id=1, source_target_pairs={{0,2},{2,4},{4,6},{6,0},{1,3},{3,5},{5,7},{7,1},{8,10},{10,12},{12... | collective-permute-start | bytes 393224 | tf_op jit(solution)/shard_map/while/body/eval_jaxpr/ppermute | solution.py:14
  62.4 1.3 log_add_fusion
  64.5 1.6 broadcast_in_dim.126
  66.1 248.8 %while.59 = (s32[]{:T(128)}, f32[128,4,8,128]{3,0,2,1:T(8,128)}, bf16[128,4,128]{2,0,1:T(8,128)(2,1)}, bf16[128,4,128]{2,0,1:T(8,128)(2,1)}, f32[128,4,128]{2,0,...) while((s32[]{:T(128)}, f32[128,4,8,128]{3,0,2,1:T(8,128)}, ...), condition=%wide.region_29.30_spmd.clone.clone, body=%wide.region_20.29_spmd.clone.clone.sunk | while | flops 676086144 | bytes 50848100 | solution.py:176
  66.1 1.3 fusion.193
  75.7 1.6 copy.184
  77.8 7.4 %conditional.30 = ((f32[128,4,8,128]{3,0,2,1:T(8,128)}, f32[128,4,128]{2,0,1:T(8,128)}, f32[128,4,128]{2,0,1:T(8,128)S(1)})) conditional(s32[]{:T(128)} %bitcast.327, (f32[128,4,8,128]{3,0,2,1:T(8,128)}, f32[128,4,128]{2,0,1:T(8,128)}, f32[128,4,128]{2,0,1:T(8,128)S(1)}) %tuple.251, (f32[128,4,8,128]{3,0,2,1:T(8,128)}, s32[2]{0:T(128)}, ...), branch_computations={%region_21.21_spmd, %region_22.22_spmd} | conditional | flops 169021504 | bytes 11515012 | solution.py:161
  79.7 1.5 fusion.29
  82.4 2.7 fusion.25
  85.1 8.6 %conditional.31 = ((f32[128,4,8,128]{3,0,2,1:T(8,128)}, f32[128,4,128]{2,0,1:T(8,128)}, f32[128,4,128]{2,0,1:T(8,128)S(1)})) conditional(s32[]{:T(128)} %bitcast.326, (f32[128,4,8,128]{3,0,2,1:T(8,128)}, f32[128,4,128]{2,0,1:T(8,128)}, f32[128,4,128]{2,0,1:T(8,128)S(1)}) %get-tuple-element.1771, (f32[128,4,8,128]{3,0,2,1:T(8,128)}, s32[2]{0:T(128)}, ...), branch_computations={%region_23.23_spmd, %region_24.24_spmd} | conditional | flops 169021504 | bytes 11515020 | solution.py:161
  88.3 1.5 fusion.53
  91.1 2.7 fusion.49
  93.7 9.6 %conditional.33 = ((f32[128,4,8,128]{3,0,2,1:T(8,128)}, f32[128,4,128]{2,0,1:T(8,128)}, f32[128,4,128]{2,0,1:T(8,128)S(1)})) conditional(s32[]{:T(128)} %bitcast.324, (f32[128,4,8,128]{3,0,2,1:T(8,128)}, f32[128,4,128]{2,0,1:T(8,128)}, f32[128,4,128]{2,0,1:T(8,128)S(1)}) %get-tuple-element.1773, (f32[128,4,8,128]{3,0,2,1:T(8,128)}, s32[2]{0:T(128)}, ...), branch_computations={%region_27.27_spmd, %region_28.28_spmd} | conditional | flops 169021504 | bytes 11548300 | solution.py:161
  93.7 1.3 slice.487
  97.9 1.5 fusion.101
  100.7 2.7 fusion.97
  103.4 5.5 %collective-permute-start.3 = (f32[128,4,128]{2,0,1:T(8,128)}, f32[128,4,128]{2,0,1:T(8,128)}, u32[]{:S(2)}, u32[]{:S(2)}) collective-permute-start(f32[128,4,128]{2,0,1:T(8,128)} %get-tuple-element.1612), channel_id=1, source_target_pairs={{0,2},{2,4},{4,6},{6,0},{1,3},{3,5},{5,7},{7,1},{8,10},{10,12},{12... | collective-permute-start | bytes 786440 | tf_op jit(solution)/shard_map/while/body/eval_jaxpr/ppermute | solution.py:14
  109.6 3.2 collective-permute-start.1
  112.9 6.3 %collective-permute-done.3 = f32[128,4,128]{2,0,1:T(8,128)} collective-permute-done((f32[128,4,128]{2,0,1:T(8,128)}, f32[128,4,128]{2,0,1:T(8,128)}, u32[]{:S(2)}, u32[]{:S(2)}) %collective-permute-start.3) | collective-permute-done | bytes 262176 | tf_op jit(solution)/shard_map/while/body/eval_jaxpr/ppermute | solution.py:14
  119.2 1.7 copy.192
  120.8 3.9 %collective-permute-done.4 = f32[128,4,128]{2,0,1:T(8,128)} collective-permute-done((f32[128,4,128]{2,0,1:T(8,128)S(1)}, f32[128,4,128]{2,0,1:T(8,128)}, u32[]{:S(2)}, u32[]{:S(2)}) %collective-permute-start.4) | collective-permute-done | bytes 262176 | tf_op jit(solution)/shard_map/while/body/eval_jaxpr/ppermute | solution.py:14
  125.7 1.9 collective-permute-done.1
  127.6 2.0 collective-permute-done.2
  129.6 1.3 fusion.193
  139.2 1.6 copy.184
  141.3 32.3 %collective-permute-start.3 = (f32[128,4,128]{2,0,1:T(8,128)}, f32[128,4,128]{2,0,1:T(8,128)}, u32[]{:S(2)}, u32[]{:S(2)}) collective-permute-start(f32[128,4,128]{2,0,1:T(8,128)} %get-tuple-element.1612), channel_id=1, source_target_pairs={{0,2},{2,4},{4,6},{6,0},{1,3},{3,5},{5,7},{7,1},{8,10},{10,12},{12... | collective-permute-start | bytes 786440 | tf_op jit(solution)/shard_map/while/body/eval_jaxpr/ppermute | solution.py:14
  173.7 6.9 %collective-permute-done.3 = f32[128,4,128]{2,0,1:T(8,128)} collective-permute-done((f32[128,4,128]{2,0,1:T(8,128)}, f32[128,4,128]{2,0,1:T(8,128)}, u32[]{:S(2)}, u32[]{:S(2)}) %collective-permute-start.3) | collective-permute-done | bytes 262176 | tf_op jit(solution)/shard_map/while/body/eval_jaxpr/ppermute | solution.py:14
  180.6 1.7 copy.192
  182.3 3.8 %collective-permute-done.4 = f32[128,4,128]{2,0,1:T(8,128)} collective-permute-done((f32[128,4,128]{2,0,1:T(8,128)S(1)}, f32[128,4,128]{2,0,1:T(8,128)}, u32[]{:S(2)}, u32[]{:S(2)}) %collective-permute-start.4) | collective-permute-done | bytes 262176 | tf_op jit(solution)/shard_map/while/body/eval_jaxpr/ppermute | solution.py:14
  187.7 1.3 collective-permute-done.2
  189.0 1.3 fusion.193
  198.6 1.6 copy.184
  200.7 20.8 %collective-permute-start.3 = (f32[128,4,128]{2,0,1:T(8,128)}, f32[128,4,128]{2,0,1:T(8,128)}, u32[]{:S(2)}, u32[]{:S(2)}) collective-permute-start(f32[128,4,128]{2,0,1:T(8,128)} %get-tuple-element.1612), channel_id=1, source_target_pairs={{0,2},{2,4},{4,6},{6,0},{1,3},{3,5},{5,7},{7,1},{8,10},{10,12},{12... | collective-permute-start | bytes 786440 | tf_op jit(solution)/shard_map/while/body/eval_jaxpr/ppermute | solution.py:14
  221.6 15.9 %collective-permute-start.4 = (f32[128,4,128]{2,0,1:T(8,128)S(1)}, f32[128,4,128]{2,0,1:T(8,128)}, u32[]{:S(2)}, u32[]{:S(2)}) collective-permute-start(f32[128,4,128]{2,0,1:T(8,128)S(1)} %get-tuple-element.1613), channel_id=1, source_target_pairs={{0,2},{2,4},{4,6},{6,0},{1,3},{3,5},{5,7},{7,1},{8,10},{10,12},{12... | collective-permute-start | bytes 786440 | tf_op jit(solution)/shard_map/while/body/eval_jaxpr/ppermute | solution.py:14
  237.6 1.7 copy.192
  239.3 4.2 %collective-permute-done.4 = f32[128,4,128]{2,0,1:T(8,128)} collective-permute-done((f32[128,4,128]{2,0,1:T(8,128)S(1)}, f32[128,4,128]{2,0,1:T(8,128)}, u32[]{:S(2)}, u32[]{:S(2)}) %collective-permute-start.4) | collective-permute-done | bytes 262176 | tf_op jit(solution)/shard_map/while/body/eval_jaxpr/ppermute | solution.py:14
  245.0 1.3 collective-permute-done.2
  246.3 1.3 fusion.193
  255.9 1.6 copy.184
  258.0 21.8 %collective-permute-start.3 = (f32[128,4,128]{2,0,1:T(8,128)}, f32[128,4,128]{2,0,1:T(8,128)}, u32[]{:S(2)}, u32[]{:S(2)}) collective-permute-start(f32[128,4,128]{2,0,1:T(8,128)} %get-tuple-element.1612), channel_id=1, source_target_pairs={{0,2},{2,4},{4,6},{6,0},{1,3},{3,5},{5,7},{7,1},{8,10},{10,12},{12... | collective-permute-start | bytes 786440 | tf_op jit(solution)/shard_map/while/body/eval_jaxpr/ppermute | solution.py:14
  279.8 21.1 %collective-permute-start.1 = (bf16[128,4,128]{2,0,1:T(8,128)(2,1)}, bf16[128,4,128]{2,0,1:T(8,128)(2,1)}, u32[]{:S(2)}, u32[]{:S(2)}) collective-permute-start(bf16[128,4,128]{2,0,1:T(8,128)(2,1)} %copy.184), channel_id=1, source_target_pairs={{0,2},{2,4},{4,6},{6,0},{1,3},{3,5},{5,7},{7,1},{8,10},{10,12},{12... | collective-permute-start | bytes 393224 | tf_op jit(solution)/shard_map/while/body/eval_jaxpr/ppermute | solution.py:14
  300.9 6.4 %collective-permute-done.3 = f32[128,4,128]{2,0,1:T(8,128)} collective-permute-done((f32[128,4,128]{2,0,1:T(8,128)}, f32[128,4,128]{2,0,1:T(8,128)}, u32[]{:S(2)}, u32[]{:S(2)}) %collective-permute-start.3) | collective-permute-done | bytes 262176 | tf_op jit(solution)/shard_map/while/body/eval_jaxpr/ppermute | solution.py:14
  307.3 1.7 copy.192
  309.0 3.1 collective-permute-done.4
  313.4 1.4 collective-permute-done.2
  314.9 3.0 copy_multiply_fusion
  318.0 2.0 fusion.118
  320.0 1.3 collective-permute-start.5
  323.4 20.0 %collective-permute-done.5 = bf16[1,128,32,128]{3,2,1,0:T(8,128)(2,1)S(1)} collective-permute-done((bf16[1,128,32,128]{3,2,1,0:T(8,128)(2,1)S(1)}, bf16[1,128,32,128]{3,2,1,0:T(8,128)(2,1)S(1)}, u32[]{:S(2)}, u32[]{:S(2)}) %collective-permute-start.5) | collective-permute-done | bytes 1048608 | tf_op jit(solution)/shard_map/ppermute | solution.py:20
  (203 shorter events, 51.5 us)
Async XLA Ops:
  0.6 16.6 %copy-start = (bf16[1,128,32,128]{3,2,1,0:T(8,128)(2,1)S(1)}, bf16[1,128,32,128]{3,2,1,0:T(8,128)(2,1)}, u32[]{:S(2)}) copy-start(bf16[1,128,32,128]{3,2,1,0:T(8,128)(2,1)} %param.50) | copy-start | bytes 3145732
  0.6 15.2 %copy-start.5 = (bf16[1,128,32,128]{3,2,1,0:T(8,128)(2,1)S(1)}, bf16[1,128,32,128]{3,2,1,0:T(8,128)(2,1)}, u32[]{:S(2)}) copy-start(bf16[1,128,32,128]{3,2,1,0:T(8,128)(2,1)} %param.54) | copy-start | bytes 3145732
  0.7 16.6 %copy-start.19 = (s32[128]{0:T(128)}, s32[128]{0:T(128)S(1)}, u32[]{:S(2)}) copy-start(s32[128]{0:T(128)S(1)} %and_select_fusion.12) | copy-start | bytes 1540
  0.7 16.5 %copy-start.21 = (s32[128]{0:T(128)}, s32[128]{0:T(128)S(1)}, u32[]{:S(2)}) copy-start(s32[128]{0:T(128)S(1)} %get-tuple-element.1428) | copy-start | bytes 1540
  0.7 16.5 %copy-start.23 = (s32[128]{0:T(128)}, s32[128]{0:T(128)S(1)}, u32[]{:S(2)}) copy-start(s32[128]{0:T(128)S(1)} %get-tuple-element.1429) | copy-start | bytes 1540
  0.7 0.5 copy-start.27
  0.7 16.5 %copy-start.25 = (s32[128]{0:T(128)}, s32[128]{0:T(128)S(1)}, u32[]{:S(2)}) copy-start(s32[128]{0:T(128)S(1)} %get-tuple-element.1426) | copy-start | bytes 1540
  0.8 0.6 copy-start.29
  0.8 0.6 copy-start.31
  13.6 2.3 copy-start.7
  14.1 2.4 copy-start.17
  17.2 4.7 %copy-start.33 = (s32[64]{0:T(128)S(1)}, s32[64]{0:T(128)}, u32[]{:S(2)}) copy-start(s32[64]{0:T(128)} %iota_add_fusion.4) | copy-start | bytes 772
  17.3 4.7 %copy-start.34 = (s32[2,64]{1,0:T(2,128)S(1)}, s32[2,64]{1,0:T(2,128)}, u32[]{:S(2)}) copy-start(s32[2,64]{1,0:T(2,128)} %iota_add_fusion.3) | copy-start | bytes 1540
  29.9 8.5 %collective-permute-start = (bf16[128,4,128]{2,0,1:T(8,128)(2,1)S(1)}, bf16[128,4,128]{2,0,1:T(8,128)(2,1)S(1)}, u32[]{:S(2)}, u32[]{:S(2)}) collective-permute-start(bf16[128,4,128]{2,0,1:T(8,128)(2,1)S(1)} %get-tuple-element.1673), channel_id=1, source_target_pairs={{0,2},{2,4},{4,6},{6,0},{1,3},{3,5},{5,7},{7,1},{8,10},{10,12},{12... | collective-permute-start | bytes 393224 | tf_op jit(solution)/shard_map/while/body/eval_jaxpr/ppermute | solution.py:14
  38.5 13.1 %collective-permute-start = (bf16[128,4,128]{2,0,1:T(8,128)(2,1)S(1)}, bf16[128,4,128]{2,0,1:T(8,128)(2,1)S(1)}, u32[]{:S(2)}, u32[]{:S(2)}) collective-permute-start(bf16[128,4,128]{2,0,1:T(8,128)(2,1)S(1)} %get-tuple-element.1673), channel_id=1, source_target_pairs={{0,2},{2,4},{4,6},{6,0},{1,3},{3,5},{5,7},{7,1},{8,10},{10,12},{12... | collective-permute-start | bytes 393224 | tf_op jit(solution)/shard_map/while/body/eval_jaxpr/ppermute | solution.py:14
  51.8 10.5 %collective-permute-start = (bf16[128,4,128]{2,0,1:T(8,128)(2,1)S(1)}, bf16[128,4,128]{2,0,1:T(8,128)(2,1)S(1)}, u32[]{:S(2)}, u32[]{:S(2)}) collective-permute-start(bf16[128,4,128]{2,0,1:T(8,128)(2,1)S(1)} %get-tuple-element.1673), channel_id=1, source_target_pairs={{0,2},{2,4},{4,6},{6,0},{1,3},{3,5},{5,7},{7,1},{8,10},{10,12},{12... | collective-permute-start | bytes 393224 | tf_op jit(solution)/shard_map/while/body/eval_jaxpr/ppermute | solution.py:14
  68.1 6.7 %copy-start.18 = (s32[2]{0:T(128)}, s32[2]{0:T(128)S(1)}, u32[]{:S(2)}) copy-start(s32[2]{0:T(128)S(1)} %dynamic_slice.33) | copy-start | bytes 28 | tf_op jit(solution)/shard_map/while
  81.2 1.0 copy-start.8
  81.5 0.9 copy-start.1
  82.4 2.7 copy-start.9
  89.8 1.0 copy-start.10
  90.1 0.9 copy-start.2
  91.1 2.7 copy-start.11
  99.4 1.0 copy-start.14
  99.7 0.9 copy-start.4
  100.7 2.7 copy-start.15
  103.4 15.8 %collective-permute-start.3 = (f32[128,4,128]{2,0,1:T(8,128)}, f32[128,4,128]{2,0,1:T(8,128)}, u32[]{:S(2)}, u32[]{:S(2)}) collective-permute-start(f32[128,4,128]{2,0,1:T(8,128)} %get-tuple-element.1612), channel_id=1, source_target_pairs={{0,2},{2,4},{4,6},{6,0},{1,3},{3,5},{5,7},{7,1},{8,10},{10,12},{12... | collective-permute-start | bytes 786440 | tf_op jit(solution)/shard_map/while/body/eval_jaxpr/ppermute | solution.py:14
  108.9 15.9 %collective-permute-start.4 = (f32[128,4,128]{2,0,1:T(8,128)S(1)}, f32[128,4,128]{2,0,1:T(8,128)}, u32[]{:S(2)}, u32[]{:S(2)}) collective-permute-start(f32[128,4,128]{2,0,1:T(8,128)S(1)} %get-tuple-element.1613), channel_id=1, source_target_pairs={{0,2},{2,4},{4,6},{6,0},{1,3},{3,5},{5,7},{7,1},{8,10},{10,12},{12... | collective-permute-start | bytes 786440 | tf_op jit(solution)/shard_map/while/body/eval_jaxpr/ppermute | solution.py:14
  109.6 18.0 %collective-permute-start.1 = (bf16[128,4,128]{2,0,1:T(8,128)(2,1)}, bf16[128,4,128]{2,0,1:T(8,128)(2,1)}, u32[]{:S(2)}, u32[]{:S(2)}) collective-permute-start(bf16[128,4,128]{2,0,1:T(8,128)(2,1)} %copy.184), channel_id=1, source_target_pairs={{0,2},{2,4},{4,6},{6,0},{1,3},{3,5},{5,7},{7,1},{8,10},{10,12},{12... | collective-permute-start | bytes 393224 | tf_op jit(solution)/shard_map/while/body/eval_jaxpr/ppermute | solution.py:14
  112.8 16.7 %collective-permute-start.2 = (bf16[128,4,128]{2,0,1:T(8,128)(2,1)S(1)}, bf16[128,4,128]{2,0,1:T(8,128)(2,1)}, u32[]{:S(2)}, u32[]{:S(2)}) collective-permute-start(bf16[128,4,128]{2,0,1:T(8,128)(2,1)S(1)} %copy.185), channel_id=1, source_target_pairs={{0,2},{2,4},{4,6},{6,0},{1,3},{3,5},{5,7},{7,1},{8,10},{10,12},{12... | collective-permute-start | bytes 393224 | tf_op jit(solution)/shard_map/while/body/eval_jaxpr/ppermute | solution.py:14
  131.6 6.7 %copy-start.18 = (s32[2]{0:T(128)}, s32[2]{0:T(128)S(1)}, u32[]{:S(2)}) copy-start(s32[2]{0:T(128)S(1)} %dynamic_slice.33) | copy-start | bytes 28 | tf_op jit(solution)/shard_map/while
  141.3 39.3 %collective-permute-start.3 = (f32[128,4,128]{2,0,1:T(8,128)}, f32[128,4,128]{2,0,1:T(8,128)}, u32[]{:S(2)}, u32[]{:S(2)}) collective-permute-start(f32[128,4,128]{2,0,1:T(8,128)} %get-tuple-element.1612), channel_id=1, source_target_pairs={{0,2},{2,4},{4,6},{6,0},{1,3},{3,5},{5,7},{7,1},{8,10},{10,12},{12... | collective-permute-start | bytes 786440 | tf_op jit(solution)/shard_map/while/body/eval_jaxpr/ppermute | solution.py:14
  173.5 12.6 %collective-permute-start.4 = (f32[128,4,128]{2,0,1:T(8,128)S(1)}, f32[128,4,128]{2,0,1:T(8,128)}, u32[]{:S(2)}, u32[]{:S(2)}) collective-permute-start(f32[128,4,128]{2,0,1:T(8,128)S(1)} %get-tuple-element.1613), channel_id=1, source_target_pairs={{0,2},{2,4},{4,6},{6,0},{1,3},{3,5},{5,7},{7,1},{8,10},{10,12},{12... | collective-permute-start | bytes 786440 | tf_op jit(solution)/shard_map/while/body/eval_jaxpr/ppermute | solution.py:14
  173.6 14.2 %collective-permute-start.1 = (bf16[128,4,128]{2,0,1:T(8,128)(2,1)}, bf16[128,4,128]{2,0,1:T(8,128)(2,1)}, u32[]{:S(2)}, u32[]{:S(2)}) collective-permute-start(bf16[128,4,128]{2,0,1:T(8,128)(2,1)} %copy.184), channel_id=1, source_target_pairs={{0,2},{2,4},{4,6},{6,0},{1,3},{3,5},{5,7},{7,1},{8,10},{10,12},{12... | collective-permute-start | bytes 393224 | tf_op jit(solution)/shard_map/while/body/eval_jaxpr/ppermute | solution.py:14
  173.6 15.5 %collective-permute-start.2 = (bf16[128,4,128]{2,0,1:T(8,128)(2,1)S(1)}, bf16[128,4,128]{2,0,1:T(8,128)(2,1)}, u32[]{:S(2)}, u32[]{:S(2)}) collective-permute-start(bf16[128,4,128]{2,0,1:T(8,128)(2,1)S(1)} %copy.185), channel_id=1, source_target_pairs={{0,2},{2,4},{4,6},{6,0},{1,3},{3,5},{5,7},{7,1},{8,10},{10,12},{12... | collective-permute-start | bytes 393224 | tf_op jit(solution)/shard_map/while/body/eval_jaxpr/ppermute | solution.py:14
  191.1 6.7 %copy-start.18 = (s32[2]{0:T(128)}, s32[2]{0:T(128)S(1)}, u32[]{:S(2)}) copy-start(s32[2]{0:T(128)S(1)} %dynamic_slice.33) | copy-start | bytes 28 | tf_op jit(solution)/shard_map/while
  200.7 36.9 %collective-permute-start.3 = (f32[128,4,128]{2,0,1:T(8,128)}, f32[128,4,128]{2,0,1:T(8,128)}, u32[]{:S(2)}, u32[]{:S(2)}) collective-permute-start(f32[128,4,128]{2,0,1:T(8,128)} %get-tuple-element.1612), channel_id=1, source_target_pairs={{0,2},{2,4},{4,6},{6,0},{1,3},{3,5},{5,7},{7,1},{8,10},{10,12},{12... | collective-permute-start | bytes 786440 | tf_op jit(solution)/shard_map/while/body/eval_jaxpr/ppermute | solution.py:14
  221.6 21.9 %collective-permute-start.4 = (f32[128,4,128]{2,0,1:T(8,128)S(1)}, f32[128,4,128]{2,0,1:T(8,128)}, u32[]{:S(2)}, u32[]{:S(2)}) collective-permute-start(f32[128,4,128]{2,0,1:T(8,128)S(1)} %get-tuple-element.1613), channel_id=1, source_target_pairs={{0,2},{2,4},{4,6},{6,0},{1,3},{3,5},{5,7},{7,1},{8,10},{10,12},{12... | collective-permute-start | bytes 786440 | tf_op jit(solution)/shard_map/while/body/eval_jaxpr/ppermute | solution.py:14
  237.5 7.5 %collective-permute-start.1 = (bf16[128,4,128]{2,0,1:T(8,128)(2,1)}, bf16[128,4,128]{2,0,1:T(8,128)(2,1)}, u32[]{:S(2)}, u32[]{:S(2)}) collective-permute-start(bf16[128,4,128]{2,0,1:T(8,128)(2,1)} %copy.184), channel_id=1, source_target_pairs={{0,2},{2,4},{4,6},{6,0},{1,3},{3,5},{5,7},{7,1},{8,10},{10,12},{12... | collective-permute-start | bytes 393224 | tf_op jit(solution)/shard_map/while/body/eval_jaxpr/ppermute | solution.py:14
  237.6 8.7 %collective-permute-start.2 = (bf16[128,4,128]{2,0,1:T(8,128)(2,1)S(1)}, bf16[128,4,128]{2,0,1:T(8,128)(2,1)}, u32[]{:S(2)}, u32[]{:S(2)}) collective-permute-start(bf16[128,4,128]{2,0,1:T(8,128)(2,1)S(1)} %copy.185), channel_id=1, source_target_pairs={{0,2},{2,4},{4,6},{6,0},{1,3},{3,5},{5,7},{7,1},{8,10},{10,12},{12... | collective-permute-start | bytes 393224 | tf_op jit(solution)/shard_map/while/body/eval_jaxpr/ppermute | solution.py:14
  248.3 6.7 %copy-start.18 = (s32[2]{0:T(128)}, s32[2]{0:T(128)S(1)}, u32[]{:S(2)}) copy-start(s32[2]{0:T(128)S(1)} %dynamic_slice.33) | copy-start | bytes 28 | tf_op jit(solution)/shard_map/while
  258.0 49.3 %collective-permute-start.3 = (f32[128,4,128]{2,0,1:T(8,128)}, f32[128,4,128]{2,0,1:T(8,128)}, u32[]{:S(2)}, u32[]{:S(2)}) collective-permute-start(f32[128,4,128]{2,0,1:T(8,128)} %get-tuple-element.1612), channel_id=1, source_target_pairs={{0,2},{2,4},{4,6},{6,0},{1,3},{3,5},{5,7},{7,1},{8,10},{10,12},{12... | collective-permute-start | bytes 786440 | tf_op jit(solution)/shard_map/while/body/eval_jaxpr/ppermute | solution.py:14
  279.8 32.3 %collective-permute-start.4 = (f32[128,4,128]{2,0,1:T(8,128)S(1)}, f32[128,4,128]{2,0,1:T(8,128)}, u32[]{:S(2)}, u32[]{:S(2)}) collective-permute-start(f32[128,4,128]{2,0,1:T(8,128)S(1)} %get-tuple-element.1613), channel_id=1, source_target_pairs={{0,2},{2,4},{4,6},{6,0},{1,3},{3,5},{5,7},{7,1},{8,10},{10,12},{12... | collective-permute-start | bytes 786440 | tf_op jit(solution)/shard_map/while/body/eval_jaxpr/ppermute | solution.py:14
  279.8 33.6 %collective-permute-start.1 = (bf16[128,4,128]{2,0,1:T(8,128)(2,1)}, bf16[128,4,128]{2,0,1:T(8,128)(2,1)}, u32[]{:S(2)}, u32[]{:S(2)}) collective-permute-start(bf16[128,4,128]{2,0,1:T(8,128)(2,1)} %copy.184), channel_id=1, source_target_pairs={{0,2},{2,4},{4,6},{6,0},{1,3},{3,5},{5,7},{7,1},{8,10},{10,12},{12... | collective-permute-start | bytes 393224 | tf_op jit(solution)/shard_map/while/body/eval_jaxpr/ppermute | solution.py:14
  300.9 14.0 %collective-permute-start.2 = (bf16[128,4,128]{2,0,1:T(8,128)(2,1)S(1)}, bf16[128,4,128]{2,0,1:T(8,128)(2,1)}, u32[]{:S(2)}, u32[]{:S(2)}) collective-permute-start(bf16[128,4,128]{2,0,1:T(8,128)(2,1)S(1)} %copy.185), channel_id=1, source_target_pairs={{0,2},{2,4},{4,6},{6,0},{1,3},{3,5},{5,7},{7,1},{8,10},{10,12},{12... | collective-permute-start | bytes 393224 | tf_op jit(solution)/shard_map/while/body/eval_jaxpr/ppermute | solution.py:14
  314.8 3.1 copy-start.6
  314.8 3.1 copy-start.20
  314.8 3.1 copy-start.22
  314.8 3.1 copy-start.24
  314.8 3.1 copy-start.26
  314.9 3.1 copy-start.28
  314.9 3.1 copy-start.30
  314.9 3.1 copy-start.32
  318.0 4.1 %copy-start.16 = (f32[128,4,128]{2,0,1:T(8,128)S(1)}, f32[128,4,128]{2,0,1:T(8,128)}, u32[]{:S(2)}) copy-start(f32[128,4,128]{2,0,1:T(8,128)} %get-tuple-element.1063) | copy-start | bytes 786436
  320.0 23.4 %collective-permute-start.5 = (bf16[1,128,32,128]{3,2,1,0:T(8,128)(2,1)S(1)}, bf16[1,128,32,128]{3,2,1,0:T(8,128)(2,1)S(1)}, u32[]{:S(2)}, u32[]{:S(2)}) collective-permute-start(bf16[1,128,32,128]{3,2,1,0:T(8,128)(2,1)S(1)} %bitcast.340), channel_id=1, source_target_pairs={{8,0},{16,8},{24,16},{9,1},{17,9},{25,17},{10,2},{18,10},{26,18},{... | collective-permute-start | bytes 3145736 | tf_op jit(solution)/shard_map/ppermute | solution.py:20
where the time goes:
time: 338 us; the launch traced here: 344 us
  starting transfers between devices  139 us (41%)
  waiting for transfers between devices  64.5 us (19%)
  local copies, waits for them, and re-layouts  56.8 us (17%)
  loops' own time  31.6 us (9%)
  matrix products  26.7 us (8%)
  other arithmetic  21.4 us (6%)
  between operations  4.17 us (1%)
    ppermute x19, starting transfers between devices, passed_along(): return lax.ppermute(value, axis, pairs)  138 us
    ppermute x19, waiting for transfers between devices, passed_along(): return lax.ppermute(value, axis, pairs)  44.5 us
    while x27, local copies, waits for them, and re-layouts  20.4 us
    ppermute x1, waiting for transfers between devices, shifted(): lax.ppermute(value, axis, [(source, source + steps) for source in range(f...  20 us
    another operation x1, loops' own time, shards(): lax.fori_loop(0, cycle_size, cycle_step, (dq_init, (k_rot, v_heads), (acc...  19.1 us
    another operation x1, loops' own time, shards(): lax.fori_loop(1, cycle_size, stat_step, (row_stats, k_rot))  9.67 us
    dot_general x3, matrix products, pair_grads(): jnp.einsum('agij,jad->iagd', dscore, k_rows, preferred_element_type=jnp.f...  8.03 us
    unnamed x51, local copies, waits for them, and re-layouts  8.02 us
  transfers between devices with their start and end apart: 20, of which 18 were waited for; matrix products, arithmetic and copies ran while one was open for 5% of the time, Pallas kernels for 0%

commit v1 on v0

v1 whole, which is shorter than its diff:
```python
import functools
import math

import jax
import jax.numpy as jnp
from jax import lax
from jax.experimental import pallas as pl
from jax.experimental.pallas import tpu as pltpu
from jax.sharding import PartitionSpec as P

NEG = -1e30
STAGES = 2
WORK = 2**20
DQ_WORK = 2**32
F32 = jnp.float32
BF16 = jnp.bfloat16


def signs(size):
    row = lax.broadcasted_iota(jnp.int32, (size, size), 0)
    col = lax.broadcasted_iota(jnp.int32, (size, size), 1)
    bits = row & col
    for step in (4, 2, 1):
        bits = bits ^ (bits >> step)
    return (1 - 2 * (bits & 1)).astype(F32).astype(BF16)


def dot(a, b, contract):
    return lax.dot_general(a, b, (contract, ((), ())), preferred_element_type=F32)


def nn(a, b):
    return dot(a, b, ((1,), (0,)))


def nt(a, b):
    return dot(a, b, ((1,), (1,)))


def split(x):
    high = x.astype(BF16)
    return high, (x - high.astype(F32)).astype(BF16)


def prep_kernel(groups, per_stage, k_hbm, v_hbm, *rest):
    outs, (rows_ref, k_ref, v_ref, sems) = rest[:-4], rest[-4:]
    copies = [
        pltpu.make_async_copy(source, target, sems.at[at])
        for at, (source, target) in enumerate(((k_hbm, k_ref), (v_hbm, v_ref)))
    ]
    for copy in copies:
        copy.start()
    tokens = k_ref.shape[0] // groups
    size = k_ref.shape[1]
    sign = signs(size)
    for part, copy in enumerate(copies):
        copy.wait()
        if part == 0:
            rows = nn(k_ref[...], sign) * (1.0 / math.sqrt(size))
        else:
            rows = v_ref[...].astype(F32)
        rows_ref[...] = rows
        for group in range(groups):
            picked = rows_ref[pl.ds(group, tokens, stride=groups), :].astype(BF16)
            outs[group // per_stage][part, group % per_stage] = picked


def finish_kernel(groups, per_stage, terms, *refs):
    count = groups // per_stage * terms
    parts, outs, rows_ref = refs[:count], refs[count:-1], refs[-1]
    tokens = parts[0].shape[2]
    for part in range(2):
        for group in range(groups):
            first = group // per_stage * terms
            rows = [ref[part, group % per_stage].astype(F32) for ref in parts[first : first + terms]]
            rows_ref[pl.ds(group, tokens, stride=groups), :] = sum(rows[1:], rows[0])
        outs[part][...] = rows_ref[...].astype(BF16)


def ring_order(count):
    return [0] + [at for at in range(count) if at % 2] + [at for at in range(count - 1, 0, -1) if at % 2 == 0]


def ring_place(count, place):
    odd = place & 1
    half = place >> 1
    return lax.rem(odd * (half + 1) + (1 - odd) * (count - half), count)


def ring_device(count, ring):
    return jnp.where(ring <= count // 2, jnp.maximum(2 * ring - 1, 0), 2 * (count - ring))


def passed(value, axis, step):
    count = lax.axis_size(axis)
    order = ring_order(count)
    return lax.ppermute(
        value, axis, [(order[at], order[(at + step) % count]) for at in range(count)]
    )


def later_pass(block, up, down, axis):
    count = lax.axis_size(axis)
    blocks = {0: block, 1: up, count - 1: down}
    for step in range(2, count // 2 + 1):
        up = blocks[step] = passed(up, axis, 1)
        if 2 * step < count:
            down = blocks[count - step] = passed(down, axis, -1)
    return [blocks[step] for step in range(count)]


def added(a, b):
    return (a.astype(F32) + b.astype(F32)).astype(BF16)


def scatter_sums(parts, axis):
    count = lax.axis_size(axis)
    terms = [parts[0]]
    for step, longest in ((1, count // 2), (-1, (count - 1) // 2)):
        moving = None
        for distance in range(longest, 0, -1):
            part = parts[(-step * distance) % count]
            moving = passed(part if moving is None else added(moving, part), axis, step)
        terms.append(moving)
    return terms


def sides_kernel(stage, groups, q_hbm, g_hbm, o_hbm, q_side_ref, g_side_ref, in_ref, sems):
    _, _, half_rows, heads, size = in_ref.shape
    per_group = heads // groups
    copies = []
    for half in range(2):
        for part, source in enumerate((q_hbm, g_hbm, o_hbm)):
            piece = source.at[pl.ds(half * half_rows, half_rows), pl.ds(stage * heads, heads)]
            copies.append(
                pltpu.make_async_copy(piece, in_ref.at[half, part], sems.at[half * 3 + part])
            )
            copies[-1].start()
    rows = half_rows * per_group
    sign = signs(size)
    root = 1.0 / math.sqrt(size)
    row_offset = lax.broadcasted_iota(jnp.int32, (rows, size), 0) // per_group
    lane = lax.broadcasted_iota(jnp.int32, (rows, size), 1)
    hide = jnp.where(row_offset == lane, NEG, 0.0).astype(BF16)
    for half in range(2):
        for copy in copies[3 * half : 3 * half + 3]:
            copy.wait()
        q_all = nn(in_ref[half, 0].reshape(half_rows * heads, size), sign) * root
        q_all = q_all.reshape(half_rows, groups, per_group, size)
        g_all = in_ref[half, 1].astype(F32).reshape(half_rows, groups, per_group, size)
        o_all = in_ref[half, 2].astype(F32).reshape(half_rows, groups, per_group, size)
        for group in range(groups):
            grad = g_all[:, group].reshape(rows, size)
            product = grad * o_all[:, group].reshape(rows, size)
            product = -(product + pltpu.roll(product, size // 2, 1))
            high = product.astype(BF16).astype(F32)
            delta = jnp.where(lane < size // 2, high, product - high)
            q_side_ref[half, group, :, :size] = q_all[:, group].reshape(rows, size).astype(BF16)
            q_side_ref[half, group, :, size:] = hide
            g_side_ref[half, group, :, :size] = grad.astype(BF16)
            g_side_ref[half, group, :, size:] = delta.astype(BF16)


def chunked(keys, chunk, body, init):
    if keys == chunk:
        return body(0, init)
    return lax.fori_loop(0, keys // chunk, body, init)


def dq_kernel(blocks, order_ref, q_side_ref, g_side_ref, *refs):
    kv_refs, (handed_ref, probs_ref, dscore_ref) = refs[:blocks], refs[blocks : blocks + 3]
    score_ref, key_ref, val_ref, back_ref = refs[blocks + 3 :]
    _, groups, tokens, size = kv_refs[0].shape
    place = lax.axis_index("ctx")
    ring = ring_place(blocks, place)
    rows = q_side_ref.shape[2]
    half_rows = tokens // 2
    per_group = rows // half_rows
    keys = blocks * tokens
    chunk = 512
    root = 1.0 / math.sqrt(size)
    power = root * math.log2(math.e)
    sign = signs(size)

    def span(index):
        return pl.ds(pl.multiple_of(index * chunk, chunk), chunk)

    at_row = lax.broadcasted_iota(jnp.int32, (half_rows, size), 0)
    at_col = lax.broadcasted_iota(jnp.int32, (half_rows, size), 1)
    for block in range(blocks):
        source = ring_device(blocks, lax.rem(ring - block + blocks, blocks))
        at = pl.ds(block * tokens, tokens)
        for half in range(2):
            q_start = order_ref[place * 2 + half]
            for k_half in range(2):
                ahead = (order_ref[source * 2 + k_half] - q_start) * half_rows
                hidden = (at_row + ahead > at_col) & (at_col < half_rows)
                hidden = jnp.where(hidden, 1.0, 0.0).astype(BF16)
                k_at = pl.ds(block * tokens + k_half * half_rows, half_rows)
                for group in range(groups):
                    key_ref[half, group, k_at, size:] = hidden
        for group in range(groups):
            key = kv_refs[block][0, group]
            for half in range(2):
                key_ref[half, group, at, :size] = key
            val_ref[group, at, :size] = kv_refs[block][1, group]
            val_ref[group, at, size:] = jnp.ones((tokens, size), BF16)
            high, low = split(nt(sign, key) * (root * root))
            back_ref[group, :size, at] = high
            back_ref[group, size:, at] = low

    for half in range(2):
        results = []
        for group in range(groups):
            slot = group % 2
            q_side = q_side_ref.at[half, group]
            g_side = g_side_ref.at[half, group]
            row_at = pl.ds(half * rows, rows)

            def scores(index, top, half=half, group=group, slot=slot, q_side=q_side):
                part = nt(key_ref[half, group, span(index), :], q_side[...])
                score_ref[slot, span(index), :] = part
                return jnp.maximum(top, jnp.max(part.reshape(chunk // 8, 8, rows), axis=0))

            top = chunked(keys, chunk, scores, jnp.full((8, rows), NEG, F32))
            top = jnp.max(top, axis=0, keepdims=True)

            def weigh(index, total, slot=slot, top=top):
                part = jnp.exp2((score_ref[slot, span(index), :] - top) * power)
                score_ref[slot, span(index), :] = part
                return total + jnp.sum(part.reshape(chunk // 8, 8, rows), axis=0)

            total = chunked(keys, chunk, weigh, jnp.zeros((8, rows), F32))
            scale = 1.0 / jnp.sum(total, axis=0, keepdims=True)

            def grads(index, dq, group=group, slot=slot, scale=scale, g_side=g_side, row_at=row_at):
                probs = score_ref[slot, span(index), :] * scale
                change = nt(val_ref[group, span(index), :], g_side[...])
                dscore = (probs * change).astype(BF16)
                probs_ref[group, span(index), row_at] = probs.astype(BF16)
                dscore_ref[group, span(index), row_at] = dscore
                return dq + nn(back_ref[group, :, span(index)], dscore)

            dq = chunked(keys, chunk, grads, jnp.zeros((2 * size, rows), F32))
            dq = (dq[:size] + dq[size:]).T + g_side[:, :size].astype(F32)
            results.append(dq.reshape(half_rows, per_group, size))
        at = pl.ds(half * half_rows, half_rows)
        handed_ref[at] = jnp.concatenate(results, axis=1).astype(BF16)


def dkv_kernel(q_side_ref, g_side_ref, probs_ref, dscore_ref, *sum_refs):
    blocks = len(sum_refs)
    _, groups, tokens, size = sum_refs[0].shape
    rows = q_side_ref.shape[2]
    scale = 1.0 / size
    sign = signs(size)
    chunk = 512
    for first in range(0, blocks * tokens, chunk):
        for group in range(groups):
            at = pl.ds(first, chunk)
            dk = dv = None
            for half in range(2):
                row_at = pl.ds(half * rows, rows)
                dk_part = nn(dscore_ref[group, at, row_at], q_side_ref[half, group, :, :size])
                dv_part = nn(probs_ref[group, at, row_at], g_side_ref[half, group, :, :size])
                dk = dk_part if dk is None else dk + dk_part
                dv = dv_part if dv is None else dv + dv_part
            high, low = split(dk)
            dk = ((nn(high, sign) + nn(low, sign)) * scale).astype(BF16)
            dv = dv.astype(BF16)
            for row in range(0, chunk, tokens):
                out = sum_refs[(first + row) // tokens]
                out[0, group] = dk[row : row + tokens]
                out[1, group] = dv[row : row + tokens]


VMEM = pl.BlockSpec(memory_space=pltpu.VMEM)
HBM = pl.BlockSpec(memory_space=pltpu.HBM)
DMA = pltpu.SemaphoreType.DMA
SMEM = pl.BlockSpec(memory_space=pltpu.SMEM)


def call(kernel, name, outs, scratch, limit, work, args, smem=False):
    shapes = [jax.ShapeDtypeStruct(*out) for out in outs]
    return pl.pallas_call(
        kernel,
        in_specs=([SMEM] if smem else []) + [VMEM] * (len(args) - smem),
        out_specs=[VMEM] * len(outs),
        out_shape=shapes,
        scratch_shapes=scratch,
        compiler_params=pltpu.CompilerParams(vmem_limit_bytes=limit * 2**20),
        cost_estimate=pl.CostEstimate(flops=work, bytes_accessed=2**16, transcendentals=0),
        name=name,
    )(*args)


def in_hbm(value):
    return pltpu.with_memory_space_constraint(value, pltpu.HBM)


def make_sides(stage, stages, groups, queries, grads, saved):
    tokens, heads, size = queries.shape
    half_rows, heads = tokens // 2, heads // stages
    rows = half_rows * heads // groups
    shape = jax.ShapeDtypeStruct((2, groups, rows, 2 * size), BF16)
    return pl.pallas_call(
        functools.partial(sides_kernel, stage, groups),
        in_specs=[HBM] * 3,
        out_specs=[VMEM] * 2,
        out_shape=[shape] * 2,
        scratch_shapes=[pltpu.VMEM((2, 3, half_rows, heads, size), BF16), DMA((6,))],
        compiler_params=pltpu.CompilerParams(vmem_limit_bytes=16 * 2**20),
        cost_estimate=pl.CostEstimate(flops=WORK, bytes_accessed=2**16, transcendentals=0),
        name="query_sides",
    )(in_hbm(queries), in_hbm(grads), in_hbm(saved))


def shards(queries, key_heads, value_heads, forward_out, output_grad, block_order):
    _, tokens, groups, size = key_heads.shape
    q_heads = queries.shape[2]
    per_group = q_heads // groups
    per_stage = groups // STAGES
    pipe = lax.axis_size("pipe")
    blocks = lax.axis_size("ctx")
    keys = blocks * tokens
    rows = tokens // 2 * per_group
    packed = ((2, per_stage, tokens, size), BF16)
    flat = ((tokens * groups, size), BF16)
    rows_scratch = pltpu.VMEM(*flat[:1], F32)
    kv_parts = pl.pallas_call(
        functools.partial(prep_kernel, groups, per_stage),
        in_specs=[HBM] * 2,
        out_specs=[VMEM] * STAGES,
        out_shape=[jax.ShapeDtypeStruct(*packed)] * STAGES,
        scratch_shapes=[rows_scratch, pltpu.VMEM(*flat), pltpu.VMEM(*flat), DMA((2,))],
        compiler_params=pltpu.CompilerParams(vmem_limit_bytes=8 * 2**20),
        cost_estimate=pl.CostEstimate(flops=WORK, bytes_accessed=2**16, transcendentals=0),
        name="pack_keys",
    )(in_hbm(key_heads.reshape(-1, size)), in_hbm(value_heads.reshape(-1, size)))
    limit = 12 + keys // 64
    def sides_of(stage, grads):
        return make_sides(stage, STAGES, per_stage, queries[0], grads, forward_out[0])

    def key_sums(probs, dscore, sides):
        return call(
            dkv_kernel, "key_grads", [packed] * blocks, [], limit, WORK, [*sides, probs, dscore]
        )

    handed, sums = [], []
    block = kv_parts[0]
    up, down = passed(block, "ctx", 1), passed(block, "ctx", -1)
    sides = sides_of(0, output_grad[0])
    for stage in range(STAGES):
        if stage == 0:
            up, sides = lax.optimization_barrier((up, sides))
        else:
            up, down, _ = lax.optimization_barrier((up, down, handed_part))
            grads, probs, _ = lax.optimization_barrier((output_grad[0], probs, up))
            parts = key_sums(probs, dscore, sides)
            sides = sides_of(stage, grads)
        gathered = later_pass(block, up, down, "ctx")
        if stage > 0:
            parts, gathered = lax.optimization_barrier((parts, gathered))
            sums.append(scatter_sums(parts, "ctx"))
        if stage + 1 < STAGES:
            block, _ = lax.optimization_barrier((kv_parts[stage + 1], down))
            up, down = passed(block, "ctx", 1), passed(block, "ctx", -1)
        handed_part, probs, dscore = call(
            functools.partial(dq_kernel, blocks),
            "query_grads",
            [((tokens, per_stage * per_group, size), BF16)]
            + [((per_stage, keys, 2 * rows), BF16)] * 2,
            [
                pltpu.VMEM((2, keys, rows), F32),
                pltpu.VMEM((2, per_stage, keys, 2 * size), BF16),
                pltpu.VMEM((per_stage, keys, 2 * size), BF16),
                pltpu.VMEM((per_stage, 2 * size, keys), BF16),
            ],
            limit,
            DQ_WORK,
            [block_order, *sides, *gathered],
            True,
        )
        handed.append(
            lax.ppermute(handed_part, "pipe", [(place, place - 1) for place in range(1, pipe)])
        )
        if stage > 0:
            probs, _ = lax.optimization_barrier((probs, handed[stage - 1]))
    parts = key_sums(probs, dscore, sides)
    sums.append(scatter_sums(parts, "ctx"))
    key_grad, value_grad = call(
        functools.partial(finish_kernel, groups, per_stage, len(sums[0])),
        "lay_out",
        [flat, flat],
        [rows_scratch],
        8,
        WORK,
        [term for terms in sums for term in terms],
    )
    shape = key_heads.shape
    return (
        key_grad.reshape(shape),
        value_grad.reshape(shape),
        jnp.concatenate(handed, axis=1)[None],
    )


def solution(mesh):
    placed = P("pipe", "ctx", "head", None)
    return jax.shard_map(
        shards,
        mesh=mesh,
        in_specs=(placed,) * 5 + (P(),),
        out_specs=(placed,) * 3,
        check_vma=False,
    )
```

time: 338 us -> 56.8 us (0.17); the launches traced: 344 us -> 56.4 us
  starting transfers between devices: 139 us -> 27.5 us
  local copies, waits for them, and re-layouts: 56.8 us -> 0.01 us
  waiting for transfers between devices: 64.5 us -> 10.5 us
  loops' own time: 31.6 us -> 0 us
  matrix products: 26.7 us -> 0 us
  other arithmetic: 21.4 us -> 1.13 us
  Pallas kernels: 0 us -> 16.6 us
  between operations: 4.17 us -> 0.76 us
    ppermute x20 -> x14, starting transfers between devices: 139 us -> 27.5 us  [the longest x12 25 us: passed(): lax.ppermute(value, axis, [(order[at], order[(at + step) % count]) for at...]
    ppermute x20 -> x14, waiting for transfers between devices: 64.5 us -> 10.5 us  [the longest x12 10.3 us: passed(): lax.ppermute(value, axis, [(order[at], order[(at + step) % count]) for at...]
    another operation x26 -> x0, loops' own time: 31.6 us -> none  [the longest x1 19.1 us: shards(): lax.fori_loop(0, cycle_size, cycle_step, (dq_init, (k_rot, v_heads), (acc...]
    dot_general x21 -> x0, matrix products: 26.7 us -> none  [the longest x3 8.03 us: pair_grads(): jnp.einsum('agij,jad->iagd', dscore, k_rows, preferred_element_type=jnp.f...]
    while x27 -> x0, local copies, waits for them, and re-layouts: 20.4 us -> none
    pallas_call x0 -> x8, Pallas kernels: none -> 16.6 us  [the longest x5 11.9 us: call(): pl.pallas_call(kernel, in_specs=([SMEM] if smem else []) + [VMEM] * (len(...]
    slice x21 -> x0, local copies, waits for them, and re-layouts: 15.6 us -> none  [the longest x4 5.21 us: absorb_grads(): q_starts[q_half]]
    add x19 -> x0, other arithmetic: 11 us -> none  [the longest x8 6.45 us: shards(): q_pos = (q_starts[:, None] * half_rows + offsets[None, :]).reshape(tok_rows)]
  transfers between devices with their start and end apart: 20 -> 14, of which waited for: 18 -> 8; matrix products, arithmetic and copies ran while one was open for 5% -> 2% of each run, Pallas kernels for 0% -> 26%
where the time goes in v1:
time: 56.8 us; the launch traced here: 56.4 us
  starting transfers between devices  27.5 us (48%)
  Pallas kernels  16.6 us (29%)
  waiting for transfers between devices  10.5 us (18%)
  other arithmetic  1.13 us (2%)
  between operations  0.76 us (1%)
    ppermute x12, starting transfers between devices, passed(): lax.ppermute(value, axis, [(order[at], order[(at + step) % count]) for at...  25 us
    pallas_call x5, Pallas kernels, call(): pl.pallas_call(kernel, in_specs=([SMEM] if smem else []) + [VMEM] * (len(...  11.9 us
    ppermute x12, waiting for transfers between devices, passed(): lax.ppermute(value, axis, [(order[at], order[(at + step) % count]) for at...  10.3 us
    pallas_call x2, Pallas kernels, make_sides(): pl.pallas_call(functools.partial(sides_kernel, stage, groups), in_specs=[...  3.54 us
    ppermute x2, starting transfers between devices, shards(): lax.ppermute(handed_part, 'pipe', [(place, place - 1) for place in range(...  2.57 us
    pallas_call x1, Pallas kernels, shards(): pl.pallas_call(functools.partial(prep_kernel, groups, per_stage), in_spec...  1.15 us
  transfers between devices with their start and end apart: 14, of which 8 were waited for; matrix products, arithmetic and copies ran while one was open for 2% of the time, Pallas kernels for 26%

profile of v1, /device:TPU:0, one launch (start us, length us, event | category | flops | bytes accessed | tf_op | source)
XLA Modules:
  0.0 56.4 jit_solution(17983261999964264629)
XLA Ops:
  0.6 0.0 copy-start
  0.6 1.1 %pack_keys.1 = (bf16[2,2,128,128]{3,2,1,0:T(8,128)(2,1)S(1)}, bf16[2,2,128,128]{3,2,1,0:T(8,128)(2,1)S(1)}) custom-call(bf16[512,128]{1,0:T(8,128)(2,1)} %bitcast.15, bf16[512,128]{1,0:T(8,128)(2,1)} %bitcast.16), custom_call_target="tpu_custom_call" | custom-call | flops 1048576 | bytes 65536 | tf_op jit(solution)/shard_map/pack_keys/pallas_call | solution.py:330
  1.8 3.1 %collective-permute-start = (bf16[2,2,128,128]{3,2,1,0:T(8,128)(2,1)S(1)}, bf16[2,2,128,128]{3,2,1,0:T(8,128)(2,1)S(1)}, u32[]{:S(2)}, u32[]{:S(2)}) collective-permute-start(bf16[2,2,128,128]{3,2,1,0:T(8,128)(2,1)S(1)} %get-tuple-element.42.refs_0_), channel_id=1, source_target_pairs={{0,2},{2,6},{6,4},{4,0},{1,3},{3,7},{7,5},{5,1},{8,10},{10,14},{14... | collective-permute-start | bytes 393224 | tf_op jit(solution)/shard_map/ppermute | solution.py:97
  4.9 1.1 %collective-permute-start.2 = (bf16[2,2,128,128]{3,2,1,0:T(8,128)(2,1)S(1)}, bf16[2,2,128,128]{3,2,1,0:T(8,128)(2,1)S(1)}, u32[]{:S(2)}, u32[]{:S(2)}) collective-permute-start(bf16[2,2,128,128]{3,2,1,0:T(8,128)(2,1)S(1)} %get-tuple-element.42.refs_0_), channel_id=1, source_target_pairs={{0,4},{2,0},{6,2},{4,6},{1,5},{3,1},{7,3},{5,7},{8,12},{10,8},{14,... | collective-permute-start | bytes 393224 | tf_op jit(solution)/shard_map/ppermute | solution.py:97
  6.0 1.8 %query_sides.2 = (bf16[2,2,512,256]{3,2,1,0:T(8,128)(2,1)S(1)}, bf16[2,2,512,256]{3,2,1,0:T(8,128)(2,1)S(1)}) custom-call(bf16[128,32,128]{2,1,0:T(8,128)(2,1)} %bitcast.9, bf16[128,32,128]{2,1,0:T(8,128)(2,1)} %bitcast.11, bf16[128,32,128]{2,1,0:T(8,128)(2,1)} %bitcast.13), custom_call_target="tpu_custom_call" | custom-call | flops 1048576 | bytes 65536 | tf_op jit(solution)/shard_map/query_sides/pallas_call | solution.py:306
  7.7 1.8 %collective-permute-done.refs_1_ = bf16[2,2,128,128]{3,2,1,0:T(8,128)(2,1)S(1)} collective-permute-done((bf16[2,2,128,128]{3,2,1,0:T(8,128)(2,1)S(1)}, bf16[2,2,128,128]{3,2,1,0:T(8,128)(2,1)S(1)}, u32[]{:S(2)}, u32[]{:S(2)}) %collective-permute-start) | collective-permute-done | bytes 131104 | tf_op jit(solution)/shard_map/ppermute | solution.py:97
  9.5 3.5 %collective-permute-start.1 = (bf16[2,2,128,128]{3,2,1,0:T(8,128)(2,1)S(1)}, bf16[2,2,128,128]{3,2,1,0:T(8,128)(2,1)S(1)}, u32[]{:S(2)}, u32[]{:S(2)}) collective-permute-start(bf16[2,2,128,128]{3,2,1,0:T(8,128)(2,1)S(1)} %collective-permute-done.refs_1_), channel_id=1, source_target_pairs={{0,2},{2,6},{6,4},{4,0},{1,3},{3,7},{7,5},{5,1},{8,10},{10,14},{14... | collective-permute-start | bytes 393224 | tf_op jit(solution)/shard_map/ppermute | solution.py:97
  13.0 0.0 collective-permute-done.2.refs_3_
  13.0 0.9 %collective-permute-start.4 = (bf16[2,2,128,128]{3,2,1,0:T(8,128)(2,1)S(1)}, bf16[2,2,128,128]{3,2,1,0:T(8,128)(2,1)S(1)}, u32[]{:S(2)}, u32[]{:S(2)}) collective-permute-start(bf16[2,2,128,128]{3,2,1,0:T(8,128)(2,1)S(1)} %get-tuple-element.67.refs_0_), channel_id=1, source_target_pairs={{0,4},{2,0},{6,2},{4,6},{1,5},{3,1},{7,3},{5,7},{8,12},{10,8},{14,... | collective-permute-start | bytes 393224 | tf_op jit(solution)/shard_map/ppermute | solution.py:97
  13.9 2.5 %collective-permute-start.3 = (bf16[2,2,128,128]{3,2,1,0:T(8,128)(2,1)S(1)}, bf16[2,2,128,128]{3,2,1,0:T(8,128)(2,1)S(1)}, u32[]{:S(2)}, u32[]{:S(2)}) collective-permute-start(bf16[2,2,128,128]{3,2,1,0:T(8,128)(2,1)S(1)} %get-tuple-element.67.refs_0_), channel_id=1, source_target_pairs={{0,2},{2,6},{6,4},{4,0},{1,3},{3,7},{7,5},{5,1},{8,10},{10,14},{14... | collective-permute-start | bytes 393224 | tf_op jit(solution)/shard_map/ppermute | solution.py:97
  16.4 0.0 collective-permute-done.1.refs_2_
  16.4 0.0 copy-done
  16.4 4.1 %query_grads.2 = (bf16[128,16,128]{2,1,0:T(8,128)(2,1)S(1)}, bf16[2,512,1024]{2,1,0:T(8,128)(2,1)S(1)}, bf16[2,512,1024]{2,1,0:T(8,128)(2,1)S(1)}) custom-call(s32[8]{0:T(128)S(1)} %copy-done, bf16[2,2,512,256]{3,2,1,0:T(8,128)(2,1)S(1)} %get-tuple-element.45.q_side_ref, bf16[2,2,512,256]{3,2,1,0:T(8,128)(2,1)S(1)} %get-tuple-element.46.g_side_ref, ...), custom_call_target="tpu_custom_call" | custom-call | flops 4294967296 | bytes 65536 | tf_op jit(solution)/shard_map/query_grads/pallas_call | solution.py:285
  20.5 1.3 %collective-permute-done.4.refs_3_ = bf16[2,2,128,128]{3,2,1,0:T(8,128)(2,1)S(1)} collective-permute-done((bf16[2,2,128,128]{3,2,1,0:T(8,128)(2,1)S(1)}, bf16[2,2,128,128]{3,2,1,0:T(8,128)(2,1)S(1)}, u32[]{:S(2)}, u32[]{:S(2)}) %collective-permute-start.4) | collective-permute-done | bytes 131104 | tf_op jit(solution)/shard_map/ppermute | solution.py:97
  21.8 0.1 collective-permute-done.3.refs_1_
  21.9 3.5 %collective-permute-start.5 = (bf16[2,2,128,128]{3,2,1,0:T(8,128)(2,1)S(1)}, bf16[2,2,128,128]{3,2,1,0:T(8,128)(2,1)S(1)}, u32[]{:S(2)}, u32[]{:S(2)}) collective-permute-start(bf16[2,2,128,128]{3,2,1,0:T(8,128)(2,1)S(1)} %collective-permute-done.3.refs_1_), channel_id=1, source_target_pairs={{0,2},{2,6},{6,4},{4,0},{1,3},{3,7},{7,5},{5,1},{8,10},{10,14},{14... | collective-permute-start | bytes 393224 | tf_op jit(solution)/shard_map/ppermute | solution.py:97
  25.5 1.3 %collective-permute-start.9 = (bf16[128,16,128]{2,1,0:T(8,128)(2,1)S(1)}, bf16[128,16,128]{2,1,0:T(8,128)(2,1)S(1)}, u32[]{:S(2)}, u32[]{:S(2)}) collective-permute-start(bf16[128,16,128]{2,1,0:T(8,128)(2,1)S(1)} %get-tuple-element.51), channel_id=1, source_target_pairs={{8,0},{16,8},{24,16},{9,1},{17,9},{25,17},{10,2},{18,10},{26,18},{... | collective-permute-start | bytes 1572872 | tf_op jit(solution)/shard_map/ppermute | solution.py:385
  26.7 1.8 %query_sides.3 = (bf16[2,2,512,256]{3,2,1,0:T(8,128)(2,1)S(1)}, bf16[2,2,512,256]{3,2,1,0:T(8,128)(2,1)S(1)}) custom-call(bf16[128,32,128]{2,1,0:T(8,128)(2,1)} %bitcast.10, bf16[128,32,128]{2,1,0:T(8,128)(2,1)} %bitcast.12, bf16[128,32,128]{2,1,0:T(8,128)(2,1)} %bitcast.14), custom_call_target="tpu_custom_call" | custom-call | flops 1048576 | bytes 65536 | tf_op jit(solution)/shard_map/query_sides/pallas_call | solution.py:306
  28.5 1.4 %key_grads.2 = (bf16[2,2,128,128]{3,2,1,0:T(8,128)(2,1)S(1)}, bf16[2,2,128,128]{3,2,1,0:T(8,128)(2,1)S(1)}, bf16[2,2,128,128]{3,2,1,0:T(8,128)(2,1)S(1)}, bf16[2,2,128,128]{3,2,1,0:T(8,128)(2,1)S(1)}) custom-call(bf16[2,2,512,256]{3,2,1,0:T(8,128)(2,1)S(1)} %get-tuple-element.45.q_side_ref, bf16[2,2,512,256]{3,2,1,0:T(8,128)(2,1)S(1)} %get-tuple-element.46.g_side_ref, ...), custom_call_target="tpu_custom_call" | custom-call | flops 1048576 | bytes 65536 | tf_op jit(solution)/shard_map/key_grads/pallas_call | solution.py:285
  30.0 0.0 collective-permute-done.5.refs_2_
  30.0 3.5 %collective-permute-start.6 = (bf16[2,2,128,128]{3,2,1,0:T(8,128)(2,1)S(1)}, bf16[2,2,128,128]{3,2,1,0:T(8,128)(2,1)S(1)}, u32[]{:S(2)}, u32[]{:S(2)}) collective-permute-start(bf16[2,2,128,128]{3,2,1,0:T(8,128)(2,1)S(1)} %get-tuple-element.61), channel_id=1, source_target_pairs={{0,2},{2,6},{6,4},{4,0},{1,3},{3,7},{7,5},{5,1},{8,10},{10,14},{14... | collective-permute-start | bytes 393224 | tf_op jit(solution)/shard_map/ppermute | solution.py:97
  33.5 4.1 %query_grads.3 = (bf16[128,16,128]{2,1,0:T(8,128)(2,1)S(1)}, bf16[2,512,1024]{2,1,0:T(8,128)(2,1)S(1)}, bf16[2,512,1024]{2,1,0:T(8,128)(2,1)S(1)}) custom-call(s32[8]{0:T(128)S(1)} %copy-done, bf16[2,2,512,256]{3,2,1,0:T(8,128)(2,1)S(1)} %get-tuple-element.65.q_side_ref, bf16[2,2,512,256]{3,2,1,0:T(8,128)(2,1)S(1)} %get-tuple-element.66.g_side_ref, ...), custom_call_target="tpu_custom_call" | custom-call | flops 4294967296 | bytes 65536 | tf_op jit(solution)/shard_map/query_grads/pallas_call | solution.py:285
  37.6 1.3 %collective-permute-start.13 = (bf16[128,16,128]{2,1,0:T(8,128)(2,1)S(1)}, bf16[128,16,128]{2,1,0:T(8,128)(2,1)S(1)}, u32[]{:S(2)}, u32[]{:S(2)}) collective-permute-start(bf16[128,16,128]{2,1,0:T(8,128)(2,1)S(1)} %get-tuple-element.80), channel_id=1, source_target_pairs={{8,0},{16,8},{24,16},{9,1},{17,9},{25,17},{10,2},{18,10},{26,18},{... | collective-permute-start | bytes 1572872 | tf_op jit(solution)/shard_map/ppermute | solution.py:385
  38.9 0.1 collective-permute-start.8
  39.0 0.0 collective-permute-done.9
  39.0 1.4 %key_grads.3 = (bf16[2,2,128,128]{3,2,1,0:T(8,128)(2,1)S(1)}, bf16[2,2,128,128]{3,2,1,0:T(8,128)(2,1)S(1)}, bf16[2,2,128,128]{3,2,1,0:T(8,128)(2,1)S(1)}, bf16[2,2,128,128]{3,2,1,0:T(8,128)(2,1)S(1)}) custom-call(bf16[2,2,512,256]{3,2,1,0:T(8,128)(2,1)S(1)} %get-tuple-element.65.q_side_ref, bf16[2,2,512,256]{3,2,1,0:T(8,128)(2,1)S(1)} %get-tuple-element.66.g_side_ref, ...), custom_call_target="tpu_custom_call" | custom-call | flops 1048576 | bytes 65536 | tf_op jit(solution)/shard_map/key_grads/pallas_call | solution.py:285
  40.4 3.8 %collective-permute-start.10 = (bf16[2,2,128,128]{3,2,1,0:T(8,128)(2,1)S(1)}, bf16[2,2,128,128]{3,2,1,0:T(8,128)(2,1)S(1)}, u32[]{:S(2)}, u32[]{:S(2)}) collective-permute-start(bf16[2,2,128,128]{3,2,1,0:T(8,128)(2,1)S(1)} %get-tuple-element.75), channel_id=1, source_target_pairs={{0,2},{2,6},{6,4},{4,0},{1,3},{3,7},{7,5},{5,1},{8,10},{10,14},{14... | collective-permute-start | bytes 393224 | tf_op jit(solution)/shard_map/ppermute | solution.py:97
  44.2 0.0 collective-permute-done.6
  44.2 1.6 %collective-permute-start.7 = (bf16[2,2,128,128]{3,2,1,0:T(8,128)(2,1)S(1)}, bf16[2,2,128,128]{3,2,1,0:T(8,128)(2,1)S(1)}, u32[]{:S(2)}, u32[]{:S(2)}) collective-permute-start(bf16[2,2,128,128]{3,2,1,0:T(8,128)(2,1)S(1)} %add_convert_fusion.1), channel_id=1, source_target_pairs={{0,2},{2,6},{6,4},{4,0},{1,3},{3,7},{7,5},{5,1},{8,10},{10,14},{14... | collective-permute-start | bytes 393224 | tf_op jit(solution)/shard_map/ppermute | solution.py:97
  45.8 1.4 %collective-permute-start.12 = (bf16[2,2,128,128]{3,2,1,0:T(8,128)(2,1)S(1)}, bf16[2,2,128,128]{3,2,1,0:T(8,128)(2,1)S(1)}, u32[]{:S(2)}, u32[]{:S(2)}) collective-permute-start(bf16[2,2,128,128]{3,2,1,0:T(8,128)(2,1)S(1)} %get-tuple-element.77), channel_id=1, source_target_pairs={{0,4},{2,0},{6,2},{4,6},{1,5},{3,1},{7,3},{5,7},{8,12},{10,8},{14,... | collective-permute-start | bytes 393224 | tf_op jit(solution)/shard_map/ppermute | solution.py:97
  47.2 2.5 %collective-permute-done.10 = bf16[2,2,128,128]{3,2,1,0:T(8,128)(2,1)S(1)} collective-permute-done((bf16[2,2,128,128]{3,2,1,0:T(8,128)(2,1)S(1)}, bf16[2,2,128,128]{3,2,1,0:T(8,128)(2,1)S(1)}, u32[]{:S(2)}, u32[]{:S(2)}) %collective-permute-start.10) | collective-permute-done | bytes 131104 | tf_op jit(solution)/shard_map/ppermute | solution.py:97
  49.7 0.1 collective-permute-start.11
  49.8 0.1 collective-permute-done.13
  49.9 1.1 %maximum_bitcast_fusion = bf16[1,128,32,128]{3,2,1,0:T(8,128)(2,1)} fusion(bf16[128,16,128]{2,1,0:T(8,128)(2,1)S(1)} %collective-permute-done.13, bf16[128,16,128]{2,1,0:T(8,128)(2,1)S(1)} %collective-permute-done.9), kind=kLoop, calls=%fused_computation | loop fusion | flops 2097152 | bytes 2097152 | tf_op jit(solution)/shard_map/broadcast_in_dim | solution.py:404
  51.0 0.0 collective-permute-done.8.refs_2_
  51.0 0.2 collective-permute-done.7.refs_1_
  51.2 1.3 %collective-permute-done.12.refs_5_ = bf16[2,2,128,128]{3,2,1,0:T(8,128)(2,1)S(1)} collective-permute-done((bf16[2,2,128,128]{3,2,1,0:T(8,128)(2,1)S(1)}, bf16[2,2,128,128]{3,2,1,0:T(8,128)(2,1)S(1)}, u32[]{:S(2)}, u32[]{:S(2)}) %collective-permute-start.12) | collective-permute-done | bytes 131104 | tf_op jit(solution)/shard_map/ppermute | solution.py:97
  52.5 3.2 %collective-permute-done.11.refs_4_ = bf16[2,2,128,128]{3,2,1,0:T(8,128)(2,1)S(1)} collective-permute-done((bf16[2,2,128,128]{3,2,1,0:T(8,128)(2,1)S(1)}, bf16[2,2,128,128]{3,2,1,0:T(8,128)(2,1)S(1)}, u32[]{:S(2)}, u32[]{:S(2)}) %collective-permute-start.11) | collective-permute-done | bytes 131104 | tf_op jit(solution)/shard_map/ppermute | solution.py:97
  55.7 0.8 %lay_out.1 = (bf16[512,128]{1,0:T(8,128)(2,1)}, bf16[512,128]{1,0:T(8,128)(2,1)}) custom-call(bf16[2,2,128,128]{3,2,1,0:T(8,128)(2,1)S(1)} %get-tuple-element.60.refs_0_, bf16[2,2,128,128]{3,2,1,0:T(8,128)(2,1)S(1)} %collective-permute-done.7.refs_1_, bf16[2,2,128,128]{3,2,1,0:T(8,128)(2,1)S(1)} %collective-permute-done.8.refs_2_, ...), custom_call_target="tpu_custom_call" | custom-call | flops 1048576 | bytes 65536 | tf_op jit(solution)/shard_map/lay_out/pallas_call | solution.py:285
  (2 shorter events, 0.1 us)
Async XLA Ops:
  0.6 15.8 %copy-start = (s32[8]{0:T(128)S(1)}, s32[8]{0:T(128)}, u32[]{:S(2)}) copy-start(s32[8]{0:T(128)} %order_ref.3) | copy-start | bytes 100
  1.8 7.7 %collective-permute-start = (bf16[2,2,128,128]{3,2,1,0:T(8,128)(2,1)S(1)}, bf16[2,2,128,128]{3,2,1,0:T(8,128)(2,1)S(1)}, u32[]{:S(2)}, u32[]{:S(2)}) collective-permute-start(bf16[2,2,128,128]{3,2,1,0:T(8,128)(2,1)S(1)} %get-tuple-element.42.refs_0_), channel_id=1, source_target_pairs={{0,2},{2,6},{6,4},{4,0},{1,3},{3,7},{7,5},{5,1},{8,10},{10,14},{14... | collective-permute-start | bytes 393224 | tf_op jit(solution)/shard_map/ppermute | solution.py:97
  4.9 8.2 %collective-permute-start.2 = (bf16[2,2,128,128]{3,2,1,0:T(8,128)(2,1)S(1)}, bf16[2,2,128,128]{3,2,1,0:T(8,128)(2,1)S(1)}, u32[]{:S(2)}, u32[]{:S(2)}) collective-permute-start(bf16[2,2,128,128]{3,2,1,0:T(8,128)(2,1)S(1)} %get-tuple-element.42.refs_0_), channel_id=1, source_target_pairs={{0,4},{2,0},{6,2},{4,6},{1,5},{3,1},{7,3},{5,7},{8,12},{10,8},{14,... | collective-permute-start | bytes 393224 | tf_op jit(solution)/shard_map/ppermute | solution.py:97
  9.5 6.9 %collective-permute-start.1 = (bf16[2,2,128,128]{3,2,1,0:T(8,128)(2,1)S(1)}, bf16[2,2,128,128]{3,2,1,0:T(8,128)(2,1)S(1)}, u32[]{:S(2)}, u32[]{:S(2)}) collective-permute-start(bf16[2,2,128,128]{3,2,1,0:T(8,128)(2,1)S(1)} %collective-permute-done.refs_1_), channel_id=1, source_target_pairs={{0,2},{2,6},{6,4},{4,0},{1,3},{3,7},{7,5},{5,1},{8,10},{10,14},{14... | collective-permute-start | bytes 393224 | tf_op jit(solution)/shard_map/ppermute | solution.py:97
  13.0 8.8 %collective-permute-start.4 = (bf16[2,2,128,128]{3,2,1,0:T(8,128)(2,1)S(1)}, bf16[2,2,128,128]{3,2,1,0:T(8,128)(2,1)S(1)}, u32[]{:S(2)}, u32[]{:S(2)}) collective-permute-start(bf16[2,2,128,128]{3,2,1,0:T(8,128)(2,1)S(1)} %get-tuple-element.67.refs_0_), channel_id=1, source_target_pairs={{0,4},{2,0},{6,2},{4,6},{1,5},{3,1},{7,3},{5,7},{8,12},{10,8},{14,... | collective-permute-start | bytes 393224 | tf_op jit(solution)/shard_map/ppermute | solution.py:97
  13.9 8.0 %collective-permute-start.3 = (bf16[2,2,128,128]{3,2,1,0:T(8,128)(2,1)S(1)}, bf16[2,2,128,128]{3,2,1,0:T(8,128)(2,1)S(1)}, u32[]{:S(2)}, u32[]{:S(2)}) collective-permute-start(bf16[2,2,128,128]{3,2,1,0:T(8,128)(2,1)S(1)} %get-tuple-element.67.refs_0_), channel_id=1, source_target_pairs={{0,2},{2,6},{6,4},{4,0},{1,3},{3,7},{7,5},{5,1},{8,10},{10,14},{14... | collective-permute-start | bytes 393224 | tf_op jit(solution)/shard_map/ppermute | solution.py:97
  21.9 8.0 %collective-permute-start.5 = (bf16[2,2,128,128]{3,2,1,0:T(8,128)(2,1)S(1)}, bf16[2,2,128,128]{3,2,1,0:T(8,128)(2,1)S(1)}, u32[]{:S(2)}, u32[]{:S(2)}) collective-permute-start(bf16[2,2,128,128]{3,2,1,0:T(8,128)(2,1)S(1)} %collective-permute-done.3.refs_1_), channel_id=1, source_target_pairs={{0,2},{2,6},{6,4},{4,0},{1,3},{3,7},{7,5},{5,1},{8,10},{10,14},{14... | collective-permute-start | bytes 393224 | tf_op jit(solution)/shard_map/ppermute | solution.py:97
  25.5 13.5 %collective-permute-start.9 = (bf16[128,16,128]{2,1,0:T(8,128)(2,1)S(1)}, bf16[128,16,128]{2,1,0:T(8,128)(2,1)S(1)}, u32[]{:S(2)}, u32[]{:S(2)}) collective-permute-start(bf16[128,16,128]{2,1,0:T(8,128)(2,1)S(1)} %get-tuple-element.51), channel_id=1, source_target_pairs={{8,0},{16,8},{24,16},{9,1},{17,9},{25,17},{10,2},{18,10},{26,18},{... | collective-permute-start | bytes 1572872 | tf_op jit(solution)/shard_map/ppermute | solution.py:385
  30.0 14.2 %collective-permute-start.6 = (bf16[2,2,128,128]{3,2,1,0:T(8,128)(2,1)S(1)}, bf16[2,2,128,128]{3,2,1,0:T(8,128)(2,1)S(1)}, u32[]{:S(2)}, u32[]{:S(2)}) collective-permute-start(bf16[2,2,128,128]{3,2,1,0:T(8,128)(2,1)S(1)} %get-tuple-element.61), channel_id=1, source_target_pairs={{0,2},{2,6},{6,4},{4,0},{1,3},{3,7},{7,5},{5,1},{8,10},{10,14},{14... | collective-permute-start | bytes 393224 | tf_op jit(solution)/shard_map/ppermute | solution.py:97
  37.6 12.3 %collective-permute-start.13 = (bf16[128,16,128]{2,1,0:T(8,128)(2,1)S(1)}, bf16[128,16,128]{2,1,0:T(8,128)(2,1)S(1)}, u32[]{:S(2)}, u32[]{:S(2)}) collective-permute-start(bf16[128,16,128]{2,1,0:T(8,128)(2,1)S(1)} %get-tuple-element.80), channel_id=1, source_target_pairs={{8,0},{16,8},{24,16},{9,1},{17,9},{25,17},{10,2},{18,10},{26,18},{... | collective-permute-start | bytes 1572872 | tf_op jit(solution)/shard_map/ppermute | solution.py:385
  38.9 12.1 %collective-permute-start.8 = (bf16[2,2,128,128]{3,2,1,0:T(8,128)(2,1)S(1)}, bf16[2,2,128,128]{3,2,1,0:T(8,128)(2,1)S(1)}, u32[]{:S(2)}, u32[]{:S(2)}) collective-permute-start(bf16[2,2,128,128]{3,2,1,0:T(8,128)(2,1)S(1)} %get-tuple-element.63), channel_id=1, source_target_pairs={{0,4},{2,0},{6,2},{4,6},{1,5},{3,1},{7,3},{5,7},{8,12},{10,8},{14,... | collective-permute-start | bytes 393224 | tf_op jit(solution)/shard_map/ppermute | solution.py:97
  40.4 9.3 %collective-permute-start.10 = (bf16[2,2,128,128]{3,2,1,0:T(8,128)(2,1)S(1)}, bf16[2,2,128,128]{3,2,1,0:T(8,128)(2,1)S(1)}, u32[]{:S(2)}, u32[]{:S(2)}) collective-permute-start(bf16[2,2,128,128]{3,2,1,0:T(8,128)(2,1)S(1)} %get-tuple-element.75), channel_id=1, source_target_pairs={{0,2},{2,6},{6,4},{4,0},{1,3},{3,7},{7,5},{5,1},{8,10},{10,14},{14... | collective-permute-start | bytes 393224 | tf_op jit(solution)/shard_map/ppermute | solution.py:97
  44.2 7.0 %collective-permute-start.7 = (bf16[2,2,128,128]{3,2,1,0:T(8,128)(2,1)S(1)}, bf16[2,2,128,128]{3,2,1,0:T(8,128)(2,1)S(1)}, u32[]{:S(2)}, u32[]{:S(2)}) collective-permute-start(bf16[2,2,128,128]{3,2,1,0:T(8,128)(2,1)S(1)} %add_convert_fusion.1), channel_id=1, source_target_pairs={{0,2},{2,6},{6,4},{4,0},{1,3},{3,7},{7,5},{5,1},{8,10},{10,14},{14... | collective-permute-start | bytes 393224 | tf_op jit(solution)/shard_map/ppermute | solution.py:97
  45.8 6.6 %collective-permute-start.12 = (bf16[2,2,128,128]{3,2,1,0:T(8,128)(2,1)S(1)}, bf16[2,2,128,128]{3,2,1,0:T(8,128)(2,1)S(1)}, u32[]{:S(2)}, u32[]{:S(2)}) collective-permute-start(bf16[2,2,128,128]{3,2,1,0:T(8,128)(2,1)S(1)} %get-tuple-element.77), channel_id=1, source_target_pairs={{0,4},{2,0},{6,2},{4,6},{1,5},{3,1},{7,3},{5,7},{8,12},{10,8},{14,... | collective-permute-start | bytes 393224 | tf_op jit(solution)/shard_map/ppermute | solution.py:97
  49.7 5.9 %collective-permute-start.11 = (bf16[2,2,128,128]{3,2,1,0:T(8,128)(2,1)S(1)}, bf16[2,2,128,128]{3,2,1,0:T(8,128)(2,1)S(1)}, u32[]{:S(2)}, u32[]{:S(2)}) collective-permute-start(bf16[2,2,128,128]{3,2,1,0:T(8,128)(2,1)S(1)} %add_convert_fusion), channel_id=1, source_target_pairs={{0,2},{2,6},{6,4},{4,0},{1,3},{3,7},{7,5},{5,1},{8,10},{10,14},{14... | collective-permute-start | bytes 393224 | tf_op jit(solution)/shard_map/ppermute | solution.py:97

commit v2 on v1

v2 whole, which is shorter than its diff:
```python
import functools
import math

import jax
import jax.numpy as jnp
from jax import lax
from jax.experimental import pallas as pl
from jax.experimental.pallas import tpu as pltpu
from jax.sharding import PartitionSpec as P

NEG = -1e30
STAGES = 2
WORK = 2**20
BIG_WORK = 2**32
F32 = jnp.float32
BF16 = jnp.bfloat16


def signs(size):
    row = lax.broadcasted_iota(jnp.int32, (size, size), 0)
    col = lax.broadcasted_iota(jnp.int32, (size, size), 1)
    bits = row & col
    for step in (4, 2, 1):
        bits = bits ^ (bits >> step)
    return (1 - 2 * (bits & 1)).astype(F32).astype(BF16)


def dot(a, b, contract):
    return lax.dot_general(a, b, (contract, ((), ())), preferred_element_type=F32)


def nn(a, b):
    return dot(a, b, ((1,), (0,)))


def nt(a, b):
    return dot(a, b, ((1,), (1,)))


def split(x):
    high = x.astype(BF16)
    return high, (x - high.astype(F32)).astype(BF16)


def prep_kernel(k_hbm, v_hbm, k_out, v_out, rows_ref, k_ref, v_ref, sems):
    copies = [
        pltpu.make_async_copy(source, target, sems.at[at])
        for at, (source, target) in enumerate(((k_hbm, k_ref), (v_hbm, v_ref)))
    ]
    for copy in copies:
        copy.start()
    groups, tokens, size = k_out.shape
    sign = signs(size)
    for copy, ref, out in zip(copies, (k_ref, v_ref), (k_out, v_out)):
        copy.wait()
        if ref is k_ref:
            rows = nn(k_ref[...], sign) * (1.0 / math.sqrt(size))
        else:
            rows = v_ref[...].astype(F32)
        rows_ref[...] = rows
        for group in range(groups):
            out[group] = rows_ref[pl.ds(group, tokens, stride=groups), :].astype(BF16)


def finish_kernel(count, *refs):
    outs, rows_ref = refs[-3:-1], refs[-1]
    for part, out in enumerate(outs):
        terms = refs[part * count : (part + 1) * count]
        groups, tokens, _ = terms[0].shape
        for group in range(groups):
            rows = [ref[group].astype(F32) for ref in terms]
            rows_ref[pl.ds(group, tokens, stride=groups), :] = sum(rows[1:], rows[0])
        out[...] = rows_ref[...].astype(BF16)


def ring_order(count):
    return [0] + [at for at in range(count) if at % 2] + [at for at in range(count - 1, 0, -1) if at % 2 == 0]


def ring_place(count, place):
    odd = place & 1
    half = place >> 1
    return lax.rem(odd * (half + 1) + (1 - odd) * (count - half), count)


def ring_device(count, ring):
    return jnp.where(ring <= count // 2, jnp.maximum(2 * ring - 1, 0), 2 * (count - ring))


def passed(value, axis, step):
    count = lax.axis_size(axis)
    order = ring_order(count)
    return lax.ppermute(
        value, axis, [(order[at], order[(at + step) % count]) for at in range(count)]
    )


def gather(block, axis, relay_after=None):
    count = lax.axis_size(axis)
    blocks = {0: block}
    for step in range(1, count // 2 + 1):
        for sign in (1, -1):
            if sign < 0 and 2 * step == count:
                continue
            if step > 1 and relay_after is not None:
                moving, shift = blocks[(sign * (step - 1)) % count], sign
                if step == 2:
                    moving, _ = lax.optimization_barrier((moving, relay_after))
            else:
                moving, shift = block, sign * step
            blocks[(sign * step) % count] = passed(moving, axis, shift)
    return [blocks[step] for step in range(count)]


def passed_down(value, axis):
    count = lax.axis_size(axis)
    return lax.ppermute(value, axis, [(at, (at - 1) % count) for at in range(count)])


def added(a, b):
    return (a.astype(F32) + b.astype(F32)).astype(BF16)


def scatter_sums(parts, axis, relay_after):
    count = lax.axis_size(axis)
    terms, relayed = [parts[0]], []
    for step, longest in ((1, count // 2), (-1, (count - 1) // 2)):
        moving = None
        for distance in range(longest, 0, -1):
            part = parts[(-step * distance) % count]
            if moving is not None:
                moving, _ = lax.optimization_barrier((moving, relay_after))
                part = added(moving, part)
                relayed.append(part)
            moving = passed(part, axis, step)
        terms.append(moving)
    return terms, relayed


def sides_kernel(groups, q_hbm, g_hbm, o_hbm, q_side_ref, g_side_ref, in_ref, sems):
    _, _, half_rows, heads, size = in_ref.shape
    per_group = heads // groups
    copies = []
    for half in range(2):
        for part, source in enumerate((q_hbm, g_hbm, o_hbm)):
            piece = source.at[pl.ds(half * half_rows, half_rows)]
            copies.append(
                pltpu.make_async_copy(piece, in_ref.at[half, part], sems.at[half * 3 + part])
            )
            copies[-1].start()
    rows = half_rows * per_group
    sign = signs(size)
    root = 1.0 / math.sqrt(size)
    row_offset = lax.broadcasted_iota(jnp.int32, (rows, size), 0) // per_group
    lane = lax.broadcasted_iota(jnp.int32, (rows, size), 1)
    hide = jnp.where(row_offset == lane, NEG, 0.0).astype(BF16)
    for half in range(2):
        for copy in copies[3 * half : 3 * half + 3]:
            copy.wait()
        q_all = nn(in_ref[half, 0].reshape(half_rows * heads, size), sign) * root
        q_all = q_all.reshape(half_rows, groups, per_group, size)
        g_all = in_ref[half, 1].astype(F32).reshape(half_rows, groups, per_group, size)
        o_all = in_ref[half, 2].astype(F32).reshape(half_rows, groups, per_group, size)
        for group in range(groups):
            grad = g_all[:, group].reshape(rows, size)
            product = grad * o_all[:, group].reshape(rows, size)
            product = -(product + pltpu.roll(product, size // 2, 1))
            high = product.astype(BF16).astype(F32)
            delta = jnp.where(lane < size // 2, high, product - high)
            q_side_ref[half, group, :, :size] = q_all[:, group].reshape(rows, size).astype(BF16)
            q_side_ref[half, group, :, size:] = hide
            g_side_ref[half, group, :, :size] = grad.astype(BF16)
            g_side_ref[half, group, :, size:] = delta.astype(BF16)


def chunked(keys, chunk, body, init):
    if keys == chunk:
        return body(0, init)
    return lax.fori_loop(0, keys // chunk, body, init)


def weights_kernel(first, blocks, order_ref, q_side_ref, g_side_ref, *refs):
    k_refs, probs_ref, sum_refs = refs[:blocks], refs[blocks], refs[blocks + 1 : 2 * blocks + 1]
    score_ref, key_ref = refs[2 * blocks + 1 :]
    groups, keys, _ = probs_ref.shape
    tokens, size = k_refs[0].shape[1:]
    place = lax.axis_index("ctx")
    ring = ring_place(blocks, place)
    rows = q_side_ref.shape[2]
    half_rows = tokens // 2
    chunk = 512
    power = math.log2(math.e) / math.sqrt(size)

    def span(index):
        return pl.ds(pl.multiple_of(index * chunk, chunk), chunk)

    at_row = lax.broadcasted_iota(jnp.int32, (half_rows, size), 0)
    at_col = lax.broadcasted_iota(jnp.int32, (half_rows, size), 1)
    for block in range(blocks):
        source = ring_device(blocks, lax.rem(ring - block + blocks, blocks))
        for half in range(2):
            q_start = order_ref[place * 2 + half]
            for k_half in range(2):
                ahead = (order_ref[source * 2 + k_half] - q_start) * half_rows
                hidden = (at_row + ahead > at_col) & (at_col < half_rows)
                hidden = jnp.where(hidden, 1.0, 0.0).astype(BF16)
                k_at = pl.ds(block * tokens + k_half * half_rows, half_rows)
                for group in range(groups):
                    key_ref[half, group, k_at, size:] = hidden
        at = pl.ds(block * tokens, tokens)
        for group in range(groups):
            key = k_refs[block][first + group]
            for half in range(2):
                key_ref[half, group, at, :size] = key

    for group in range(groups):
        for half in range(2):
            q_side = q_side_ref.at[half, first + group]
            row_at = pl.ds(half * rows, rows)

            def scores(index, top, half=half, group=group, q_side=q_side):
                part = nt(key_ref[half, group, span(index), :], q_side[...])
                score_ref[half, span(index), :] = part
                return jnp.maximum(top, jnp.max(part.reshape(chunk // 8, 8, rows), axis=0))

            top = chunked(keys, chunk, scores, jnp.full((8, rows), NEG, F32))
            top = jnp.max(top, axis=0, keepdims=True)

            def weigh(index, total, half=half, top=top):
                part = jnp.exp2((score_ref[half, span(index), :] - top) * power)
                score_ref[half, span(index), :] = part
                return total + jnp.sum(part.reshape(chunk // 8, 8, rows), axis=0)

            total = chunked(keys, chunk, weigh, jnp.zeros((8, rows), F32))
            scale = 1.0 / jnp.sum(total, axis=0, keepdims=True)

            def settle(index, carried, half=half, group=group, scale=scale, row_at=row_at):
                probs = score_ref[half, span(index), :] * scale
                probs_ref[group, span(index), row_at] = probs.astype(probs_ref.dtype)
                return carried

            chunked(keys, chunk, settle, 0)
        for row in range(0, keys, chunk):
            dv = None
            for half in range(2):
                probs = probs_ref[group, pl.ds(row, chunk), pl.ds(half * rows, rows)]
                part = nn(probs.astype(BF16), g_side_ref[half, first + group, :, :size])
                dv = part if dv is None else dv + part
            dv = dv.astype(BF16)
            for at in range(0, chunk, tokens):
                sum_refs[(row + at) // tokens][group] = dv[at : at + tokens]


def dq_kernel(first, blocks, g_side_ref, probs_ref, *refs):
    k_refs, v_refs = refs[:blocks], refs[blocks : 2 * blocks]
    handed_ref, dscore_ref, val_ref, back_ref = refs[2 * blocks :]
    groups, keys, _ = probs_ref.shape
    tokens, size = k_refs[0].shape[1:]
    rows = g_side_ref.shape[2]
    half_rows = tokens // 2
    per_group = rows // half_rows
    chunk = 512
    sign = signs(size)

    def span(index):
        return pl.ds(pl.multiple_of(index * chunk, chunk), chunk)

    for block in range(blocks):
        at = pl.ds(block * tokens, tokens)
        for group in range(groups):
            val_ref[group, at, :size] = v_refs[block][first + group]
            val_ref[group, at, size:] = jnp.ones((tokens, size), BF16)
            high, low = split(nt(sign, k_refs[block][first + group]) * (1.0 / size))
            back_ref[group, :size, at] = high
            back_ref[group, size:, at] = low

    for half in range(2):
        results = []
        for group in range(groups):
            g_side = g_side_ref.at[half, first + group]
            row_at = pl.ds(half * rows, rows)

            def grads(index, dq, group=group, g_side=g_side, row_at=row_at):
                change = nt(val_ref[group, span(index), :], g_side[...])
                probs = probs_ref[group, span(index), row_at].astype(F32)
                dscore = (probs * change).astype(BF16)
                dscore_ref[group, span(index), row_at] = dscore
                return dq + nn(back_ref[group, :, span(index)], dscore)

            dq = chunked(keys, chunk, grads, jnp.zeros((2 * size, rows), F32))
            dq = (dq[:size] + dq[size:]).T + g_side[:, :size].astype(F32)
            results.append(dq.reshape(half_rows, per_group, size))
        at = pl.ds(half * half_rows, half_rows)
        handed_ref[at] = jnp.concatenate(results, axis=1).astype(BF16)


def dk_kernel(stages, q_side_ref, *refs):
    dscore_refs, sum_refs = refs[:stages], refs[stages:]
    tokens, size = sum_refs[0].shape[1:]
    rows = q_side_ref.shape[2]
    sign = signs(size)
    chunk = 512
    per_stage, keys, _ = dscore_refs[0].shape
    for row in range(0, keys, chunk):
        for group in range(stages * per_stage):
            dk = None
            for half in range(2):
                dscore = dscore_refs[group // per_stage].at[group % per_stage]
                dscore = dscore[pl.ds(row, chunk), pl.ds(half * rows, rows)]
                part = nn(dscore, q_side_ref[half, group, :, :size])
                dk = part if dk is None else dk + part
            high, low = split(dk)
            dk = ((nn(high, sign) + nn(low, sign)) * (1.0 / size)).astype(BF16)
            for at in range(0, chunk, tokens):
                sum_refs[(row + at) // tokens][group] = dk[at : at + tokens]


VMEM = pl.BlockSpec(memory_space=pltpu.VMEM)
HBM = pl.BlockSpec(memory_space=pltpu.HBM)
DMA = pltpu.SemaphoreType.DMA
SMEM = pl.BlockSpec(memory_space=pltpu.SMEM)


def call(kernel, name, outs, scratch, limit, work, args, smem=False):
    shapes = [jax.ShapeDtypeStruct(*out) for out in outs]
    return pl.pallas_call(
        kernel,
        in_specs=([SMEM] if smem else []) + [VMEM] * (len(args) - smem),
        out_specs=[VMEM] * len(outs),
        out_shape=shapes,
        scratch_shapes=scratch,
        compiler_params=pltpu.CompilerParams(vmem_limit_bytes=limit * 2**20),
        cost_estimate=pl.CostEstimate(flops=work, bytes_accessed=2**16, transcendentals=0),
        name=name,
    )(*args)


def in_hbm(value):
    return pltpu.with_memory_space_constraint(value, pltpu.HBM)


def make_sides(groups, queries, grads, saved):
    tokens, heads, size = queries.shape
    half_rows = tokens // 2
    rows = half_rows * heads // groups
    shape = jax.ShapeDtypeStruct((2, groups, rows, 2 * size), BF16)
    return pl.pallas_call(
        functools.partial(sides_kernel, groups),
        in_specs=[HBM] * 3,
        out_specs=[VMEM] * 2,
        out_shape=[shape] * 2,
        scratch_shapes=[pltpu.VMEM((2, 3, half_rows, heads, size), BF16), DMA((6,))],
        compiler_params=pltpu.CompilerParams(vmem_limit_bytes=24 * 2**20),
        cost_estimate=pl.CostEstimate(flops=WORK, bytes_accessed=2**16, transcendentals=0),
        name="query_sides",
    )(in_hbm(queries), in_hbm(grads), in_hbm(saved))


def shards(queries, key_heads, value_heads, forward_out, output_grad, block_order):
    _, tokens, groups, size = key_heads.shape
    q_heads = queries.shape[2]
    per_group = q_heads // groups
    per_stage = groups // STAGES
    blocks = lax.axis_size("ctx")
    keys = blocks * tokens
    rows = tokens // 2 * per_group
    probs_type = F32 if keys <= 1024 else BF16
    packed = ((groups, tokens, size), BF16)
    part = ((per_stage, tokens, size), BF16)
    flat = ((tokens * groups, size), BF16)
    rows_scratch = pltpu.VMEM(*flat[:1], F32)
    limit = 12 + keys // 64
    after = lax.optimization_barrier
    k_block, v_block = pl.pallas_call(
        prep_kernel,
        in_specs=[HBM] * 2,
        out_specs=[VMEM] * 2,
        out_shape=[jax.ShapeDtypeStruct(*packed)] * 2,
        scratch_shapes=[rows_scratch, pltpu.VMEM(*flat), pltpu.VMEM(*flat), DMA((2,))],
        compiler_params=pltpu.CompilerParams(vmem_limit_bytes=8 * 2**20),
        cost_estimate=pl.CostEstimate(flops=WORK, bytes_accessed=2**16, transcendentals=0),
        name="pack_keys",
    )(in_hbm(key_heads.reshape(-1, size)), in_hbm(value_heads.reshape(-1, size)))

    q_side, g_side = make_sides(groups, queries[0], output_grad[0], forward_out[0])
    k_all = gather(k_block, "ctx", (q_side, g_side))
    v_block, _ = after((v_block, (k_all[1], k_all[-1], q_side)))

    probs, dv_parts = [], []
    for stage in range(STAGES):
        stage_probs, *parts = call(
            functools.partial(weights_kernel, stage * per_stage, blocks),
            "weights",
            [((per_stage, keys, 2 * rows), probs_type)] + [part] * blocks,
            [
                pltpu.VMEM((2, keys, rows), F32),
                pltpu.VMEM((2, per_stage, keys, 2 * size), BF16),
            ],
            limit,
            BIG_WORK,
            [block_order, q_side, g_side, *k_all],
            True,
        )
        if stage == 0:
            v_all = gather(v_block, "ctx", stage_probs)
            q_side, _ = after((q_side, stage_probs))
        probs.append(stage_probs)
        dv_parts.append(parts)
    dv_parts = [jnp.concatenate(parts, axis=0) for parts in zip(*dv_parts)]

    handed, dscores = [], []
    for stage in range(STAGES):
        handed_part, dscore = call(
            functools.partial(dq_kernel, stage * per_stage, blocks),
            "query_grads",
            [((tokens, per_stage * per_group, size), BF16)]
            + [((per_stage, keys, 2 * rows), BF16)],
            [
                pltpu.VMEM((per_stage, keys, 2 * size), BF16),
                pltpu.VMEM((per_stage, 2 * size, keys), BF16),
            ],
            limit,
            BIG_WORK,
            [g_side, probs[stage], *k_all, *v_all],
        )
        if stage == 0:
            g_side, _ = after((g_side, handed_part))
        handed.append(passed_down(handed_part, "pipe"))
        dscores.append(dscore)
    dv_terms, dv_relayed = scatter_sums(dv_parts, "ctx", ())
    dscores, _ = after((dscores, (dv_relayed, dv_terms[-1])))
    dk_parts = call(
        functools.partial(dk_kernel, STAGES),
        "key_grads",
        [packed] * blocks,
        [],
        limit,
        WORK,
        [q_side, *dscores],
    )
    dk_terms, _ = scatter_sums(dk_parts, "ctx", ())
    key_grad, value_grad = call(
        functools.partial(finish_kernel, len(dk_terms)),
        "lay_out",
        [flat, flat],
        [rows_scratch],
        8,
        WORK,
        [*dk_terms, *dv_terms],
    )
    handed = jnp.concatenate(handed, axis=1)[None]
    last = lax.axis_index("pipe") == lax.axis_size("pipe") - 1
    shape = key_heads.shape
    return (
        key_grad.reshape(shape),
        value_grad.reshape(shape),
        jnp.where(last, jnp.zeros_like(handed), handed),
    )


def solution(mesh):
    placed = P("pipe", "ctx", "head", None)
    return jax.shard_map(
        shards,
        mesh=mesh,
        in_specs=(placed,) * 5 + (P(),),
        out_specs=(placed,) * 3,
        check_vma=False,
    )
```

time: 56.8 us -> 56.7 us (level)
  waiting for transfers between devices: 10.5 us -> 6.94 us
  starting transfers between devices: 27.5 us -> 30.1 us
  Pallas kernels: 16.6 us -> 17.4 us
    ppermute x12, waiting for transfers between devices: 10.3 us -> 6.93 us  [passed(): lax.ppermute(value, axis, [(order[at], order[(at + step) % count]) for at...]
    ppermute x12, starting transfers between devices: 25 us -> 27 us  [passed(): lax.ppermute(value, axis, [(order[at], order[(at + step) % count]) for at...]
    pallas_call x5 -> x6, Pallas kernels: 11.9 us -> 13.8 us  [call(): pl.pallas_call(kernel, in_specs=([SMEM] if smem else []) + [VMEM] * (len(...]
    select_n x0 -> x1, other arithmetic: none -> 1.18 us  [shards(): jnp.where(last, jnp.zeros_like(handed), handed)]
    pallas_call x3 -> x2, Pallas kernels: 4.69 us -> 3.63 us  [the longest x1 2.48 us: make_sides(): pl.pallas_call(functools.partial(sides_kernel, groups), in_specs=[HBM] *...]
    broadcast_in_dim x1 -> x0, other arithmetic: 1.05 us -> none  [shards(): jnp.concatenate(handed, axis=1)[None]]
  transfers between devices with their start and end apart: 14 -> 14, of which waited for: 8 -> 5; matrix products, arithmetic and copies ran while one was open for 2% -> 0% of each run, Pallas kernels for 26% -> 29%
where the time goes in v2:
time: 56.7 us; the launch traced here: 56.6 us
  starting transfers between devices  30.1 us (53%)
  Pallas kernels  17.4 us (31%)
  waiting for transfers between devices  6.94 us (12%)
  other arithmetic  1.3 us (2%)
  between operations  0.77 us (1%)
    ppermute x12, starting transfers between devices, passed(): lax.ppermute(value, axis, [(order[at], order[(at + step) % count]) for at...  27 us
    pallas_call x6, Pallas kernels, call(): pl.pallas_call(kernel, in_specs=([SMEM] if smem else []) + [VMEM] * (len(...  13.8 us
    ppermute x12, waiting for transfers between devices, passed(): lax.ppermute(value, axis, [(order[at], order[(at + step) % count]) for at...  6.93 us
    ppermute x2, starting transfers between devices, passed_down(): lax.ppermute(value, axis, [(at, (at - 1) % count) for at in range(count)])  3.09 us
    pallas_call x1, Pallas kernels, make_sides(): pl.pallas_call(functools.partial(sides_kernel, groups), in_specs=[HBM] *...  2.48 us
    select_n x1, other arithmetic, shards(): jnp.where(last, jnp.zeros_like(handed), handed)  1.18 us
    pallas_call x1, Pallas kernels, shards(): pl.pallas_call(prep_kernel, in_specs=[HBM] * 2, out_specs=[VMEM] * 2, out...  1.15 us
  transfers between devices with their start and end apart: 14, of which 5 were waited for; matrix products, arithmetic and copies ran while one was open for 0% of the time, Pallas kernels for 29%

profile of v2, /device:TPU:0, one launch (start us, length us, event | category | flops | bytes accessed | tf_op | source)
XLA Modules:
  0.0 56.6 jit_solution(10442318523861114282)
XLA Ops:
  0.6 0.0 copy-start
  0.6 1.1 %pack_keys.1 = (bf16[4,128,128]{2,1,0:T(8,128)(2,1)S(1)}, bf16[4,128,128]{2,1,0:T(8,128)(2,1)S(1)}) custom-call(bf16[512,128]{1,0:T(8,128)(2,1)} %bitcast.14, bf16[512,128]{1,0:T(8,128)(2,1)} %bitcast.15), custom_call_target="tpu_custom_call" | custom-call | flops 1048576 | bytes 65536 | tf_op jit(solution)/shard_map/pack_keys/pallas_call | solution.py:374
  1.8 3.1 %collective-permute-start = (bf16[4,128,128]{2,1,0:T(8,128)(2,1)S(1)}, bf16[4,128,128]{2,1,0:T(8,128)(2,1)S(1)}, u32[]{:S(2)}, u32[]{:S(2)}) collective-permute-start(bf16[4,128,128]{2,1,0:T(8,128)(2,1)S(1)} %get-tuple-element.36.refs_0_), channel_id=1, source_target_pairs={{0,2},{2,6},{6,4},{4,0},{1,3},{3,7},{7,5},{5,1},{8,10},{10,14},{14... | collective-permute-start | bytes 393224 | tf_op jit(solution)/shard_map/ppermute | solution.py:93
  4.9 1.1 %collective-permute-start.2 = (bf16[4,128,128]{2,1,0:T(8,128)(2,1)S(1)}, bf16[4,128,128]{2,1,0:T(8,128)(2,1)S(1)}, u32[]{:S(2)}, u32[]{:S(2)}) collective-permute-start(bf16[4,128,128]{2,1,0:T(8,128)(2,1)S(1)} %get-tuple-element.36.refs_0_), channel_id=1, source_target_pairs={{0,4},{2,0},{6,2},{4,6},{1,5},{3,1},{7,3},{5,7},{8,12},{10,8},{14,... | collective-permute-start | bytes 393224 | tf_op jit(solution)/shard_map/ppermute | solution.py:93
  6.0 2.5 %query_sides.1 = (bf16[2,4,512,256]{3,2,1,0:T(8,128)(2,1)S(1)}, bf16[2,4,512,256]{3,2,1,0:T(8,128)(2,1)S(1)}) custom-call(bf16[128,32,128]{2,1,0:T(8,128)(2,1)} %bitcast.9, bf16[128,32,128]{2,1,0:T(8,128)(2,1)} %bitcast.10, bf16[128,32,128]{2,1,0:T(8,128)(2,1)} %bitcast.11), custom_call_target="tpu_custom_call" | custom-call | flops 1048576 | bytes 65536 | tf_op jit(solution)/shard_map/query_sides/pallas_call | solution.py:347
  8.4 1.0 %collective-permute-done.refs_1_ = bf16[4,128,128]{2,1,0:T(8,128)(2,1)S(1)} collective-permute-done((bf16[4,128,128]{2,1,0:T(8,128)(2,1)S(1)}, bf16[4,128,128]{2,1,0:T(8,128)(2,1)S(1)}, u32[]{:S(2)}, u32[]{:S(2)}) %collective-permute-start) | collective-permute-done | bytes 131104 | tf_op jit(solution)/shard_map/ppermute | solution.py:93
  9.5 3.5 %collective-permute-start.1 = (bf16[4,128,128]{2,1,0:T(8,128)(2,1)S(1)}, bf16[4,128,128]{2,1,0:T(8,128)(2,1)S(1)}, u32[]{:S(2)}, u32[]{:S(2)}) collective-permute-start(bf16[4,128,128]{2,1,0:T(8,128)(2,1)S(1)} %collective-permute-done.refs_1_), channel_id=1, source_target_pairs={{0,2},{2,6},{6,4},{4,0},{1,3},{3,7},{7,5},{5,1},{8,10},{10,14},{14... | collective-permute-start | bytes 393224 | tf_op jit(solution)/shard_map/ppermute | solution.py:93
  13.0 0.0 collective-permute-done.2.refs_3_
  13.0 3.4 %collective-permute-start.3 = (bf16[4,128,128]{2,1,0:T(8,128)(2,1)S(1)}, bf16[4,128,128]{2,1,0:T(8,128)(2,1)S(1)}, u32[]{:S(2)}, u32[]{:S(2)}) collective-permute-start(bf16[4,128,128]{2,1,0:T(8,128)(2,1)S(1)} %get-tuple-element.41.refs_4_), channel_id=1, source_target_pairs={{0,2},{2,6},{6,4},{4,0},{1,3},{3,7},{7,5},{5,1},{8,10},{10,14},{14... | collective-permute-start | bytes 393224 | tf_op jit(solution)/shard_map/ppermute | solution.py:93
  16.4 0.0 collective-permute-start.5
  16.4 0.2 collective-permute-done.1.refs_2_
  16.6 0.0 copy-done
  16.6 3.2 %weights.2 = (f32[2,512,1024]{2,1,0:T(8,128)S(1)}, bf16[2,128,128]{2,1,0:T(8,128)(2,1)S(1)}, bf16[2,128,128]{2,1,0:T(8,128)(2,1)S(1)}, bf16[2,128,128]{2,1,0:T(8,128)(2,1)S(1)}, bf16[2,128,128]{2,1,0:T(8,128)(2,1)S(1)}) custom-call(s32[8]{0:T(128)S(1)} %copy-done, bf16[2,4,512,256]{3,2,1,0:T(8,128)(2,1)S(1)} %get-tuple-element.39.q_side_ref, ...), custom_call_target="tpu_custom_call" | custom-call | flops 4294967296 | bytes 65536 | tf_op jit(solution)/shard_map/weights/pallas_call | solution.py:326
  19.8 0.0 collective-permute-done.3.refs_5_
  19.8 5.0 %collective-permute-start.4 = (bf16[4,128,128]{2,1,0:T(8,128)(2,1)S(1)}, bf16[4,128,128]{2,1,0:T(8,128)(2,1)S(1)}, u32[]{:S(2)}, u32[]{:S(2)}) collective-permute-start(bf16[4,128,128]{2,1,0:T(8,128)(2,1)S(1)} %collective-permute-done.3.refs_5_), channel_id=1, source_target_pairs={{0,2},{2,6},{6,4},{4,0},{1,3},{3,7},{7,5},{5,1},{8,10},{10,14},{14... | collective-permute-start | bytes 393224 | tf_op jit(solution)/shard_map/ppermute | solution.py:93
  24.8 3.2 %weights.3 = (f32[2,512,1024]{2,1,0:T(8,128)S(1)}, bf16[2,128,128]{2,1,0:T(8,128)(2,1)S(1)}, bf16[2,128,128]{2,1,0:T(8,128)(2,1)S(1)}, bf16[2,128,128]{2,1,0:T(8,128)(2,1)S(1)}, bf16[2,128,128]{2,1,0:T(8,128)(2,1)S(1)}) custom-call(s32[8]{0:T(128)S(1)} %copy-done, bf16[2,4,512,256]{3,2,1,0:T(8,128)(2,1)S(1)} %get-tuple-element.39.q_side_ref, ...), custom_call_target="tpu_custom_call" | custom-call | flops 4294967296 | bytes 65536 | tf_op jit(solution)/shard_map/weights/pallas_call | solution.py:326
  28.0 4.8 %collective-permute-start.6 = (bf16[4,128,128]{2,1,0:T(8,128)(2,1)S(1)}, bf16[4,128,128]{2,1,0:T(8,128)(2,1)S(1)}, u32[]{:S(2)}, u32[]{:S(2)}) collective-permute-start(bf16[4,128,128]{2,1,0:T(8,128)(2,1)S(1)} %pad_maximum_fusion), channel_id=1, source_target_pairs={{0,2},{2,6},{6,4},{4,0},{1,3},{3,7},{7,5},{5,1},{8,10},{10,14},{14... | collective-permute-start | bytes 393224 | tf_op jit(solution)/shard_map/ppermute | solution.py:93
  32.8 0.1 collective-permute-start.7
  32.8 0.0 collective-permute-done.5.refs_7_
  32.8 0.0 collective-permute-done.4.refs_6_
  32.9 1.9 %query_grads.2 = (bf16[128,16,128]{2,1,0:T(8,128)(2,1)S(1)}, bf16[2,512,1024]{2,1,0:T(8,128)(2,1)S(1)}) custom-call(bf16[2,4,512,256]{3,2,1,0:T(8,128)(2,1)S(1)} %get-tuple-element.45.g_side_ref, f32[2,512,1024]{2,1,0:T(8,128)S(1)} %get-tuple-element.38.probs_ref, bf16[4,128,128]{2,1,0:T(8,128)(2,1)S(1)} %get-tuple-element.36.refs_0_, ...), custom_call_target="tpu_custom_call" | custom-call | flops 4294967296 | bytes 65536 | tf_op jit(solution)/shard_map/query_grads/pallas_call | solution.py:326
  34.8 2.5 %collective-permute-start.12 = (bf16[128,16,128]{2,1,0:T(8,128)(2,1)S(1)}, bf16[128,16,128]{2,1,0:T(8,128)(2,1)S(1)}, u32[]{:S(2)}, u32[]{:S(2)}) collective-permute-start(bf16[128,16,128]{2,1,0:T(8,128)(2,1)S(1)} %get-tuple-element.44), channel_id=1, source_target_pairs={{0,24},{8,0},{16,8},{24,16},{1,25},{9,1},{17,9},{25,17},{2,26},{10... | collective-permute-start | bytes 1572872 | tf_op jit(solution)/shard_map/ppermute | solution.py:117
  37.3 1.9 %query_grads.3 = (bf16[128,16,128]{2,1,0:T(8,128)(2,1)S(1)}, bf16[2,512,1024]{2,1,0:T(8,128)(2,1)S(1)}) custom-call(bf16[2,4,512,256]{3,2,1,0:T(8,128)(2,1)S(1)} %get-tuple-element.45.g_side_ref, f32[2,512,1024]{2,1,0:T(8,128)S(1)} %get-tuple-element.46.probs_ref, bf16[4,128,128]{2,1,0:T(8,128)(2,1)S(1)} %get-tuple-element.36.refs_0_, ...), custom_call_target="tpu_custom_call" | custom-call | flops 4294967296 | bytes 65536 | tf_op jit(solution)/shard_map/query_grads/pallas_call | solution.py:326
  39.2 0.6 %collective-permute-start.13 = (bf16[128,16,128]{2,1,0:T(8,128)(2,1)S(1)}, bf16[128,16,128]{2,1,0:T(8,128)(2,1)S(1)}, u32[]{:S(2)}, u32[]{:S(2)}) collective-permute-start(bf16[128,16,128]{2,1,0:T(8,128)(2,1)S(1)} %get-tuple-element.64), channel_id=1, source_target_pairs={{0,24},{8,0},{16,8},{24,16},{1,25},{9,1},{17,9},{25,17},{2,26},{10... | collective-permute-start | bytes 1572872 | tf_op jit(solution)/shard_map/ppermute | solution.py:117
  39.8 0.0 collective-permute-done.6
  39.8 0.0 collective-permute-done.7.refs_5_
  39.8 2.9 %key_grads.1 = (bf16[4,128,128]{2,1,0:T(8,128)(2,1)S(1)}, bf16[4,128,128]{2,1,0:T(8,128)(2,1)S(1)}, bf16[4,128,128]{2,1,0:T(8,128)(2,1)S(1)}, bf16[4,128,128]{2,1,0:T(8,128)(2,1)S(1)}) custom-call(bf16[2,4,512,256]{3,2,1,0:T(8,128)(2,1)S(1)} %get-tuple-element.39.q_side_ref, bf16[2,512,1024]{2,1,0:T(8,128)(2,1)S(1)} %get-tuple-element.54.refs_0_, ...), custom_call_target="tpu_custom_call" | custom-call | flops 1048576 | bytes 65536 | tf_op jit(solution)/shard_map/key_grads/pallas_call | solution.py:326
  42.7 2.0 %collective-permute-start.8 = (bf16[4,128,128]{2,1,0:T(8,128)(2,1)S(1)}, bf16[4,128,128]{2,1,0:T(8,128)(2,1)S(1)}, u32[]{:S(2)}, u32[]{:S(2)}) collective-permute-start(bf16[4,128,128]{2,1,0:T(8,128)(2,1)S(1)} %get-tuple-element.57), channel_id=1, source_target_pairs={{0,2},{2,6},{6,4},{4,0},{1,3},{3,7},{7,5},{5,1},{8,10},{10,14},{14... | collective-permute-start | bytes 393224 | tf_op jit(solution)/shard_map/ppermute | solution.py:93
  44.7 1.9 %collective-permute-start.11 = (bf16[4,128,128]{2,1,0:T(8,128)(2,1)S(1)}, bf16[4,128,128]{2,1,0:T(8,128)(2,1)S(1)}, u32[]{:S(2)}, u32[]{:S(2)}) collective-permute-start(bf16[4,128,128]{2,1,0:T(8,128)(2,1)S(1)} %add_convert_fusion.1), channel_id=1, source_target_pairs={{0,2},{2,6},{6,4},{4,0},{1,3},{3,7},{7,5},{5,1},{8,10},{10,14},{14... | collective-permute-start | bytes 393224 | tf_op jit(solution)/shard_map/ppermute | solution.py:93
  46.7 1.0 %collective-permute-start.10 = (bf16[4,128,128]{2,1,0:T(8,128)(2,1)S(1)}, bf16[4,128,128]{2,1,0:T(8,128)(2,1)S(1)}, u32[]{:S(2)}, u32[]{:S(2)}) collective-permute-start(bf16[4,128,128]{2,1,0:T(8,128)(2,1)S(1)} %get-tuple-element.59), channel_id=1, source_target_pairs={{0,4},{2,0},{6,2},{4,6},{1,5},{3,1},{7,3},{5,7},{8,12},{10,8},{14,... | collective-permute-start | bytes 393224 | tf_op jit(solution)/shard_map/ppermute | solution.py:93
  47.7 0.9 %collective-permute-done.8 = bf16[4,128,128]{2,1,0:T(8,128)(2,1)S(1)} collective-permute-done((bf16[4,128,128]{2,1,0:T(8,128)(2,1)S(1)}, bf16[4,128,128]{2,1,0:T(8,128)(2,1)S(1)}, u32[]{:S(2)}, u32[]{:S(2)}) %collective-permute-start.8) | collective-permute-done | bytes 131104 | tf_op jit(solution)/shard_map/ppermute | solution.py:93
  48.7 1.1 %collective-permute-start.9 = (bf16[4,128,128]{2,1,0:T(8,128)(2,1)S(1)}, bf16[4,128,128]{2,1,0:T(8,128)(2,1)S(1)}, u32[]{:S(2)}, u32[]{:S(2)}) collective-permute-start(bf16[4,128,128]{2,1,0:T(8,128)(2,1)S(1)} %add_convert_fusion), channel_id=1, source_target_pairs={{0,2},{2,6},{6,4},{4,0},{1,3},{3,7},{7,5},{5,1},{8,10},{10,14},{14... | collective-permute-start | bytes 393224 | tf_op jit(solution)/shard_map/ppermute | solution.py:93
  49.8 2.2 %collective-permute-done.10.refs_2_ = bf16[4,128,128]{2,1,0:T(8,128)(2,1)S(1)} collective-permute-done((bf16[4,128,128]{2,1,0:T(8,128)(2,1)S(1)}, bf16[4,128,128]{2,1,0:T(8,128)(2,1)S(1)}, u32[]{:S(2)}, u32[]{:S(2)}) %collective-permute-start.10) | collective-permute-done | bytes 131104 | tf_op jit(solution)/shard_map/ppermute | solution.py:93
  52.0 0.0 collective-permute-done.11.refs_4_
  52.0 2.6 %collective-permute-done.9.refs_1_ = bf16[4,128,128]{2,1,0:T(8,128)(2,1)S(1)} collective-permute-done((bf16[4,128,128]{2,1,0:T(8,128)(2,1)S(1)}, bf16[4,128,128]{2,1,0:T(8,128)(2,1)S(1)}, u32[]{:S(2)}, u32[]{:S(2)}) %collective-permute-start.9) | collective-permute-done | bytes 131104 | tf_op jit(solution)/shard_map/ppermute | solution.py:93
  54.6 0.8 %lay_out.1 = (bf16[512,128]{1,0:T(8,128)(2,1)}, bf16[512,128]{1,0:T(8,128)(2,1)}) custom-call(bf16[4,128,128]{2,1,0:T(8,128)(2,1)S(1)} %get-tuple-element.56.refs_0_, bf16[4,128,128]{2,1,0:T(8,128)(2,1)S(1)} %collective-permute-done.9.refs_1_, bf16[4,128,128]{2,1,0:T(8,128)(2,1)S(1)} %collective-permute-done.10.refs_2_, ...), custom_call_target="tpu_custom_call" | custom-call | flops 1048576 | bytes 65536 | tf_op jit(solution)/shard_map/lay_out/pallas_call | solution.py:326
  55.4 0.0 collective-permute-done.13
  55.4 0.0 collective-permute-done.12
  55.4 1.2 %maximum_select_fusion = bf16[1,128,32,128]{3,2,1,0:T(8,128)(2,1)} fusion(bf16[1,128,16,128]{3,2,1,0:T(8,128)(2,1)S(1)} %bitcast.13, bf16[1,128,16,128]{3,2,1,0:T(8,128)(2,1)S(1)} %bitcast.12, pred[]{:T(512)S(6)} %eq.3), kind=kLoop, calls=%fused_computation | loop fusion | flops 2621440 | bytes 2097153 | tf_op jit(solution)/shard_map/jit(_where)/select_n | solution.py:457
  (5 shorter events, 0.1 us)
Async XLA Ops:
  0.6 16.0 %copy-start = (s32[8]{0:T(128)S(1)}, s32[8]{0:T(128)}, u32[]{:S(2)}) copy-start(s32[8]{0:T(128)} %order_ref.3) | copy-start | bytes 100
  1.8 7.7 %collective-permute-start = (bf16[4,128,128]{2,1,0:T(8,128)(2,1)S(1)}, bf16[4,128,128]{2,1,0:T(8,128)(2,1)S(1)}, u32[]{:S(2)}, u32[]{:S(2)}) collective-permute-start(bf16[4,128,128]{2,1,0:T(8,128)(2,1)S(1)} %get-tuple-element.36.refs_0_), channel_id=1, source_target_pairs={{0,2},{2,6},{6,4},{4,0},{1,3},{3,7},{7,5},{5,1},{8,10},{10,14},{14... | collective-permute-start | bytes 393224 | tf_op jit(solution)/shard_map/ppermute | solution.py:93
  4.9 8.2 %collective-permute-start.2 = (bf16[4,128,128]{2,1,0:T(8,128)(2,1)S(1)}, bf16[4,128,128]{2,1,0:T(8,128)(2,1)S(1)}, u32[]{:S(2)}, u32[]{:S(2)}) collective-permute-start(bf16[4,128,128]{2,1,0:T(8,128)(2,1)S(1)} %get-tuple-element.36.refs_0_), channel_id=1, source_target_pairs={{0,4},{2,0},{6,2},{4,6},{1,5},{3,1},{7,3},{5,7},{8,12},{10,8},{14,... | collective-permute-start | bytes 393224 | tf_op jit(solution)/shard_map/ppermute | solution.py:93
  9.5 7.1 %collective-permute-start.1 = (bf16[4,128,128]{2,1,0:T(8,128)(2,1)S(1)}, bf16[4,128,128]{2,1,0:T(8,128)(2,1)S(1)}, u32[]{:S(2)}, u32[]{:S(2)}) collective-permute-start(bf16[4,128,128]{2,1,0:T(8,128)(2,1)S(1)} %collective-permute-done.refs_1_), channel_id=1, source_target_pairs={{0,2},{2,6},{6,4},{4,0},{1,3},{3,7},{7,5},{5,1},{8,10},{10,14},{14... | collective-permute-start | bytes 393224 | tf_op jit(solution)/shard_map/ppermute | solution.py:93
  13.0 6.8 %collective-permute-start.3 = (bf16[4,128,128]{2,1,0:T(8,128)(2,1)S(1)}, bf16[4,128,128]{2,1,0:T(8,128)(2,1)S(1)}, u32[]{:S(2)}, u32[]{:S(2)}) collective-permute-start(bf16[4,128,128]{2,1,0:T(8,128)(2,1)S(1)} %get-tuple-element.41.refs_4_), channel_id=1, source_target_pairs={{0,2},{2,6},{6,4},{4,0},{1,3},{3,7},{7,5},{5,1},{8,10},{10,14},{14... | collective-permute-start | bytes 393224 | tf_op jit(solution)/shard_map/ppermute | solution.py:93
  16.4 16.4 %collective-permute-start.5 = (bf16[4,128,128]{2,1,0:T(8,128)(2,1)S(1)}, bf16[4,128,128]{2,1,0:T(8,128)(2,1)S(1)}, u32[]{:S(2)}, u32[]{:S(2)}) collective-permute-start(bf16[4,128,128]{2,1,0:T(8,128)(2,1)S(1)} %get-tuple-element.41.refs_4_), channel_id=1, source_target_pairs={{0,4},{2,0},{6,2},{4,6},{1,5},{3,1},{7,3},{5,7},{8,12},{10,8},{14,... | collective-permute-start | bytes 393224 | tf_op jit(solution)/shard_map/ppermute | solution.py:93
  19.8 13.0 %collective-permute-start.4 = (bf16[4,128,128]{2,1,0:T(8,128)(2,1)S(1)}, bf16[4,128,128]{2,1,0:T(8,128)(2,1)S(1)}, u32[]{:S(2)}, u32[]{:S(2)}) collective-permute-start(bf16[4,128,128]{2,1,0:T(8,128)(2,1)S(1)} %collective-permute-done.3.refs_5_), channel_id=1, source_target_pairs={{0,2},{2,6},{6,4},{4,0},{1,3},{3,7},{7,5},{5,1},{8,10},{10,14},{14... | collective-permute-start | bytes 393224 | tf_op jit(solution)/shard_map/ppermute | solution.py:93
  28.0 11.8 %collective-permute-start.6 = (bf16[4,128,128]{2,1,0:T(8,128)(2,1)S(1)}, bf16[4,128,128]{2,1,0:T(8,128)(2,1)S(1)}, u32[]{:S(2)}, u32[]{:S(2)}) collective-permute-start(bf16[4,128,128]{2,1,0:T(8,128)(2,1)S(1)} %pad_maximum_fusion), channel_id=1, source_target_pairs={{0,2},{2,6},{6,4},{4,0},{1,3},{3,7},{7,5},{5,1},{8,10},{10,14},{14... | collective-permute-start | bytes 393224 | tf_op jit(solution)/shard_map/ppermute | solution.py:93
  32.8 7.0 %collective-permute-start.7 = (bf16[4,128,128]{2,1,0:T(8,128)(2,1)S(1)}, bf16[4,128,128]{2,1,0:T(8,128)(2,1)S(1)}, u32[]{:S(2)}, u32[]{:S(2)}) collective-permute-start(bf16[4,128,128]{2,1,0:T(8,128)(2,1)S(1)} %pad_maximum_fusion.1), channel_id=1, source_target_pairs={{0,4},{2,0},{6,2},{4,6},{1,5},{3,1},{7,3},{5,7},{8,12},{10,8},{14,... | collective-permute-start | bytes 393224 | tf_op jit(solution)/shard_map/ppermute | solution.py:93
  34.8 20.6 %collective-permute-start.12 = (bf16[128,16,128]{2,1,0:T(8,128)(2,1)S(1)}, bf16[128,16,128]{2,1,0:T(8,128)(2,1)S(1)}, u32[]{:S(2)}, u32[]{:S(2)}) collective-permute-start(bf16[128,16,128]{2,1,0:T(8,128)(2,1)S(1)} %get-tuple-element.44), channel_id=1, source_target_pairs={{0,24},{8,0},{16,8},{24,16},{1,25},{9,1},{17,9},{25,17},{2,26},{10... | collective-permute-start | bytes 1572872 | tf_op jit(solution)/shard_map/ppermute | solution.py:117
  39.2 16.2 %collective-permute-start.13 = (bf16[128,16,128]{2,1,0:T(8,128)(2,1)S(1)}, bf16[128,16,128]{2,1,0:T(8,128)(2,1)S(1)}, u32[]{:S(2)}, u32[]{:S(2)}) collective-permute-start(bf16[128,16,128]{2,1,0:T(8,128)(2,1)S(1)} %get-tuple-element.64), channel_id=1, source_target_pairs={{0,24},{8,0},{16,8},{24,16},{1,25},{9,1},{17,9},{25,17},{2,26},{10... | collective-permute-start | bytes 1572872 | tf_op jit(solution)/shard_map/ppermute | solution.py:117
  42.7 5.9 %collective-permute-start.8 = (bf16[4,128,128]{2,1,0:T(8,128)(2,1)S(1)}, bf16[4,128,128]{2,1,0:T(8,128)(2,1)S(1)}, u32[]{:S(2)}, u32[]{:S(2)}) collective-permute-start(bf16[4,128,128]{2,1,0:T(8,128)(2,1)S(1)} %get-tuple-element.57), channel_id=1, source_target_pairs={{0,2},{2,6},{6,4},{4,0},{1,3},{3,7},{7,5},{5,1},{8,10},{10,14},{14... | collective-permute-start | bytes 393224 | tf_op jit(solution)/shard_map/ppermute | solution.py:93
  44.7 7.3 %collective-permute-start.11 = (bf16[4,128,128]{2,1,0:T(8,128)(2,1)S(1)}, bf16[4,128,128]{2,1,0:T(8,128)(2,1)S(1)}, u32[]{:S(2)}, u32[]{:S(2)}) collective-permute-start(bf16[4,128,128]{2,1,0:T(8,128)(2,1)S(1)} %add_convert_fusion.1), channel_id=1, source_target_pairs={{0,2},{2,6},{6,4},{4,0},{1,3},{3,7},{7,5},{5,1},{8,10},{10,14},{14... | collective-permute-start | bytes 393224 | tf_op jit(solution)/shard_map/ppermute | solution.py:93
  46.7 5.3 %collective-permute-start.10 = (bf16[4,128,128]{2,1,0:T(8,128)(2,1)S(1)}, bf16[4,128,128]{2,1,0:T(8,128)(2,1)S(1)}, u32[]{:S(2)}, u32[]{:S(2)}) collective-permute-start(bf16[4,128,128]{2,1,0:T(8,128)(2,1)S(1)} %get-tuple-element.59), channel_id=1, source_target_pairs={{0,4},{2,0},{6,2},{4,6},{1,5},{3,1},{7,3},{5,7},{8,12},{10,8},{14,... | collective-permute-start | bytes 393224 | tf_op jit(solution)/shard_map/ppermute | solution.py:93
  48.7 5.9 %collective-permute-start.9 = (bf16[4,128,128]{2,1,0:T(8,128)(2,1)S(1)}, bf16[4,128,128]{2,1,0:T(8,128)(2,1)S(1)}, u32[]{:S(2)}, u32[]{:S(2)}) collective-permute-start(bf16[4,128,128]{2,1,0:T(8,128)(2,1)S(1)} %add_convert_fusion), channel_id=1, source_target_pairs={{0,2},{2,6},{6,4},{4,0},{1,3},{3,7},{7,5},{5,1},{8,10},{10,14},{14... | collective-permute-start | bytes 393224 | tf_op jit(solution)/shard_map/ppermute | solution.py:93

commit v3 on v2

--- a/solution.py
+++ b/solution.py
@@ -173,31 +173,25 @@
             g_side_ref[half, group, :, size:] = delta.astype(BF16)
 
 
-def chunked(keys, chunk, body, init):
-    if keys == chunk:
-        return body(0, init)
-    return lax.fori_loop(0, keys // chunk, body, init)
+def far_last(count):
+    return [step for step in range(count) if step != count // 2] + [count // 2]
 
 
 def weights_kernel(first, blocks, order_ref, q_side_ref, g_side_ref, *refs):
-    k_refs, probs_ref, sum_refs = refs[:blocks], refs[blocks], refs[blocks + 1 : 2 * blocks + 1]
-    score_ref, key_ref = refs[2 * blocks + 1 :]
-    groups, keys, _ = probs_ref.shape
+    k_refs, (weight_ref, scale_ref) = refs[:blocks], refs[blocks : blocks + 2]
+    sum_refs, key_ref = refs[blocks + 2 : 2 * blocks + 2], refs[-1]
+    groups, keys, _ = weight_ref.shape
     tokens, size = k_refs[0].shape[1:]
     place = lax.axis_index("ctx")
     ring = ring_place(blocks, place)
     rows = q_side_ref.shape[2]
     half_rows = tokens // 2
-    chunk = 512
     power = math.log2(math.e) / math.sqrt(size)
-
-    def span(index):
-        return pl.ds(pl.multiple_of(index * chunk, chunk), chunk)
 
     at_row = lax.broadcasted_iota(jnp.int32, (half_rows, size), 0)
     at_col = lax.broadcasted_iota(jnp.int32, (half_rows, size), 1)
-    for block in range(blocks):
-        source = ring_device(blocks, lax.rem(ring - block + blocks, blocks))
+    for block, distance in enumerate(far_last(blocks)):
+        source = ring_device(blocks, lax.rem(ring - distance + blocks, blocks))
         for half in range(2):
             q_start = order_ref[place * 2 + half]
             for k_half in range(2):
@@ -213,57 +207,56 @@
             for half in range(2):
                 key_ref[half, group, at, :size] = key
 
-    for group in range(groups):
-        for half in range(2):
-            q_side = q_side_ref.at[half, first + group]
-            row_at = pl.ds(half * rows, rows)
-
-            def scores(index, top, half=half, group=group, q_side=q_side):
-                part = nt(key_ref[half, group, span(index), :], q_side[...])
-                score_ref[half, span(index), :] = part
-                return jnp.maximum(top, jnp.max(part.reshape(chunk // 8, 8, rows), axis=0))
-
-            top = chunked(keys, chunk, scores, jnp.full((8, rows), NEG, F32))
-            top = jnp.max(top, axis=0, keepdims=True)
-
-            def weigh(index, total, half=half, top=top):
-                part = jnp.exp2((score_ref[half, span(index), :] - top) * power)
-                score_ref[half, span(index), :] = part
-                return total + jnp.sum(part.reshape(chunk // 8, 8, rows), axis=0)
-
-            total = chunked(keys, chunk, weigh, jnp.zeros((8, rows), F32))
+    chunk = 256
+    units = [(group, half) for group in range(groups) for half in range(2)]
+    tops, scales = {}, {}
+    for step in range(len(units) + 1):
+        top = total = None
+        for row in range(0, keys, chunk):
+            k_at = pl.ds(row, chunk)
+            if step < len(units):
+                group, half = units[step]
+                part = nt(key_ref[half, group, k_at, :], q_side_ref[half, first + group])
+                weight_ref[group, k_at, pl.ds(half * rows, rows)] = part
+                part = jnp.max(part.reshape(chunk // 8, 8, rows), axis=0)
+                top = part if top is None else jnp.maximum(top, part)
+            if step > 0:
+                group, half = units[step - 1]
+                part = weight_ref[group, k_at, pl.ds(half * rows, rows)]
+                part = jnp.exp2((part - tops[step - 1]) * power)
+                weight_ref[group, k_at, pl.ds(half * rows, rows)] = part
+                part = jnp.sum(part.reshape(chunk // 8, 8, rows), axis=0)
+                total = part if total is None else total + part
+        if step < len(units):
+            tops[step] = jnp.max(top, axis=0, keepdims=True)
+        if step > 0:
+            group, half = units[step - 1]
             scale = 1.0 / jnp.sum(total, axis=0, keepdims=True)
-
-            def settle(index, carried, half=half, group=group, scale=scale, row_at=row_at):
-                probs = score_ref[half, span(index), :] * scale
-                probs_ref[group, span(index), row_at] = probs.astype(probs_ref.dtype)
-                return carried
-
-            chunked(keys, chunk, settle, 0)
-        for row in range(0, keys, chunk):
+            scale_ref[group, :, pl.ds(half * rows, rows)] = jnp.broadcast_to(scale, (8, rows))
+            scales[half] = scale
+        if step == 0 or units[step - 1][1] == 0:
+            continue
+        for row in range(0, keys, 512):
             dv = None
             for half in range(2):
-                probs = probs_ref[group, pl.ds(row, chunk), pl.ds(half * rows, rows)]
+                probs = weight_ref[group, pl.ds(row, 512), pl.ds(half * rows, rows)] * scales[half]
                 part = nn(probs.astype(BF16), g_side_ref[half, first + group, :, :size])
                 dv = part if dv is None else dv + part
             dv = dv.astype(BF16)
-            for at in range(0, chunk, tokens):
+            for at in range(0, 512, tokens):
                 sum_refs[(row + at) // tokens][group] = dv[at : at + tokens]
 
 
-def dq_kernel(first, blocks, g_side_ref, probs_ref, *refs):
+def dq_kernel(first, blocks, g_side_ref, weight_ref, scale_ref, *refs):
     k_refs, v_refs = refs[:blocks], refs[blocks : 2 * blocks]
     handed_ref, dscore_ref, val_ref, back_ref = refs[2 * blocks :]
-    groups, keys, _ = probs_ref.shape
+    groups, keys, _ = weight_ref.shape
     tokens, size = k_refs[0].shape[1:]
     rows = g_side_ref.shape[2]
     half_rows = tokens // 2
     per_group = rows // half_rows
     chunk = 512
     sign = signs(size)
-
-    def span(index):
-        return pl.ds(pl.multiple_of(index * chunk, chunk), chunk)
 
     for block in range(blocks):
         at = pl.ds(block * tokens, tokens)
@@ -274,44 +267,53 @@
             back_ref[group, :size, at] = high
             back_ref[group, size:, at] = low
 
-    for half in range(2):
-        results = []
-        for group in range(groups):
-            g_side = g_side_ref.at[half, first + group]
-            row_at = pl.ds(half * rows, rows)
-
-            def grads(index, dq, group=group, g_side=g_side, row_at=row_at):
-                change = nt(val_ref[group, span(index), :], g_side[...])
-                probs = probs_ref[group, span(index), row_at].astype(F32)
-                dscore = (probs * change).astype(BF16)
-                dscore_ref[group, span(index), row_at] = dscore
-                return dq + nn(back_ref[group, :, span(index)], dscore)
-
-            dq = chunked(keys, chunk, grads, jnp.zeros((2 * size, rows), F32))
-            dq = (dq[:size] + dq[size:]).T + g_side[:, :size].astype(F32)
+    def change(unit, row):
+        half, group = unit
+        return nt(val_ref[group, pl.ds(row, chunk), :], g_side_ref[half, first + group])
+
+    units = [(half, group) for half in range(2) for group in range(groups)]
+    steps = [(unit, row) for unit in units for row in range(0, keys, chunk)]
+    ahead = change(*steps[0])
+    results, dq = [], None
+    for step, ((half, group), row) in enumerate(steps):
+        now = ahead
+        if step + 1 < len(steps):
+            ahead = change(*steps[step + 1])
+        k_at, row_at = pl.ds(row, chunk), pl.ds(half * rows, rows)
+        probs = weight_ref[group, k_at, row_at] * scale_ref[group, :1, row_at]
+        dscore = (probs * now).astype(BF16)
+        dscore_ref[group, k_at, row_at] = dscore
+        part = nn(back_ref[group, :, k_at], dscore)
+        dq = part if dq is None else dq + part
+        if row + chunk == keys:
+            dq = (dq[:size] + dq[size:]).T + g_side_ref[half, first + group, :, :size].astype(F32)
             results.append(dq.reshape(half_rows, per_group, size))
-        at = pl.ds(half * half_rows, half_rows)
-        handed_ref[at] = jnp.concatenate(results, axis=1).astype(BF16)
-
-
-def dk_kernel(stages, q_side_ref, *refs):
+            dq = None
+        if len(results) == groups:
+            at = pl.ds(half * half_rows, half_rows)
+            handed_ref[at] = jnp.concatenate(results, axis=1).astype(BF16)
+            results = []
+
+
+def dk_kernel(stages, start, q_side_ref, *refs):
     dscore_refs, sum_refs = refs[:stages], refs[stages:]
     tokens, size = sum_refs[0].shape[1:]
     rows = q_side_ref.shape[2]
-    sign = signs(size)
+    signs_twice = jnp.concatenate([signs(size)] * 2, axis=0)
     chunk = 512
-    per_stage, keys, _ = dscore_refs[0].shape
-    for row in range(0, keys, chunk):
+    per_stage = dscore_refs[0].shape[0]
+    count = len(sum_refs) * tokens
+    for row in range(0, count, chunk):
+        length = min(chunk, count - row)
         for group in range(stages * per_stage):
             dk = None
             for half in range(2):
                 dscore = dscore_refs[group // per_stage].at[group % per_stage]
-                dscore = dscore[pl.ds(row, chunk), pl.ds(half * rows, rows)]
+                dscore = dscore[pl.ds(start * tokens + row, length), pl.ds(half * rows, rows)]
                 part = nn(dscore, q_side_ref[half, group, :, :size])
                 dk = part if dk is None else dk + part
-            high, low = split(dk)
-            dk = ((nn(high, sign) + nn(low, sign)) * (1.0 / size)).astype(BF16)
-            for at in range(0, chunk, tokens):
+            dk = (nn(jnp.concatenate(split(dk), axis=1), signs_twice) * (1.0 / size)).astype(BF16)
+            for at in range(0, length, tokens):
                 sum_refs[(row + at) // tokens][group] = dk[at : at + tokens]
 
 
@@ -364,7 +366,6 @@
     blocks = lax.axis_size("ctx")
     keys = blocks * tokens
     rows = tokens // 2 * per_group
-    probs_type = F32 if keys <= 1024 else BF16
     packed = ((groups, tokens, size), BF16)
     part = ((per_stage, tokens, size), BF16)
     flat = ((tokens * groups, size), BF16)
@@ -382,32 +383,32 @@
         name="pack_keys",
     )(in_hbm(key_heads.reshape(-1, size)), in_hbm(value_heads.reshape(-1, size)))
 
-    q_side, g_side = make_sides(groups, queries[0], output_grad[0], forward_out[0])
-    k_all = gather(k_block, "ctx", (q_side, g_side))
-    v_block, _ = after((v_block, (k_all[1], k_all[-1], q_side)))
-
-    probs, dv_parts = [], []
+    k_all = gather(k_block, "ctx", ())
+    q_loads, _ = after((queries[0], k_all[1]))
+    q_side, g_side = make_sides(groups, q_loads, output_grad[0], forward_out[0])
+    v_block, _ = after((v_block, q_side))
+    v_all = gather(v_block, "ctx")
+    slots = far_last(blocks)
+    k_all, v_all = [k_all[step] for step in slots], [v_all[step] for step in slots]
+
+    weights, dv_parts = [], []
     for stage in range(STAGES):
-        stage_probs, *parts = call(
+        weight, scale, *parts = call(
             functools.partial(weights_kernel, stage * per_stage, blocks),
             "weights",
-            [((per_stage, keys, 2 * rows), probs_type)] + [part] * blocks,
-            [
-                pltpu.VMEM((2, keys, rows), F32),
-                pltpu.VMEM((2, per_stage, keys, 2 * size), BF16),
-            ],
+            [((per_stage, keys, 2 * rows), F32), ((per_stage, 8, 2 * rows), F32)] + [part] * blocks,
+            [pltpu.VMEM((2, per_stage, keys, 2 * size), BF16)],
             limit,
             BIG_WORK,
             [block_order, q_side, g_side, *k_all],
             True,
         )
         if stage == 0:
-            v_all = gather(v_block, "ctx", stage_probs)
-            q_side, _ = after((q_side, stage_probs))
-        probs.append(stage_probs)
+            q_side, _ = after((q_side, scale))
+        weights.append((weight, scale))
         dv_parts.append(parts)
-    dv_parts = [jnp.concatenate(parts, axis=0) for parts in zip(*dv_parts)]
-
+
+    g_side, _ = after((g_side, weights[-1][1]))
     handed, dscores = [], []
     for stage in range(STAGES):
         handed_part, dscore = call(
@@ -421,24 +422,36 @@
             ],
             limit,
             BIG_WORK,
-            [g_side, probs[stage], *k_all, *v_all],
+            [g_side, *weights[stage], *k_all, *v_all],
         )
         if stage == 0:
-            g_side, _ = after((g_side, handed_part))
+            g_side, dv_parts, _ = after((g_side, dv_parts, handed_part))
         handed.append(passed_down(handed_part, "pipe"))
         dscores.append(dscore)
+    dv_parts = [jnp.concatenate(parts, axis=0) for parts in zip(*dv_parts)]
+    dv_parts = [dv_parts[slots.index(step)] for step in range(blocks)]
     dv_terms, dv_relayed = scatter_sums(dv_parts, "ctx", ())
-    dscores, _ = after((dscores, (dv_relayed, dv_terms[-1])))
-    dk_parts = call(
-        functools.partial(dk_kernel, STAGES),
-        "key_grads",
-        [packed] * blocks,
-        [],
-        limit,
-        WORK,
-        [q_side, *dscores],
-    )
-    dk_terms, _ = scatter_sums(dk_parts, "ctx", ())
+
+    def key_sums(start, stop, dscores):
+        return call(
+            functools.partial(dk_kernel, STAGES, start),
+            "key_grads",
+            [packed] * (stop - start),
+            [],
+            limit,
+            WORK,
+            [q_side, *dscores],
+        )
+
+    far_parts = key_sums(blocks - 1, blocks, dscores)
+    dscores, _ = after((dscores, (far_parts, dv_relayed, dv_terms[-1])))
+    dk_parts = key_sums(0, blocks - 1, dscores) + far_parts
+    dk_parts = [dk_parts[slots.index(step)] for step in range(blocks)]
+    dk_terms, _ = scatter_sums(dk_parts, "ctx", (dk_parts[0], dv_terms[1]))
+    handed = jnp.concatenate(handed, axis=1)[None]
+    last = lax.axis_index("pipe") == lax.axis_size("pipe") - 1
+    handed = jnp.where(last, jnp.zeros_like(handed), handed)
+    dk_terms[0], _ = after((dk_terms[0], handed))
     key_grad, value_grad = call(
         functools.partial(finish_kernel, len(dk_terms)),
         "lay_out",
@@ -448,13 +461,11 @@
         WORK,
         [*dk_terms, *dv_terms],
     )
-    handed = jnp.concatenate(handed, axis=1)[None]
-    last = lax.axis_index("pipe") == lax.axis_size("pipe") - 1
     shape = key_heads.shape
     return (
         key_grad.reshape(shape),
         value_grad.reshape(shape),
-        jnp.where(last, jnp.zeros_like(handed), handed),
+        handed,
     )
 
 

time: 56.7 us -> 59.8 us (1.055)
  starting transfers between devices: 30.1 us -> 25.8 us
  local copies, waits for them, and re-layouts: 0.01 us -> 3.56 us
  waiting for transfers between devices: 6.94 us -> 9.82 us
  other arithmetic: 1.3 us -> 2.49 us
    ppermute x12, starting transfers between devices: 27 us -> 22.8 us  [passed(): lax.ppermute(value, axis, [(order[at], order[(at + step) % count]) for at...]
    unnamed x2 -> x10, local copies, waits for them, and re-layouts: 0.01 us -> 3.56 us
    ppermute x2, waiting for transfers between devices: 0.01 us -> 1.97 us  [passed_down(): lax.ppermute(value, axis, [(at, (at - 1) % count) for at in range(count)])]
    select_n x1, other arithmetic: 1.18 us -> 2.38 us  [shards(): handed = jnp.where(last, jnp.zeros_like(handed), handed)]
    ppermute x12, waiting for transfers between devices: 6.93 us -> 7.85 us  [passed(): lax.ppermute(value, axis, [(order[at], order[(at + step) % count]) for at...]
    pallas_call x6 -> x7, Pallas kernels: 13.8 us -> 13.4 us  [call(): pl.pallas_call(kernel, in_specs=([SMEM] if smem else []) + [VMEM] * (len(...]
  transfers between devices with their start and end apart: 14 -> 14, of which waited for: 5 -> 5; matrix products, arithmetic and copies ran while one was open for 0% -> 4% of each run, Pallas kernels for 29% -> 23%
where the time goes in v3:
time: 59.8 us; the launch traced here: 59.5 us
  starting transfers between devices  25.8 us (43%)
  Pallas kernels  17.1 us (29%)
  waiting for transfers between devices  9.82 us (16%)
  local copies, waits for them, and re-layouts  3.56 us (6%)
  other arithmetic  2.49 us (4%)
  between operations  0.8 us (1%)
    ppermute x12, starting transfers between devices, passed(): lax.ppermute(value, axis, [(order[at], order[(at + step) % count]) for at...  22.8 us
    pallas_call x7, Pallas kernels, call(): pl.pallas_call(kernel, in_specs=([SMEM] if smem else []) + [VMEM] * (len(...  13.4 us
    ppermute x12, waiting for transfers between devices, passed(): lax.ppermute(value, axis, [(order[at], order[(at + step) % count]) for at...  7.85 us
    unnamed x10, local copies, waits for them, and re-layouts  3.56 us
    ppermute x2, starting transfers between devices, passed_down(): lax.ppermute(value, axis, [(at, (at - 1) % count) for at in range(count)])  2.97 us
    pallas_call x1, Pallas kernels, make_sides(): pl.pallas_call(functools.partial(sides_kernel, groups), in_specs=[HBM] *...  2.48 us
    select_n x1, other arithmetic, shards(): handed = jnp.where(last, jnp.zeros_like(handed), handed)  2.38 us
    ppermute x2, waiting for transfers between devices, passed_down(): lax.ppermute(value, axis, [(at, (at - 1) % count) for at in range(count)])  1.97 us
  transfers between devices with their start and end apart: 14, of which 5 were waited for; matrix products, arithmetic and copies ran while one was open for 4% of the time, Pallas kernels for 23%

profile of v3, /device:TPU:0, one launch (start us, length us, event | category | flops | bytes accessed | tf_op | source)
XLA Modules:
  0.0 59.5 jit_solution(9022001132433109133)
XLA Ops:
  0.6 0.0 copy-start.4
  0.6 1.1 %pack_keys.1 = (bf16[4,128,128]{2,1,0:T(8,128)(2,1)S(1)}, bf16[4,128,128]{2,1,0:T(8,128)(2,1)S(1)}) custom-call(bf16[512,128]{1,0:T(8,128)(2,1)} %bitcast.12, bf16[512,128]{1,0:T(8,128)(2,1)} %bitcast.13), custom_call_target="tpu_custom_call" | custom-call | flops 1048576 | bytes 65536 | tf_op jit(solution)/shard_map/pack_keys/pallas_call | solution.py:375
  1.8 3.1 %collective-permute-start = (bf16[4,128,128]{2,1,0:T(8,128)(2,1)S(1)}, bf16[4,128,128]{2,1,0:T(8,128)(2,1)S(1)}, u32[]{:S(2)}, u32[]{:S(2)}) collective-permute-start(bf16[4,128,128]{2,1,0:T(8,128)(2,1)S(1)} %get-tuple-element.45.refs_0_), channel_id=1, source_target_pairs={{0,2},{2,6},{6,4},{4,0},{1,3},{3,7},{7,5},{5,1},{8,10},{10,14},{14... | collective-permute-start | bytes 393224 | tf_op jit(solution)/shard_map/ppermute | solution.py:93
  4.9 1.1 %collective-permute-start.1 = (bf16[4,128,128]{2,1,0:T(8,128)(2,1)S(1)}, bf16[4,128,128]{2,1,0:T(8,128)(2,1)S(1)}, u32[]{:S(2)}, u32[]{:S(2)}) collective-permute-start(bf16[4,128,128]{2,1,0:T(8,128)(2,1)S(1)} %get-tuple-element.45.refs_0_), channel_id=1, source_target_pairs={{0,4},{2,0},{6,2},{4,6},{1,5},{3,1},{7,3},{5,7},{8,12},{10,8},{14,... | collective-permute-start | bytes 393224 | tf_op jit(solution)/shard_map/ppermute | solution.py:93
  6.0 3.5 %collective-permute-done.refs_1_ = bf16[4,128,128]{2,1,0:T(8,128)(2,1)S(1)} collective-permute-done((bf16[4,128,128]{2,1,0:T(8,128)(2,1)S(1)}, bf16[4,128,128]{2,1,0:T(8,128)(2,1)S(1)}, u32[]{:S(2)}, u32[]{:S(2)}) %collective-permute-start) | collective-permute-done | bytes 131104 | tf_op jit(solution)/shard_map/ppermute | solution.py:93
  9.5 3.5 %collective-permute-start.2 = (bf16[4,128,128]{2,1,0:T(8,128)(2,1)S(1)}, bf16[4,128,128]{2,1,0:T(8,128)(2,1)S(1)}, u32[]{:S(2)}, u32[]{:S(2)}) collective-permute-start(bf16[4,128,128]{2,1,0:T(8,128)(2,1)S(1)} %collective-permute-done.refs_1_), channel_id=1, source_target_pairs={{0,2},{2,6},{6,4},{4,0},{1,3},{3,7},{7,5},{5,1},{8,10},{10,14},{14... | collective-permute-start | bytes 393224 | tf_op jit(solution)/shard_map/ppermute | solution.py:93
  13.0 2.5 %query_sides.1 = (bf16[2,4,512,256]{3,2,1,0:T(8,128)(2,1)S(1)}, bf16[2,4,512,256]{3,2,1,0:T(8,128)(2,1)S(1)}) custom-call(bf16[128,32,128]{2,1,0:T(8,128)(2,1)} %bitcast.9, bf16[128,32,128]{2,1,0:T(8,128)(2,1)} %bitcast.10, bf16[128,32,128]{2,1,0:T(8,128)(2,1)} %bitcast.11), custom_call_target="tpu_custom_call" | custom-call | flops 1048576 | bytes 65536 | tf_op jit(solution)/shard_map/query_sides/pallas_call | solution.py:349
  15.5 3.4 %collective-permute-start.3 = (bf16[4,128,128]{2,1,0:T(8,128)(2,1)S(1)}, bf16[4,128,128]{2,1,0:T(8,128)(2,1)S(1)}, u32[]{:S(2)}, u32[]{:S(2)}) collective-permute-start(bf16[4,128,128]{2,1,0:T(8,128)(2,1)S(1)} %get-tuple-element.55.refs_4_), channel_id=1, source_target_pairs={{0,2},{2,6},{6,4},{4,0},{1,3},{3,7},{7,5},{5,1},{8,10},{10,14},{14... | collective-permute-start | bytes 393224 | tf_op jit(solution)/shard_map/ppermute | solution.py:93
  19.0 0.0 collective-permute-start.4
  19.0 2.4 %collective-permute-start.5 = (bf16[4,128,128]{2,1,0:T(8,128)(2,1)S(1)}, bf16[4,128,128]{2,1,0:T(8,128)(2,1)S(1)}, u32[]{:S(2)}, u32[]{:S(2)}) collective-permute-start(bf16[4,128,128]{2,1,0:T(8,128)(2,1)S(1)} %get-tuple-element.55.refs_4_), channel_id=1, source_target_pairs={{0,6},{2,4},{6,0},{4,2},{1,7},{3,5},{7,1},{5,3},{8,14},{10,12},{14... | collective-permute-start | bytes 393224 | tf_op jit(solution)/shard_map/ppermute | solution.py:93
  21.4 0.0 collective-permute-done.1.refs_2_
  21.4 0.0 collective-permute-done.2.refs_3_
  21.4 0.0 copy-done.4
  21.4 2.7 %weights.2 = (f32[2,512,1024]{2,1,0:T(8,128)S(1)}, f32[2,8,1024]{2,1,0:T(8,128)S(1)}, bf16[2,128,128]{2,1,0:T(8,128)(2,1)S(1)}, bf16[2,128,128]{2,1,0:T(8,128)(2...) custom-call(s32[8]{0:T(128)S(1)} %copy-done.4, ...), custom_call_target="tpu_custom_call" | custom-call | flops 4294967296 | bytes 65536 | tf_op jit(solution)/shard_map/weights/pallas_call | solution.py:328
  24.1 2.7 %weights.3 = (f32[2,512,1024]{2,1,0:T(8,128)S(1)}, f32[2,8,1024]{2,1,0:T(8,128)S(1)}, bf16[2,128,128]{2,1,0:T(8,128)(2,1)S(1)}, bf16[2,128,128]{2,1,0:T(8,128)(2...) custom-call(s32[8]{0:T(128)S(1)} %copy-done.4, ...), custom_call_target="tpu_custom_call" | custom-call | flops 4294967296 | bytes 65536 | tf_op jit(solution)/shard_map/weights/pallas_call | solution.py:328
  26.9 0.0 collective-permute-done.3.refs_5_
  26.9 0.0 collective-permute-done.4.refs_6_
  26.9 0.4 collective-permute-done.5.refs_7_
  27.3 1.6 %query_grads.2 = (bf16[128,16,128]{2,1,0:T(8,128)(2,1)S(1)}, bf16[2,512,1024]{2,1,0:T(8,128)(2,1)S(1)}) custom-call(bf16[2,4,512,256]{3,2,1,0:T(8,128)(2,1)S(1)} %get-tuple-element.66.g_side_ref, f32[2,512,1024]{2,1,0:T(8,128)S(1)} %get-tuple-element.53.weight_ref, f32[2,8,1024]{2,1,0:T(8,128)S(1)} %get-tuple-element.49.scale_ref, ...), custom_call_target="tpu_custom_call" | custom-call | flops 4294967296 | bytes 65536 | tf_op jit(solution)/shard_map/query_grads/pallas_call | solution.py:328
  28.9 0.0 copy-start
  29.0 2.4 %collective-permute-start.8 = (bf16[128,16,128]{2,1,0:T(8,128)(2,1)S(1)}, bf16[128,16,128]{2,1,0:T(8,128)(2,1)}, u32[]{:S(2)}, u32[]{:S(2)}) collective-permute-start(bf16[128,16,128]{2,1,0:T(8,128)(2,1)S(1)} %get-tuple-element.65), channel_id=1, source_target_pairs={{0,24},{8,0},{16,8},{24,16},{1,25},{9,1},{17,9},{25,17},{2,26},{10... | collective-permute-start | bytes 1572872 | tf_op jit(solution)/shard_map/ppermute | solution.py:117
  31.4 4.9 %collective-permute-start.7 = (bf16[4,128,128]{2,1,0:T(8,128)(2,1)S(1)}, bf16[4,128,128]{2,1,0:T(8,128)(2,1)S(1)}, u32[]{:S(2)}, u32[]{:S(2)}) collective-permute-start(bf16[4,128,128]{2,1,0:T(8,128)(2,1)S(1)} %pad_maximum_fusion.1), channel_id=1, source_target_pairs={{0,4},{2,0},{6,2},{4,6},{1,5},{3,1},{7,3},{5,7},{8,12},{10,8},{14,... | collective-permute-start | bytes 393224 | tf_op jit(solution)/shard_map/ppermute | solution.py:93
  36.3 0.1 collective-permute-start.6
  36.4 2.4 %query_grads.3 = (bf16[128,16,128]{2,1,0:T(8,128)(2,1)}, bf16[2,512,1024]{2,1,0:T(8,128)(2,1)S(1)}) custom-call(bf16[2,4,512,256]{3,2,1,0:T(8,128)(2,1)S(1)} %get-tuple-element.66.g_side_ref, f32[2,512,1024]{2,1,0:T(8,128)S(1)} %get-tuple-element.67.weight_ref, f32[2,8,1024]{2,1,0:T(8,128)S(1)} %get-tuple-element.51.scale_ref, ...), custom_call_target="tpu_custom_call" | custom-call | flops 4294967296 | bytes 65536 | tf_op jit(solution)/shard_map/query_grads/pallas_call | solution.py:328
  38.8 0.0 copy-start.2
  38.8 0.0 copy-done
  38.8 0.9 %key_grads.2 = bf16[4,128,128]{2,1,0:T(8,128)(2,1)S(1)} custom-call(bf16[2,4,512,256]{3,2,1,0:T(8,128)(2,1)S(1)} %get-tuple-element.50.q_side_ref, bf16[2,512,1024]{2,1,0:T(8,128)(2,1)S(1)} %get-tuple-element.75.refs_0_, bf16[2,512,1024]{2,1,0:T(8,128)(2,1)S(1)} %get-tuple-element.76.refs_1_), custom_call_target="tpu_custom_call" | custom-call | flops 1048576 | bytes 65536 | tf_op jit(solution)/shard_map/key_grads/pallas_call | solution.py:328
  39.7 0.4 copy-done.2
  40.1 1.2 %collective-permute-start.10 = (bf16[4,128,128]{2,1,0:T(8,128)(2,1)S(1)}, bf16[4,128,128]{2,1,0:T(8,128)(2,1)S(1)}, u32[]{:S(2)}, u32[]{:S(2)}) collective-permute-start(bf16[4,128,128]{2,1,0:T(8,128)(2,1)S(1)} %key_grads.2), channel_id=1, source_target_pairs={{0,2},{2,6},{6,4},{4,0},{1,3},{3,7},{7,5},{5,1},{8,10},{10,14},{14... | collective-permute-start | bytes 393224 | tf_op jit(solution)/shard_map/ppermute | solution.py:93
  41.3 0.5 collective-permute-start.9
  41.9 1.8 %collective-permute-done.6 = bf16[4,128,128]{2,1,0:T(8,128)(2,1)S(1)} collective-permute-done((bf16[4,128,128]{2,1,0:T(8,128)(2,1)S(1)}, bf16[4,128,128]{2,1,0:T(8,128)(2,1)S(1)}, u32[]{:S(2)}, u32[]{:S(2)}) %collective-permute-start.6) | collective-permute-done | bytes 131104 | tf_op jit(solution)/shard_map/ppermute | solution.py:93
  43.7 0.1 collective-permute-start.11
  43.8 0.0 collective-permute-done.7.refs_5_
  43.8 0.0 copy-start.1
  43.8 1.6 %copy-done.1 = bf16[2,512,1024]{2,1,0:T(8,128)(2,1)S(1)} copy-done((bf16[2,512,1024]{2,1,0:T(8,128)(2,1)S(1)}, bf16[2,512,1024]{2,1,0:T(8,128)(2,1)}, u32[]{:S(2)}) %copy-start.1) | copy-done | bytes 2097176
  45.4 0.0 copy-start.3
  45.4 1.6 %copy-done.3 = bf16[2,512,1024]{2,1,0:T(8,128)(2,1)S(1)} copy-done((bf16[2,512,1024]{2,1,0:T(8,128)(2,1)S(1)}, bf16[2,512,1024]{2,1,0:T(8,128)(2,1)}, u32[]{:S(2)}) %copy-start.3) | copy-done | bytes 2097176
  47.0 2.3 %key_grads.3 = (bf16[4,128,128]{2,1,0:T(8,128)(2,1)S(1)}, bf16[4,128,128]{2,1,0:T(8,128)(2,1)S(1)}, bf16[4,128,128]{2,1,0:T(8,128)(2,1)S(1)}) custom-call(bf16[2,4,512,256]{3,2,1,0:T(8,128)(2,1)S(1)} %get-tuple-element.50.q_side_ref, bf16[2,512,1024]{2,1,0:T(8,128)(2,1)S(1)} %copy-done.1, bf16[2,512,1024]{2,1,0:T(8,128)(2,1)S(1)} %copy-done.3), custom_call_target="tpu_custom_call" | custom-call | flops 1048576 | bytes 65536 | tf_op jit(solution)/shard_map/key_grads/pallas_call | solution.py:328
  49.2 3.0 %collective-permute-start.13 = (bf16[4,128,128]{2,1,0:T(8,128)(2,1)S(1)}, bf16[4,128,128]{2,1,0:T(8,128)(2,1)S(1)}, u32[]{:S(2)}, u32[]{:S(2)}) collective-permute-start(bf16[4,128,128]{2,1,0:T(8,128)(2,1)S(1)} %get-tuple-element.82), channel_id=1, source_target_pairs={{0,4},{2,0},{6,2},{4,6},{1,5},{3,1},{7,3},{5,7},{8,12},{10,8},{14,... | collective-permute-start | bytes 393224 | tf_op jit(solution)/shard_map/ppermute | solution.py:93
  52.2 0.0 collective-permute-done.10
  52.2 0.0 collective-permute-done.11.refs_4_
  52.2 0.1 collective-permute-start.12
  52.3 2.0 %collective-permute-done.9 = bf16[128,16,128]{2,1,0:T(8,128)(2,1)} collective-permute-done((bf16[128,16,128]{2,1,0:T(8,128)(2,1)}, bf16[128,16,128]{2,1,0:T(8,128)(2,1)}, u32[]{:S(2)}, u32[]{:S(2)}) %collective-permute-start.9) | collective-permute-done | bytes 524320 | tf_op jit(solution)/shard_map/ppermute | solution.py:117
  54.3 0.0 collective-permute-done.8
  54.3 2.4 %maximum_select_fusion = bf16[1,128,32,128]{3,2,1,0:T(8,128)(2,1)} fusion(bf16[1,128,16,128]{3,2,1,0:T(8,128)(2,1)} %bitcast.6, bf16[1,128,16,128]{3,2,1,0:T(8,128)(2,1)} %bitcast.5, pred[]{:T(512)S(6)} %eq.3), kind=kLoop, calls=%fused_computation | loop fusion | flops 2621440 | bytes 2097153 | tf_op jit(solution)/shard_map/jit(_where)/select_n | solution.py:453
  56.7 0.0 collective-permute-done.13.refs_2_
  56.7 2.1 %collective-permute-done.12.refs_1_ = bf16[4,128,128]{2,1,0:T(8,128)(2,1)S(1)} collective-permute-done((bf16[4,128,128]{2,1,0:T(8,128)(2,1)S(1)}, bf16[4,128,128]{2,1,0:T(8,128)(2,1)S(1)}, u32[]{:S(2)}, u32[]{:S(2)}) %collective-permute-start.12) | collective-permute-done | bytes 131104 | tf_op jit(solution)/shard_map/ppermute | solution.py:93
  58.7 0.8 %lay_out.1 = (bf16[512,128]{1,0:T(8,128)(2,1)}, bf16[512,128]{1,0:T(8,128)(2,1)}) custom-call(bf16[4,128,128]{2,1,0:T(8,128)(2,1)S(1)} %get-tuple-element.79.refs_0_, bf16[4,128,128]{2,1,0:T(8,128)(2,1)S(1)} %collective-permute-done.12.refs_1_, bf16[4,128,128]{2,1,0:T(8,128)(2,1)S(1)} %collective-permute-done.13.refs_2_, ...), custom_call_target="tpu_custom_call" | custom-call | flops 1048576 | bytes 65536 | tf_op jit(solution)/shard_map/lay_out/pallas_call | solution.py:328
  (5 shorter events, 0.1 us)
Async XLA Ops:
  0.6 20.8 %copy-start.4 = (s32[8]{0:T(128)S(1)}, s32[8]{0:T(128)}, u32[]{:S(2)}) copy-start(s32[8]{0:T(128)} %order_ref.3) | copy-start | bytes 100
  1.8 7.7 %collective-permute-start = (bf16[4,128,128]{2,1,0:T(8,128)(2,1)S(1)}, bf16[4,128,128]{2,1,0:T(8,128)(2,1)S(1)}, u32[]{:S(2)}, u32[]{:S(2)}) collective-permute-start(bf16[4,128,128]{2,1,0:T(8,128)(2,1)S(1)} %get-tuple-element.45.refs_0_), channel_id=1, source_target_pairs={{0,2},{2,6},{6,4},{4,0},{1,3},{3,7},{7,5},{5,1},{8,10},{10,14},{14... | collective-permute-start | bytes 393224 | tf_op jit(solution)/shard_map/ppermute | solution.py:93
  4.9 16.5 %collective-permute-start.1 = (bf16[4,128,128]{2,1,0:T(8,128)(2,1)S(1)}, bf16[4,128,128]{2,1,0:T(8,128)(2,1)S(1)}, u32[]{:S(2)}, u32[]{:S(2)}) collective-permute-start(bf16[4,128,128]{2,1,0:T(8,128)(2,1)S(1)} %get-tuple-element.45.refs_0_), channel_id=1, source_target_pairs={{0,4},{2,0},{6,2},{4,6},{1,5},{3,1},{7,3},{5,7},{8,12},{10,8},{14,... | collective-permute-start | bytes 393224 | tf_op jit(solution)/shard_map/ppermute | solution.py:93
  9.5 11.9 %collective-permute-start.2 = (bf16[4,128,128]{2,1,0:T(8,128)(2,1)S(1)}, bf16[4,128,128]{2,1,0:T(8,128)(2,1)S(1)}, u32[]{:S(2)}, u32[]{:S(2)}) collective-permute-start(bf16[4,128,128]{2,1,0:T(8,128)(2,1)S(1)} %collective-permute-done.refs_1_), channel_id=1, source_target_pairs={{0,2},{2,6},{6,4},{4,0},{1,3},{3,7},{7,5},{5,1},{8,10},{10,14},{14... | collective-permute-start | bytes 393224 | tf_op jit(solution)/shard_map/ppermute | solution.py:93
  15.5 11.3 %collective-permute-start.3 = (bf16[4,128,128]{2,1,0:T(8,128)(2,1)S(1)}, bf16[4,128,128]{2,1,0:T(8,128)(2,1)S(1)}, u32[]{:S(2)}, u32[]{:S(2)}) collective-permute-start(bf16[4,128,128]{2,1,0:T(8,128)(2,1)S(1)} %get-tuple-element.55.refs_4_), channel_id=1, source_target_pairs={{0,2},{2,6},{6,4},{4,0},{1,3},{3,7},{7,5},{5,1},{8,10},{10,14},{14... | collective-permute-start | bytes 393224 | tf_op jit(solution)/shard_map/ppermute | solution.py:93
  19.0 7.9 %collective-permute-start.4 = (bf16[4,128,128]{2,1,0:T(8,128)(2,1)S(1)}, bf16[4,128,128]{2,1,0:T(8,128)(2,1)S(1)}, u32[]{:S(2)}, u32[]{:S(2)}) collective-permute-start(bf16[4,128,128]{2,1,0:T(8,128)(2,1)S(1)} %get-tuple-element.55.refs_4_), channel_id=1, source_target_pairs={{0,4},{2,0},{6,2},{4,6},{1,5},{3,1},{7,3},{5,7},{8,12},{10,8},{14,... | collective-permute-start | bytes 393224 | tf_op jit(solution)/shard_map/ppermute | solution.py:93
  19.0 8.4 %collective-permute-start.5 = (bf16[4,128,128]{2,1,0:T(8,128)(2,1)S(1)}, bf16[4,128,128]{2,1,0:T(8,128)(2,1)S(1)}, u32[]{:S(2)}, u32[]{:S(2)}) collective-permute-start(bf16[4,128,128]{2,1,0:T(8,128)(2,1)S(1)} %get-tuple-element.55.refs_4_), channel_id=1, source_target_pairs={{0,6},{2,4},{6,0},{4,2},{1,7},{3,5},{7,1},{5,3},{8,14},{10,12},{14... | collective-permute-start | bytes 393224 | tf_op jit(solution)/shard_map/ppermute | solution.py:93
  28.9 9.8 %copy-start = (bf16[2,512,1024]{2,1,0:T(8,128)(2,1)}, bf16[2,512,1024]{2,1,0:T(8,128)(2,1)S(1)}, u32[]{:S(2)}) copy-start(bf16[2,512,1024]{2,1,0:T(8,128)(2,1)S(1)} %get-tuple-element.75.refs_0_) | copy-start | bytes 6291460
  29.0 25.3 %collective-permute-start.8 = (bf16[128,16,128]{2,1,0:T(8,128)(2,1)S(1)}, bf16[128,16,128]{2,1,0:T(8,128)(2,1)}, u32[]{:S(2)}, u32[]{:S(2)}) collective-permute-start(bf16[128,16,128]{2,1,0:T(8,128)(2,1)S(1)} %get-tuple-element.65), channel_id=1, source_target_pairs={{0,24},{8,0},{16,8},{24,16},{1,25},{9,1},{17,9},{25,17},{2,26},{10... | collective-permute-start | bytes 1572872 | tf_op jit(solution)/shard_map/ppermute | solution.py:117
  31.4 12.4 %collective-permute-start.7 = (bf16[4,128,128]{2,1,0:T(8,128)(2,1)S(1)}, bf16[4,128,128]{2,1,0:T(8,128)(2,1)S(1)}, u32[]{:S(2)}, u32[]{:S(2)}) collective-permute-start(bf16[4,128,128]{2,1,0:T(8,128)(2,1)S(1)} %pad_maximum_fusion.1), channel_id=1, source_target_pairs={{0,4},{2,0},{6,2},{4,6},{1,5},{3,1},{7,3},{5,7},{8,12},{10,8},{14,... | collective-permute-start | bytes 393224 | tf_op jit(solution)/shard_map/ppermute | solution.py:93
  36.3 7.3 %collective-permute-start.6 = (bf16[4,128,128]{2,1,0:T(8,128)(2,1)S(1)}, bf16[4,128,128]{2,1,0:T(8,128)(2,1)S(1)}, u32[]{:S(2)}, u32[]{:S(2)}) collective-permute-start(bf16[4,128,128]{2,1,0:T(8,128)(2,1)S(1)} %pad_maximum_fusion), channel_id=1, source_target_pairs={{0,2},{2,6},{6,4},{4,0},{1,3},{3,7},{7,5},{5,1},{8,10},{10,14},{14... | collective-permute-start | bytes 393224 | tf_op jit(solution)/shard_map/ppermute | solution.py:93
  38.8 1.3 %copy-start.2 = (bf16[2,512,1024]{2,1,0:T(8,128)(2,1)}, bf16[2,512,1024]{2,1,0:T(8,128)(2,1)S(1)}, u32[]{:S(2)}) copy-start(bf16[2,512,1024]{2,1,0:T(8,128)(2,1)S(1)} %get-tuple-element.76.refs_1_) | copy-start | bytes 6291460
  40.1 12.1 %collective-permute-start.10 = (bf16[4,128,128]{2,1,0:T(8,128)(2,1)S(1)}, bf16[4,128,128]{2,1,0:T(8,128)(2,1)S(1)}, u32[]{:S(2)}, u32[]{:S(2)}) collective-permute-start(bf16[4,128,128]{2,1,0:T(8,128)(2,1)S(1)} %key_grads.2), channel_id=1, source_target_pairs={{0,2},{2,6},{6,4},{4,0},{1,3},{3,7},{7,5},{5,1},{8,10},{10,14},{14... | collective-permute-start | bytes 393224 | tf_op jit(solution)/shard_map/ppermute | solution.py:93
  41.3 12.9 %collective-permute-start.9 = (bf16[128,16,128]{2,1,0:T(8,128)(2,1)}, bf16[128,16,128]{2,1,0:T(8,128)(2,1)}, u32[]{:S(2)}, u32[]{:S(2)}) collective-permute-start(bf16[128,16,128]{2,1,0:T(8,128)(2,1)} %get-tuple-element.78), channel_id=1, source_target_pairs={{0,24},{8,0},{16,8},{24,16},{1,25},{9,1},{17,9},{25,17},{2,26},{10... | collective-permute-start | bytes 1572872 | tf_op jit(solution)/shard_map/ppermute | solution.py:117
  43.7 8.5 %collective-permute-start.11 = (bf16[4,128,128]{2,1,0:T(8,128)(2,1)S(1)}, bf16[4,128,128]{2,1,0:T(8,128)(2,1)S(1)}, u32[]{:S(2)}, u32[]{:S(2)}) collective-permute-start(bf16[4,128,128]{2,1,0:T(8,128)(2,1)S(1)} %add_convert_fusion.1), channel_id=1, source_target_pairs={{0,2},{2,6},{6,4},{4,0},{1,3},{3,7},{7,5},{5,1},{8,10},{10,14},{14... | collective-permute-start | bytes 393224 | tf_op jit(solution)/shard_map/ppermute | solution.py:93
  43.8 1.6 %copy-start.1 = (bf16[2,512,1024]{2,1,0:T(8,128)(2,1)S(1)}, bf16[2,512,1024]{2,1,0:T(8,128)(2,1)}, u32[]{:S(2)}) copy-start(bf16[2,512,1024]{2,1,0:T(8,128)(2,1)} %copy-done) | copy-start | bytes 6291460
  45.4 1.6 %copy-start.3 = (bf16[2,512,1024]{2,1,0:T(8,128)(2,1)S(1)}, bf16[2,512,1024]{2,1,0:T(8,128)(2,1)}, u32[]{:S(2)}) copy-start(bf16[2,512,1024]{2,1,0:T(8,128)(2,1)} %copy-done.2) | copy-start | bytes 6291460
  49.2 7.4 %collective-permute-start.13 = (bf16[4,128,128]{2,1,0:T(8,128)(2,1)S(1)}, bf16[4,128,128]{2,1,0:T(8,128)(2,1)S(1)}, u32[]{:S(2)}, u32[]{:S(2)}) collective-permute-start(bf16[4,128,128]{2,1,0:T(8,128)(2,1)S(1)} %get-tuple-element.82), channel_id=1, source_target_pairs={{0,4},{2,0},{6,2},{4,6},{1,5},{3,1},{7,3},{5,7},{8,12},{10,8},{14,... | collective-permute-start | bytes 393224 | tf_op jit(solution)/shard_map/ppermute | solution.py:93
  52.2 6.5 %collective-permute-start.12 = (bf16[4,128,128]{2,1,0:T(8,128)(2,1)S(1)}, bf16[4,128,128]{2,1,0:T(8,128)(2,1)S(1)}, u32[]{:S(2)}, u32[]{:S(2)}) collective-permute-start(bf16[4,128,128]{2,1,0:T(8,128)(2,1)S(1)} %add_convert_fusion), channel_id=1, source_target_pairs={{0,2},{2,6},{6,4},{4,0},{1,3},{3,7},{7,5},{5,1},{8,10},{10,14},{14... | collective-permute-start | bytes 393224 | tf_op jit(solution)/shard_map/ppermute | solution.py:93

commit v4 on v3

--- a/solution.py
+++ b/solution.py
@@ -11,7 +11,7 @@
 NEG = -1e30
 STAGES = 2
 WORK = 2**20
-BIG_WORK = 2**32
+BIG_WORK = (2**32, 2**30)
 F32 = jnp.float32
 BF16 = jnp.bfloat16
 
@@ -42,33 +42,41 @@
     return high, (x - high.astype(F32)).astype(BF16)
 
 
-def prep_kernel(k_hbm, v_hbm, k_out, v_out, rows_ref, k_ref, v_ref, sems):
+def prep_kernel(k_hbm, v_hbm, *refs):
+    outs, (rows_ref, k_ref, v_ref, sems) = refs[:-4], refs[-4:]
     copies = [
         pltpu.make_async_copy(source, target, sems.at[at])
         for at, (source, target) in enumerate(((k_hbm, k_ref), (v_hbm, v_ref)))
     ]
     for copy in copies:
         copy.start()
-    groups, tokens, size = k_out.shape
+    both, tokens, size = outs[0].shape
+    per_stage = both // 2
+    groups = per_stage * len(outs)
     sign = signs(size)
-    for copy, ref, out in zip(copies, (k_ref, v_ref), (k_out, v_out)):
+    for part, copy in enumerate(copies):
         copy.wait()
-        if ref is k_ref:
+        if part == 0:
             rows = nn(k_ref[...], sign) * (1.0 / math.sqrt(size))
         else:
             rows = v_ref[...].astype(F32)
         rows_ref[...] = rows
         for group in range(groups):
-            out[group] = rows_ref[pl.ds(group, tokens, stride=groups), :].astype(BF16)
-
-
-def finish_kernel(count, *refs):
-    outs, rows_ref = refs[-3:-1], refs[-1]
+            picked = rows_ref[pl.ds(group, tokens, stride=groups), :].astype(BF16)
+            outs[group // per_stage][part * per_stage + group % per_stage] = picked
+
+
+def finish_kernel(stages, *refs):
+    parts, outs, rows_ref = refs[:-3], refs[-3:-1], refs[-1]
+    terms = len(parts) // stages
+    both, tokens, _ = parts[0].shape
+    per_stage = both // 2
+    groups = per_stage * stages
     for part, out in enumerate(outs):
-        terms = refs[part * count : (part + 1) * count]
-        groups, tokens, _ = terms[0].shape
-        for group in range(groups):
-            rows = [ref[group].astype(F32) for ref in terms]
+        for group in range(groups):
+            first = group // per_stage * terms
+            at = part * per_stage + group % per_stage
+            rows = [ref[at].astype(F32) for ref in parts[first : first + terms]]
             rows_ref[pl.ds(group, tokens, stride=groups), :] = sum(rows[1:], rows[0])
         out[...] = rows_ref[...].astype(BF16)
 
@@ -203,7 +211,7 @@
                     key_ref[half, group, k_at, size:] = hidden
         at = pl.ds(block * tokens, tokens)
         for group in range(groups):
-            key = k_refs[block][first + group]
+            key = k_refs[block][group]
             for half in range(2):
                 key_ref[half, group, at, :size] = key
 
@@ -248,10 +256,10 @@
 
 
 def dq_kernel(first, blocks, g_side_ref, weight_ref, scale_ref, *refs):
-    k_refs, v_refs = refs[:blocks], refs[blocks : 2 * blocks]
-    handed_ref, dscore_ref, val_ref, back_ref = refs[2 * blocks :]
+    kv_refs = refs[:blocks]
+    handed_ref, dscore_ref, val_ref, back_ref = refs[blocks:]
     groups, keys, _ = weight_ref.shape
-    tokens, size = k_refs[0].shape[1:]
+    tokens, size = kv_refs[0].shape[1:]
     rows = g_side_ref.shape[2]
     half_rows = tokens // 2
     per_group = rows // half_rows
@@ -261,9 +269,9 @@
     for block in range(blocks):
         at = pl.ds(block * tokens, tokens)
         for group in range(groups):
-            val_ref[group, at, :size] = v_refs[block][first + group]
+            val_ref[group, at, :size] = kv_refs[block][groups + group]
             val_ref[group, at, size:] = jnp.ones((tokens, size), BF16)
-            high, low = split(nt(sign, k_refs[block][first + group]) * (1.0 / size))
+            high, low = split(nt(sign, kv_refs[block][group]) * (1.0 / size))
             back_ref[group, :size, at] = high
             back_ref[group, size:, at] = low
 
@@ -295,25 +303,20 @@
             results = []
 
 
-def dk_kernel(stages, start, q_side_ref, *refs):
-    dscore_refs, sum_refs = refs[:stages], refs[stages:]
+def dk_kernel(first, q_side_ref, dscore_ref, *sum_refs):
     tokens, size = sum_refs[0].shape[1:]
+    groups, keys, _ = dscore_ref.shape
     rows = q_side_ref.shape[2]
     signs_twice = jnp.concatenate([signs(size)] * 2, axis=0)
-    chunk = 512
-    per_stage = dscore_refs[0].shape[0]
-    count = len(sum_refs) * tokens
-    for row in range(0, count, chunk):
-        length = min(chunk, count - row)
-        for group in range(stages * per_stage):
+    for row in range(0, keys, 512):
+        for group in range(groups):
             dk = None
             for half in range(2):
-                dscore = dscore_refs[group // per_stage].at[group % per_stage]
-                dscore = dscore[pl.ds(start * tokens + row, length), pl.ds(half * rows, rows)]
-                part = nn(dscore, q_side_ref[half, group, :, :size])
+                dscore = dscore_ref[group, pl.ds(row, 512), pl.ds(half * rows, rows)]
+                part = nn(dscore, q_side_ref[half, first + group, :, :size])
                 dk = part if dk is None else dk + part
             dk = (nn(jnp.concatenate(split(dk), axis=1), signs_twice) * (1.0 / size)).astype(BF16)
-            for at in range(0, length, tokens):
+            for at in range(0, 512, tokens):
                 sum_refs[(row + at) // tokens][group] = dk[at : at + tokens]
 
 
@@ -352,7 +355,7 @@
         out_specs=[VMEM] * 2,
         out_shape=[shape] * 2,
         scratch_shapes=[pltpu.VMEM((2, 3, half_rows, heads, size), BF16), DMA((6,))],
-        compiler_params=pltpu.CompilerParams(vmem_limit_bytes=24 * 2**20),
+        compiler_params=pltpu.CompilerParams(vmem_limit_bytes=12 * 2**20),
         cost_estimate=pl.CostEstimate(flops=WORK, bytes_accessed=2**16, transcendentals=0),
         name="query_sides",
     )(in_hbm(queries), in_hbm(grads), in_hbm(saved))
@@ -366,51 +369,57 @@
     blocks = lax.axis_size("ctx")
     keys = blocks * tokens
     rows = tokens // 2 * per_group
-    packed = ((groups, tokens, size), BF16)
+    packed = ((2 * per_stage, tokens, size), BF16)
     part = ((per_stage, tokens, size), BF16)
     flat = ((tokens * groups, size), BF16)
     rows_scratch = pltpu.VMEM(*flat[:1], F32)
-    limit = 12 + keys // 64
+    limit = 6 + keys // 64
     after = lax.optimization_barrier
-    k_block, v_block = pl.pallas_call(
+    slots = far_last(blocks)
+    kv_blocks = pl.pallas_call(
         prep_kernel,
         in_specs=[HBM] * 2,
-        out_specs=[VMEM] * 2,
-        out_shape=[jax.ShapeDtypeStruct(*packed)] * 2,
+        out_specs=[VMEM] * STAGES,
+        out_shape=[jax.ShapeDtypeStruct(*packed)] * STAGES,
         scratch_shapes=[rows_scratch, pltpu.VMEM(*flat), pltpu.VMEM(*flat), DMA((2,))],
         compiler_params=pltpu.CompilerParams(vmem_limit_bytes=8 * 2**20),
         cost_estimate=pl.CostEstimate(flops=WORK, bytes_accessed=2**16, transcendentals=0),
         name="pack_keys",
     )(in_hbm(key_heads.reshape(-1, size)), in_hbm(value_heads.reshape(-1, size)))
 
-    k_all = gather(k_block, "ctx", ())
-    q_loads, _ = after((queries[0], k_all[1]))
+    gathered = [gather(kv_blocks[0], "ctx", ())]
+    q_loads, _ = after((queries[0], gathered[0][1]))
     q_side, g_side = make_sides(groups, q_loads, output_grad[0], forward_out[0])
-    v_block, _ = after((v_block, q_side))
-    v_all = gather(v_block, "ctx")
-    slots = far_last(blocks)
-    k_all, v_all = [k_all[step] for step in slots], [v_all[step] for step in slots]
-
-    weights, dv_parts = [], []
+    for stage in range(1, STAGES):
+        block, _ = after((kv_blocks[stage], q_side))
+        gathered.append(gather(block, "ctx"))
+
+    def sums_of(stage, dscore, dv_parts):
+        dk_parts = call(
+            functools.partial(dk_kernel, stage * per_stage),
+            "key_grads",
+            [part] * blocks,
+            [],
+            limit,
+            WORK,
+            [q_side, dscore],
+        )
+        parts = [jnp.concatenate(pair, axis=0) for pair in zip(dk_parts, dv_parts)]
+        return [parts[slots.index(step)] for step in range(blocks)]
+
+    handed, terms = [], []
     for stage in range(STAGES):
-        weight, scale, *parts = call(
+        kv_all = [gathered[stage][step] for step in slots]
+        weight, scale, *dv_parts = call(
             functools.partial(weights_kernel, stage * per_stage, blocks),
             "weights",
             [((per_stage, keys, 2 * rows), F32), ((per_stage, 8, 2 * rows), F32)] + [part] * blocks,
             [pltpu.VMEM((2, per_stage, keys, 2 * size), BF16)],
             limit,
-            BIG_WORK,
-            [block_order, q_side, g_side, *k_all],
+            BIG_WORK[min(stage, 1)],
+            [block_order, q_side, g_side, *kv_all],
             True,
         )
-        if stage == 0:
-            q_side, _ = after((q_side, scale))
-        weights.append((weight, scale))
-        dv_parts.append(parts)
-
-    g_side, _ = after((g_side, weights[-1][1]))
-    handed, dscores = [], []
-    for stage in range(STAGES):
         handed_part, dscore = call(
             functools.partial(dq_kernel, stage * per_stage, blocks),
             "query_grads",
@@ -421,46 +430,22 @@
                 pltpu.VMEM((per_stage, 2 * size, keys), BF16),
             ],
             limit,
-            BIG_WORK,
-            [g_side, *weights[stage], *k_all, *v_all],
+            BIG_WORK[min(stage, 1)],
+            [g_side, weight, scale, *kv_all],
         )
-        if stage == 0:
-            g_side, dv_parts, _ = after((g_side, dv_parts, handed_part))
         handed.append(passed_down(handed_part, "pipe"))
-        dscores.append(dscore)
-    dv_parts = [jnp.concatenate(parts, axis=0) for parts in zip(*dv_parts)]
-    dv_parts = [dv_parts[slots.index(step)] for step in range(blocks)]
-    dv_terms, dv_relayed = scatter_sums(dv_parts, "ctx", ())
-
-    def key_sums(start, stop, dscores):
-        return call(
-            functools.partial(dk_kernel, STAGES, start),
-            "key_grads",
-            [packed] * (stop - start),
-            [],
-            limit,
-            WORK,
-            [q_side, *dscores],
-        )
-
-    far_parts = key_sums(blocks - 1, blocks, dscores)
-    dscores, _ = after((dscores, (far_parts, dv_relayed, dv_terms[-1])))
-    dk_parts = key_sums(0, blocks - 1, dscores) + far_parts
-    dk_parts = [dk_parts[slots.index(step)] for step in range(blocks)]
-    dk_terms, _ = scatter_sums(dk_parts, "ctx", (dk_parts[0], dv_terms[1]))
+        if stage > 0:
+            dscore, _ = after((dscore, (relayed, terms[-1], handed[0])))
+        parts = sums_of(stage, dscore, dv_parts)
+        q_side, _ = after((q_side, parts))
+        stage_terms, relayed = scatter_sums(parts, "ctx", handed[:stage])
+        terms += stage_terms
+    key_grad, value_grad = call(
+        functools.partial(finish_kernel, STAGES), "lay_out", [flat, flat], [rows_scratch], 8, WORK, terms
+    )
     handed = jnp.concatenate(handed, axis=1)[None]
     last = lax.axis_index("pipe") == lax.axis_size("pipe") - 1
     handed = jnp.where(last, jnp.zeros_like(handed), handed)
-    dk_terms[0], _ = after((dk_terms[0], handed))
-    key_grad, value_grad = call(
-        functools.partial(finish_kernel, len(dk_terms)),
-        "lay_out",
-        [flat, flat],
-        [rows_scratch],
-        8,
-        WORK,
-        [*dk_terms, *dv_terms],
-    )
     shape = key_heads.shape
     return (
         key_grad.reshape(shape),

time: 59.8 us -> 58.6 us (0.980)
  waiting for transfers between devices: 9.82 us -> 13.9 us
  local copies, waits for them, and re-layouts: 3.56 us -> 0.08 us
  other arithmetic: 2.49 us -> 1.3 us
  Pallas kernels: 17.1 us -> 16.1 us
    ppermute x12, waiting for transfers between devices: 7.85 us -> 12.7 us  [passed(): lax.ppermute(value, axis, [(order[at], order[(at + step) % count]) for at...]
    unnamed x10 -> x6, local copies, waits for them, and re-layouts: 3.56 us -> 0.03 us
    select_n x1, other arithmetic: 2.38 us -> 1.18 us  [shards(): handed = jnp.where(last, jnp.zeros_like(handed), handed)]
    pallas_call x7, Pallas kernels: 13.4 us -> 12.5 us  [call(): pl.pallas_call(kernel, in_specs=([SMEM] if smem else []) + [VMEM] * (len(...]
    ppermute x2, waiting for transfers between devices: 1.97 us -> 1.11 us  [passed_down(): lax.ppermute(value, axis, [(at, (at - 1) % count) for at in range(count)])]
  transfers between devices with their start and end apart: 14 -> 14, of which waited for: 5 -> 4; matrix products, arithmetic and copies ran while one was open for 4% -> 2% of each run, Pallas kernels for 23% -> 24%
where the time goes in v4:
time: 58.6 us; the launch traced here: 58.1 us
  starting transfers between devices  25.9 us (44%)
  Pallas kernels  16.1 us (27%)
  waiting for transfers between devices  13.9 us (24%)
  other arithmetic  1.3 us (2%)
  between operations  0.81 us (1%)
    ppermute x12, starting transfers between devices, passed(): lax.ppermute(value, axis, [(order[at], order[(at + step) % count]) for at...  22.8 us
    ppermute x12, waiting for transfers between devices, passed(): lax.ppermute(value, axis, [(order[at], order[(at + step) % count]) for at...  12.7 us
    pallas_call x7, Pallas kernels, call(): pl.pallas_call(kernel, in_specs=([SMEM] if smem else []) + [VMEM] * (len(...  12.5 us
    ppermute x2, starting transfers between devices, passed_down(): lax.ppermute(value, axis, [(at, (at - 1) % count) for at in range(count)])  3.08 us
    pallas_call x1, Pallas kernels, make_sides(): pl.pallas_call(functools.partial(sides_kernel, groups), in_specs=[HBM] *...  2.48 us
    select_n x1, other arithmetic, shards(): handed = jnp.where(last, jnp.zeros_like(handed), handed)  1.18 us
  transfers between devices with their start and end apart: 14, of which 4 were waited for; matrix products, arithmetic and copies ran while one was open for 2% of the time, Pallas kernels for 24%

profile of v4, /device:TPU:0, one launch (start us, length us, event | category | flops | bytes accessed | tf_op | source)
XLA Modules:
  0.0 58.1 jit_solution(5751995363287583861)
XLA Ops:
  0.6 0.0 copy-start
  0.6 1.1 %pack_keys.1 = (bf16[4,128,128]{2,1,0:T(8,128)(2,1)S(1)}, bf16[4,128,128]{2,1,0:T(8,128)(2,1)S(1)}) custom-call(bf16[512,128]{1,0:T(8,128)(2,1)} %bitcast.14, bf16[512,128]{1,0:T(8,128)(2,1)} %bitcast.15), custom_call_target="tpu_custom_call" | custom-call | flops 1048576 | bytes 65536 | tf_op jit(solution)/shard_map/pack_keys/pallas_call | solution.py:379
  1.8 3.1 %collective-permute-start = (bf16[4,128,128]{2,1,0:T(8,128)(2,1)S(1)}, bf16[4,128,128]{2,1,0:T(8,128)(2,1)S(1)}, u32[]{:S(2)}, u32[]{:S(2)}) collective-permute-start(bf16[4,128,128]{2,1,0:T(8,128)(2,1)S(1)} %get-tuple-element.38.refs_0_), channel_id=1, source_target_pairs={{0,2},{2,6},{6,4},{4,0},{1,3},{3,7},{7,5},{5,1},{8,10},{10,14},{14... | collective-permute-start | bytes 393224 | tf_op jit(solution)/shard_map/ppermute | solution.py:101
  4.9 1.1 %collective-permute-start.1 = (bf16[4,128,128]{2,1,0:T(8,128)(2,1)S(1)}, bf16[4,128,128]{2,1,0:T(8,128)(2,1)S(1)}, u32[]{:S(2)}, u32[]{:S(2)}) collective-permute-start(bf16[4,128,128]{2,1,0:T(8,128)(2,1)S(1)} %get-tuple-element.38.refs_0_), channel_id=1, source_target_pairs={{0,4},{2,0},{6,2},{4,6},{1,5},{3,1},{7,3},{5,7},{8,12},{10,8},{14,... | collective-permute-start | bytes 393224 | tf_op jit(solution)/shard_map/ppermute | solution.py:101
  6.0 3.5 %collective-permute-done.refs_1_ = bf16[4,128,128]{2,1,0:T(8,128)(2,1)S(1)} collective-permute-done((bf16[4,128,128]{2,1,0:T(8,128)(2,1)S(1)}, bf16[4,128,128]{2,1,0:T(8,128)(2,1)S(1)}, u32[]{:S(2)}, u32[]{:S(2)}) %collective-permute-start) | collective-permute-done | bytes 131104 | tf_op jit(solution)/shard_map/ppermute | solution.py:101
  9.5 3.5 %collective-permute-start.2 = (bf16[4,128,128]{2,1,0:T(8,128)(2,1)S(1)}, bf16[4,128,128]{2,1,0:T(8,128)(2,1)S(1)}, u32[]{:S(2)}, u32[]{:S(2)}) collective-permute-start(bf16[4,128,128]{2,1,0:T(8,128)(2,1)S(1)} %collective-permute-done.refs_1_), channel_id=1, source_target_pairs={{0,2},{2,6},{6,4},{4,0},{1,3},{3,7},{7,5},{5,1},{8,10},{10,14},{14... | collective-permute-start | bytes 393224 | tf_op jit(solution)/shard_map/ppermute | solution.py:101
  13.0 2.5 %query_sides.1 = (bf16[2,4,512,256]{3,2,1,0:T(8,128)(2,1)S(1)}, bf16[2,4,512,256]{3,2,1,0:T(8,128)(2,1)S(1)}) custom-call(bf16[128,32,128]{2,1,0:T(8,128)(2,1)} %bitcast.9, bf16[128,32,128]{2,1,0:T(8,128)(2,1)} %bitcast.10, bf16[128,32,128]{2,1,0:T(8,128)(2,1)} %bitcast.11), custom_call_target="tpu_custom_call" | custom-call | flops 1048576 | bytes 65536 | tf_op jit(solution)/shard_map/query_sides/pallas_call | solution.py:352
  15.5 3.4 %collective-permute-start.6 = (bf16[4,128,128]{2,1,0:T(8,128)(2,1)S(1)}, bf16[4,128,128]{2,1,0:T(8,128)(2,1)S(1)}, u32[]{:S(2)}, u32[]{:S(2)}) collective-permute-start(bf16[4,128,128]{2,1,0:T(8,128)(2,1)S(1)} %get-tuple-element.55.refs_0_), channel_id=1, source_target_pairs={{0,2},{2,6},{6,4},{4,0},{1,3},{3,7},{7,5},{5,1},{8,10},{10,14},{14... | collective-permute-start | bytes 393224 | tf_op jit(solution)/shard_map/ppermute | solution.py:101
  19.0 0.0 collective-permute-start.7
  19.0 2.4 %collective-permute-start.8 = (bf16[4,128,128]{2,1,0:T(8,128)(2,1)S(1)}, bf16[4,128,128]{2,1,0:T(8,128)(2,1)S(1)}, u32[]{:S(2)}, u32[]{:S(2)}) collective-permute-start(bf16[4,128,128]{2,1,0:T(8,128)(2,1)S(1)} %get-tuple-element.55.refs_0_), channel_id=1, source_target_pairs={{0,6},{2,4},{6,0},{4,2},{1,7},{3,5},{7,1},{5,3},{8,14},{10,12},{14... | collective-permute-start | bytes 393224 | tf_op jit(solution)/shard_map/ppermute | solution.py:101
  21.4 0.0 collective-permute-done.1.refs_2_
  21.4 0.0 collective-permute-done.2.refs_3_
  21.4 0.0 copy-done
  21.4 2.7 %weights.2 = (f32[2,512,1024]{2,1,0:T(8,128)S(1)}, f32[2,8,1024]{2,1,0:T(8,128)S(1)}, bf16[2,128,128]{2,1,0:T(8,128)(2,1)S(1)}, bf16[2,128,128]{2,1,0:T(8,128)(2...) custom-call(s32[8]{0:T(128)S(1)} %copy-done, ...), custom_call_target="tpu_custom_call" | custom-call | flops 4294967296 | bytes 65536 | tf_op jit(solution)/shard_map/weights/pallas_call | solution.py:331
  24.1 1.6 %query_grads.2 = (bf16[128,16,128]{2,1,0:T(8,128)(2,1)S(1)}, bf16[2,512,1024]{2,1,0:T(8,128)(2,1)S(1)}) custom-call(bf16[2,4,512,256]{3,2,1,0:T(8,128)(2,1)S(1)} %get-tuple-element.41.g_side_ref, f32[2,512,1024]{2,1,0:T(8,128)S(1)} %get-tuple-element.42.weight_ref, f32[2,8,1024]{2,1,0:T(8,128)S(1)} %get-tuple-element.43.scale_ref, ...), custom_call_target="tpu_custom_call" | custom-call | flops 4294967296 | bytes 65536 | tf_op jit(solution)/shard_map/query_grads/pallas_call | solution.py:331
  25.8 1.5 %key_grads.2 = (bf16[2,128,128]{2,1,0:T(8,128)(2,1)S(1)}, bf16[2,128,128]{2,1,0:T(8,128)(2,1)S(1)}, bf16[2,128,128]{2,1,0:T(8,128)(2,1)S(1)}, bf16[2,128,128]{2,1,0:T(8,128)(2,1)S(1)}) custom-call(bf16[2,4,512,256]{3,2,1,0:T(8,128)(2,1)S(1)} %get-tuple-element.53.q_side_ref, bf16[2,512,1024]{2,1,0:T(8,128)(2,1)S(1)} %get-tuple-element.44.dscore_ref), custom_call_target="tpu_custom_call" | custom-call | flops 1048576 | bytes 65536 | tf_op jit(solution)/shard_map/key_grads/pallas_call | solution.py:331
  27.3 2.5 %collective-permute-start.9 = (bf16[128,16,128]{2,1,0:T(8,128)(2,1)S(1)}, bf16[128,16,128]{2,1,0:T(8,128)(2,1)S(1)}, u32[]{:S(2)}, u32[]{:S(2)}) collective-permute-start(bf16[128,16,128]{2,1,0:T(8,128)(2,1)S(1)} %get-tuple-element.59), channel_id=1, source_target_pairs={{0,24},{8,0},{16,8},{24,16},{1,25},{9,1},{17,9},{25,17},{2,26},{10... | collective-permute-start | bytes 1572872 | tf_op jit(solution)/shard_map/ppermute | solution.py:125
  29.8 1.1 %collective-permute-start.5 = (bf16[4,128,128]{2,1,0:T(8,128)(2,1)S(1)}, bf16[4,128,128]{2,1,0:T(8,128)(2,1)S(1)}, u32[]{:S(2)}, u32[]{:S(2)}) collective-permute-start(bf16[4,128,128]{2,1,0:T(8,128)(2,1)S(1)} %constant_dynamic-update-slice_fusion.6), channel_id=1, source_target_pairs={{0,4},{2,0},{6,2},{4,6},{1,5},{3,1},{7,3},{5,7},{8,12},{10,8},{14,... | collective-permute-start | bytes 393224 | tf_op jit(solution)/shard_map/ppermute | solution.py:101
  31.0 0.0 collective-permute-done.6.refs_1_
  31.0 1.0 %collective-permute-start.3 = (bf16[4,128,128]{2,1,0:T(8,128)(2,1)S(1)}, bf16[4,128,128]{2,1,0:T(8,128)(2,1)S(1)}, u32[]{:S(2)}, u32[]{:S(2)}) collective-permute-start(bf16[4,128,128]{2,1,0:T(8,128)(2,1)S(1)} %constant_dynamic-update-slice_fusion.2), channel_id=1, source_target_pairs={{0,2},{2,6},{6,4},{4,0},{1,3},{3,7},{7,5},{5,1},{8,10},{10,14},{14... | collective-permute-start | bytes 393224 | tf_op jit(solution)/shard_map/ppermute | solution.py:101
  32.0 0.0 collective-permute-done.7.refs_2_
  32.0 0.0 collective-permute-done.8.refs_3_
  32.0 2.7 %weights.3 = (f32[2,512,1024]{2,1,0:T(8,128)S(1)}, f32[2,8,1024]{2,1,0:T(8,128)S(1)}, bf16[2,128,128]{2,1,0:T(8,128)(2,1)S(1)}, bf16[2,128,128]{2,1,0:T(8,128)(2...) custom-call(s32[8]{0:T(128)S(1)} %copy-done, ...), custom_call_target="tpu_custom_call" | custom-call | flops 1073741824 | bytes 65536 | tf_op jit(solution)/shard_map/weights/pallas_call | solution.py:331
  34.8 1.6 %query_grads.3 = (bf16[128,16,128]{2,1,0:T(8,128)(2,1)S(1)}, bf16[2,512,1024]{2,1,0:T(8,128)(2,1)S(1)}) custom-call(bf16[2,4,512,256]{3,2,1,0:T(8,128)(2,1)S(1)} %get-tuple-element.41.g_side_ref, f32[2,512,1024]{2,1,0:T(8,128)S(1)} %get-tuple-element.56.weight_ref, f32[2,8,1024]{2,1,0:T(8,128)S(1)} %get-tuple-element.57.scale_ref, ...), custom_call_target="tpu_custom_call" | custom-call | flops 1073741824 | bytes 65536 | tf_op jit(solution)/shard_map/query_grads/pallas_call | solution.py:331
  36.4 0.6 %collective-permute-start.13 = (bf16[128,16,128]{2,1,0:T(8,128)(2,1)S(1)}, bf16[128,16,128]{2,1,0:T(8,128)(2,1)S(1)}, u32[]{:S(2)}, u32[]{:S(2)}) collective-permute-start(bf16[128,16,128]{2,1,0:T(8,128)(2,1)S(1)} %get-tuple-element.72), channel_id=1, source_target_pairs={{0,24},{8,0},{16,8},{24,16},{1,25},{9,1},{17,9},{25,17},{2,26},{10... | collective-permute-start | bytes 1572872 | tf_op jit(solution)/shard_map/ppermute | solution.py:125
  37.0 0.0 collective-permute-done.3
  37.0 4.1 %collective-permute-start.4 = (bf16[4,128,128]{2,1,0:T(8,128)(2,1)S(1)}, bf16[4,128,128]{2,1,0:T(8,128)(2,1)S(1)}, u32[]{:S(2)}, u32[]{:S(2)}) collective-permute-start(bf16[4,128,128]{2,1,0:T(8,128)(2,1)S(1)} %add_convert_fusion.1), channel_id=1, source_target_pairs={{0,2},{2,6},{6,4},{4,0},{1,3},{3,7},{7,5},{5,1},{8,10},{10,14},{14... | collective-permute-start | bytes 393224 | tf_op jit(solution)/shard_map/ppermute | solution.py:101
  41.1 0.0 collective-permute-done.5.refs_2_
  41.1 1.1 %collective-permute-done.9 = bf16[128,16,128]{2,1,0:T(8,128)(2,1)S(1)} collective-permute-done((bf16[128,16,128]{2,1,0:T(8,128)(2,1)S(1)}, bf16[128,16,128]{2,1,0:T(8,128)(2,1)S(1)}, u32[]{:S(2)}, u32[]{:S(2)}) %collective-permute-start.9) | collective-permute-done | bytes 524320 | tf_op jit(solution)/shard_map/ppermute | solution.py:125
  42.2 1.5 %key_grads.3 = (bf16[2,128,128]{2,1,0:T(8,128)(2,1)S(1)}, bf16[2,128,128]{2,1,0:T(8,128)(2,1)S(1)}, bf16[2,128,128]{2,1,0:T(8,128)(2,1)S(1)}, bf16[2,128,128]{2,1,0:T(8,128)(2,1)S(1)}) custom-call(bf16[2,4,512,256]{3,2,1,0:T(8,128)(2,1)S(1)} %get-tuple-element.53.q_side_ref, bf16[2,512,1024]{2,1,0:T(8,128)(2,1)S(1)} %get-tuple-element.60.dscore_ref), custom_call_target="tpu_custom_call" | custom-call | flops 1048576 | bytes 65536 | tf_op jit(solution)/shard_map/key_grads/pallas_call | solution.py:331
  43.7 0.1 collective-permute-start.10
  43.8 3.0 %collective-permute-start.12 = (bf16[4,128,128]{2,1,0:T(8,128)(2,1)S(1)}, bf16[4,128,128]{2,1,0:T(8,128)(2,1)S(1)}, u32[]{:S(2)}, u32[]{:S(2)}) collective-permute-start(bf16[4,128,128]{2,1,0:T(8,128)(2,1)S(1)} %pad_maximum_fusion.2), channel_id=1, source_target_pairs={{0,4},{2,0},{6,2},{4,6},{1,5},{3,1},{7,3},{5,7},{8,12},{10,8},{14,... | collective-permute-start | bytes 393224 | tf_op jit(solution)/shard_map/ppermute | solution.py:101
  46.8 4.5 %collective-permute-done.10 = bf16[4,128,128]{2,1,0:T(8,128)(2,1)S(1)} collective-permute-done((bf16[4,128,128]{2,1,0:T(8,128)(2,1)S(1)}, bf16[4,128,128]{2,1,0:T(8,128)(2,1)S(1)}, u32[]{:S(2)}, u32[]{:S(2)}) %collective-permute-start.10) | collective-permute-done | bytes 131104 | tf_op jit(solution)/shard_map/ppermute | solution.py:101
  51.4 0.1 collective-permute-start.11
  51.4 0.0 collective-permute-done.13
  51.5 1.2 %maximum_select_fusion = bf16[1,128,32,128]{3,2,1,0:T(8,128)(2,1)} fusion(bf16[1,128,16,128]{3,2,1,0:T(8,128)(2,1)S(1)} %bitcast.13, bf16[1,128,16,128]{3,2,1,0:T(8,128)(2,1)S(1)} %bitcast.12, pred[]{:T(512)S(6)} %eq.3), kind=kLoop, calls=%fused_computation | loop fusion | flops 2621440 | bytes 2097153 | tf_op jit(solution)/shard_map/jit(_where)/select_n | solution.py:448
  52.6 0.0 collective-permute-done.4.refs_1_
  52.6 0.0 collective-permute-done.12.refs_5_
  52.6 4.7 %collective-permute-done.11.refs_4_ = bf16[4,128,128]{2,1,0:T(8,128)(2,1)S(1)} collective-permute-done((bf16[4,128,128]{2,1,0:T(8,128)(2,1)S(1)}, bf16[4,128,128]{2,1,0:T(8,128)(2,1)S(1)}, u32[]{:S(2)}, u32[]{:S(2)}) %collective-permute-start.11) | collective-permute-done | bytes 131104 | tf_op jit(solution)/shard_map/ppermute | solution.py:101
  57.3 0.8 %lay_out.1 = (bf16[512,128]{1,0:T(8,128)(2,1)}, bf16[512,128]{1,0:T(8,128)(2,1)}) custom-call(bf16[4,128,128]{2,1,0:T(8,128)(2,1)S(1)} %constant_dynamic-update-slice_fusion.refs_0_, bf16[4,128,128]{2,1,0:T(8,128)(2,1)S(1)} %collective-permute-done.4.refs_1_, bf16[4,128,128]{2,1,0:T(8,128)(2,1)S(1)} %collective-permute-done.5.refs_2_, ...), custom_call_target="tpu_custom_call" | custom-call | flops 1048576 | bytes 65536 | tf_op jit(solution)/shard_map/lay_out/pallas_call | solution.py:331
  (13 shorter events, 0.2 us)
Async XLA Ops:
  0.6 20.8 %copy-start = (s32[8]{0:T(128)S(1)}, s32[8]{0:T(128)}, u32[]{:S(2)}) copy-start(s32[8]{0:T(128)} %order_ref.3) | copy-start | bytes 100
  1.8 7.7 %collective-permute-start = (bf16[4,128,128]{2,1,0:T(8,128)(2,1)S(1)}, bf16[4,128,128]{2,1,0:T(8,128)(2,1)S(1)}, u32[]{:S(2)}, u32[]{:S(2)}) collective-permute-start(bf16[4,128,128]{2,1,0:T(8,128)(2,1)S(1)} %get-tuple-element.38.refs_0_), channel_id=1, source_target_pairs={{0,2},{2,6},{6,4},{4,0},{1,3},{3,7},{7,5},{5,1},{8,10},{10,14},{14... | collective-permute-start | bytes 393224 | tf_op jit(solution)/shard_map/ppermute | solution.py:101
  4.9 16.5 %collective-permute-start.1 = (bf16[4,128,128]{2,1,0:T(8,128)(2,1)S(1)}, bf16[4,128,128]{2,1,0:T(8,128)(2,1)S(1)}, u32[]{:S(2)}, u32[]{:S(2)}) collective-permute-start(bf16[4,128,128]{2,1,0:T(8,128)(2,1)S(1)} %get-tuple-element.38.refs_0_), channel_id=1, source_target_pairs={{0,4},{2,0},{6,2},{4,6},{1,5},{3,1},{7,3},{5,7},{8,12},{10,8},{14,... | collective-permute-start | bytes 393224 | tf_op jit(solution)/shard_map/ppermute | solution.py:101
  9.5 11.9 %collective-permute-start.2 = (bf16[4,128,128]{2,1,0:T(8,128)(2,1)S(1)}, bf16[4,128,128]{2,1,0:T(8,128)(2,1)S(1)}, u32[]{:S(2)}, u32[]{:S(2)}) collective-permute-start(bf16[4,128,128]{2,1,0:T(8,128)(2,1)S(1)} %collective-permute-done.refs_1_), channel_id=1, source_target_pairs={{0,2},{2,6},{6,4},{4,0},{1,3},{3,7},{7,5},{5,1},{8,10},{10,14},{14... | collective-permute-start | bytes 393224 | tf_op jit(solution)/shard_map/ppermute | solution.py:101
  15.5 15.5 %collective-permute-start.6 = (bf16[4,128,128]{2,1,0:T(8,128)(2,1)S(1)}, bf16[4,128,128]{2,1,0:T(8,128)(2,1)S(1)}, u32[]{:S(2)}, u32[]{:S(2)}) collective-permute-start(bf16[4,128,128]{2,1,0:T(8,128)(2,1)S(1)} %get-tuple-element.55.refs_0_), channel_id=1, source_target_pairs={{0,2},{2,6},{6,4},{4,0},{1,3},{3,7},{7,5},{5,1},{8,10},{10,14},{14... | collective-permute-start | bytes 393224 | tf_op jit(solution)/shard_map/ppermute | solution.py:101
  19.0 13.1 %collective-permute-start.7 = (bf16[4,128,128]{2,1,0:T(8,128)(2,1)S(1)}, bf16[4,128,128]{2,1,0:T(8,128)(2,1)S(1)}, u32[]{:S(2)}, u32[]{:S(2)}) collective-permute-start(bf16[4,128,128]{2,1,0:T(8,128)(2,1)S(1)} %get-tuple-element.55.refs_0_), channel_id=1, source_target_pairs={{0,4},{2,0},{6,2},{4,6},{1,5},{3,1},{7,3},{5,7},{8,12},{10,8},{14,... | collective-permute-start | bytes 393224 | tf_op jit(solution)/shard_map/ppermute | solution.py:101
  19.0 13.1 %collective-permute-start.8 = (bf16[4,128,128]{2,1,0:T(8,128)(2,1)S(1)}, bf16[4,128,128]{2,1,0:T(8,128)(2,1)S(1)}, u32[]{:S(2)}, u32[]{:S(2)}) collective-permute-start(bf16[4,128,128]{2,1,0:T(8,128)(2,1)S(1)} %get-tuple-element.55.refs_0_), channel_id=1, source_target_pairs={{0,6},{2,4},{6,0},{4,2},{1,7},{3,5},{7,1},{5,3},{8,14},{10,12},{14... | collective-permute-start | bytes 393224 | tf_op jit(solution)/shard_map/ppermute | solution.py:101
  27.3 14.9 %collective-permute-start.9 = (bf16[128,16,128]{2,1,0:T(8,128)(2,1)S(1)}, bf16[128,16,128]{2,1,0:T(8,128)(2,1)S(1)}, u32[]{:S(2)}, u32[]{:S(2)}) collective-permute-start(bf16[128,16,128]{2,1,0:T(8,128)(2,1)S(1)} %get-tuple-element.59), channel_id=1, source_target_pairs={{0,24},{8,0},{16,8},{24,16},{1,25},{9,1},{17,9},{25,17},{2,26},{10... | collective-permute-start | bytes 1572872 | tf_op jit(solution)/shard_map/ppermute | solution.py:125
  29.8 11.3 %collective-permute-start.5 = (bf16[4,128,128]{2,1,0:T(8,128)(2,1)S(1)}, bf16[4,128,128]{2,1,0:T(8,128)(2,1)S(1)}, u32[]{:S(2)}, u32[]{:S(2)}) collective-permute-start(bf16[4,128,128]{2,1,0:T(8,128)(2,1)S(1)} %constant_dynamic-update-slice_fusion.6), channel_id=1, source_target_pairs={{0,4},{2,0},{6,2},{4,6},{1,5},{3,1},{7,3},{5,7},{8,12},{10,8},{14,... | collective-permute-start | bytes 393224 | tf_op jit(solution)/shard_map/ppermute | solution.py:101
  31.0 6.0 %collective-permute-start.3 = (bf16[4,128,128]{2,1,0:T(8,128)(2,1)S(1)}, bf16[4,128,128]{2,1,0:T(8,128)(2,1)S(1)}, u32[]{:S(2)}, u32[]{:S(2)}) collective-permute-start(bf16[4,128,128]{2,1,0:T(8,128)(2,1)S(1)} %constant_dynamic-update-slice_fusion.2), channel_id=1, source_target_pairs={{0,2},{2,6},{6,4},{4,0},{1,3},{3,7},{7,5},{5,1},{8,10},{10,14},{14... | collective-permute-start | bytes 393224 | tf_op jit(solution)/shard_map/ppermute | solution.py:101
  36.4 15.0 %collective-permute-start.13 = (bf16[128,16,128]{2,1,0:T(8,128)(2,1)S(1)}, bf16[128,16,128]{2,1,0:T(8,128)(2,1)S(1)}, u32[]{:S(2)}, u32[]{:S(2)}) collective-permute-start(bf16[128,16,128]{2,1,0:T(8,128)(2,1)S(1)} %get-tuple-element.72), channel_id=1, source_target_pairs={{0,24},{8,0},{16,8},{24,16},{1,25},{9,1},{17,9},{25,17},{2,26},{10... | collective-permute-start | bytes 1572872 | tf_op jit(solution)/shard_map/ppermute | solution.py:125
  37.0 15.6 %collective-permute-start.4 = (bf16[4,128,128]{2,1,0:T(8,128)(2,1)S(1)}, bf16[4,128,128]{2,1,0:T(8,128)(2,1)S(1)}, u32[]{:S(2)}, u32[]{:S(2)}) collective-permute-start(bf16[4,128,128]{2,1,0:T(8,128)(2,1)S(1)} %add_convert_fusion.1), channel_id=1, source_target_pairs={{0,2},{2,6},{6,4},{4,0},{1,3},{3,7},{7,5},{5,1},{8,10},{10,14},{14... | collective-permute-start | bytes 393224 | tf_op jit(solution)/shard_map/ppermute | solution.py:101
  43.7 7.6 %collective-permute-start.10 = (bf16[4,128,128]{2,1,0:T(8,128)(2,1)S(1)}, bf16[4,128,128]{2,1,0:T(8,128)(2,1)S(1)}, u32[]{:S(2)}, u32[]{:S(2)}) collective-permute-start(bf16[4,128,128]{2,1,0:T(8,128)(2,1)S(1)} %pad_maximum_fusion.1), channel_id=1, source_target_pairs={{0,2},{2,6},{6,4},{4,0},{1,3},{3,7},{7,5},{5,1},{8,10},{10,14},{14... | collective-permute-start | bytes 393224 | tf_op jit(solution)/shard_map/ppermute | solution.py:101
  43.8 8.8 %collective-permute-start.12 = (bf16[4,128,128]{2,1,0:T(8,128)(2,1)S(1)}, bf16[4,128,128]{2,1,0:T(8,128)(2,1)S(1)}, u32[]{:S(2)}, u32[]{:S(2)}) collective-permute-start(bf16[4,128,128]{2,1,0:T(8,128)(2,1)S(1)} %pad_maximum_fusion.2), channel_id=1, source_target_pairs={{0,4},{2,0},{6,2},{4,6},{1,5},{3,1},{7,3},{5,7},{8,12},{10,8},{14,... | collective-permute-start | bytes 393224 | tf_op jit(solution)/shard_map/ppermute | solution.py:101
  51.4 5.9 %collective-permute-start.11 = (bf16[4,128,128]{2,1,0:T(8,128)(2,1)S(1)}, bf16[4,128,128]{2,1,0:T(8,128)(2,1)S(1)}, u32[]{:S(2)}, u32[]{:S(2)}) collective-permute-start(bf16[4,128,128]{2,1,0:T(8,128)(2,1)S(1)} %add_convert_fusion), channel_id=1, source_target_pairs={{0,2},{2,6},{6,4},{4,0},{1,3},{3,7},{7,5},{5,1},{8,10},{10,14},{14... | collective-permute-start | bytes 393224 | tf_op jit(solution)/shard_map/ppermute | solution.py:101

commit v5 on v4

--- a/solution.py
+++ b/solution.py
@@ -11,7 +11,7 @@
 NEG = -1e30
 STAGES = 2
 WORK = 2**20
-BIG_WORK = (2**32, 2**30)
+BIG_WORK = (2**32, 2**32, 2**32)
 F32 = jnp.float32
 BF16 = jnp.bfloat16
 
@@ -66,17 +66,17 @@
             outs[group // per_stage][part * per_stage + group % per_stage] = picked
 
 
-def finish_kernel(stages, *refs):
+def finish_kernel(counts, *refs):
     parts, outs, rows_ref = refs[:-3], refs[-3:-1], refs[-1]
-    terms = len(parts) // stages
     both, tokens, _ = parts[0].shape
     per_stage = both // 2
-    groups = per_stage * stages
+    groups = per_stage * len(counts)
     for part, out in enumerate(outs):
         for group in range(groups):
-            first = group // per_stage * terms
+            stage = group // per_stage
+            terms = parts[sum(counts[:stage]) : sum(counts[: stage + 1])]
             at = part * per_stage + group % per_stage
-            rows = [ref[at].astype(F32) for ref in parts[first : first + terms]]
+            rows = [ref[at].astype(F32) for ref in terms]
             rows_ref[pl.ds(group, tokens, stride=groups), :] = sum(rows[1:], rows[0])
         out[...] = rows_ref[...].astype(BF16)
 
@@ -103,20 +103,13 @@
     )
 
 
-def gather(block, axis, relay_after=None):
+def gather_rest(block, up, down, axis):
     count = lax.axis_size(axis)
-    blocks = {0: block}
-    for step in range(1, count // 2 + 1):
-        for sign in (1, -1):
-            if sign < 0 and 2 * step == count:
-                continue
-            if step > 1 and relay_after is not None:
-                moving, shift = blocks[(sign * (step - 1)) % count], sign
-                if step == 2:
-                    moving, _ = lax.optimization_barrier((moving, relay_after))
-            else:
-                moving, shift = block, sign * step
-            blocks[(sign * step) % count] = passed(moving, axis, shift)
+    blocks = {0: block, 1: up, count - 1: down}
+    for step in range(2, count // 2 + 1):
+        up = blocks[step] = passed(up, axis, 1)
+        if 2 * step < count:
+            down = blocks[count - step] = passed(down, axis, -1)
     return [blocks[step] for step in range(count)]
 
 
@@ -129,20 +122,29 @@
     return (a.astype(F32) + b.astype(F32)).astype(BF16)
 
 
-def scatter_sums(parts, axis, relay_after):
+def up_sums(parts, axis, joined=None, relay_after=()):
     count = lax.axis_size(axis)
-    terms, relayed = [parts[0]], []
-    for step, longest in ((1, count // 2), (-1, (count - 1) // 2)):
-        moving = None
-        for distance in range(longest, 0, -1):
-            part = parts[(-step * distance) % count]
-            if moving is not None:
-                moving, _ = lax.optimization_barrier((moving, relay_after))
-                part = added(moving, part)
-                relayed.append(part)
-            moving = passed(part, axis, step)
-        terms.append(moving)
-    return terms, relayed
+    longest = count // 2
+    part = parts[count - longest]
+    arrived = None
+    for distance in range(longest - 1, 0, -1):
+        if arrived is None and joined is not None:
+            both = passed(jnp.concatenate([joined, part], axis=0), axis, 1)
+            arrived, moving = both[: joined.shape[0]], both[joined.shape[0] :]
+        else:
+            moving = passed(part, axis, 1)
+        moving, _ = lax.optimization_barrier((moving, relay_after))
+        part = added(moving, parts[count - distance])
+    return part, arrived
+
+
+def down_sums(parts, axis):
+    count = lax.axis_size(axis)
+    moving = None
+    for distance in range((count - 1) // 2, 0, -1):
+        part = parts[distance]
+        moving = passed(part if moving is None else added(moving, part), axis, -1)
+    return moving
 
 
 def sides_kernel(groups, q_hbm, g_hbm, o_hbm, q_side_ref, g_side_ref, in_ref, sems):
@@ -387,12 +389,12 @@
         name="pack_keys",
     )(in_hbm(key_heads.reshape(-1, size)), in_hbm(value_heads.reshape(-1, size)))
 
-    gathered = [gather(kv_blocks[0], "ctx", ())]
-    q_loads, _ = after((queries[0], gathered[0][1]))
+    near = [(passed(kv_blocks[0], "ctx", 1), passed(kv_blocks[0], "ctx", -1))]
+    q_loads, _ = after((queries[0], near[0][0]))
     q_side, g_side = make_sides(groups, q_loads, output_grad[0], forward_out[0])
     for stage in range(1, STAGES):
         block, _ = after((kv_blocks[stage], q_side))
-        gathered.append(gather(block, "ctx"))
+        near.append((passed(block, "ctx", 1), passed(block, "ctx", -1)))
 
     def sums_of(stage, dscore, dv_parts):
         dk_parts = call(
@@ -408,8 +410,10 @@
         return [parts[slots.index(step)] for step in range(blocks)]
 
     handed, terms = [], []
+    gathered = gather_rest(kv_blocks[0], *near[0], "ctx")
+    last_hop = None
     for stage in range(STAGES):
-        kv_all = [gathered[stage][step] for step in slots]
+        kv_all = [gathered[step] for step in slots]
         weight, scale, *dv_parts = call(
             functools.partial(weights_kernel, stage * per_stage, blocks),
             "weights",
@@ -420,6 +424,10 @@
             [block_order, q_side, g_side, *kv_all],
             True,
         )
+        if stage + 1 < STAGES:
+            up, down = near[stage + 1]
+            up, scale = after((up, scale))
+            gathered = gather_rest(kv_blocks[stage + 1], up, down, "ctx")
         handed_part, dscore = call(
             functools.partial(dq_kernel, stage * per_stage, blocks),
             "query_grads",
@@ -430,22 +438,36 @@
                 pltpu.VMEM((per_stage, 2 * size, keys), BF16),
             ],
             limit,
-            BIG_WORK[min(stage, 1)],
+            BIG_WORK[2 * min(stage, 1)],
             [g_side, weight, scale, *kv_all],
         )
-        handed.append(passed_down(handed_part, "pipe"))
-        if stage > 0:
-            dscore, _ = after((dscore, (relayed, terms[-1], handed[0])))
+        if stage == 0:
+            handed.append(passed_down(handed_part, "pipe"))
+        else:
+            dscore, _ = after((dscore, (last_hop, terms[-1])))
         parts = sums_of(stage, dscore, dv_parts)
         q_side, _ = after((q_side, parts))
-        stage_terms, relayed = scatter_sums(parts, "ctx", handed[:stage])
-        terms += stage_terms
-    key_grad, value_grad = call(
-        functools.partial(finish_kernel, STAGES), "lay_out", [flat, flat], [rows_scratch], 8, WORK, terms
-    )
+        if stage > 0:
+            handed_part, _ = after((handed_part, parts))
+            handed.append(passed_down(handed_part, "pipe"))
+        last_hop, arrived = up_sums(parts, "ctx", last_hop, handed[:stage])
+        if arrived is not None:
+            terms[-1] = terms[-1] + [arrived]
+        terms.append([parts[0], down_sums(parts, "ctx")])
+    terms[-1].append(passed(last_hop, "ctx", 1))
     handed = jnp.concatenate(handed, axis=1)[None]
     last = lax.axis_index("pipe") == lax.axis_size("pipe") - 1
     handed = jnp.where(last, jnp.zeros_like(handed), handed)
+    terms[0][0], _ = after((terms[0][0], handed))
+    key_grad, value_grad = call(
+        functools.partial(finish_kernel, [len(found) for found in terms]),
+        "lay_out",
+        [flat, flat],
+        [rows_scratch],
+        8,
+        WORK,
+        sum(terms, []),
+    )
     shape = key_heads.shape
     return (
         key_grad.reshape(shape),

time: 58.6 us -> 57.7 us (0.985)
  waiting for transfers between devices: 13.9 us -> 12.8 us
    ppermute x2, starting transfers between devices: 3.08 us -> 5 us  [passed_down(): lax.ppermute(value, axis, [(at, (at - 1) % count) for at in range(count)])]
    ppermute x12 -> x11, starting transfers between devices: 22.8 us -> 21.2 us  [passed(): lax.ppermute(value, axis, [(order[at], order[(at + step) % count]) for at...]
    ppermute x2, waiting for transfers between devices: 1.11 us -> 0.52 us  [passed_down(): lax.ppermute(value, axis, [(at, (at - 1) % count) for at in range(count)])]
    ppermute x12 -> x11, waiting for transfers between devices: 12.7 us -> 12.3 us  [passed(): lax.ppermute(value, axis, [(order[at], order[(at + step) % count]) for at...]
  transfers between devices with their start and end apart: 14 -> 13, of which waited for: 4 -> 6; matrix products, arithmetic and copies ran while one was open for 2% -> 2% of each run, Pallas kernels for 24% -> 25%
where the time goes in v5:
time: 57.7 us; the launch traced here: 57.6 us
  starting transfers between devices  26.2 us (45%)
  Pallas kernels  16.3 us (28%)
  waiting for transfers between devices  12.8 us (22%)
  other arithmetic  1.29 us (2%)
  between operations  0.81 us (1%)
    ppermute x11, starting transfers between devices, passed(): lax.ppermute(value, axis, [(order[at], order[(at + step) % count]) for at...  21.2 us
    pallas_call x7, Pallas kernels, call(): pl.pallas_call(kernel, in_specs=([SMEM] if smem else []) + [VMEM] * (len(...  12.7 us
    ppermute x11, waiting for transfers between devices, passed(): lax.ppermute(value, axis, [(order[at], order[(at + step) % count]) for at...  12.3 us
    ppermute x2, starting transfers between devices, passed_down(): lax.ppermute(value, axis, [(at, (at - 1) % count) for at in range(count)])  5 us
    pallas_call x1, Pallas kernels, make_sides(): pl.pallas_call(functools.partial(sides_kernel, groups), in_specs=[HBM] *...  2.48 us
    select_n x1, other arithmetic, shards(): handed = jnp.where(last, jnp.zeros_like(handed), handed)  1.17 us
  transfers between devices with their start and end apart: 13, of which 6 were waited for; matrix products, arithmetic and copies ran while one was open for 2% of the time, Pallas kernels for 25%

profile of v5, /device:TPU:0, one launch (start us, length us, event | category | flops | bytes accessed | tf_op | source)
XLA Modules:
  0.0 57.6 jit_solution(14000975118723979163)
XLA Ops:
  0.6 0.0 copy-start
  0.6 1.1 %pack_keys.1 = (bf16[4,128,128]{2,1,0:T(8,128)(2,1)S(1)}, bf16[4,128,128]{2,1,0:T(8,128)(2,1)S(1)}) custom-call(bf16[512,128]{1,0:T(8,128)(2,1)} %bitcast.14, bf16[512,128]{1,0:T(8,128)(2,1)} %bitcast.15), custom_call_target="tpu_custom_call" | custom-call | flops 1048576 | bytes 65536 | tf_op jit(solution)/shard_map/pack_keys/pallas_call | solution.py:381
  1.8 3.1 %collective-permute-start = (bf16[4,128,128]{2,1,0:T(8,128)(2,1)S(1)}, bf16[4,128,128]{2,1,0:T(8,128)(2,1)S(1)}, u32[]{:S(2)}, u32[]{:S(2)}) collective-permute-start(bf16[4,128,128]{2,1,0:T(8,128)(2,1)S(1)} %get-tuple-element.42.refs_0_), channel_id=1, source_target_pairs={{0,2},{2,6},{6,4},{4,0},{1,3},{3,7},{7,5},{5,1},{8,10},{10,14},{14... | collective-permute-start | bytes 393224 | tf_op jit(solution)/shard_map/ppermute | solution.py:101
  4.9 1.1 %collective-permute-start.1 = (bf16[4,128,128]{2,1,0:T(8,128)(2,1)S(1)}, bf16[4,128,128]{2,1,0:T(8,128)(2,1)S(1)}, u32[]{:S(2)}, u32[]{:S(2)}) collective-permute-start(bf16[4,128,128]{2,1,0:T(8,128)(2,1)S(1)} %get-tuple-element.42.refs_0_), channel_id=1, source_target_pairs={{0,4},{2,0},{6,2},{4,6},{1,5},{3,1},{7,3},{5,7},{8,12},{10,8},{14,... | collective-permute-start | bytes 393224 | tf_op jit(solution)/shard_map/ppermute | solution.py:101
  6.0 3.5 %collective-permute-done.refs_1_ = bf16[4,128,128]{2,1,0:T(8,128)(2,1)S(1)} collective-permute-done((bf16[4,128,128]{2,1,0:T(8,128)(2,1)S(1)}, bf16[4,128,128]{2,1,0:T(8,128)(2,1)S(1)}, u32[]{:S(2)}, u32[]{:S(2)}) %collective-permute-start) | collective-permute-done | bytes 131104 | tf_op jit(solution)/shard_map/ppermute | solution.py:101
  9.5 3.5 %collective-permute-start.2 = (bf16[4,128,128]{2,1,0:T(8,128)(2,1)S(1)}, bf16[4,128,128]{2,1,0:T(8,128)(2,1)S(1)}, u32[]{:S(2)}, u32[]{:S(2)}) collective-permute-start(bf16[4,128,128]{2,1,0:T(8,128)(2,1)S(1)} %collective-permute-done.refs_1_), channel_id=1, source_target_pairs={{0,2},{2,6},{6,4},{4,0},{1,3},{3,7},{7,5},{5,1},{8,10},{10,14},{14... | collective-permute-start | bytes 393224 | tf_op jit(solution)/shard_map/ppermute | solution.py:101
  13.0 2.5 %query_sides.1 = (bf16[2,4,512,256]{3,2,1,0:T(8,128)(2,1)S(1)}, bf16[2,4,512,256]{3,2,1,0:T(8,128)(2,1)S(1)}) custom-call(bf16[128,32,128]{2,1,0:T(8,128)(2,1)} %bitcast.9, bf16[128,32,128]{2,1,0:T(8,128)(2,1)} %bitcast.10, bf16[128,32,128]{2,1,0:T(8,128)(2,1)} %bitcast.11), custom_call_target="tpu_custom_call" | custom-call | flops 1048576 | bytes 65536 | tf_op jit(solution)/shard_map/query_sides/pallas_call | solution.py:354
  15.5 3.4 %collective-permute-start.3 = (bf16[4,128,128]{2,1,0:T(8,128)(2,1)S(1)}, bf16[4,128,128]{2,1,0:T(8,128)(2,1)S(1)}, u32[]{:S(2)}, u32[]{:S(2)}) collective-permute-start(bf16[4,128,128]{2,1,0:T(8,128)(2,1)S(1)} %get-tuple-element.48.refs_0_), channel_id=1, source_target_pairs={{0,2},{2,6},{6,4},{4,0},{1,3},{3,7},{7,5},{5,1},{8,10},{10,14},{14... | collective-permute-start | bytes 393224 | tf_op jit(solution)/shard_map/ppermute | solution.py:101
  19.0 0.0 collective-permute-start.5
  19.0 0.0 collective-permute-done.1.refs_2_
  19.0 0.0 collective-permute-done.2.refs_3_
  19.0 0.0 copy-done
  19.0 2.8 %weights.2 = (f32[2,512,1024]{2,1,0:T(8,128)S(1)}, f32[2,8,1024]{2,1,0:T(8,128)S(1)}, bf16[2,128,128]{2,1,0:T(8,128)(2,1)S(1)}, bf16[2,128,128]{2,1,0:T(8,128)(2...) custom-call(s32[8]{0:T(128)S(1)} %copy-done, ...), custom_call_target="tpu_custom_call" | custom-call | flops 4294967296 | bytes 65536 | tf_op jit(solution)/shard_map/weights/pallas_call | solution.py:333
  21.7 0.5 collective-permute-done.3.refs_1_
  22.3 1.7 %query_grads.2 = (bf16[128,16,128]{2,1,0:T(8,128)(2,1)S(1)}, bf16[2,512,1024]{2,1,0:T(8,128)(2,1)S(1)}) custom-call(bf16[2,4,512,256]{3,2,1,0:T(8,128)(2,1)S(1)} %get-tuple-element.45.g_side_ref, f32[2,512,1024]{2,1,0:T(8,128)S(1)} %get-tuple-element.46.weight_ref, f32[2,8,1024]{2,1,0:T(8,128)S(1)} %get-tuple-element.50.scale_ref, ...), custom_call_target="tpu_custom_call" | custom-call | flops 4294967296 | bytes 65536 | tf_op jit(solution)/shard_map/query_grads/pallas_call | solution.py:333
  24.0 1.5 %key_grads.2 = (bf16[2,128,128]{2,1,0:T(8,128)(2,1)S(1)}, bf16[2,128,128]{2,1,0:T(8,128)(2,1)S(1)}, bf16[2,128,128]{2,1,0:T(8,128)(2,1)S(1)}, bf16[2,128,128]{2,1,0:T(8,128)(2,1)S(1)}) custom-call(bf16[2,4,512,256]{3,2,1,0:T(8,128)(2,1)S(1)} %get-tuple-element.61.q_side_ref, bf16[2,512,1024]{2,1,0:T(8,128)(2,1)S(1)} %get-tuple-element.51.dscore_ref), custom_call_target="tpu_custom_call" | custom-call | flops 1048576 | bytes 65536 | tf_op jit(solution)/shard_map/key_grads/pallas_call | solution.py:333
  25.5 2.5 %collective-permute-start.7 = (bf16[4,128,128]{2,1,0:T(8,128)(2,1)S(1)}, bf16[4,128,128]{2,1,0:T(8,128)(2,1)S(1)}, u32[]{:S(2)}, u32[]{:S(2)}) collective-permute-start(bf16[4,128,128]{2,1,0:T(8,128)(2,1)S(1)} %constant_dynamic-update-slice_fusion.4), channel_id=1, source_target_pairs={{0,2},{2,6},{6,4},{4,0},{1,3},{3,7},{7,5},{5,1},{8,10},{10,14},{14... | collective-permute-start | bytes 393224 | tf_op jit(solution)/shard_map/ppermute | solution.py:101
  28.1 1.9 %collective-permute-start.6 = (bf16[4,128,128]{2,1,0:T(8,128)(2,1)S(1)}, bf16[4,128,128]{2,1,0:T(8,128)(2,1)S(1)}, u32[]{:S(2)}, u32[]{:S(2)}) collective-permute-start(bf16[4,128,128]{2,1,0:T(8,128)(2,1)S(1)} %collective-permute-done.3.refs_1_), channel_id=1, source_target_pairs={{0,2},{2,6},{6,4},{4,0},{1,3},{3,7},{7,5},{5,1},{8,10},{10,14},{14... | collective-permute-start | bytes 393224 | tf_op jit(solution)/shard_map/ppermute | solution.py:101
  30.0 1.1 %collective-permute-start.8 = (bf16[4,128,128]{2,1,0:T(8,128)(2,1)S(1)}, bf16[4,128,128]{2,1,0:T(8,128)(2,1)S(1)}, u32[]{:S(2)}, u32[]{:S(2)}) collective-permute-start(bf16[4,128,128]{2,1,0:T(8,128)(2,1)S(1)} %constant_dynamic-update-slice_fusion.2), channel_id=1, source_target_pairs={{0,4},{2,0},{6,2},{4,6},{1,5},{3,1},{7,3},{5,7},{8,12},{10,8},{14,... | collective-permute-start | bytes 393224 | tf_op jit(solution)/shard_map/ppermute | solution.py:101
  31.1 2.5 %collective-permute-start.4 = (bf16[128,16,128]{2,1,0:T(8,128)(2,1)S(1)}, bf16[128,16,128]{2,1,0:T(8,128)(2,1)S(1)}, u32[]{:S(2)}, u32[]{:S(2)}) collective-permute-start(bf16[128,16,128]{2,1,0:T(8,128)(2,1)S(1)} %get-tuple-element.54), channel_id=1, source_target_pairs={{0,24},{8,0},{16,8},{24,16},{1,25},{9,1},{17,9},{25,17},{2,26},{10... | collective-permute-start | bytes 1572872 | tf_op jit(solution)/shard_map/ppermute | solution.py:118
  33.6 0.0 collective-permute-done.7
  33.6 0.0 collective-permute-done.5.refs_2_
  33.6 0.8 %collective-permute-done.6.refs_3_ = bf16[4,128,128]{2,1,0:T(8,128)(2,1)S(1)} collective-permute-done((bf16[4,128,128]{2,1,0:T(8,128)(2,1)S(1)}, bf16[4,128,128]{2,1,0:T(8,128)(2,1)S(1)}, u32[]{:S(2)}, u32[]{:S(2)}) %collective-permute-start.6) | collective-permute-done | bytes 131104 | tf_op jit(solution)/shard_map/ppermute | solution.py:101
  34.5 2.7 %weights.3 = (f32[2,512,1024]{2,1,0:T(8,128)S(1)}, f32[2,8,1024]{2,1,0:T(8,128)S(1)}, bf16[2,128,128]{2,1,0:T(8,128)(2,1)S(1)}, bf16[2,128,128]{2,1,0:T(8,128)(2...) custom-call(s32[8]{0:T(128)S(1)} %copy-done, ...), custom_call_target="tpu_custom_call" | custom-call | flops 4294967296 | bytes 65536 | tf_op jit(solution)/shard_map/weights/pallas_call | solution.py:333
  37.2 1.7 %query_grads.3 = (bf16[128,16,128]{2,1,0:T(8,128)(2,1)S(1)}, bf16[2,512,1024]{2,1,0:T(8,128)(2,1)S(1)}) custom-call(bf16[2,4,512,256]{3,2,1,0:T(8,128)(2,1)S(1)} %get-tuple-element.45.g_side_ref, f32[2,512,1024]{2,1,0:T(8,128)S(1)} %get-tuple-element.63.weight_ref, f32[2,8,1024]{2,1,0:T(8,128)S(1)} %get-tuple-element.64.scale_ref, ...), custom_call_target="tpu_custom_call" | custom-call | flops 4294967296 | bytes 65536 | tf_op jit(solution)/shard_map/query_grads/pallas_call | solution.py:333
  39.0 0.0 collective-permute-done.8.refs_1_
  39.0 1.5 %key_grads.3 = (bf16[2,128,128]{2,1,0:T(8,128)(2,1)S(1)}, bf16[2,128,128]{2,1,0:T(8,128)(2,1)S(1)}, bf16[2,128,128]{2,1,0:T(8,128)(2,1)S(1)}, bf16[2,128,128]{2,1,0:T(8,128)(2,1)S(1)}) custom-call(bf16[2,4,512,256]{3,2,1,0:T(8,128)(2,1)S(1)} %get-tuple-element.61.q_side_ref, bf16[2,512,1024]{2,1,0:T(8,128)(2,1)S(1)} %get-tuple-element.67.dscore_ref), custom_call_target="tpu_custom_call" | custom-call | flops 1048576 | bytes 65536 | tf_op jit(solution)/shard_map/key_grads/pallas_call | solution.py:333
  40.6 1.0 %collective-permute-start.10 = (bf16[8,128,128]{2,1,0:T(8,128)(2,1)S(1)}, bf16[8,128,128]{2,1,0:T(8,128)(2,1)S(1)}, u32[]{:S(2)}, u32[]{:S(2)}) collective-permute-start(bf16[8,128,128]{2,1,0:T(8,128)(2,1)S(1)} %pad_maximum_fusion), channel_id=1, source_target_pairs={{0,2},{2,6},{6,4},{4,0},{1,3},{3,7},{7,5},{5,1},{8,10},{10,14},{14... | collective-permute-start | bytes 786440 | tf_op jit(solution)/shard_map/ppermute | solution.py:101
  41.6 2.5 %collective-permute-start.9 = (bf16[128,16,128]{2,1,0:T(8,128)(2,1)S(1)}, bf16[128,16,128]{2,1,0:T(8,128)(2,1)S(1)}, u32[]{:S(2)}, u32[]{:S(2)}) collective-permute-start(bf16[128,16,128]{2,1,0:T(8,128)(2,1)S(1)} %get-tuple-element.74), channel_id=1, source_target_pairs={{0,24},{8,0},{16,8},{24,16},{1,25},{9,1},{17,9},{25,17},{2,26},{10... | collective-permute-start | bytes 1572872 | tf_op jit(solution)/shard_map/ppermute | solution.py:118
  44.1 2.0 %collective-permute-start.11 = (bf16[4,128,128]{2,1,0:T(8,128)(2,1)S(1)}, bf16[4,128,128]{2,1,0:T(8,128)(2,1)S(1)}, u32[]{:S(2)}, u32[]{:S(2)}) collective-permute-start(bf16[4,128,128]{2,1,0:T(8,128)(2,1)S(1)} %constant_dynamic-update-slice_fusion.10), channel_id=1, source_target_pairs={{0,4},{2,0},{6,2},{4,6},{1,5},{3,1},{7,3},{5,7},{8,12},{10,8},{14,... | collective-permute-start | bytes 393224 | tf_op jit(solution)/shard_map/ppermute | solution.py:101
  46.1 4.7 %collective-permute-done.10 = bf16[8,128,128]{2,1,0:T(8,128)(2,1)S(1)} collective-permute-done((bf16[8,128,128]{2,1,0:T(8,128)(2,1)S(1)}, bf16[8,128,128]{2,1,0:T(8,128)(2,1)S(1)}, u32[]{:S(2)}, u32[]{:S(2)}) %collective-permute-start.10) | collective-permute-done | bytes 262176 | tf_op jit(solution)/shard_map/ppermute | solution.py:101
  50.8 0.0 collective-permute-done.4
  50.9 1.5 %collective-permute-start.12 = (bf16[4,128,128]{2,1,0:T(8,128)(2,1)S(1)}, bf16[4,128,128]{2,1,0:T(8,128)(2,1)S(1)}, u32[]{:S(2)}, u32[]{:S(2)}) collective-permute-start(bf16[4,128,128]{2,1,0:T(8,128)(2,1)S(1)} %add_convert_fusion), channel_id=1, source_target_pairs={{0,2},{2,6},{6,4},{4,0},{1,3},{3,7},{7,5},{5,1},{8,10},{10,14},{14... | collective-permute-start | bytes 393224 | tf_op jit(solution)/shard_map/ppermute | solution.py:101
  52.3 0.5 collective-permute-done.9
  52.9 1.2 %maximum_select_fusion = bf16[1,128,32,128]{3,2,1,0:T(8,128)(2,1)} fusion(bf16[1,128,16,128]{3,2,1,0:T(8,128)(2,1)S(1)} %bitcast.13, bf16[1,128,16,128]{3,2,1,0:T(8,128)(2,1)S(1)} %bitcast.12, pred[]{:T(512)S(6)} %eq.3), kind=kLoop, calls=%fused_computation | loop fusion | flops 2621440 | bytes 2097153 | tf_op jit(solution)/shard_map/jit(_where)/select_n | solution.py:460
  54.0 0.0 collective-permute-done.11.refs_4_
  54.0 2.7 %collective-permute-done.12.refs_5_ = bf16[4,128,128]{2,1,0:T(8,128)(2,1)S(1)} collective-permute-done((bf16[4,128,128]{2,1,0:T(8,128)(2,1)S(1)}, bf16[4,128,128]{2,1,0:T(8,128)(2,1)S(1)}, u32[]{:S(2)}, u32[]{:S(2)}) %collective-permute-start.12) | collective-permute-done | bytes 131104 | tf_op jit(solution)/shard_map/ppermute | solution.py:101
  56.8 0.8 %lay_out.1 = (bf16[512,128]{1,0:T(8,128)(2,1)}, bf16[512,128]{1,0:T(8,128)(2,1)}) custom-call(bf16[4,128,128]{2,1,0:T(8,128)(2,1)S(1)} %get-tuple-element.75.refs_0_, bf16[4,128,128]{2,1,0:T(8,128)(2,1)S(1)} %collective-permute-done.8.refs_1_, bf16[4,128,128]{2,1,0:T(8,128)(2,1)S(1)} %get-tuple-element.82.refs_2_, ...), custom_call_target="tpu_custom_call" | custom-call | flops 1048576 | bytes 65536 | tf_op jit(solution)/shard_map/lay_out/pallas_call | solution.py:333
  (17 shorter events, 0.3 us)
Async XLA Ops:
  0.6 18.3 %copy-start = (s32[8]{0:T(128)S(1)}, s32[8]{0:T(128)}, u32[]{:S(2)}) copy-start(s32[8]{0:T(128)} %order_ref.3) | copy-start | bytes 100
  1.8 7.7 %collective-permute-start = (bf16[4,128,128]{2,1,0:T(8,128)(2,1)S(1)}, bf16[4,128,128]{2,1,0:T(8,128)(2,1)S(1)}, u32[]{:S(2)}, u32[]{:S(2)}) collective-permute-start(bf16[4,128,128]{2,1,0:T(8,128)(2,1)S(1)} %get-tuple-element.42.refs_0_), channel_id=1, source_target_pairs={{0,2},{2,6},{6,4},{4,0},{1,3},{3,7},{7,5},{5,1},{8,10},{10,14},{14... | collective-permute-start | bytes 393224 | tf_op jit(solution)/shard_map/ppermute | solution.py:101
  4.9 14.1 %collective-permute-start.1 = (bf16[4,128,128]{2,1,0:T(8,128)(2,1)S(1)}, bf16[4,128,128]{2,1,0:T(8,128)(2,1)S(1)}, u32[]{:S(2)}, u32[]{:S(2)}) collective-permute-start(bf16[4,128,128]{2,1,0:T(8,128)(2,1)S(1)} %get-tuple-element.42.refs_0_), channel_id=1, source_target_pairs={{0,4},{2,0},{6,2},{4,6},{1,5},{3,1},{7,3},{5,7},{8,12},{10,8},{14,... | collective-permute-start | bytes 393224 | tf_op jit(solution)/shard_map/ppermute | solution.py:101
  9.5 9.5 %collective-permute-start.2 = (bf16[4,128,128]{2,1,0:T(8,128)(2,1)S(1)}, bf16[4,128,128]{2,1,0:T(8,128)(2,1)S(1)}, u32[]{:S(2)}, u32[]{:S(2)}) collective-permute-start(bf16[4,128,128]{2,1,0:T(8,128)(2,1)S(1)} %collective-permute-done.refs_1_), channel_id=1, source_target_pairs={{0,2},{2,6},{6,4},{4,0},{1,3},{3,7},{7,5},{5,1},{8,10},{10,14},{14... | collective-permute-start | bytes 393224 | tf_op jit(solution)/shard_map/ppermute | solution.py:101
  15.5 6.7 %collective-permute-start.3 = (bf16[4,128,128]{2,1,0:T(8,128)(2,1)S(1)}, bf16[4,128,128]{2,1,0:T(8,128)(2,1)S(1)}, u32[]{:S(2)}, u32[]{:S(2)}) collective-permute-start(bf16[4,128,128]{2,1,0:T(8,128)(2,1)S(1)} %get-tuple-element.48.refs_0_), channel_id=1, source_target_pairs={{0,2},{2,6},{6,4},{4,0},{1,3},{3,7},{7,5},{5,1},{8,10},{10,14},{14... | collective-permute-start | bytes 393224 | tf_op jit(solution)/shard_map/ppermute | solution.py:101
  19.0 14.7 %collective-permute-start.5 = (bf16[4,128,128]{2,1,0:T(8,128)(2,1)S(1)}, bf16[4,128,128]{2,1,0:T(8,128)(2,1)S(1)}, u32[]{:S(2)}, u32[]{:S(2)}) collective-permute-start(bf16[4,128,128]{2,1,0:T(8,128)(2,1)S(1)} %get-tuple-element.48.refs_0_), channel_id=1, source_target_pairs={{0,4},{2,0},{6,2},{4,6},{1,5},{3,1},{7,3},{5,7},{8,12},{10,8},{14,... | collective-permute-start | bytes 393224 | tf_op jit(solution)/shard_map/ppermute | solution.py:101
  25.5 8.1 %collective-permute-start.7 = (bf16[4,128,128]{2,1,0:T(8,128)(2,1)S(1)}, bf16[4,128,128]{2,1,0:T(8,128)(2,1)S(1)}, u32[]{:S(2)}, u32[]{:S(2)}) collective-permute-start(bf16[4,128,128]{2,1,0:T(8,128)(2,1)S(1)} %constant_dynamic-update-slice_fusion.4), channel_id=1, source_target_pairs={{0,2},{2,6},{6,4},{4,0},{1,3},{3,7},{7,5},{5,1},{8,10},{10,14},{14... | collective-permute-start | bytes 393224 | tf_op jit(solution)/shard_map/ppermute | solution.py:101
  28.1 6.4 %collective-permute-start.6 = (bf16[4,128,128]{2,1,0:T(8,128)(2,1)S(1)}, bf16[4,128,128]{2,1,0:T(8,128)(2,1)S(1)}, u32[]{:S(2)}, u32[]{:S(2)}) collective-permute-start(bf16[4,128,128]{2,1,0:T(8,128)(2,1)S(1)} %collective-permute-done.3.refs_1_), channel_id=1, source_target_pairs={{0,2},{2,6},{6,4},{4,0},{1,3},{3,7},{7,5},{5,1},{8,10},{10,14},{14... | collective-permute-start | bytes 393224 | tf_op jit(solution)/shard_map/ppermute | solution.py:101
  30.0 9.0 %collective-permute-start.8 = (bf16[4,128,128]{2,1,0:T(8,128)(2,1)S(1)}, bf16[4,128,128]{2,1,0:T(8,128)(2,1)S(1)}, u32[]{:S(2)}, u32[]{:S(2)}) collective-permute-start(bf16[4,128,128]{2,1,0:T(8,128)(2,1)S(1)} %constant_dynamic-update-slice_fusion.2), channel_id=1, source_target_pairs={{0,4},{2,0},{6,2},{4,6},{1,5},{3,1},{7,3},{5,7},{8,12},{10,8},{14,... | collective-permute-start | bytes 393224 | tf_op jit(solution)/shard_map/ppermute | solution.py:101
  31.1 19.7 %collective-permute-start.4 = (bf16[128,16,128]{2,1,0:T(8,128)(2,1)S(1)}, bf16[128,16,128]{2,1,0:T(8,128)(2,1)S(1)}, u32[]{:S(2)}, u32[]{:S(2)}) collective-permute-start(bf16[128,16,128]{2,1,0:T(8,128)(2,1)S(1)} %get-tuple-element.54), channel_id=1, source_target_pairs={{0,24},{8,0},{16,8},{24,16},{1,25},{9,1},{17,9},{25,17},{2,26},{10... | collective-permute-start | bytes 1572872 | tf_op jit(solution)/shard_map/ppermute | solution.py:118
  40.6 10.2 %collective-permute-start.10 = (bf16[8,128,128]{2,1,0:T(8,128)(2,1)S(1)}, bf16[8,128,128]{2,1,0:T(8,128)(2,1)S(1)}, u32[]{:S(2)}, u32[]{:S(2)}) collective-permute-start(bf16[8,128,128]{2,1,0:T(8,128)(2,1)S(1)} %pad_maximum_fusion), channel_id=1, source_target_pairs={{0,2},{2,6},{6,4},{4,0},{1,3},{3,7},{7,5},{5,1},{8,10},{10,14},{14... | collective-permute-start | bytes 786440 | tf_op jit(solution)/shard_map/ppermute | solution.py:101
  41.6 11.3 %collective-permute-start.9 = (bf16[128,16,128]{2,1,0:T(8,128)(2,1)S(1)}, bf16[128,16,128]{2,1,0:T(8,128)(2,1)S(1)}, u32[]{:S(2)}, u32[]{:S(2)}) collective-permute-start(bf16[128,16,128]{2,1,0:T(8,128)(2,1)S(1)} %get-tuple-element.74), channel_id=1, source_target_pairs={{0,24},{8,0},{16,8},{24,16},{1,25},{9,1},{17,9},{25,17},{2,26},{10... | collective-permute-start | bytes 1572872 | tf_op jit(solution)/shard_map/ppermute | solution.py:118
  44.1 9.9 %collective-permute-start.11 = (bf16[4,128,128]{2,1,0:T(8,128)(2,1)S(1)}, bf16[4,128,128]{2,1,0:T(8,128)(2,1)S(1)}, u32[]{:S(2)}, u32[]{:S(2)}) collective-permute-start(bf16[4,128,128]{2,1,0:T(8,128)(2,1)S(1)} %constant_dynamic-update-slice_fusion.10), channel_id=1, source_target_pairs={{0,4},{2,0},{6,2},{4,6},{1,5},{3,1},{7,3},{5,7},{8,12},{10,8},{14,... | collective-permute-start | bytes 393224 | tf_op jit(solution)/shard_map/ppermute | solution.py:101
  50.9 5.9 %collective-permute-start.12 = (bf16[4,128,128]{2,1,0:T(8,128)(2,1)S(1)}, bf16[4,128,128]{2,1,0:T(8,128)(2,1)S(1)}, u32[]{:S(2)}, u32[]{:S(2)}) collective-permute-start(bf16[4,128,128]{2,1,0:T(8,128)(2,1)S(1)} %add_convert_fusion), channel_id=1, source_target_pairs={{0,2},{2,6},{6,4},{4,0},{1,3},{3,7},{7,5},{5,1},{8,10},{10,14},{14... | collective-permute-start | bytes 393224 | tf_op jit(solution)/shard_map/ppermute | solution.py:101

commit v6 on v3

--- a/solution.py
+++ b/solution.py
@@ -95,20 +95,13 @@
     )
 
 
-def gather(block, axis, relay_after=None):
+def gather_rest(block, up, down, axis):
     count = lax.axis_size(axis)
-    blocks = {0: block}
-    for step in range(1, count // 2 + 1):
-        for sign in (1, -1):
-            if sign < 0 and 2 * step == count:
-                continue
-            if step > 1 and relay_after is not None:
-                moving, shift = blocks[(sign * (step - 1)) % count], sign
-                if step == 2:
-                    moving, _ = lax.optimization_barrier((moving, relay_after))
-            else:
-                moving, shift = block, sign * step
-            blocks[(sign * step) % count] = passed(moving, axis, shift)
+    blocks = {0: block, 1: up, count - 1: down}
+    for step in range(2, count // 2 + 1):
+        up = blocks[step] = passed(up, axis, 1)
+        if 2 * step < count:
+            down = blocks[count - step] = passed(down, axis, -1)
     return [blocks[step] for step in range(count)]
 
 
@@ -352,7 +345,7 @@
         out_specs=[VMEM] * 2,
         out_shape=[shape] * 2,
         scratch_shapes=[pltpu.VMEM((2, 3, half_rows, heads, size), BF16), DMA((6,))],
-        compiler_params=pltpu.CompilerParams(vmem_limit_bytes=24 * 2**20),
+        compiler_params=pltpu.CompilerParams(vmem_limit_bytes=12 * 2**20),
         cost_estimate=pl.CostEstimate(flops=WORK, bytes_accessed=2**16, transcendentals=0),
         name="query_sides",
     )(in_hbm(queries), in_hbm(grads), in_hbm(saved))
@@ -370,7 +363,7 @@
     part = ((per_stage, tokens, size), BF16)
     flat = ((tokens * groups, size), BF16)
     rows_scratch = pltpu.VMEM(*flat[:1], F32)
-    limit = 12 + keys // 64
+    limit = 6 + keys // 64
     after = lax.optimization_barrier
     k_block, v_block = pl.pallas_call(
         prep_kernel,
@@ -383,14 +376,15 @@
         name="pack_keys",
     )(in_hbm(key_heads.reshape(-1, size)), in_hbm(value_heads.reshape(-1, size)))
 
-    k_all = gather(k_block, "ctx", ())
-    q_loads, _ = after((queries[0], k_all[1]))
+    up, down = passed(k_block, "ctx", 1), passed(k_block, "ctx", -1)
+    q_loads, _ = after((queries[0], up))
     q_side, g_side = make_sides(groups, q_loads, output_grad[0], forward_out[0])
+    k_all = gather_rest(k_block, up, down, "ctx")
     v_block, _ = after((v_block, q_side))
-    v_all = gather(v_block, "ctx")
+    up, down = passed(v_block, "ctx", 1), passed(v_block, "ctx", -1)
+
     slots = far_last(blocks)
-    k_all, v_all = [k_all[step] for step in slots], [v_all[step] for step in slots]
-
+    k_all = [k_all[step] for step in slots]
     weights, dv_parts = [], []
     for stage in range(STAGES):
         weight, scale, *parts = call(
@@ -404,11 +398,12 @@
             True,
         )
         if stage == 0:
-            q_side, _ = after((q_side, scale))
+            up, q_side = after((up, q_side, scale))[:2]
+            v_all = gather_rest(v_block, up, down, "ctx")
         weights.append((weight, scale))
         dv_parts.append(parts)
 
-    g_side, _ = after((g_side, weights[-1][1]))
+    v_all = [v_all[step] for step in slots]
     handed, dscores = [], []
     for stage in range(STAGES):
         handed_part, dscore = call(
@@ -425,33 +420,28 @@
             [g_side, *weights[stage], *k_all, *v_all],
         )
         if stage == 0:
-            g_side, dv_parts, _ = after((g_side, dv_parts, handed_part))
+            g_side, _ = after((g_side, handed_part))
         handed.append(passed_down(handed_part, "pipe"))
         dscores.append(dscore)
     dv_parts = [jnp.concatenate(parts, axis=0) for parts in zip(*dv_parts)]
     dv_parts = [dv_parts[slots.index(step)] for step in range(blocks)]
     dv_terms, dv_relayed = scatter_sums(dv_parts, "ctx", ())
 
-    def key_sums(start, stop, dscores):
-        return call(
-            functools.partial(dk_kernel, STAGES, start),
-            "key_grads",
-            [packed] * (stop - start),
-            [],
-            limit,
-            WORK,
-            [q_side, *dscores],
-        )
-
-    far_parts = key_sums(blocks - 1, blocks, dscores)
-    dscores, _ = after((dscores, (far_parts, dv_relayed, dv_terms[-1])))
-    dk_parts = key_sums(0, blocks - 1, dscores) + far_parts
+    dscores, _ = after((dscores, (dv_relayed, dv_terms[-1])))
+    dk_parts = call(
+        functools.partial(dk_kernel, STAGES, 0),
+        "key_grads",
+        [packed] * blocks,
+        [],
+        limit,
+        WORK,
+        [q_side, *dscores],
+    )
     dk_parts = [dk_parts[slots.index(step)] for step in range(blocks)]
-    dk_terms, _ = scatter_sums(dk_parts, "ctx", (dk_parts[0], dv_terms[1]))
+    dk_terms, _ = scatter_sums(dk_parts, "ctx", ())
     handed = jnp.concatenate(handed, axis=1)[None]
     last = lax.axis_index("pipe") == lax.axis_size("pipe") - 1
     handed = jnp.where(last, jnp.zeros_like(handed), handed)
-    dk_terms[0], _ = after((dk_terms[0], handed))
     key_grad, value_grad = call(
         functools.partial(finish_kernel, len(dk_terms)),
         "lay_out",

time: 59.8 us -> 55.3 us (0.925)
  waiting for transfers between devices: 9.82 us -> 13.4 us
  local copies, waits for them, and re-layouts: 3.56 us -> 0.01 us
  starting transfers between devices: 25.8 us -> 23.8 us
  Pallas kernels: 17.1 us -> 15.9 us
  other arithmetic: 2.49 us -> 1.3 us
    ppermute x12, waiting for transfers between devices: 7.85 us -> 13.3 us  [passed(): lax.ppermute(value, axis, [(order[at], order[(at + step) % count]) for at...]
    unnamed x10 -> x2, local copies, waits for them, and re-layouts: 3.56 us -> 0.01 us
    ppermute x12, starting transfers between devices: 22.8 us -> 20.7 us  [passed(): lax.ppermute(value, axis, [(order[at], order[(at + step) % count]) for at...]
    ppermute x2, waiting for transfers between devices: 1.97 us -> 0.08 us  [passed_down(): lax.ppermute(value, axis, [(at, (at - 1) % count) for at in range(count)])]
    select_n x1, other arithmetic: 2.38 us -> 1.18 us  [shards(): handed = jnp.where(last, jnp.zeros_like(handed), handed)]
    pallas_call x7 -> x6, Pallas kernels: 13.4 us -> 12.3 us  [call(): pl.pallas_call(kernel, in_specs=([SMEM] if smem else []) + [VMEM] * (len(...]
  transfers between devices with their start and end apart: 14 -> 14, of which waited for: 5 -> 7; matrix products, arithmetic and copies ran while one was open for 4% -> 0% of each run, Pallas kernels for 23% -> 27%
where the time goes in v6:
time: 55.3 us; the launch traced here: 55.1 us
  starting transfers between devices  23.8 us (43%)
  Pallas kernels  15.9 us (29%)
  waiting for transfers between devices  13.4 us (24%)
  other arithmetic  1.3 us (2%)
  between operations  0.76 us (1%)
    ppermute x12, starting transfers between devices, passed(): lax.ppermute(value, axis, [(order[at], order[(at + step) % count]) for at...  20.7 us
    ppermute x12, waiting for transfers between devices, passed(): lax.ppermute(value, axis, [(order[at], order[(at + step) % count]) for at...  13.3 us
    pallas_call x6, Pallas kernels, call(): pl.pallas_call(kernel, in_specs=([SMEM] if smem else []) + [VMEM] * (len(...  12.3 us
    ppermute x2, starting transfers between devices, passed_down(): lax.ppermute(value, axis, [(at, (at - 1) % count) for at in range(count)])  3.09 us
    pallas_call x1, Pallas kernels, make_sides(): pl.pallas_call(functools.partial(sides_kernel, groups), in_specs=[HBM] *...  2.48 us
    select_n x1, other arithmetic, shards(): handed = jnp.where(last, jnp.zeros_like(handed), handed)  1.18 us
    pallas_call x1, Pallas kernels, shards(): pl.pallas_call(prep_kernel, in_specs=[HBM] * 2, out_specs=[VMEM] * 2, out...  1.15 us
  transfers between devices with their start and end apart: 14, of which 7 were waited for; matrix products, arithmetic and copies ran while one was open for 0% of the time, Pallas kernels for 27%

profile of v6, /device:TPU:0, one launch (start us, length us, event | category | flops | bytes accessed | tf_op | source)
XLA Modules:
  0.0 55.1 jit_solution(2593523074139697522)
XLA Ops:
  0.6 0.0 copy-start
  0.6 1.1 %pack_keys.1 = (bf16[4,128,128]{2,1,0:T(8,128)(2,1)S(1)}, bf16[4,128,128]{2,1,0:T(8,128)(2,1)S(1)}) custom-call(bf16[512,128]{1,0:T(8,128)(2,1)} %bitcast.14, bf16[512,128]{1,0:T(8,128)(2,1)} %bitcast.15), custom_call_target="tpu_custom_call" | custom-call | flops 1048576 | bytes 65536 | tf_op jit(solution)/shard_map/pack_keys/pallas_call | solution.py:368
  1.8 3.1 %collective-permute-start = (bf16[4,128,128]{2,1,0:T(8,128)(2,1)S(1)}, bf16[4,128,128]{2,1,0:T(8,128)(2,1)S(1)}, u32[]{:S(2)}, u32[]{:S(2)}) collective-permute-start(bf16[4,128,128]{2,1,0:T(8,128)(2,1)S(1)} %get-tuple-element.37.refs_0_), channel_id=1, source_target_pairs={{0,2},{2,6},{6,4},{4,0},{1,3},{3,7},{7,5},{5,1},{8,10},{10,14},{14... | collective-permute-start | bytes 393224 | tf_op jit(solution)/shard_map/ppermute | solution.py:93
  4.9 1.1 %collective-permute-start.2 = (bf16[4,128,128]{2,1,0:T(8,128)(2,1)S(1)}, bf16[4,128,128]{2,1,0:T(8,128)(2,1)S(1)}, u32[]{:S(2)}, u32[]{:S(2)}) collective-permute-start(bf16[4,128,128]{2,1,0:T(8,128)(2,1)S(1)} %get-tuple-element.37.refs_0_), channel_id=1, source_target_pairs={{0,4},{2,0},{6,2},{4,6},{1,5},{3,1},{7,3},{5,7},{8,12},{10,8},{14,... | collective-permute-start | bytes 393224 | tf_op jit(solution)/shard_map/ppermute | solution.py:93
  6.0 3.5 %collective-permute-done.refs_1_ = bf16[4,128,128]{2,1,0:T(8,128)(2,1)S(1)} collective-permute-done((bf16[4,128,128]{2,1,0:T(8,128)(2,1)S(1)}, bf16[4,128,128]{2,1,0:T(8,128)(2,1)S(1)}, u32[]{:S(2)}, u32[]{:S(2)}) %collective-permute-start) | collective-permute-done | bytes 131104 | tf_op jit(solution)/shard_map/ppermute | solution.py:93
  9.5 3.5 %collective-permute-start.3 = (bf16[4,128,128]{2,1,0:T(8,128)(2,1)S(1)}, bf16[4,128,128]{2,1,0:T(8,128)(2,1)S(1)}, u32[]{:S(2)}, u32[]{:S(2)}) collective-permute-start(bf16[4,128,128]{2,1,0:T(8,128)(2,1)S(1)} %collective-permute-done.refs_1_), channel_id=1, source_target_pairs={{0,2},{2,6},{6,4},{4,0},{1,3},{3,7},{7,5},{5,1},{8,10},{10,14},{14... | collective-permute-start | bytes 393224 | tf_op jit(solution)/shard_map/ppermute | solution.py:93
  13.0 2.5 %query_sides.1 = (bf16[2,4,512,256]{3,2,1,0:T(8,128)(2,1)S(1)}, bf16[2,4,512,256]{3,2,1,0:T(8,128)(2,1)S(1)}) custom-call(bf16[128,32,128]{2,1,0:T(8,128)(2,1)} %bitcast.9, bf16[128,32,128]{2,1,0:T(8,128)(2,1)} %bitcast.10, bf16[128,32,128]{2,1,0:T(8,128)(2,1)} %bitcast.11), custom_call_target="tpu_custom_call" | custom-call | flops 1048576 | bytes 65536 | tf_op jit(solution)/shard_map/query_sides/pallas_call | solution.py:342
  15.5 3.4 %collective-permute-start.1 = (bf16[4,128,128]{2,1,0:T(8,128)(2,1)S(1)}, bf16[4,128,128]{2,1,0:T(8,128)(2,1)S(1)}, u32[]{:S(2)}, u32[]{:S(2)}) collective-permute-start(bf16[4,128,128]{2,1,0:T(8,128)(2,1)S(1)} %get-tuple-element.40.refs_4_), channel_id=1, source_target_pairs={{0,2},{2,6},{6,4},{4,0},{1,3},{3,7},{7,5},{5,1},{8,10},{10,14},{14... | collective-permute-start | bytes 393224 | tf_op jit(solution)/shard_map/ppermute | solution.py:93
  19.0 0.0 collective-permute-start.4
  19.0 0.0 collective-permute-done.2.refs_2_
  19.0 0.0 collective-permute-done.3.refs_3_
  19.0 0.0 copy-done
  19.0 2.7 %weights.2 = (f32[2,512,1024]{2,1,0:T(8,128)S(1)}, f32[2,8,1024]{2,1,0:T(8,128)S(1)}, bf16[2,128,128]{2,1,0:T(8,128)(2,1)S(1)}, bf16[2,128,128]{2,1,0:T(8,128)(2...) custom-call(s32[8]{0:T(128)S(1)} %copy-done, ...), custom_call_target="tpu_custom_call" | custom-call | flops 4294967296 | bytes 65536 | tf_op jit(solution)/shard_map/weights/pallas_call | solution.py:321
  21.7 0.5 collective-permute-done.1.refs_5_
  22.3 2.5 %collective-permute-start.5 = (bf16[4,128,128]{2,1,0:T(8,128)(2,1)S(1)}, bf16[4,128,128]{2,1,0:T(8,128)(2,1)S(1)}, u32[]{:S(2)}, u32[]{:S(2)}) collective-permute-start(bf16[4,128,128]{2,1,0:T(8,128)(2,1)S(1)} %collective-permute-done.1.refs_5_), channel_id=1, source_target_pairs={{0,2},{2,6},{6,4},{4,0},{1,3},{3,7},{7,5},{5,1},{8,10},{10,14},{14... | collective-permute-start | bytes 393224 | tf_op jit(solution)/shard_map/ppermute | solution.py:93
  24.7 2.7 %weights.3 = (f32[2,512,1024]{2,1,0:T(8,128)S(1)}, f32[2,8,1024]{2,1,0:T(8,128)S(1)}, bf16[2,128,128]{2,1,0:T(8,128)(2,1)S(1)}, bf16[2,128,128]{2,1,0:T(8,128)(2...) custom-call(s32[8]{0:T(128)S(1)} %copy-done, ...), custom_call_target="tpu_custom_call" | custom-call | flops 4294967296 | bytes 65536 | tf_op jit(solution)/shard_map/weights/pallas_call | solution.py:321
  27.5 1.9 %collective-permute-start.6 = (bf16[4,128,128]{2,1,0:T(8,128)(2,1)S(1)}, bf16[4,128,128]{2,1,0:T(8,128)(2,1)S(1)}, u32[]{:S(2)}, u32[]{:S(2)}) collective-permute-start(bf16[4,128,128]{2,1,0:T(8,128)(2,1)S(1)} %pad_maximum_fusion), channel_id=1, source_target_pairs={{0,2},{2,6},{6,4},{4,0},{1,3},{3,7},{7,5},{5,1},{8,10},{10,14},{14... | collective-permute-start | bytes 393224 | tf_op jit(solution)/shard_map/ppermute | solution.py:93
  29.5 1.1 %collective-permute-start.7 = (bf16[4,128,128]{2,1,0:T(8,128)(2,1)S(1)}, bf16[4,128,128]{2,1,0:T(8,128)(2,1)S(1)}, u32[]{:S(2)}, u32[]{:S(2)}) collective-permute-start(bf16[4,128,128]{2,1,0:T(8,128)(2,1)S(1)} %pad_maximum_fusion.1), channel_id=1, source_target_pairs={{0,4},{2,0},{6,2},{4,6},{1,5},{3,1},{7,3},{5,7},{8,12},{10,8},{14,... | collective-permute-start | bytes 393224 | tf_op jit(solution)/shard_map/ppermute | solution.py:93
  30.6 0.0 collective-permute-done.4.refs_6_
  30.6 0.0 collective-permute-done.5.refs_7_
  30.6 1.6 %query_grads.2 = (bf16[128,16,128]{2,1,0:T(8,128)(2,1)S(1)}, bf16[2,512,1024]{2,1,0:T(8,128)(2,1)S(1)}) custom-call(bf16[2,4,512,256]{3,2,1,0:T(8,128)(2,1)S(1)} %get-tuple-element.48.g_side_ref, f32[2,512,1024]{2,1,0:T(8,128)S(1)} %get-tuple-element.44.weight_ref, f32[2,8,1024]{2,1,0:T(8,128)S(1)} %get-tuple-element.42.scale_ref, ...), custom_call_target="tpu_custom_call" | custom-call | flops 4294967296 | bytes 65536 | tf_op jit(solution)/shard_map/query_grads/pallas_call | solution.py:321
  32.2 2.5 %collective-permute-start.12 = (bf16[128,16,128]{2,1,0:T(8,128)(2,1)S(1)}, bf16[128,16,128]{2,1,0:T(8,128)(2,1)S(1)}, u32[]{:S(2)}, u32[]{:S(2)}) collective-permute-start(bf16[128,16,128]{2,1,0:T(8,128)(2,1)S(1)} %get-tuple-element.47), channel_id=1, source_target_pairs={{0,24},{8,0},{16,8},{24,16},{1,25},{9,1},{17,9},{25,17},{2,26},{10... | collective-permute-start | bytes 1572872 | tf_op jit(solution)/shard_map/ppermute | solution.py:110
  34.7 1.6 %query_grads.3 = (bf16[128,16,128]{2,1,0:T(8,128)(2,1)S(1)}, bf16[2,512,1024]{2,1,0:T(8,128)(2,1)S(1)}) custom-call(bf16[2,4,512,256]{3,2,1,0:T(8,128)(2,1)S(1)} %get-tuple-element.48.g_side_ref, f32[2,512,1024]{2,1,0:T(8,128)S(1)} %get-tuple-element.49.weight_ref, f32[2,8,1024]{2,1,0:T(8,128)S(1)} %get-tuple-element.50.scale_ref, ...), custom_call_target="tpu_custom_call" | custom-call | flops 4294967296 | bytes 65536 | tf_op jit(solution)/shard_map/query_grads/pallas_call | solution.py:321
  36.3 0.6 %collective-permute-start.13 = (bf16[128,16,128]{2,1,0:T(8,128)(2,1)S(1)}, bf16[128,16,128]{2,1,0:T(8,128)(2,1)S(1)}, u32[]{:S(2)}, u32[]{:S(2)}) collective-permute-start(bf16[128,16,128]{2,1,0:T(8,128)(2,1)S(1)} %get-tuple-element.68), channel_id=1, source_target_pairs={{0,24},{8,0},{16,8},{24,16},{1,25},{9,1},{17,9},{25,17},{2,26},{10... | collective-permute-start | bytes 1572872 | tf_op jit(solution)/shard_map/ppermute | solution.py:110
  36.9 0.0 collective-permute-done.6
  36.9 0.0 collective-permute-done.7.refs_5_
  36.9 2.8 %key_grads.1 = (bf16[4,128,128]{2,1,0:T(8,128)(2,1)S(1)}, bf16[4,128,128]{2,1,0:T(8,128)(2,1)S(1)}, bf16[4,128,128]{2,1,0:T(8,128)(2,1)S(1)}, bf16[4,128,128]{2,1,0:T(8,128)(2,1)S(1)}) custom-call(bf16[2,4,512,256]{3,2,1,0:T(8,128)(2,1)S(1)} %get-tuple-element.43.q_side_ref, bf16[2,512,1024]{2,1,0:T(8,128)(2,1)S(1)} %get-tuple-element.58.refs_0_, ...), custom_call_target="tpu_custom_call" | custom-call | flops 1048576 | bytes 65536 | tf_op jit(solution)/shard_map/key_grads/pallas_call | solution.py:321
  39.8 1.0 %collective-permute-start.8 = (bf16[4,128,128]{2,1,0:T(8,128)(2,1)S(1)}, bf16[4,128,128]{2,1,0:T(8,128)(2,1)S(1)}, u32[]{:S(2)}, u32[]{:S(2)}) collective-permute-start(bf16[4,128,128]{2,1,0:T(8,128)(2,1)S(1)} %get-tuple-element.61), channel_id=1, source_target_pairs={{0,2},{2,6},{6,4},{4,0},{1,3},{3,7},{7,5},{5,1},{8,10},{10,14},{14... | collective-permute-start | bytes 393224 | tf_op jit(solution)/shard_map/ppermute | solution.py:93
  40.8 1.8 %collective-permute-start.11 = (bf16[4,128,128]{2,1,0:T(8,128)(2,1)S(1)}, bf16[4,128,128]{2,1,0:T(8,128)(2,1)S(1)}, u32[]{:S(2)}, u32[]{:S(2)}) collective-permute-start(bf16[4,128,128]{2,1,0:T(8,128)(2,1)S(1)} %add_convert_fusion.1), channel_id=1, source_target_pairs={{0,2},{2,6},{6,4},{4,0},{1,3},{3,7},{7,5},{5,1},{8,10},{10,14},{14... | collective-permute-start | bytes 393224 | tf_op jit(solution)/shard_map/ppermute | solution.py:93
  42.6 1.2 %collective-permute-start.10 = (bf16[4,128,128]{2,1,0:T(8,128)(2,1)S(1)}, bf16[4,128,128]{2,1,0:T(8,128)(2,1)S(1)}, u32[]{:S(2)}, u32[]{:S(2)}) collective-permute-start(bf16[4,128,128]{2,1,0:T(8,128)(2,1)S(1)} %get-tuple-element.63), channel_id=1, source_target_pairs={{0,4},{2,0},{6,2},{4,6},{1,5},{3,1},{7,3},{5,7},{8,12},{10,8},{14,... | collective-permute-start | bytes 393224 | tf_op jit(solution)/shard_map/ppermute | solution.py:93
  43.7 3.4 %collective-permute-done.8 = bf16[4,128,128]{2,1,0:T(8,128)(2,1)S(1)} collective-permute-done((bf16[4,128,128]{2,1,0:T(8,128)(2,1)S(1)}, bf16[4,128,128]{2,1,0:T(8,128)(2,1)S(1)}, u32[]{:S(2)}, u32[]{:S(2)}) %collective-permute-start.8) | collective-permute-done | bytes 131104 | tf_op jit(solution)/shard_map/ppermute | solution.py:93
  47.2 0.1 collective-permute-start.9
  47.3 2.0 %collective-permute-done.10.refs_2_ = bf16[4,128,128]{2,1,0:T(8,128)(2,1)S(1)} collective-permute-done((bf16[4,128,128]{2,1,0:T(8,128)(2,1)S(1)}, bf16[4,128,128]{2,1,0:T(8,128)(2,1)S(1)}, u32[]{:S(2)}, u32[]{:S(2)}) %collective-permute-start.10) | collective-permute-done | bytes 131104 | tf_op jit(solution)/shard_map/ppermute | solution.py:93
  49.2 0.6 %collective-permute-done.11.refs_4_ = bf16[4,128,128]{2,1,0:T(8,128)(2,1)S(1)} collective-permute-done((bf16[4,128,128]{2,1,0:T(8,128)(2,1)S(1)}, bf16[4,128,128]{2,1,0:T(8,128)(2,1)S(1)}, u32[]{:S(2)}, u32[]{:S(2)}) %collective-permute-start.11) | collective-permute-done | bytes 131104 | tf_op jit(solution)/shard_map/ppermute | solution.py:93
  49.8 3.2 %collective-permute-done.9.refs_1_ = bf16[4,128,128]{2,1,0:T(8,128)(2,1)S(1)} collective-permute-done((bf16[4,128,128]{2,1,0:T(8,128)(2,1)S(1)}, bf16[4,128,128]{2,1,0:T(8,128)(2,1)S(1)}, u32[]{:S(2)}, u32[]{:S(2)}) %collective-permute-start.9) | collective-permute-done | bytes 131104 | tf_op jit(solution)/shard_map/ppermute | solution.py:93
  53.1 0.8 %lay_out.1 = (bf16[512,128]{1,0:T(8,128)(2,1)}, bf16[512,128]{1,0:T(8,128)(2,1)}) custom-call(bf16[4,128,128]{2,1,0:T(8,128)(2,1)S(1)} %get-tuple-element.60.refs_0_, bf16[4,128,128]{2,1,0:T(8,128)(2,1)S(1)} %collective-permute-done.9.refs_1_, bf16[4,128,128]{2,1,0:T(8,128)(2,1)S(1)} %collective-permute-done.10.refs_2_, ...), custom_call_target="tpu_custom_call" | custom-call | flops 1048576 | bytes 65536 | tf_op jit(solution)/shard_map/lay_out/pallas_call | solution.py:321
  53.9 0.1 collective-permute-done.13
  53.9 0.0 collective-permute-done.12
  54.0 1.2 %maximum_select_fusion = bf16[1,128,32,128]{3,2,1,0:T(8,128)(2,1)} fusion(bf16[1,128,16,128]{3,2,1,0:T(8,128)(2,1)S(1)} %bitcast.13, bf16[1,128,16,128]{3,2,1,0:T(8,128)(2,1)S(1)} %bitcast.12, pred[]{:T(512)S(6)} %eq.3), kind=kLoop, calls=%fused_computation | loop fusion | flops 2621440 | bytes 2097153 | tf_op jit(solution)/shard_map/jit(_where)/select_n | solution.py:444
  (5 shorter events, 0.1 us)
Async XLA Ops:
  0.6 18.3 %copy-start = (s32[8]{0:T(128)S(1)}, s32[8]{0:T(128)}, u32[]{:S(2)}) copy-start(s32[8]{0:T(128)} %order_ref.3) | copy-start | bytes 100
  1.8 7.7 %collective-permute-start = (bf16[4,128,128]{2,1,0:T(8,128)(2,1)S(1)}, bf16[4,128,128]{2,1,0:T(8,128)(2,1)S(1)}, u32[]{:S(2)}, u32[]{:S(2)}) collective-permute-start(bf16[4,128,128]{2,1,0:T(8,128)(2,1)S(1)} %get-tuple-element.37.refs_0_), channel_id=1, source_target_pairs={{0,2},{2,6},{6,4},{4,0},{1,3},{3,7},{7,5},{5,1},{8,10},{10,14},{14... | collective-permute-start | bytes 393224 | tf_op jit(solution)/shard_map/ppermute | solution.py:93
  4.9 14.1 %collective-permute-start.2 = (bf16[4,128,128]{2,1,0:T(8,128)(2,1)S(1)}, bf16[4,128,128]{2,1,0:T(8,128)(2,1)S(1)}, u32[]{:S(2)}, u32[]{:S(2)}) collective-permute-start(bf16[4,128,128]{2,1,0:T(8,128)(2,1)S(1)} %get-tuple-element.37.refs_0_), channel_id=1, source_target_pairs={{0,4},{2,0},{6,2},{4,6},{1,5},{3,1},{7,3},{5,7},{8,12},{10,8},{14,... | collective-permute-start | bytes 393224 | tf_op jit(solution)/shard_map/ppermute | solution.py:93
  9.5 9.5 %collective-permute-start.3 = (bf16[4,128,128]{2,1,0:T(8,128)(2,1)S(1)}, bf16[4,128,128]{2,1,0:T(8,128)(2,1)S(1)}, u32[]{:S(2)}, u32[]{:S(2)}) collective-permute-start(bf16[4,128,128]{2,1,0:T(8,128)(2,1)S(1)} %collective-permute-done.refs_1_), channel_id=1, source_target_pairs={{0,2},{2,6},{6,4},{4,0},{1,3},{3,7},{7,5},{5,1},{8,10},{10,14},{14... | collective-permute-start | bytes 393224 | tf_op jit(solution)/shard_map/ppermute | solution.py:93
  15.5 6.7 %collective-permute-start.1 = (bf16[4,128,128]{2,1,0:T(8,128)(2,1)S(1)}, bf16[4,128,128]{2,1,0:T(8,128)(2,1)S(1)}, u32[]{:S(2)}, u32[]{:S(2)}) collective-permute-start(bf16[4,128,128]{2,1,0:T(8,128)(2,1)S(1)} %get-tuple-element.40.refs_4_), channel_id=1, source_target_pairs={{0,2},{2,6},{6,4},{4,0},{1,3},{3,7},{7,5},{5,1},{8,10},{10,14},{14... | collective-permute-start | bytes 393224 | tf_op jit(solution)/shard_map/ppermute | solution.py:93
  19.0 11.6 %collective-permute-start.4 = (bf16[4,128,128]{2,1,0:T(8,128)(2,1)S(1)}, bf16[4,128,128]{2,1,0:T(8,128)(2,1)S(1)}, u32[]{:S(2)}, u32[]{:S(2)}) collective-permute-start(bf16[4,128,128]{2,1,0:T(8,128)(2,1)S(1)} %get-tuple-element.40.refs_4_), channel_id=1, source_target_pairs={{0,4},{2,0},{6,2},{4,6},{1,5},{3,1},{7,3},{5,7},{8,12},{10,8},{14,... | collective-permute-start | bytes 393224 | tf_op jit(solution)/shard_map/ppermute | solution.py:93
  22.3 8.3 %collective-permute-start.5 = (bf16[4,128,128]{2,1,0:T(8,128)(2,1)S(1)}, bf16[4,128,128]{2,1,0:T(8,128)(2,1)S(1)}, u32[]{:S(2)}, u32[]{:S(2)}) collective-permute-start(bf16[4,128,128]{2,1,0:T(8,128)(2,1)S(1)} %collective-permute-done.1.refs_5_), channel_id=1, source_target_pairs={{0,2},{2,6},{6,4},{4,0},{1,3},{3,7},{7,5},{5,1},{8,10},{10,14},{14... | collective-permute-start | bytes 393224 | tf_op jit(solution)/shard_map/ppermute | solution.py:93
  27.5 9.4 %collective-permute-start.6 = (bf16[4,128,128]{2,1,0:T(8,128)(2,1)S(1)}, bf16[4,128,128]{2,1,0:T(8,128)(2,1)S(1)}, u32[]{:S(2)}, u32[]{:S(2)}) collective-permute-start(bf16[4,128,128]{2,1,0:T(8,128)(2,1)S(1)} %pad_maximum_fusion), channel_id=1, source_target_pairs={{0,2},{2,6},{6,4},{4,0},{1,3},{3,7},{7,5},{5,1},{8,10},{10,14},{14... | collective-permute-start | bytes 393224 | tf_op jit(solution)/shard_map/ppermute | solution.py:93
  29.5 7.5 %collective-permute-start.7 = (bf16[4,128,128]{2,1,0:T(8,128)(2,1)S(1)}, bf16[4,128,128]{2,1,0:T(8,128)(2,1)S(1)}, u32[]{:S(2)}, u32[]{:S(2)}) collective-permute-start(bf16[4,128,128]{2,1,0:T(8,128)(2,1)S(1)} %pad_maximum_fusion.1), channel_id=1, source_target_pairs={{0,4},{2,0},{6,2},{4,6},{1,5},{3,1},{7,3},{5,7},{8,12},{10,8},{14,... | collective-permute-start | bytes 393224 | tf_op jit(solution)/shard_map/ppermute | solution.py:93
  32.2 21.8 %collective-permute-start.12 = (bf16[128,16,128]{2,1,0:T(8,128)(2,1)S(1)}, bf16[128,16,128]{2,1,0:T(8,128)(2,1)S(1)}, u32[]{:S(2)}, u32[]{:S(2)}) collective-permute-start(bf16[128,16,128]{2,1,0:T(8,128)(2,1)S(1)} %get-tuple-element.47), channel_id=1, source_target_pairs={{0,24},{8,0},{16,8},{24,16},{1,25},{9,1},{17,9},{25,17},{2,26},{10... | collective-permute-start | bytes 1572872 | tf_op jit(solution)/shard_map/ppermute | solution.py:110
  36.3 17.7 %collective-permute-start.13 = (bf16[128,16,128]{2,1,0:T(8,128)(2,1)S(1)}, bf16[128,16,128]{2,1,0:T(8,128)(2,1)S(1)}, u32[]{:S(2)}, u32[]{:S(2)}) collective-permute-start(bf16[128,16,128]{2,1,0:T(8,128)(2,1)S(1)} %get-tuple-element.68), channel_id=1, source_target_pairs={{0,24},{8,0},{16,8},{24,16},{1,25},{9,1},{17,9},{25,17},{2,26},{10... | collective-permute-start | bytes 1572872 | tf_op jit(solution)/shard_map/ppermute | solution.py:110
  39.8 7.4 %collective-permute-start.8 = (bf16[4,128,128]{2,1,0:T(8,128)(2,1)S(1)}, bf16[4,128,128]{2,1,0:T(8,128)(2,1)S(1)}, u32[]{:S(2)}, u32[]{:S(2)}) collective-permute-start(bf16[4,128,128]{2,1,0:T(8,128)(2,1)S(1)} %get-tuple-element.61), channel_id=1, source_target_pairs={{0,2},{2,6},{6,4},{4,0},{1,3},{3,7},{7,5},{5,1},{8,10},{10,14},{14... | collective-permute-start | bytes 393224 | tf_op jit(solution)/shard_map/ppermute | solution.py:93
  40.8 9.0 %collective-permute-start.11 = (bf16[4,128,128]{2,1,0:T(8,128)(2,1)S(1)}, bf16[4,128,128]{2,1,0:T(8,128)(2,1)S(1)}, u32[]{:S(2)}, u32[]{:S(2)}) collective-permute-start(bf16[4,128,128]{2,1,0:T(8,128)(2,1)S(1)} %add_convert_fusion.1), channel_id=1, source_target_pairs={{0,2},{2,6},{6,4},{4,0},{1,3},{3,7},{7,5},{5,1},{8,10},{10,14},{14... | collective-permute-start | bytes 393224 | tf_op jit(solution)/shard_map/ppermute | solution.py:93
  42.6 6.7 %collective-permute-start.10 = (bf16[4,128,128]{2,1,0:T(8,128)(2,1)S(1)}, bf16[4,128,128]{2,1,0:T(8,128)(2,1)S(1)}, u32[]{:S(2)}, u32[]{:S(2)}) collective-permute-start(bf16[4,128,128]{2,1,0:T(8,128)(2,1)S(1)} %get-tuple-element.63), channel_id=1, source_target_pairs={{0,4},{2,0},{6,2},{4,6},{1,5},{3,1},{7,3},{5,7},{8,12},{10,8},{14,... | collective-permute-start | bytes 393224 | tf_op jit(solution)/shard_map/ppermute | solution.py:93
  47.2 5.9 %collective-permute-start.9 = (bf16[4,128,128]{2,1,0:T(8,128)(2,1)S(1)}, bf16[4,128,128]{2,1,0:T(8,128)(2,1)S(1)}, u32[]{:S(2)}, u32[]{:S(2)}) collective-permute-start(bf16[4,128,128]{2,1,0:T(8,128)(2,1)S(1)} %add_convert_fusion), channel_id=1, source_target_pairs={{0,2},{2,6},{6,4},{4,0},{1,3},{3,7},{7,5},{5,1},{8,10},{10,14},{14... | collective-permute-start | bytes 393224 | tf_op jit(solution)/shard_map/ppermute | solution.py:93

commit v7 on v6

--- a/solution.py
+++ b/solution.py
@@ -172,7 +172,7 @@
 
 def weights_kernel(first, blocks, order_ref, q_side_ref, g_side_ref, *refs):
     k_refs, (weight_ref, scale_ref) = refs[:blocks], refs[blocks : blocks + 2]
-    sum_refs, key_ref = refs[blocks + 2 : 2 * blocks + 2], refs[-1]
+    sum_refs, mask_ref = refs[blocks + 2 : 2 * blocks + 2], refs[-1]
     groups, keys, _ = weight_ref.shape
     tokens, size = k_refs[0].shape[1:]
     place = lax.axis_index("ctx")
@@ -192,13 +192,12 @@
                 hidden = (at_row + ahead > at_col) & (at_col < half_rows)
                 hidden = jnp.where(hidden, 1.0, 0.0).astype(BF16)
                 k_at = pl.ds(block * tokens + k_half * half_rows, half_rows)
-                for group in range(groups):
-                    key_ref[half, group, k_at, size:] = hidden
-        at = pl.ds(block * tokens, tokens)
-        for group in range(groups):
-            key = k_refs[block][first + group]
-            for half in range(2):
-                key_ref[half, group, at, :size] = key
+                mask_ref[half, k_at, :] = hidden
+
+    def key_side(group, half, row):
+        near = range(row // tokens, (row + chunk) // tokens)
+        keys_here = jnp.concatenate([k_refs[block][first + group] for block in near], axis=0)
+        return jnp.concatenate([keys_here, mask_ref[half, pl.ds(row, chunk), :]], axis=1)
 
     chunk = 256
     units = [(group, half) for group in range(groups) for half in range(2)]
@@ -209,7 +208,7 @@
             k_at = pl.ds(row, chunk)
             if step < len(units):
                 group, half = units[step]
-                part = nt(key_ref[half, group, k_at, :], q_side_ref[half, first + group])
+                part = nt(key_side(group, half, row), q_side_ref[half, first + group])
                 weight_ref[group, k_at, pl.ds(half * rows, rows)] = part
                 part = jnp.max(part.reshape(chunk // 8, 8, rows), axis=0)
                 top = part if top is None else jnp.maximum(top, part)
@@ -242,7 +241,7 @@
 
 def dq_kernel(first, blocks, g_side_ref, weight_ref, scale_ref, *refs):
     k_refs, v_refs = refs[:blocks], refs[blocks : 2 * blocks]
-    handed_ref, dscore_ref, val_ref, back_ref = refs[2 * blocks :]
+    handed_ref, dscore_ref, back_ref = refs[2 * blocks :]
     groups, keys, _ = weight_ref.shape
     tokens, size = k_refs[0].shape[1:]
     rows = g_side_ref.shape[2]
@@ -254,15 +253,16 @@
     for block in range(blocks):
         at = pl.ds(block * tokens, tokens)
         for group in range(groups):
-            val_ref[group, at, :size] = v_refs[block][first + group]
-            val_ref[group, at, size:] = jnp.ones((tokens, size), BF16)
             high, low = split(nt(sign, k_refs[block][first + group]) * (1.0 / size))
             back_ref[group, :size, at] = high
             back_ref[group, size:, at] = low
 
     def change(unit, row):
         half, group = unit
-        return nt(val_ref[group, pl.ds(row, chunk), :], g_side_ref[half, first + group])
+        near = range(row // tokens, (row + chunk) // tokens)
+        values = jnp.concatenate([v_refs[block][first + group] for block in near], axis=0)
+        values = jnp.concatenate([values, jnp.ones_like(values)], axis=1)
+        return nt(values, g_side_ref[half, first + group])
 
     units = [(half, group) for half in range(2) for group in range(groups)]
     steps = [(unit, row) for unit in units for row in range(0, keys, chunk)]
@@ -391,7 +391,7 @@
             functools.partial(weights_kernel, stage * per_stage, blocks),
             "weights",
             [((per_stage, keys, 2 * rows), F32), ((per_stage, 8, 2 * rows), F32)] + [part] * blocks,
-            [pltpu.VMEM((2, per_stage, keys, 2 * size), BF16)],
+            [pltpu.VMEM((2, keys, size), BF16)],
             limit,
             BIG_WORK,
             [block_order, q_side, g_side, *k_all],
@@ -412,7 +412,6 @@
             [((tokens, per_stage * per_group, size), BF16)]
             + [((per_stage, keys, 2 * rows), BF16)],
             [
-                pltpu.VMEM((per_stage, keys, 2 * size), BF16),
                 pltpu.VMEM((per_stage, 2 * size, keys), BF16),
             ],
             limit,
@@ -421,10 +420,12 @@
         )
         if stage == 0:
             g_side, _ = after((g_side, handed_part))
+            first_handed = handed_part
         handed.append(passed_down(handed_part, "pipe"))
         dscores.append(dscore)
     dv_parts = [jnp.concatenate(parts, axis=0) for parts in zip(*dv_parts)]
     dv_parts = [dv_parts[slots.index(step)] for step in range(blocks)]
+    dv_parts[1], _ = after((dv_parts[1], first_handed))
     dv_terms, dv_relayed = scatter_sums(dv_parts, "ctx", ())
 
     dscores, _ = after((dscores, (dv_relayed, dv_terms[-1])))

time: 55.3 us -> 56.6 us (1.024)
  starting transfers between devices: 23.8 us -> 24.6 us
    ppermute x12, starting transfers between devices: 20.7 us -> 21.5 us  [passed(): lax.ppermute(value, axis, [(order[at], order[(at + step) % count]) for at...]
  transfers between devices with their start and end apart: 14 -> 14, of which waited for: 7 -> 6; matrix products, arithmetic and copies ran while one was open for 0% -> 0% of each run, Pallas kernels for 27% -> 26%
where the time goes in v7:
time: 56.6 us; the launch traced here: 56.4 us
  starting transfers between devices  24.6 us (43%)
  Pallas kernels  15.9 us (28%)
  waiting for transfers between devices  13.8 us (24%)
  other arithmetic  1.3 us (2%)
  between operations  0.77 us (1%)
    ppermute x12, starting transfers between devices, passed(): lax.ppermute(value, axis, [(order[at], order[(at + step) % count]) for at...  21.5 us
    ppermute x12, waiting for transfers between devices, passed(): lax.ppermute(value, axis, [(order[at], order[(at + step) % count]) for at...  13.8 us
    pallas_call x6, Pallas kernels, call(): pl.pallas_call(kernel, in_specs=([SMEM] if smem else []) + [VMEM] * (len(...  12.3 us
    ppermute x2, starting transfers between devices, passed_down(): lax.ppermute(value, axis, [(at, (at - 1) % count) for at in range(count)])  3.09 us
    pallas_call x1, Pallas kernels, make_sides(): pl.pallas_call(functools.partial(sides_kernel, groups), in_specs=[HBM] *...  2.48 us
    select_n x1, other arithmetic, shards(): handed = jnp.where(last, jnp.zeros_like(handed), handed)  1.18 us
    pallas_call x1, Pallas kernels, shards(): pl.pallas_call(prep_kernel, in_specs=[HBM] * 2, out_specs=[VMEM] * 2, out...  1.15 us
  transfers between devices with their start and end apart: 14, of which 6 were waited for; matrix products, arithmetic and copies ran while one was open for 0% of the time, Pallas kernels for 26%

profile of v7, /device:TPU:0, one launch (start us, length us, event | category | flops | bytes accessed | tf_op | source)
XLA Modules:
  0.0 56.4 jit_solution(1031127173200445608)
XLA Ops:
  0.6 0.0 copy-start
  0.6 1.1 %pack_keys.1 = (bf16[4,128,128]{2,1,0:T(8,128)(2,1)S(1)}, bf16[4,128,128]{2,1,0:T(8,128)(2,1)S(1)}) custom-call(bf16[512,128]{1,0:T(8,128)(2,1)} %bitcast.14, bf16[512,128]{1,0:T(8,128)(2,1)} %bitcast.15), custom_call_target="tpu_custom_call" | custom-call | flops 1048576 | bytes 65536 | tf_op jit(solution)/shard_map/pack_keys/pallas_call | solution.py:368
  1.8 3.1 %collective-permute-start = (bf16[4,128,128]{2,1,0:T(8,128)(2,1)S(1)}, bf16[4,128,128]{2,1,0:T(8,128)(2,1)S(1)}, u32[]{:S(2)}, u32[]{:S(2)}) collective-permute-start(bf16[4,128,128]{2,1,0:T(8,128)(2,1)S(1)} %get-tuple-element.38.refs_0_), channel_id=1, source_target_pairs={{0,2},{2,6},{6,4},{4,0},{1,3},{3,7},{7,5},{5,1},{8,10},{10,14},{14... | collective-permute-start | bytes 393224 | tf_op jit(solution)/shard_map/ppermute | solution.py:93
  4.9 1.1 %collective-permute-start.2 = (bf16[4,128,128]{2,1,0:T(8,128)(2,1)S(1)}, bf16[4,128,128]{2,1,0:T(8,128)(2,1)S(1)}, u32[]{:S(2)}, u32[]{:S(2)}) collective-permute-start(bf16[4,128,128]{2,1,0:T(8,128)(2,1)S(1)} %get-tuple-element.38.refs_0_), channel_id=1, source_target_pairs={{0,4},{2,0},{6,2},{4,6},{1,5},{3,1},{7,3},{5,7},{8,12},{10,8},{14,... | collective-permute-start | bytes 393224 | tf_op jit(solution)/shard_map/ppermute | solution.py:93
  6.0 3.5 %collective-permute-done.refs_1_ = bf16[4,128,128]{2,1,0:T(8,128)(2,1)S(1)} collective-permute-done((bf16[4,128,128]{2,1,0:T(8,128)(2,1)S(1)}, bf16[4,128,128]{2,1,0:T(8,128)(2,1)S(1)}, u32[]{:S(2)}, u32[]{:S(2)}) %collective-permute-start) | collective-permute-done | bytes 131104 | tf_op jit(solution)/shard_map/ppermute | solution.py:93
  9.5 3.5 %collective-permute-start.3 = (bf16[4,128,128]{2,1,0:T(8,128)(2,1)S(1)}, bf16[4,128,128]{2,1,0:T(8,128)(2,1)S(1)}, u32[]{:S(2)}, u32[]{:S(2)}) collective-permute-start(bf16[4,128,128]{2,1,0:T(8,128)(2,1)S(1)} %collective-permute-done.refs_1_), channel_id=1, source_target_pairs={{0,2},{2,6},{6,4},{4,0},{1,3},{3,7},{7,5},{5,1},{8,10},{10,14},{14... | collective-permute-start | bytes 393224 | tf_op jit(solution)/shard_map/ppermute | solution.py:93
  13.0 2.5 %query_sides.1 = (bf16[2,4,512,256]{3,2,1,0:T(8,128)(2,1)S(1)}, bf16[2,4,512,256]{3,2,1,0:T(8,128)(2,1)S(1)}) custom-call(bf16[128,32,128]{2,1,0:T(8,128)(2,1)} %bitcast.9, bf16[128,32,128]{2,1,0:T(8,128)(2,1)} %bitcast.10, bf16[128,32,128]{2,1,0:T(8,128)(2,1)} %bitcast.11), custom_call_target="tpu_custom_call" | custom-call | flops 1048576 | bytes 65536 | tf_op jit(solution)/shard_map/query_sides/pallas_call | solution.py:342
  15.5 3.4 %collective-permute-start.1 = (bf16[4,128,128]{2,1,0:T(8,128)(2,1)S(1)}, bf16[4,128,128]{2,1,0:T(8,128)(2,1)S(1)}, u32[]{:S(2)}, u32[]{:S(2)}) collective-permute-start(bf16[4,128,128]{2,1,0:T(8,128)(2,1)S(1)} %get-tuple-element.41.refs_4_), channel_id=1, source_target_pairs={{0,2},{2,6},{6,4},{4,0},{1,3},{3,7},{7,5},{5,1},{8,10},{10,14},{14... | collective-permute-start | bytes 393224 | tf_op jit(solution)/shard_map/ppermute | solution.py:93
  19.0 0.0 collective-permute-start.4
  19.0 0.0 collective-permute-done.2.refs_2_
  19.0 0.0 collective-permute-done.3.refs_3_
  19.0 0.0 copy-done
  19.0 2.7 %weights.2 = (f32[2,512,1024]{2,1,0:T(8,128)S(1)}, f32[2,8,1024]{2,1,0:T(8,128)S(1)}, bf16[2,128,128]{2,1,0:T(8,128)(2,1)S(1)}, bf16[2,128,128]{2,1,0:T(8,128)(2...) custom-call(s32[8]{0:T(128)S(1)} %copy-done, ...), custom_call_target="tpu_custom_call" | custom-call | flops 4294967296 | bytes 65536 | tf_op jit(solution)/shard_map/weights/pallas_call | solution.py:321
  21.7 0.5 collective-permute-done.1.refs_5_
  22.3 2.5 %collective-permute-start.5 = (bf16[4,128,128]{2,1,0:T(8,128)(2,1)S(1)}, bf16[4,128,128]{2,1,0:T(8,128)(2,1)S(1)}, u32[]{:S(2)}, u32[]{:S(2)}) collective-permute-start(bf16[4,128,128]{2,1,0:T(8,128)(2,1)S(1)} %collective-permute-done.1.refs_5_), channel_id=1, source_target_pairs={{0,2},{2,6},{6,4},{4,0},{1,3},{3,7},{7,5},{5,1},{8,10},{10,14},{14... | collective-permute-start | bytes 393224 | tf_op jit(solution)/shard_map/ppermute | solution.py:93
  24.7 2.7 %weights.3 = (f32[2,512,1024]{2,1,0:T(8,128)S(1)}, f32[2,8,1024]{2,1,0:T(8,128)S(1)}, bf16[2,128,128]{2,1,0:T(8,128)(2,1)S(1)}, bf16[2,128,128]{2,1,0:T(8,128)(2...) custom-call(s32[8]{0:T(128)S(1)} %copy-done, ...), custom_call_target="tpu_custom_call" | custom-call | flops 4294967296 | bytes 65536 | tf_op jit(solution)/shard_map/weights/pallas_call | solution.py:321
  27.5 1.9 %collective-permute-start.6 = (bf16[4,128,128]{2,1,0:T(8,128)(2,1)S(1)}, bf16[4,128,128]{2,1,0:T(8,128)(2,1)S(1)}, u32[]{:S(2)}, u32[]{:S(2)}) collective-permute-start(bf16[4,128,128]{2,1,0:T(8,128)(2,1)S(1)} %pad_maximum_fusion), channel_id=1, source_target_pairs={{0,2},{2,6},{6,4},{4,0},{1,3},{3,7},{7,5},{5,1},{8,10},{10,14},{14... | collective-permute-start | bytes 393224 | tf_op jit(solution)/shard_map/ppermute | solution.py:93
  29.5 0.0 collective-permute-done.4.refs_6_
  29.5 0.0 collective-permute-done.5.refs_7_
  29.5 1.6 %query_grads.2 = (bf16[128,16,128]{2,1,0:T(8,128)(2,1)S(1)}, bf16[2,512,1024]{2,1,0:T(8,128)(2,1)S(1)}) custom-call(bf16[2,4,512,256]{3,2,1,0:T(8,128)(2,1)S(1)} %get-tuple-element.49.g_side_ref, f32[2,512,1024]{2,1,0:T(8,128)S(1)} %get-tuple-element.45.weight_ref, f32[2,8,1024]{2,1,0:T(8,128)S(1)} %get-tuple-element.43.scale_ref, ...), custom_call_target="tpu_custom_call" | custom-call | flops 4294967296 | bytes 65536 | tf_op jit(solution)/shard_map/query_grads/pallas_call | solution.py:321
  31.1 2.5 %collective-permute-start.12 = (bf16[128,16,128]{2,1,0:T(8,128)(2,1)S(1)}, bf16[128,16,128]{2,1,0:T(8,128)(2,1)S(1)}, u32[]{:S(2)}, u32[]{:S(2)}) collective-permute-start(bf16[128,16,128]{2,1,0:T(8,128)(2,1)S(1)} %get-tuple-element.48), channel_id=1, source_target_pairs={{0,24},{8,0},{16,8},{24,16},{1,25},{9,1},{17,9},{25,17},{2,26},{10... | collective-permute-start | bytes 1572872 | tf_op jit(solution)/shard_map/ppermute | solution.py:110
  33.6 1.2 %collective-permute-start.7 = (bf16[4,128,128]{2,1,0:T(8,128)(2,1)S(1)}, bf16[4,128,128]{2,1,0:T(8,128)(2,1)S(1)}, u32[]{:S(2)}, u32[]{:S(2)}) collective-permute-start(bf16[4,128,128]{2,1,0:T(8,128)(2,1)S(1)} %pad_maximum_fusion.1), channel_id=1, source_target_pairs={{0,4},{2,0},{6,2},{4,6},{1,5},{3,1},{7,3},{5,7},{8,12},{10,8},{14,... | collective-permute-start | bytes 393224 | tf_op jit(solution)/shard_map/ppermute | solution.py:93
  34.8 1.6 %query_grads.3 = (bf16[128,16,128]{2,1,0:T(8,128)(2,1)S(1)}, bf16[2,512,1024]{2,1,0:T(8,128)(2,1)S(1)}) custom-call(bf16[2,4,512,256]{3,2,1,0:T(8,128)(2,1)S(1)} %get-tuple-element.49.g_side_ref, f32[2,512,1024]{2,1,0:T(8,128)S(1)} %get-tuple-element.50.weight_ref, f32[2,8,1024]{2,1,0:T(8,128)S(1)} %get-tuple-element.51.scale_ref, ...), custom_call_target="tpu_custom_call" | custom-call | flops 4294967296 | bytes 65536 | tf_op jit(solution)/shard_map/query_grads/pallas_call | solution.py:321
  36.5 0.6 %collective-permute-start.13 = (bf16[128,16,128]{2,1,0:T(8,128)(2,1)S(1)}, bf16[128,16,128]{2,1,0:T(8,128)(2,1)S(1)}, u32[]{:S(2)}, u32[]{:S(2)}) collective-permute-start(bf16[128,16,128]{2,1,0:T(8,128)(2,1)S(1)} %get-tuple-element.70), channel_id=1, source_target_pairs={{0,24},{8,0},{16,8},{24,16},{1,25},{9,1},{17,9},{25,17},{2,26},{10... | collective-permute-start | bytes 1572872 | tf_op jit(solution)/shard_map/ppermute | solution.py:110
  37.0 0.0 collective-permute-done.6
  37.1 1.5 %collective-permute-done.7.refs_5_ = bf16[4,128,128]{2,1,0:T(8,128)(2,1)S(1)} collective-permute-done((bf16[4,128,128]{2,1,0:T(8,128)(2,1)S(1)}, bf16[4,128,128]{2,1,0:T(8,128)(2,1)S(1)}, u32[]{:S(2)}, u32[]{:S(2)}) %collective-permute-start.7) | collective-permute-done | bytes 131104 | tf_op jit(solution)/shard_map/ppermute | solution.py:93
  38.6 2.8 %key_grads.1 = (bf16[4,128,128]{2,1,0:T(8,128)(2,1)S(1)}, bf16[4,128,128]{2,1,0:T(8,128)(2,1)S(1)}, bf16[4,128,128]{2,1,0:T(8,128)(2,1)S(1)}, bf16[4,128,128]{2,1,0:T(8,128)(2,1)S(1)}) custom-call(bf16[2,4,512,256]{3,2,1,0:T(8,128)(2,1)S(1)} %get-tuple-element.44.q_side_ref, bf16[2,512,1024]{2,1,0:T(8,128)(2,1)S(1)} %get-tuple-element.60.refs_0_, ...), custom_call_target="tpu_custom_call" | custom-call | flops 1048576 | bytes 65536 | tf_op jit(solution)/shard_map/key_grads/pallas_call | solution.py:321
  41.4 1.7 %collective-permute-start.8 = (bf16[4,128,128]{2,1,0:T(8,128)(2,1)S(1)}, bf16[4,128,128]{2,1,0:T(8,128)(2,1)S(1)}, u32[]{:S(2)}, u32[]{:S(2)}) collective-permute-start(bf16[4,128,128]{2,1,0:T(8,128)(2,1)S(1)} %get-tuple-element.63), channel_id=1, source_target_pairs={{0,2},{2,6},{6,4},{4,0},{1,3},{3,7},{7,5},{5,1},{8,10},{10,14},{14... | collective-permute-start | bytes 393224 | tf_op jit(solution)/shard_map/ppermute | solution.py:93
  43.1 2.0 %collective-permute-start.11 = (bf16[4,128,128]{2,1,0:T(8,128)(2,1)S(1)}, bf16[4,128,128]{2,1,0:T(8,128)(2,1)S(1)}, u32[]{:S(2)}, u32[]{:S(2)}) collective-permute-start(bf16[4,128,128]{2,1,0:T(8,128)(2,1)S(1)} %add_convert_fusion.1), channel_id=1, source_target_pairs={{0,2},{2,6},{6,4},{4,0},{1,3},{3,7},{7,5},{5,1},{8,10},{10,14},{14... | collective-permute-start | bytes 393224 | tf_op jit(solution)/shard_map/ppermute | solution.py:93
  45.1 0.9 %collective-permute-start.10 = (bf16[4,128,128]{2,1,0:T(8,128)(2,1)S(1)}, bf16[4,128,128]{2,1,0:T(8,128)(2,1)S(1)}, u32[]{:S(2)}, u32[]{:S(2)}) collective-permute-start(bf16[4,128,128]{2,1,0:T(8,128)(2,1)S(1)} %get-tuple-element.65), channel_id=1, source_target_pairs={{0,4},{2,0},{6,2},{4,6},{1,5},{3,1},{7,3},{5,7},{8,12},{10,8},{14,... | collective-permute-start | bytes 393224 | tf_op jit(solution)/shard_map/ppermute | solution.py:93
  46.0 2.4 %collective-permute-done.8 = bf16[4,128,128]{2,1,0:T(8,128)(2,1)S(1)} collective-permute-done((bf16[4,128,128]{2,1,0:T(8,128)(2,1)S(1)}, bf16[4,128,128]{2,1,0:T(8,128)(2,1)S(1)}, u32[]{:S(2)}, u32[]{:S(2)}) %collective-permute-start.8) | collective-permute-done | bytes 131104 | tf_op jit(solution)/shard_map/ppermute | solution.py:93
  48.5 0.1 collective-permute-start.9
  48.6 2.9 %collective-permute-done.11.refs_4_ = bf16[4,128,128]{2,1,0:T(8,128)(2,1)S(1)} collective-permute-done((bf16[4,128,128]{2,1,0:T(8,128)(2,1)S(1)}, bf16[4,128,128]{2,1,0:T(8,128)(2,1)S(1)}, u32[]{:S(2)}, u32[]{:S(2)}) %collective-permute-start.11) | collective-permute-done | bytes 131104 | tf_op jit(solution)/shard_map/ppermute | solution.py:93
  51.5 0.0 collective-permute-done.10.refs_2_
  51.5 2.9 %collective-permute-done.9.refs_1_ = bf16[4,128,128]{2,1,0:T(8,128)(2,1)S(1)} collective-permute-done((bf16[4,128,128]{2,1,0:T(8,128)(2,1)S(1)}, bf16[4,128,128]{2,1,0:T(8,128)(2,1)S(1)}, u32[]{:S(2)}, u32[]{:S(2)}) %collective-permute-start.9) | collective-permute-done | bytes 131104 | tf_op jit(solution)/shard_map/ppermute | solution.py:93
  54.4 0.8 %lay_out.1 = (bf16[512,128]{1,0:T(8,128)(2,1)}, bf16[512,128]{1,0:T(8,128)(2,1)}) custom-call(bf16[4,128,128]{2,1,0:T(8,128)(2,1)S(1)} %get-tuple-element.62.refs_0_, bf16[4,128,128]{2,1,0:T(8,128)(2,1)S(1)} %collective-permute-done.9.refs_1_, bf16[4,128,128]{2,1,0:T(8,128)(2,1)S(1)} %collective-permute-done.10.refs_2_, ...), custom_call_target="tpu_custom_call" | custom-call | flops 1048576 | bytes 65536 | tf_op jit(solution)/shard_map/lay_out/pallas_call | solution.py:321
  55.2 0.0 collective-permute-done.13
  55.2 0.0 collective-permute-done.12
  55.2 1.2 %maximum_select_fusion = bf16[1,128,32,128]{3,2,1,0:T(8,128)(2,1)} fusion(bf16[1,128,16,128]{3,2,1,0:T(8,128)(2,1)S(1)} %bitcast.13, bf16[1,128,16,128]{3,2,1,0:T(8,128)(2,1)S(1)} %bitcast.12, pred[]{:T(512)S(6)} %eq.3), kind=kLoop, calls=%fused_computation | loop fusion | flops 2621440 | bytes 2097153 | tf_op jit(solution)/shard_map/jit(_where)/select_n | solution.py:445
  (5 shorter events, 0.1 us)
Async XLA Ops:
  0.6 18.3 %copy-start = (s32[8]{0:T(128)S(1)}, s32[8]{0:T(128)}, u32[]{:S(2)}) copy-start(s32[8]{0:T(128)} %order_ref.3) | copy-start | bytes 100
  1.8 7.7 %collective-permute-start = (bf16[4,128,128]{2,1,0:T(8,128)(2,1)S(1)}, bf16[4,128,128]{2,1,0:T(8,128)(2,1)S(1)}, u32[]{:S(2)}, u32[]{:S(2)}) collective-permute-start(bf16[4,128,128]{2,1,0:T(8,128)(2,1)S(1)} %get-tuple-element.38.refs_0_), channel_id=1, source_target_pairs={{0,2},{2,6},{6,4},{4,0},{1,3},{3,7},{7,5},{5,1},{8,10},{10,14},{14... | collective-permute-start | bytes 393224 | tf_op jit(solution)/shard_map/ppermute | solution.py:93
  4.9 14.1 %collective-permute-start.2 = (bf16[4,128,128]{2,1,0:T(8,128)(2,1)S(1)}, bf16[4,128,128]{2,1,0:T(8,128)(2,1)S(1)}, u32[]{:S(2)}, u32[]{:S(2)}) collective-permute-start(bf16[4,128,128]{2,1,0:T(8,128)(2,1)S(1)} %get-tuple-element.38.refs_0_), channel_id=1, source_target_pairs={{0,4},{2,0},{6,2},{4,6},{1,5},{3,1},{7,3},{5,7},{8,12},{10,8},{14,... | collective-permute-start | bytes 393224 | tf_op jit(solution)/shard_map/ppermute | solution.py:93
  9.5 9.5 %collective-permute-start.3 = (bf16[4,128,128]{2,1,0:T(8,128)(2,1)S(1)}, bf16[4,128,128]{2,1,0:T(8,128)(2,1)S(1)}, u32[]{:S(2)}, u32[]{:S(2)}) collective-permute-start(bf16[4,128,128]{2,1,0:T(8,128)(2,1)S(1)} %collective-permute-done.refs_1_), channel_id=1, source_target_pairs={{0,2},{2,6},{6,4},{4,0},{1,3},{3,7},{7,5},{5,1},{8,10},{10,14},{14... | collective-permute-start | bytes 393224 | tf_op jit(solution)/shard_map/ppermute | solution.py:93
  15.5 6.7 %collective-permute-start.1 = (bf16[4,128,128]{2,1,0:T(8,128)(2,1)S(1)}, bf16[4,128,128]{2,1,0:T(8,128)(2,1)S(1)}, u32[]{:S(2)}, u32[]{:S(2)}) collective-permute-start(bf16[4,128,128]{2,1,0:T(8,128)(2,1)S(1)} %get-tuple-element.41.refs_4_), channel_id=1, source_target_pairs={{0,2},{2,6},{6,4},{4,0},{1,3},{3,7},{7,5},{5,1},{8,10},{10,14},{14... | collective-permute-start | bytes 393224 | tf_op jit(solution)/shard_map/ppermute | solution.py:93
  19.0 10.5 %collective-permute-start.4 = (bf16[4,128,128]{2,1,0:T(8,128)(2,1)S(1)}, bf16[4,128,128]{2,1,0:T(8,128)(2,1)S(1)}, u32[]{:S(2)}, u32[]{:S(2)}) collective-permute-start(bf16[4,128,128]{2,1,0:T(8,128)(2,1)S(1)} %get-tuple-element.41.refs_4_), channel_id=1, source_target_pairs={{0,4},{2,0},{6,2},{4,6},{1,5},{3,1},{7,3},{5,7},{8,12},{10,8},{14,... | collective-permute-start | bytes 393224 | tf_op jit(solution)/shard_map/ppermute | solution.py:93
  22.3 7.2 %collective-permute-start.5 = (bf16[4,128,128]{2,1,0:T(8,128)(2,1)S(1)}, bf16[4,128,128]{2,1,0:T(8,128)(2,1)S(1)}, u32[]{:S(2)}, u32[]{:S(2)}) collective-permute-start(bf16[4,128,128]{2,1,0:T(8,128)(2,1)S(1)} %collective-permute-done.1.refs_5_), channel_id=1, source_target_pairs={{0,2},{2,6},{6,4},{4,0},{1,3},{3,7},{7,5},{5,1},{8,10},{10,14},{14... | collective-permute-start | bytes 393224 | tf_op jit(solution)/shard_map/ppermute | solution.py:93
  27.5 9.5 %collective-permute-start.6 = (bf16[4,128,128]{2,1,0:T(8,128)(2,1)S(1)}, bf16[4,128,128]{2,1,0:T(8,128)(2,1)S(1)}, u32[]{:S(2)}, u32[]{:S(2)}) collective-permute-start(bf16[4,128,128]{2,1,0:T(8,128)(2,1)S(1)} %pad_maximum_fusion), channel_id=1, source_target_pairs={{0,2},{2,6},{6,4},{4,0},{1,3},{3,7},{7,5},{5,1},{8,10},{10,14},{14... | collective-permute-start | bytes 393224 | tf_op jit(solution)/shard_map/ppermute | solution.py:93
  31.1 24.1 %collective-permute-start.12 = (bf16[128,16,128]{2,1,0:T(8,128)(2,1)S(1)}, bf16[128,16,128]{2,1,0:T(8,128)(2,1)S(1)}, u32[]{:S(2)}, u32[]{:S(2)}) collective-permute-start(bf16[128,16,128]{2,1,0:T(8,128)(2,1)S(1)} %get-tuple-element.48), channel_id=1, source_target_pairs={{0,24},{8,0},{16,8},{24,16},{1,25},{9,1},{17,9},{25,17},{2,26},{10... | collective-permute-start | bytes 1572872 | tf_op jit(solution)/shard_map/ppermute | solution.py:110
  33.6 5.0 %collective-permute-start.7 = (bf16[4,128,128]{2,1,0:T(8,128)(2,1)S(1)}, bf16[4,128,128]{2,1,0:T(8,128)(2,1)S(1)}, u32[]{:S(2)}, u32[]{:S(2)}) collective-permute-start(bf16[4,128,128]{2,1,0:T(8,128)(2,1)S(1)} %pad_maximum_fusion.1), channel_id=1, source_target_pairs={{0,4},{2,0},{6,2},{4,6},{1,5},{3,1},{7,3},{5,7},{8,12},{10,8},{14,... | collective-permute-start | bytes 393224 | tf_op jit(solution)/shard_map/ppermute | solution.py:93
  36.5 18.8 %collective-permute-start.13 = (bf16[128,16,128]{2,1,0:T(8,128)(2,1)S(1)}, bf16[128,16,128]{2,1,0:T(8,128)(2,1)S(1)}, u32[]{:S(2)}, u32[]{:S(2)}) collective-permute-start(bf16[128,16,128]{2,1,0:T(8,128)(2,1)S(1)} %get-tuple-element.70), channel_id=1, source_target_pairs={{0,24},{8,0},{16,8},{24,16},{1,25},{9,1},{17,9},{25,17},{2,26},{10... | collective-permute-start | bytes 1572872 | tf_op jit(solution)/shard_map/ppermute | solution.py:110
  41.4 7.1 %collective-permute-start.8 = (bf16[4,128,128]{2,1,0:T(8,128)(2,1)S(1)}, bf16[4,128,128]{2,1,0:T(8,128)(2,1)S(1)}, u32[]{:S(2)}, u32[]{:S(2)}) collective-permute-start(bf16[4,128,128]{2,1,0:T(8,128)(2,1)S(1)} %get-tuple-element.63), channel_id=1, source_target_pairs={{0,2},{2,6},{6,4},{4,0},{1,3},{3,7},{7,5},{5,1},{8,10},{10,14},{14... | collective-permute-start | bytes 393224 | tf_op jit(solution)/shard_map/ppermute | solution.py:93
  43.1 8.4 %collective-permute-start.11 = (bf16[4,128,128]{2,1,0:T(8,128)(2,1)S(1)}, bf16[4,128,128]{2,1,0:T(8,128)(2,1)S(1)}, u32[]{:S(2)}, u32[]{:S(2)}) collective-permute-start(bf16[4,128,128]{2,1,0:T(8,128)(2,1)S(1)} %add_convert_fusion.1), channel_id=1, source_target_pairs={{0,2},{2,6},{6,4},{4,0},{1,3},{3,7},{7,5},{5,1},{8,10},{10,14},{14... | collective-permute-start | bytes 393224 | tf_op jit(solution)/shard_map/ppermute | solution.py:93
  45.1 6.4 %collective-permute-start.10 = (bf16[4,128,128]{2,1,0:T(8,128)(2,1)S(1)}, bf16[4,128,128]{2,1,0:T(8,128)(2,1)S(1)}, u32[]{:S(2)}, u32[]{:S(2)}) collective-permute-start(bf16[4,128,128]{2,1,0:T(8,128)(2,1)S(1)} %get-tuple-element.65), channel_id=1, source_target_pairs={{0,4},{2,0},{6,2},{4,6},{1,5},{3,1},{7,3},{5,7},{8,12},{10,8},{14,... | collective-permute-start | bytes 393224 | tf_op jit(solution)/shard_map/ppermute | solution.py:93
  48.5 5.9 %collective-permute-start.9 = (bf16[4,128,128]{2,1,0:T(8,128)(2,1)S(1)}, bf16[4,128,128]{2,1,0:T(8,128)(2,1)S(1)}, u32[]{:S(2)}, u32[]{:S(2)}) collective-permute-start(bf16[4,128,128]{2,1,0:T(8,128)(2,1)S(1)} %add_convert_fusion), channel_id=1, source_target_pairs={{0,2},{2,6},{6,4},{4,0},{1,3},{3,7},{7,5},{5,1},{8,10},{10,14},{14... | collective-permute-start | bytes 393224 | tf_op jit(solution)/shard_map/ppermute | solution.py:93

commit v8 on v7

--- a/solution.py
+++ b/solution.py
@@ -130,40 +130,59 @@
     return terms, relayed
 
 
-def sides_kernel(groups, q_hbm, g_hbm, o_hbm, q_side_ref, g_side_ref, in_ref, sems):
+def fetch(sources, in_ref, sems):
+    half_rows = in_ref.shape[2]
+    copies = []
+    for half in range(2):
+        for part, source in enumerate(sources):
+            piece = source.at[pl.ds(half * half_rows, half_rows)]
+            sem = sems.at[half * len(sources) + part]
+            copies.append(pltpu.make_async_copy(piece, in_ref.at[half, part], sem))
+            copies[-1].start()
+
+    def wait(half):
+        for copy in copies[half * len(sources) : (half + 1) * len(sources)]:
+            copy.wait()
+
+    return wait
+
+
+def query_side_kernel(groups, q_hbm, side_ref, in_ref, sems):
+    wait = fetch((q_hbm,), in_ref, sems)
     _, _, half_rows, heads, size = in_ref.shape
     per_group = heads // groups
-    copies = []
-    for half in range(2):
-        for part, source in enumerate((q_hbm, g_hbm, o_hbm)):
-            piece = source.at[pl.ds(half * half_rows, half_rows)]
-            copies.append(
-                pltpu.make_async_copy(piece, in_ref.at[half, part], sems.at[half * 3 + part])
-            )
-            copies[-1].start()
     rows = half_rows * per_group
     sign = signs(size)
-    root = 1.0 / math.sqrt(size)
     row_offset = lax.broadcasted_iota(jnp.int32, (rows, size), 0) // per_group
     lane = lax.broadcasted_iota(jnp.int32, (rows, size), 1)
     hide = jnp.where(row_offset == lane, NEG, 0.0).astype(BF16)
     for half in range(2):
-        for copy in copies[3 * half : 3 * half + 3]:
-            copy.wait()
-        q_all = nn(in_ref[half, 0].reshape(half_rows * heads, size), sign) * root
+        wait(half)
+        q_all = nn(in_ref[half, 0].reshape(half_rows * heads, size), sign) * (1.0 / math.sqrt(size))
         q_all = q_all.reshape(half_rows, groups, per_group, size)
-        g_all = in_ref[half, 1].astype(F32).reshape(half_rows, groups, per_group, size)
-        o_all = in_ref[half, 2].astype(F32).reshape(half_rows, groups, per_group, size)
+        for group in range(groups):
+            side_ref[half, group, :, :size] = q_all[:, group].reshape(rows, size).astype(BF16)
+            side_ref[half, group, :, size:] = hide
+
+
+def grad_side_kernel(groups, g_hbm, o_hbm, side_ref, in_ref, sems):
+    wait = fetch((g_hbm, o_hbm), in_ref, sems)
+    _, _, half_rows, heads, size = in_ref.shape
+    per_group = heads // groups
+    rows = half_rows * per_group
+    lane = lax.broadcasted_iota(jnp.int32, (rows, size), 1)
+    for half in range(2):
+        wait(half)
+        g_all = in_ref[half, 0].astype(F32).reshape(half_rows, groups, per_group, size)
+        o_all = in_ref[half, 1].astype(F32).reshape(half_rows, groups, per_group, size)
         for group in range(groups):
             grad = g_all[:, group].reshape(rows, size)
             product = grad * o_all[:, group].reshape(rows, size)
             product = -(product + pltpu.roll(product, size // 2, 1))
             high = product.astype(BF16).astype(F32)
             delta = jnp.where(lane < size // 2, high, product - high)
-            q_side_ref[half, group, :, :size] = q_all[:, group].reshape(rows, size).astype(BF16)
-            q_side_ref[half, group, :, size:] = hide
-            g_side_ref[half, group, :, :size] = grad.astype(BF16)
-            g_side_ref[half, group, :, size:] = delta.astype(BF16)
+            side_ref[half, group, :, :size] = grad.astype(BF16)
+            side_ref[half, group, :, size:] = delta.astype(BF16)
 
 
 def far_last(count):
@@ -334,21 +353,21 @@
     return pltpu.with_memory_space_constraint(value, pltpu.HBM)
 
 
-def make_sides(groups, queries, grads, saved):
-    tokens, heads, size = queries.shape
+def make_side(kernel, name, groups, *sources):
+    tokens, heads, size = sources[0].shape
     half_rows = tokens // 2
     rows = half_rows * heads // groups
-    shape = jax.ShapeDtypeStruct((2, groups, rows, 2 * size), BF16)
+    count = len(sources)
     return pl.pallas_call(
-        functools.partial(sides_kernel, groups),
-        in_specs=[HBM] * 3,
-        out_specs=[VMEM] * 2,
-        out_shape=[shape] * 2,
-        scratch_shapes=[pltpu.VMEM((2, 3, half_rows, heads, size), BF16), DMA((6,))],
+        functools.partial(kernel, groups),
+        in_specs=[HBM] * count,
+        out_specs=VMEM,
+        out_shape=jax.ShapeDtypeStruct((2, groups, rows, 2 * size), BF16),
+        scratch_shapes=[pltpu.VMEM((2, count, half_rows, heads, size), BF16), DMA((2 * count,))],
         compiler_params=pltpu.CompilerParams(vmem_limit_bytes=12 * 2**20),
         cost_estimate=pl.CostEstimate(flops=WORK, bytes_accessed=2**16, transcendentals=0),
-        name="query_sides",
-    )(in_hbm(queries), in_hbm(grads), in_hbm(saved))
+        name=name,
+    )(*[in_hbm(source) for source in sources])
 
 
 def shards(queries, key_heads, value_heads, forward_out, output_grad, block_order):
@@ -377,8 +396,10 @@
     )(in_hbm(key_heads.reshape(-1, size)), in_hbm(value_heads.reshape(-1, size)))
 
     up, down = passed(k_block, "ctx", 1), passed(k_block, "ctx", -1)
+    g_side = make_side(grad_side_kernel, "grad_side", groups, output_grad[0], forward_out[0])
+    up, g_side = after((up, g_side))
     q_loads, _ = after((queries[0], up))
-    q_side, g_side = make_sides(groups, q_loads, output_grad[0], forward_out[0])
+    q_side = make_side(query_side_kernel, "query_side", groups, q_loads)
     k_all = gather_rest(k_block, up, down, "ctx")
     v_block, _ = after((v_block, q_side))
     up, down = passed(v_block, "ctx", 1), passed(v_block, "ctx", -1)
@@ -420,12 +441,10 @@
         )
         if stage == 0:
             g_side, _ = after((g_side, handed_part))
-            first_handed = handed_part
         handed.append(passed_down(handed_part, "pipe"))
         dscores.append(dscore)
     dv_parts = [jnp.concatenate(parts, axis=0) for parts in zip(*dv_parts)]
     dv_parts = [dv_parts[slots.index(step)] for step in range(blocks)]
-    dv_parts[1], _ = after((dv_parts[1], first_handed))
     dv_terms, dv_relayed = scatter_sums(dv_parts, "ctx", ())
 
     dscores, _ = after((dscores, (dv_relayed, dv_terms[-1])))

time: 56.6 us -> 55.4 us (0.979)
  waiting for transfers between devices: 13.8 us -> 10.4 us
  Pallas kernels: 15.9 us -> 17.4 us
  starting transfers between devices: 24.6 us -> 25.4 us
    ppermute x12, waiting for transfers between devices: 13.8 us -> 9.14 us  [passed(): lax.ppermute(value, axis, [(order[at], order[(at + step) % count]) for at...]
    pallas_call x1 -> x2, Pallas kernels: 2.48 us -> 3.98 us  [make_side(): pl.pallas_call(functools.partial(kernel, groups), in_specs=[HBM] * count,...]
    ppermute x2, waiting for transfers between devices: 0.01 us -> 1.27 us  [passed_down(): lax.ppermute(value, axis, [(at, (at - 1) % count) for at in range(count)])]
    ppermute x12, starting transfers between devices: 21.5 us -> 22.3 us  [passed(): lax.ppermute(value, axis, [(order[at], order[(at + step) % count]) for at...]
  transfers between devices with their start and end apart: 14 -> 14, of which waited for: 6 -> 6; matrix products, arithmetic and copies ran while one was open for 0% -> 0% of each run, Pallas kernels for 26% -> 29%
where the time goes in v8:
time: 55.4 us; the launch traced here: 55.2 us
  starting transfers between devices  25.4 us (46%)
  Pallas kernels  17.4 us (31%)
  waiting for transfers between devices  10.4 us (19%)
  other arithmetic  1.3 us (2%)
  between operations  0.75 us (1%)
    ppermute x12, starting transfers between devices, passed(): lax.ppermute(value, axis, [(order[at], order[(at + step) % count]) for at...  22.3 us
    pallas_call x6, Pallas kernels, call(): pl.pallas_call(kernel, in_specs=([SMEM] if smem else []) + [VMEM] * (len(...  12.3 us
    ppermute x12, waiting for transfers between devices, passed(): lax.ppermute(value, axis, [(order[at], order[(at + step) % count]) for at...  9.14 us
    pallas_call x2, Pallas kernels, make_side(): pl.pallas_call(functools.partial(kernel, groups), in_specs=[HBM] * count,...  3.98 us
    ppermute x2, starting transfers between devices, passed_down(): lax.ppermute(value, axis, [(at, (at - 1) % count) for at in range(count)])  3.08 us
    ppermute x2, waiting for transfers between devices, passed_down(): lax.ppermute(value, axis, [(at, (at - 1) % count) for at in range(count)])  1.27 us
    select_n x1, other arithmetic, shards(): handed = jnp.where(last, jnp.zeros_like(handed), handed)  1.18 us
    pallas_call x1, Pallas kernels, shards(): pl.pallas_call(prep_kernel, in_specs=[HBM] * 2, out_specs=[VMEM] * 2, out...  1.14 us
  transfers between devices with their start and end apart: 14, of which 6 were waited for; matrix products, arithmetic and copies ran while one was open for 0% of the time, Pallas kernels for 29%

profile of v8, /device:TPU:0, one launch (start us, length us, event | category | flops | bytes accessed | tf_op | source)
XLA Modules:
  0.0 55.2 jit_solution(6276879956814032257)
XLA Ops:
  0.6 1.1 %pack_keys.1 = (bf16[4,128,128]{2,1,0:T(8,128)(2,1)S(1)}, bf16[4,128,128]{2,1,0:T(8,128)(2,1)S(1)}) custom-call(bf16[512,128]{1,0:T(8,128)(2,1)} %bitcast.14, bf16[512,128]{1,0:T(8,128)(2,1)} %bitcast.15), custom_call_target="tpu_custom_call" | custom-call | flops 1048576 | bytes 65536 | tf_op jit(solution)/shard_map/pack_keys/pallas_call | solution.py:387
  1.8 3.1 %collective-permute-start = (bf16[4,128,128]{2,1,0:T(8,128)(2,1)S(1)}, bf16[4,128,128]{2,1,0:T(8,128)(2,1)S(1)}, u32[]{:S(2)}, u32[]{:S(2)}) collective-permute-start(bf16[4,128,128]{2,1,0:T(8,128)(2,1)S(1)} %get-tuple-element.37.refs_0_), channel_id=1, source_target_pairs={{0,2},{2,6},{6,4},{4,0},{1,3},{3,7},{7,5},{5,1},{8,10},{10,14},{14... | collective-permute-start | bytes 393224 | tf_op jit(solution)/shard_map/ppermute | solution.py:93
  4.9 1.1 %collective-permute-start.2 = (bf16[4,128,128]{2,1,0:T(8,128)(2,1)S(1)}, bf16[4,128,128]{2,1,0:T(8,128)(2,1)S(1)}, u32[]{:S(2)}, u32[]{:S(2)}) collective-permute-start(bf16[4,128,128]{2,1,0:T(8,128)(2,1)S(1)} %get-tuple-element.37.refs_0_), channel_id=1, source_target_pairs={{0,4},{2,0},{6,2},{4,6},{1,5},{3,1},{7,3},{5,7},{8,12},{10,8},{14,... | collective-permute-start | bytes 393224 | tf_op jit(solution)/shard_map/ppermute | solution.py:93
  5.9 2.0 %grad_side.1.g_side_ref = bf16[2,4,512,256]{3,2,1,0:T(8,128)(2,1)S(1)} custom-call(bf16[128,32,128]{2,1,0:T(8,128)(2,1)} %bitcast.10, bf16[128,32,128]{2,1,0:T(8,128)(2,1)} %bitcast.11), custom_call_target="tpu_custom_call" | custom-call | flops 1048576 | bytes 65536 | tf_op jit(solution)/shard_map/grad_side/pallas_call | solution.py:361
  8.0 0.0 copy-start
  8.0 1.5 %collective-permute-done.refs_1_ = bf16[4,128,128]{2,1,0:T(8,128)(2,1)S(1)} collective-permute-done((bf16[4,128,128]{2,1,0:T(8,128)(2,1)S(1)}, bf16[4,128,128]{2,1,0:T(8,128)(2,1)S(1)}, u32[]{:S(2)}, u32[]{:S(2)}) %collective-permute-start) | collective-permute-done | bytes 131104 | tf_op jit(solution)/shard_map/ppermute | solution.py:93
  9.5 3.5 %collective-permute-start.3 = (bf16[4,128,128]{2,1,0:T(8,128)(2,1)S(1)}, bf16[4,128,128]{2,1,0:T(8,128)(2,1)S(1)}, u32[]{:S(2)}, u32[]{:S(2)}) collective-permute-start(bf16[4,128,128]{2,1,0:T(8,128)(2,1)S(1)} %collective-permute-done.refs_1_), channel_id=1, source_target_pairs={{0,2},{2,6},{6,4},{4,0},{1,3},{3,7},{7,5},{5,1},{8,10},{10,14},{14... | collective-permute-start | bytes 393224 | tf_op jit(solution)/shard_map/ppermute | solution.py:93
  13.0 2.0 %query_side.1.q_side_ref = bf16[2,4,512,256]{3,2,1,0:T(8,128)(2,1)S(1)} custom-call(bf16[128,32,128]{2,1,0:T(8,128)(2,1)} %bitcast.9), custom_call_target="tpu_custom_call" | custom-call | flops 1048576 | bytes 65536 | tf_op jit(solution)/shard_map/query_side/pallas_call | solution.py:361
  15.0 3.4 %collective-permute-start.1 = (bf16[4,128,128]{2,1,0:T(8,128)(2,1)S(1)}, bf16[4,128,128]{2,1,0:T(8,128)(2,1)S(1)}, u32[]{:S(2)}, u32[]{:S(2)}) collective-permute-start(bf16[4,128,128]{2,1,0:T(8,128)(2,1)S(1)} %get-tuple-element.40.refs_4_), channel_id=1, source_target_pairs={{0,2},{2,6},{6,4},{4,0},{1,3},{3,7},{7,5},{5,1},{8,10},{10,14},{14... | collective-permute-start | bytes 393224 | tf_op jit(solution)/shard_map/ppermute | solution.py:93
  18.4 0.0 collective-permute-start.4
  18.4 0.0 collective-permute-done.2.refs_2_
  18.4 0.0 collective-permute-done.3.refs_3_
  18.4 0.0 copy-done
  18.4 2.7 %weights.2 = (f32[2,512,1024]{2,1,0:T(8,128)S(1)}, f32[2,8,1024]{2,1,0:T(8,128)S(1)}, bf16[2,128,128]{2,1,0:T(8,128)(2,1)S(1)}, bf16[2,128,128]{2,1,0:T(8,128)(2...) custom-call(s32[8]{0:T(128)S(1)} %copy-done, ...), custom_call_target="tpu_custom_call" | custom-call | flops 4294967296 | bytes 65536 | tf_op jit(solution)/shard_map/weights/pallas_call | solution.py:340
  21.2 0.5 collective-permute-done.1.refs_5_
  21.7 2.5 %collective-permute-start.5 = (bf16[4,128,128]{2,1,0:T(8,128)(2,1)S(1)}, bf16[4,128,128]{2,1,0:T(8,128)(2,1)S(1)}, u32[]{:S(2)}, u32[]{:S(2)}) collective-permute-start(bf16[4,128,128]{2,1,0:T(8,128)(2,1)S(1)} %collective-permute-done.1.refs_5_), channel_id=1, source_target_pairs={{0,2},{2,6},{6,4},{4,0},{1,3},{3,7},{7,5},{5,1},{8,10},{10,14},{14... | collective-permute-start | bytes 393224 | tf_op jit(solution)/shard_map/ppermute | solution.py:93
  24.2 2.7 %weights.3 = (f32[2,512,1024]{2,1,0:T(8,128)S(1)}, f32[2,8,1024]{2,1,0:T(8,128)S(1)}, bf16[2,128,128]{2,1,0:T(8,128)(2,1)S(1)}, bf16[2,128,128]{2,1,0:T(8,128)(2...) custom-call(s32[8]{0:T(128)S(1)} %copy-done, ...), custom_call_target="tpu_custom_call" | custom-call | flops 4294967296 | bytes 65536 | tf_op jit(solution)/shard_map/weights/pallas_call | solution.py:340
  27.0 2.4 %collective-permute-start.6 = (bf16[4,128,128]{2,1,0:T(8,128)(2,1)S(1)}, bf16[4,128,128]{2,1,0:T(8,128)(2,1)S(1)}, u32[]{:S(2)}, u32[]{:S(2)}) collective-permute-start(bf16[4,128,128]{2,1,0:T(8,128)(2,1)S(1)} %pad_maximum_fusion), channel_id=1, source_target_pairs={{0,2},{2,6},{6,4},{4,0},{1,3},{3,7},{7,5},{5,1},{8,10},{10,14},{14... | collective-permute-start | bytes 393224 | tf_op jit(solution)/shard_map/ppermute | solution.py:93
  29.4 0.6 %collective-permute-start.7 = (bf16[4,128,128]{2,1,0:T(8,128)(2,1)S(1)}, bf16[4,128,128]{2,1,0:T(8,128)(2,1)S(1)}, u32[]{:S(2)}, u32[]{:S(2)}) collective-permute-start(bf16[4,128,128]{2,1,0:T(8,128)(2,1)S(1)} %pad_maximum_fusion.1), channel_id=1, source_target_pairs={{0,4},{2,0},{6,2},{4,6},{1,5},{3,1},{7,3},{5,7},{8,12},{10,8},{14,... | collective-permute-start | bytes 393224 | tf_op jit(solution)/shard_map/ppermute | solution.py:93
  30.0 0.0 collective-permute-done.4.refs_6_
  30.0 0.0 collective-permute-done.5.refs_7_
  30.0 1.6 %query_grads.2 = (bf16[128,16,128]{2,1,0:T(8,128)(2,1)S(1)}, bf16[2,512,1024]{2,1,0:T(8,128)(2,1)S(1)}) custom-call(bf16[2,4,512,256]{3,2,1,0:T(8,128)(2,1)S(1)} %grad_side.1.g_side_ref, f32[2,512,1024]{2,1,0:T(8,128)S(1)} %get-tuple-element.44.weight_ref, f32[2,8,1024]{2,1,0:T(8,128)S(1)} %get-tuple-element.42.scale_ref, ...), custom_call_target="tpu_custom_call" | custom-call | flops 4294967296 | bytes 65536 | tf_op jit(solution)/shard_map/query_grads/pallas_call | solution.py:340
  31.7 2.5 %collective-permute-start.12 = (bf16[128,16,128]{2,1,0:T(8,128)(2,1)S(1)}, bf16[128,16,128]{2,1,0:T(8,128)(2,1)S(1)}, u32[]{:S(2)}, u32[]{:S(2)}) collective-permute-start(bf16[128,16,128]{2,1,0:T(8,128)(2,1)S(1)} %get-tuple-element.47), channel_id=1, source_target_pairs={{0,24},{8,0},{16,8},{24,16},{1,25},{9,1},{17,9},{25,17},{2,26},{10... | collective-permute-start | bytes 1572872 | tf_op jit(solution)/shard_map/ppermute | solution.py:110
  34.1 1.6 %query_grads.3 = (bf16[128,16,128]{2,1,0:T(8,128)(2,1)S(1)}, bf16[2,512,1024]{2,1,0:T(8,128)(2,1)S(1)}) custom-call(bf16[2,4,512,256]{3,2,1,0:T(8,128)(2,1)S(1)} %grad_side.1.g_side_ref, f32[2,512,1024]{2,1,0:T(8,128)S(1)} %get-tuple-element.49.weight_ref, f32[2,8,1024]{2,1,0:T(8,128)S(1)} %get-tuple-element.50.scale_ref, ...), custom_call_target="tpu_custom_call" | custom-call | flops 4294967296 | bytes 65536 | tf_op jit(solution)/shard_map/query_grads/pallas_call | solution.py:340
  35.8 0.6 %collective-permute-start.13 = (bf16[128,16,128]{2,1,0:T(8,128)(2,1)S(1)}, bf16[128,16,128]{2,1,0:T(8,128)(2,1)S(1)}, u32[]{:S(2)}, u32[]{:S(2)}) collective-permute-start(bf16[128,16,128]{2,1,0:T(8,128)(2,1)S(1)} %get-tuple-element.68), channel_id=1, source_target_pairs={{0,24},{8,0},{16,8},{24,16},{1,25},{9,1},{17,9},{25,17},{2,26},{10... | collective-permute-start | bytes 1572872 | tf_op jit(solution)/shard_map/ppermute | solution.py:110
  36.3 0.0 collective-permute-done.6
  36.4 0.0 collective-permute-done.7.refs_5_
  36.4 2.8 %key_grads.1 = (bf16[4,128,128]{2,1,0:T(8,128)(2,1)S(1)}, bf16[4,128,128]{2,1,0:T(8,128)(2,1)S(1)}, bf16[4,128,128]{2,1,0:T(8,128)(2,1)S(1)}, bf16[4,128,128]{2,1,0:T(8,128)(2,1)S(1)}) custom-call(bf16[2,4,512,256]{3,2,1,0:T(8,128)(2,1)S(1)} %query_side.1.q_side_ref, bf16[2,512,1024]{2,1,0:T(8,128)(2,1)S(1)} %get-tuple-element.58.refs_0_, ...), custom_call_target="tpu_custom_call" | custom-call | flops 1048576 | bytes 65536 | tf_op jit(solution)/shard_map/key_grads/pallas_call | solution.py:340
  39.2 1.5 %collective-permute-start.8 = (bf16[4,128,128]{2,1,0:T(8,128)(2,1)S(1)}, bf16[4,128,128]{2,1,0:T(8,128)(2,1)S(1)}, u32[]{:S(2)}, u32[]{:S(2)}) collective-permute-start(bf16[4,128,128]{2,1,0:T(8,128)(2,1)S(1)} %get-tuple-element.61), channel_id=1, source_target_pairs={{0,2},{2,6},{6,4},{4,0},{1,3},{3,7},{7,5},{5,1},{8,10},{10,14},{14... | collective-permute-start | bytes 393224 | tf_op jit(solution)/shard_map/ppermute | solution.py:93
  40.8 2.2 %collective-permute-start.11 = (bf16[4,128,128]{2,1,0:T(8,128)(2,1)S(1)}, bf16[4,128,128]{2,1,0:T(8,128)(2,1)S(1)}, u32[]{:S(2)}, u32[]{:S(2)}) collective-permute-start(bf16[4,128,128]{2,1,0:T(8,128)(2,1)S(1)} %add_convert_fusion.1), channel_id=1, source_target_pairs={{0,2},{2,6},{6,4},{4,0},{1,3},{3,7},{7,5},{5,1},{8,10},{10,14},{14... | collective-permute-start | bytes 393224 | tf_op jit(solution)/shard_map/ppermute | solution.py:93
  43.0 0.7 %collective-permute-start.10 = (bf16[4,128,128]{2,1,0:T(8,128)(2,1)S(1)}, bf16[4,128,128]{2,1,0:T(8,128)(2,1)S(1)}, u32[]{:S(2)}, u32[]{:S(2)}) collective-permute-start(bf16[4,128,128]{2,1,0:T(8,128)(2,1)S(1)} %get-tuple-element.63), channel_id=1, source_target_pairs={{0,4},{2,0},{6,2},{4,6},{1,5},{3,1},{7,3},{5,7},{8,12},{10,8},{14,... | collective-permute-start | bytes 393224 | tf_op jit(solution)/shard_map/ppermute | solution.py:93
  43.7 2.4 %collective-permute-done.8 = bf16[4,128,128]{2,1,0:T(8,128)(2,1)S(1)} collective-permute-done((bf16[4,128,128]{2,1,0:T(8,128)(2,1)S(1)}, bf16[4,128,128]{2,1,0:T(8,128)(2,1)S(1)}, u32[]{:S(2)}, u32[]{:S(2)}) %collective-permute-start.8) | collective-permute-done | bytes 131104 | tf_op jit(solution)/shard_map/ppermute | solution.py:93
  46.1 1.2 %collective-permute-start.9 = (bf16[4,128,128]{2,1,0:T(8,128)(2,1)S(1)}, bf16[4,128,128]{2,1,0:T(8,128)(2,1)S(1)}, u32[]{:S(2)}, u32[]{:S(2)}) collective-permute-start(bf16[4,128,128]{2,1,0:T(8,128)(2,1)S(1)} %add_convert_fusion), channel_id=1, source_target_pairs={{0,2},{2,6},{6,4},{4,0},{1,3},{3,7},{7,5},{5,1},{8,10},{10,14},{14... | collective-permute-start | bytes 393224 | tf_op jit(solution)/shard_map/ppermute | solution.py:93
  47.3 2.1 %collective-permute-done.10.refs_2_ = bf16[4,128,128]{2,1,0:T(8,128)(2,1)S(1)} collective-permute-done((bf16[4,128,128]{2,1,0:T(8,128)(2,1)S(1)}, bf16[4,128,128]{2,1,0:T(8,128)(2,1)S(1)}, u32[]{:S(2)}, u32[]{:S(2)}) %collective-permute-start.10) | collective-permute-done | bytes 131104 | tf_op jit(solution)/shard_map/ppermute | solution.py:93
  49.4 0.0 collective-permute-done.11.refs_4_
  49.4 2.6 %collective-permute-done.9.refs_1_ = bf16[4,128,128]{2,1,0:T(8,128)(2,1)S(1)} collective-permute-done((bf16[4,128,128]{2,1,0:T(8,128)(2,1)S(1)}, bf16[4,128,128]{2,1,0:T(8,128)(2,1)S(1)}, u32[]{:S(2)}, u32[]{:S(2)}) %collective-permute-start.9) | collective-permute-done | bytes 131104 | tf_op jit(solution)/shard_map/ppermute | solution.py:93
  52.0 0.8 %lay_out.1 = (bf16[512,128]{1,0:T(8,128)(2,1)}, bf16[512,128]{1,0:T(8,128)(2,1)}) custom-call(bf16[4,128,128]{2,1,0:T(8,128)(2,1)S(1)} %get-tuple-element.60.refs_0_, bf16[4,128,128]{2,1,0:T(8,128)(2,1)S(1)} %collective-permute-done.9.refs_1_, bf16[4,128,128]{2,1,0:T(8,128)(2,1)S(1)} %collective-permute-done.10.refs_2_, ...), custom_call_target="tpu_custom_call" | custom-call | flops 1048576 | bytes 65536 | tf_op jit(solution)/shard_map/lay_out/pallas_call | solution.py:340
  52.8 1.3 %collective-permute-done.13 = bf16[128,16,128]{2,1,0:T(8,128)(2,1)S(1)} collective-permute-done((bf16[128,16,128]{2,1,0:T(8,128)(2,1)S(1)}, bf16[128,16,128]{2,1,0:T(8,128)(2,1)S(1)}, u32[]{:S(2)}, u32[]{:S(2)}) %collective-permute-start.13) | collective-permute-done | bytes 524320 | tf_op jit(solution)/shard_map/ppermute | solution.py:110
  54.1 0.0 collective-permute-done.12
  54.1 1.2 %maximum_select_fusion = bf16[1,128,32,128]{3,2,1,0:T(8,128)(2,1)} fusion(bf16[1,128,16,128]{3,2,1,0:T(8,128)(2,1)S(1)} %bitcast.13, bf16[1,128,16,128]{3,2,1,0:T(8,128)(2,1)S(1)} %bitcast.12, pred[]{:T(512)S(6)} %eq.3), kind=kLoop, calls=%fused_computation | loop fusion | flops 2621440 | bytes 2097153 | tf_op jit(solution)/shard_map/jit(_where)/select_n | solution.py:464
  (5 shorter events, 0.1 us)
Async XLA Ops:
  1.8 7.7 %collective-permute-start = (bf16[4,128,128]{2,1,0:T(8,128)(2,1)S(1)}, bf16[4,128,128]{2,1,0:T(8,128)(2,1)S(1)}, u32[]{:S(2)}, u32[]{:S(2)}) collective-permute-start(bf16[4,128,128]{2,1,0:T(8,128)(2,1)S(1)} %get-tuple-element.37.refs_0_), channel_id=1, source_target_pairs={{0,2},{2,6},{6,4},{4,0},{1,3},{3,7},{7,5},{5,1},{8,10},{10,14},{14... | collective-permute-start | bytes 393224 | tf_op jit(solution)/shard_map/ppermute | solution.py:93
  4.9 13.6 %collective-permute-start.2 = (bf16[4,128,128]{2,1,0:T(8,128)(2,1)S(1)}, bf16[4,128,128]{2,1,0:T(8,128)(2,1)S(1)}, u32[]{:S(2)}, u32[]{:S(2)}) collective-permute-start(bf16[4,128,128]{2,1,0:T(8,128)(2,1)S(1)} %get-tuple-element.37.refs_0_), channel_id=1, source_target_pairs={{0,4},{2,0},{6,2},{4,6},{1,5},{3,1},{7,3},{5,7},{8,12},{10,8},{14,... | collective-permute-start | bytes 393224 | tf_op jit(solution)/shard_map/ppermute | solution.py:93
  8.0 10.5 %copy-start = (s32[8]{0:T(128)S(1)}, s32[8]{0:T(128)}, u32[]{:S(2)}) copy-start(s32[8]{0:T(128)} %order_ref.3) | copy-start | bytes 100
  9.5 9.0 %collective-permute-start.3 = (bf16[4,128,128]{2,1,0:T(8,128)(2,1)S(1)}, bf16[4,128,128]{2,1,0:T(8,128)(2,1)S(1)}, u32[]{:S(2)}, u32[]{:S(2)}) collective-permute-start(bf16[4,128,128]{2,1,0:T(8,128)(2,1)S(1)} %collective-permute-done.refs_1_), channel_id=1, source_target_pairs={{0,2},{2,6},{6,4},{4,0},{1,3},{3,7},{7,5},{5,1},{8,10},{10,14},{14... | collective-permute-start | bytes 393224 | tf_op jit(solution)/shard_map/ppermute | solution.py:93
  15.0 6.7 %collective-permute-start.1 = (bf16[4,128,128]{2,1,0:T(8,128)(2,1)S(1)}, bf16[4,128,128]{2,1,0:T(8,128)(2,1)S(1)}, u32[]{:S(2)}, u32[]{:S(2)}) collective-permute-start(bf16[4,128,128]{2,1,0:T(8,128)(2,1)S(1)} %get-tuple-element.40.refs_4_), channel_id=1, source_target_pairs={{0,2},{2,6},{6,4},{4,0},{1,3},{3,7},{7,5},{5,1},{8,10},{10,14},{14... | collective-permute-start | bytes 393224 | tf_op jit(solution)/shard_map/ppermute | solution.py:93
  18.4 11.6 %collective-permute-start.4 = (bf16[4,128,128]{2,1,0:T(8,128)(2,1)S(1)}, bf16[4,128,128]{2,1,0:T(8,128)(2,1)S(1)}, u32[]{:S(2)}, u32[]{:S(2)}) collective-permute-start(bf16[4,128,128]{2,1,0:T(8,128)(2,1)S(1)} %get-tuple-element.40.refs_4_), channel_id=1, source_target_pairs={{0,4},{2,0},{6,2},{4,6},{1,5},{3,1},{7,3},{5,7},{8,12},{10,8},{14,... | collective-permute-start | bytes 393224 | tf_op jit(solution)/shard_map/ppermute | solution.py:93
  21.7 8.3 %collective-permute-start.5 = (bf16[4,128,128]{2,1,0:T(8,128)(2,1)S(1)}, bf16[4,128,128]{2,1,0:T(8,128)(2,1)S(1)}, u32[]{:S(2)}, u32[]{:S(2)}) collective-permute-start(bf16[4,128,128]{2,1,0:T(8,128)(2,1)S(1)} %collective-permute-done.1.refs_5_), channel_id=1, source_target_pairs={{0,2},{2,6},{6,4},{4,0},{1,3},{3,7},{7,5},{5,1},{8,10},{10,14},{14... | collective-permute-start | bytes 393224 | tf_op jit(solution)/shard_map/ppermute | solution.py:93
  27.0 9.4 %collective-permute-start.6 = (bf16[4,128,128]{2,1,0:T(8,128)(2,1)S(1)}, bf16[4,128,128]{2,1,0:T(8,128)(2,1)S(1)}, u32[]{:S(2)}, u32[]{:S(2)}) collective-permute-start(bf16[4,128,128]{2,1,0:T(8,128)(2,1)S(1)} %pad_maximum_fusion), channel_id=1, source_target_pairs={{0,2},{2,6},{6,4},{4,0},{1,3},{3,7},{7,5},{5,1},{8,10},{10,14},{14... | collective-permute-start | bytes 393224 | tf_op jit(solution)/shard_map/ppermute | solution.py:93
  29.4 7.0 %collective-permute-start.7 = (bf16[4,128,128]{2,1,0:T(8,128)(2,1)S(1)}, bf16[4,128,128]{2,1,0:T(8,128)(2,1)S(1)}, u32[]{:S(2)}, u32[]{:S(2)}) collective-permute-start(bf16[4,128,128]{2,1,0:T(8,128)(2,1)S(1)} %pad_maximum_fusion.1), channel_id=1, source_target_pairs={{0,4},{2,0},{6,2},{4,6},{1,5},{3,1},{7,3},{5,7},{8,12},{10,8},{14,... | collective-permute-start | bytes 393224 | tf_op jit(solution)/shard_map/ppermute | solution.py:93
  31.7 22.4 %collective-permute-start.12 = (bf16[128,16,128]{2,1,0:T(8,128)(2,1)S(1)}, bf16[128,16,128]{2,1,0:T(8,128)(2,1)S(1)}, u32[]{:S(2)}, u32[]{:S(2)}) collective-permute-start(bf16[128,16,128]{2,1,0:T(8,128)(2,1)S(1)} %get-tuple-element.47), channel_id=1, source_target_pairs={{0,24},{8,0},{16,8},{24,16},{1,25},{9,1},{17,9},{25,17},{2,26},{10... | collective-permute-start | bytes 1572872 | tf_op jit(solution)/shard_map/ppermute | solution.py:110
  35.8 18.3 %collective-permute-start.13 = (bf16[128,16,128]{2,1,0:T(8,128)(2,1)S(1)}, bf16[128,16,128]{2,1,0:T(8,128)(2,1)S(1)}, u32[]{:S(2)}, u32[]{:S(2)}) collective-permute-start(bf16[128,16,128]{2,1,0:T(8,128)(2,1)S(1)} %get-tuple-element.68), channel_id=1, source_target_pairs={{0,24},{8,0},{16,8},{24,16},{1,25},{9,1},{17,9},{25,17},{2,26},{10... | collective-permute-start | bytes 1572872 | tf_op jit(solution)/shard_map/ppermute | solution.py:110
  39.2 6.8 %collective-permute-start.8 = (bf16[4,128,128]{2,1,0:T(8,128)(2,1)S(1)}, bf16[4,128,128]{2,1,0:T(8,128)(2,1)S(1)}, u32[]{:S(2)}, u32[]{:S(2)}) collective-permute-start(bf16[4,128,128]{2,1,0:T(8,128)(2,1)S(1)} %get-tuple-element.61), channel_id=1, source_target_pairs={{0,2},{2,6},{6,4},{4,0},{1,3},{3,7},{7,5},{5,1},{8,10},{10,14},{14... | collective-permute-start | bytes 393224 | tf_op jit(solution)/shard_map/ppermute | solution.py:93
  40.8 8.6 %collective-permute-start.11 = (bf16[4,128,128]{2,1,0:T(8,128)(2,1)S(1)}, bf16[4,128,128]{2,1,0:T(8,128)(2,1)S(1)}, u32[]{:S(2)}, u32[]{:S(2)}) collective-permute-start(bf16[4,128,128]{2,1,0:T(8,128)(2,1)S(1)} %add_convert_fusion.1), channel_id=1, source_target_pairs={{0,2},{2,6},{6,4},{4,0},{1,3},{3,7},{7,5},{5,1},{8,10},{10,14},{14... | collective-permute-start | bytes 393224 | tf_op jit(solution)/shard_map/ppermute | solution.py:93
  43.0 6.4 %collective-permute-start.10 = (bf16[4,128,128]{2,1,0:T(8,128)(2,1)S(1)}, bf16[4,128,128]{2,1,0:T(8,128)(2,1)S(1)}, u32[]{:S(2)}, u32[]{:S(2)}) collective-permute-start(bf16[4,128,128]{2,1,0:T(8,128)(2,1)S(1)} %get-tuple-element.63), channel_id=1, source_target_pairs={{0,4},{2,0},{6,2},{4,6},{1,5},{3,1},{7,3},{5,7},{8,12},{10,8},{14,... | collective-permute-start | bytes 393224 | tf_op jit(solution)/shard_map/ppermute | solution.py:93
  46.1 5.9 %collective-permute-start.9 = (bf16[4,128,128]{2,1,0:T(8,128)(2,1)S(1)}, bf16[4,128,128]{2,1,0:T(8,128)(2,1)S(1)}, u32[]{:S(2)}, u32[]{:S(2)}) collective-permute-start(bf16[4,128,128]{2,1,0:T(8,128)(2,1)S(1)} %add_convert_fusion), channel_id=1, source_target_pairs={{0,2},{2,6},{6,4},{4,0},{1,3},{3,7},{7,5},{5,1},{8,10},{10,14},{14... | collective-permute-start | bytes 393224 | tf_op jit(solution)/shard_map/ppermute | solution.py:93

commit v9 on v8

--- a/solution.py
+++ b/solution.py
@@ -91,7 +91,7 @@
     count = lax.axis_size(axis)
     order = ring_order(count)
     return lax.ppermute(
-        value, axis, [(order[at], order[(at + step) % count]) for at in range(count)]
+        value, axis, [(order[at], order[(at - step) % count]) for at in range(count)]
     )
 
 
@@ -203,7 +203,7 @@
     at_row = lax.broadcasted_iota(jnp.int32, (half_rows, size), 0)
     at_col = lax.broadcasted_iota(jnp.int32, (half_rows, size), 1)
     for block, distance in enumerate(far_last(blocks)):
-        source = ring_device(blocks, lax.rem(ring - distance + blocks, blocks))
+        source = ring_device(blocks, lax.rem(ring + distance, blocks))
         for half in range(2):
             q_start = order_ref[place * 2 + half]
             for k_half in range(2):

time: 55.4 us -> 51.7 us (0.933)
  waiting for transfers between devices: 10.4 us -> 8.26 us
  starting transfers between devices: 25.4 us -> 23.8 us
    ppermute x12, starting transfers between devices: 22.3 us -> 20.7 us  [passed(): lax.ppermute(value, axis, [(order[at], order[(at - step) % count]) for at...]
    ppermute x12, waiting for transfers between devices: 9.14 us -> 7.96 us  [passed(): lax.ppermute(value, axis, [(order[at], order[(at - step) % count]) for at...]
    ppermute x2, waiting for transfers between devices: 1.27 us -> 0.3 us  [passed_down(): lax.ppermute(value, axis, [(at, (at - 1) % count) for at in range(count)])]
  transfers between devices with their start and end apart: 14 -> 14, of which waited for: 6 -> 6; matrix products, arithmetic and copies ran while one was open for 0% -> 0% of each run, Pallas kernels for 29% -> 32%
where the time goes in v9:
time: 51.7 us; the launch traced here: 51.5 us
  starting transfers between devices  23.8 us (46%)
  Pallas kernels  17.4 us (34%)
  waiting for transfers between devices  8.26 us (16%)
  other arithmetic  1.3 us (3%)
  between operations  0.75 us (1%)
    ppermute x12, starting transfers between devices, passed(): lax.ppermute(value, axis, [(order[at], order[(at - step) % count]) for at...  20.7 us
    pallas_call x6, Pallas kernels, call(): pl.pallas_call(kernel, in_specs=([SMEM] if smem else []) + [VMEM] * (len(...  12.3 us
    ppermute x12, waiting for transfers between devices, passed(): lax.ppermute(value, axis, [(order[at], order[(at - step) % count]) for at...  7.96 us
    pallas_call x2, Pallas kernels, make_side(): pl.pallas_call(functools.partial(kernel, groups), in_specs=[HBM] * count,...  3.98 us
    ppermute x2, starting transfers between devices, passed_down(): lax.ppermute(value, axis, [(at, (at - 1) % count) for at in range(count)])  3.08 us
    select_n x1, other arithmetic, shards(): handed = jnp.where(last, jnp.zeros_like(handed), handed)  1.18 us
    pallas_call x1, Pallas kernels, shards(): pl.pallas_call(prep_kernel, in_specs=[HBM] * 2, out_specs=[VMEM] * 2, out...  1.14 us
  transfers between devices with their start and end apart: 14, of which 6 were waited for; matrix products, arithmetic and copies ran while one was open for 0% of the time, Pallas kernels for 32%

profile of v9, /device:TPU:0, one launch (start us, length us, event | category | flops | bytes accessed | tf_op | source)
XLA Modules:
  0.0 51.5 jit_solution(950013970353456264)
XLA Ops:
  0.6 1.1 %pack_keys.1 = (bf16[4,128,128]{2,1,0:T(8,128)(2,1)S(1)}, bf16[4,128,128]{2,1,0:T(8,128)(2,1)S(1)}) custom-call(bf16[512,128]{1,0:T(8,128)(2,1)} %bitcast.14, bf16[512,128]{1,0:T(8,128)(2,1)} %bitcast.15), custom_call_target="tpu_custom_call" | custom-call | flops 1048576 | bytes 65536 | tf_op jit(solution)/shard_map/pack_keys/pallas_call | solution.py:387
  1.8 4.1 %collective-permute-start = (bf16[4,128,128]{2,1,0:T(8,128)(2,1)S(1)}, bf16[4,128,128]{2,1,0:T(8,128)(2,1)S(1)}, u32[]{:S(2)}, u32[]{:S(2)}) collective-permute-start(bf16[4,128,128]{2,1,0:T(8,128)(2,1)S(1)} %get-tuple-element.37.refs_0_), channel_id=1, source_target_pairs={{0,4},{2,0},{6,2},{4,6},{1,5},{3,1},{7,3},{5,7},{8,12},{10,8},{14,... | collective-permute-start | bytes 393224 | tf_op jit(solution)/shard_map/ppermute | solution.py:93
  5.9 0.0 collective-permute-start.2
  5.9 2.0 %grad_side.1.g_side_ref = bf16[2,4,512,256]{3,2,1,0:T(8,128)(2,1)S(1)} custom-call(bf16[128,32,128]{2,1,0:T(8,128)(2,1)} %bitcast.10, bf16[128,32,128]{2,1,0:T(8,128)(2,1)} %bitcast.11), custom_call_target="tpu_custom_call" | custom-call | flops 1048576 | bytes 65536 | tf_op jit(solution)/shard_map/grad_side/pallas_call | solution.py:361
  7.9 0.0 copy-start
  7.9 1.9 %collective-permute-done.refs_1_ = bf16[4,128,128]{2,1,0:T(8,128)(2,1)S(1)} collective-permute-done((bf16[4,128,128]{2,1,0:T(8,128)(2,1)S(1)}, bf16[4,128,128]{2,1,0:T(8,128)(2,1)S(1)}, u32[]{:S(2)}, u32[]{:S(2)}) %collective-permute-start) | collective-permute-done | bytes 131104 | tf_op jit(solution)/shard_map/ppermute | solution.py:93
  9.8 3.4 %collective-permute-start.3 = (bf16[4,128,128]{2,1,0:T(8,128)(2,1)S(1)}, bf16[4,128,128]{2,1,0:T(8,128)(2,1)S(1)}, u32[]{:S(2)}, u32[]{:S(2)}) collective-permute-start(bf16[4,128,128]{2,1,0:T(8,128)(2,1)S(1)} %collective-permute-done.refs_1_), channel_id=1, source_target_pairs={{0,4},{2,0},{6,2},{4,6},{1,5},{3,1},{7,3},{5,7},{8,12},{10,8},{14,... | collective-permute-start | bytes 393224 | tf_op jit(solution)/shard_map/ppermute | solution.py:93
  13.2 2.0 %query_side.1.q_side_ref = bf16[2,4,512,256]{3,2,1,0:T(8,128)(2,1)S(1)} custom-call(bf16[128,32,128]{2,1,0:T(8,128)(2,1)} %bitcast.9), custom_call_target="tpu_custom_call" | custom-call | flops 1048576 | bytes 65536 | tf_op jit(solution)/shard_map/query_side/pallas_call | solution.py:361
  15.1 0.1 collective-permute-start.1
  15.2 2.0 %collective-permute-start.4 = (bf16[4,128,128]{2,1,0:T(8,128)(2,1)S(1)}, bf16[4,128,128]{2,1,0:T(8,128)(2,1)S(1)}, u32[]{:S(2)}, u32[]{:S(2)}) collective-permute-start(bf16[4,128,128]{2,1,0:T(8,128)(2,1)S(1)} %get-tuple-element.40.refs_4_), channel_id=1, source_target_pairs={{0,2},{2,6},{6,4},{4,0},{1,3},{3,7},{7,5},{5,1},{8,10},{10,14},{14... | collective-permute-start | bytes 393224 | tf_op jit(solution)/shard_map/ppermute | solution.py:93
  17.2 0.0 collective-permute-done.2.refs_2_
  17.2 0.0 collective-permute-done.3.refs_3_
  17.2 0.0 copy-done
  17.2 2.7 %weights.2 = (f32[2,512,1024]{2,1,0:T(8,128)S(1)}, f32[2,8,1024]{2,1,0:T(8,128)S(1)}, bf16[2,128,128]{2,1,0:T(8,128)(2,1)S(1)}, bf16[2,128,128]{2,1,0:T(8,128)(2...) custom-call(s32[8]{0:T(128)S(1)} %copy-done, ...), custom_call_target="tpu_custom_call" | custom-call | flops 4294967296 | bytes 65536 | tf_op jit(solution)/shard_map/weights/pallas_call | solution.py:340
  20.0 0.7 %collective-permute-done.1.refs_5_ = bf16[4,128,128]{2,1,0:T(8,128)(2,1)S(1)} collective-permute-done((bf16[4,128,128]{2,1,0:T(8,128)(2,1)S(1)}, bf16[4,128,128]{2,1,0:T(8,128)(2,1)S(1)}, u32[]{:S(2)}, u32[]{:S(2)}) %collective-permute-start.1) | collective-permute-done | bytes 131104 | tf_op jit(solution)/shard_map/ppermute | solution.py:93
  20.6 2.6 %collective-permute-start.5 = (bf16[4,128,128]{2,1,0:T(8,128)(2,1)S(1)}, bf16[4,128,128]{2,1,0:T(8,128)(2,1)S(1)}, u32[]{:S(2)}, u32[]{:S(2)}) collective-permute-start(bf16[4,128,128]{2,1,0:T(8,128)(2,1)S(1)} %collective-permute-done.1.refs_5_), channel_id=1, source_target_pairs={{0,4},{2,0},{6,2},{4,6},{1,5},{3,1},{7,3},{5,7},{8,12},{10,8},{14,... | collective-permute-start | bytes 393224 | tf_op jit(solution)/shard_map/ppermute | solution.py:93
  23.2 2.7 %weights.3 = (f32[2,512,1024]{2,1,0:T(8,128)S(1)}, f32[2,8,1024]{2,1,0:T(8,128)S(1)}, bf16[2,128,128]{2,1,0:T(8,128)(2,1)S(1)}, bf16[2,128,128]{2,1,0:T(8,128)(2...) custom-call(s32[8]{0:T(128)S(1)} %copy-done, ...), custom_call_target="tpu_custom_call" | custom-call | flops 4294967296 | bytes 65536 | tf_op jit(solution)/shard_map/weights/pallas_call | solution.py:340
  26.0 0.1 collective-permute-start.6
  26.1 2.0 %collective-permute-start.7 = (bf16[4,128,128]{2,1,0:T(8,128)(2,1)S(1)}, bf16[4,128,128]{2,1,0:T(8,128)(2,1)S(1)}, u32[]{:S(2)}, u32[]{:S(2)}) collective-permute-start(bf16[4,128,128]{2,1,0:T(8,128)(2,1)S(1)} %pad_maximum_fusion.1), channel_id=1, source_target_pairs={{0,2},{2,6},{6,4},{4,0},{1,3},{3,7},{7,5},{5,1},{8,10},{10,14},{14... | collective-permute-start | bytes 393224 | tf_op jit(solution)/shard_map/ppermute | solution.py:93
  28.1 0.0 collective-permute-done.4.refs_6_
  28.1 0.0 collective-permute-done.5.refs_7_
  28.1 1.6 %query_grads.2 = (bf16[128,16,128]{2,1,0:T(8,128)(2,1)S(1)}, bf16[2,512,1024]{2,1,0:T(8,128)(2,1)S(1)}) custom-call(bf16[2,4,512,256]{3,2,1,0:T(8,128)(2,1)S(1)} %grad_side.1.g_side_ref, f32[2,512,1024]{2,1,0:T(8,128)S(1)} %get-tuple-element.44.weight_ref, f32[2,8,1024]{2,1,0:T(8,128)S(1)} %get-tuple-element.42.scale_ref, ...), custom_call_target="tpu_custom_call" | custom-call | flops 4294967296 | bytes 65536 | tf_op jit(solution)/shard_map/query_grads/pallas_call | solution.py:340
  29.8 2.5 %collective-permute-start.12 = (bf16[128,16,128]{2,1,0:T(8,128)(2,1)S(1)}, bf16[128,16,128]{2,1,0:T(8,128)(2,1)S(1)}, u32[]{:S(2)}, u32[]{:S(2)}) collective-permute-start(bf16[128,16,128]{2,1,0:T(8,128)(2,1)S(1)} %get-tuple-element.47), channel_id=1, source_target_pairs={{0,24},{8,0},{16,8},{24,16},{1,25},{9,1},{17,9},{25,17},{2,26},{10... | collective-permute-start | bytes 1572872 | tf_op jit(solution)/shard_map/ppermute | solution.py:110
  32.3 1.6 %query_grads.3 = (bf16[128,16,128]{2,1,0:T(8,128)(2,1)S(1)}, bf16[2,512,1024]{2,1,0:T(8,128)(2,1)S(1)}) custom-call(bf16[2,4,512,256]{3,2,1,0:T(8,128)(2,1)S(1)} %grad_side.1.g_side_ref, f32[2,512,1024]{2,1,0:T(8,128)S(1)} %get-tuple-element.49.weight_ref, f32[2,8,1024]{2,1,0:T(8,128)S(1)} %get-tuple-element.50.scale_ref, ...), custom_call_target="tpu_custom_call" | custom-call | flops 4294967296 | bytes 65536 | tf_op jit(solution)/shard_map/query_grads/pallas_call | solution.py:340
  33.9 0.6 %collective-permute-start.13 = (bf16[128,16,128]{2,1,0:T(8,128)(2,1)S(1)}, bf16[128,16,128]{2,1,0:T(8,128)(2,1)S(1)}, u32[]{:S(2)}, u32[]{:S(2)}) collective-permute-start(bf16[128,16,128]{2,1,0:T(8,128)(2,1)S(1)} %get-tuple-element.68), channel_id=1, source_target_pairs={{0,24},{8,0},{16,8},{24,16},{1,25},{9,1},{17,9},{25,17},{2,26},{10... | collective-permute-start | bytes 1572872 | tf_op jit(solution)/shard_map/ppermute | solution.py:110
  34.4 0.0 collective-permute-done.6
  34.5 0.0 collective-permute-done.7.refs_5_
  34.5 2.8 %key_grads.1 = (bf16[4,128,128]{2,1,0:T(8,128)(2,1)S(1)}, bf16[4,128,128]{2,1,0:T(8,128)(2,1)S(1)}, bf16[4,128,128]{2,1,0:T(8,128)(2,1)S(1)}, bf16[4,128,128]{2,1,0:T(8,128)(2,1)S(1)}) custom-call(bf16[2,4,512,256]{3,2,1,0:T(8,128)(2,1)S(1)} %query_side.1.q_side_ref, bf16[2,512,1024]{2,1,0:T(8,128)(2,1)S(1)} %get-tuple-element.58.refs_0_, ...), custom_call_target="tpu_custom_call" | custom-call | flops 1048576 | bytes 65536 | tf_op jit(solution)/shard_map/key_grads/pallas_call | solution.py:340
  37.3 2.4 %collective-permute-start.8 = (bf16[4,128,128]{2,1,0:T(8,128)(2,1)S(1)}, bf16[4,128,128]{2,1,0:T(8,128)(2,1)S(1)}, u32[]{:S(2)}, u32[]{:S(2)}) collective-permute-start(bf16[4,128,128]{2,1,0:T(8,128)(2,1)S(1)} %get-tuple-element.61), channel_id=1, source_target_pairs={{0,4},{2,0},{6,2},{4,6},{1,5},{3,1},{7,3},{5,7},{8,12},{10,8},{14,... | collective-permute-start | bytes 393224 | tf_op jit(solution)/shard_map/ppermute | solution.py:93
  39.7 0.1 collective-permute-start.11
  39.8 2.0 %collective-permute-start.10 = (bf16[4,128,128]{2,1,0:T(8,128)(2,1)S(1)}, bf16[4,128,128]{2,1,0:T(8,128)(2,1)S(1)}, u32[]{:S(2)}, u32[]{:S(2)}) collective-permute-start(bf16[4,128,128]{2,1,0:T(8,128)(2,1)S(1)} %get-tuple-element.63), channel_id=1, source_target_pairs={{0,2},{2,6},{6,4},{4,0},{1,3},{3,7},{7,5},{5,1},{8,10},{10,14},{14... | collective-permute-start | bytes 393224 | tf_op jit(solution)/shard_map/ppermute | solution.py:93
  41.7 2.4 %collective-permute-done.8 = bf16[4,128,128]{2,1,0:T(8,128)(2,1)S(1)} collective-permute-done((bf16[4,128,128]{2,1,0:T(8,128)(2,1)S(1)}, bf16[4,128,128]{2,1,0:T(8,128)(2,1)S(1)}, u32[]{:S(2)}, u32[]{:S(2)}) %collective-permute-start.8) | collective-permute-done | bytes 131104 | tf_op jit(solution)/shard_map/ppermute | solution.py:93
  44.2 2.0 %collective-permute-start.9 = (bf16[4,128,128]{2,1,0:T(8,128)(2,1)S(1)}, bf16[4,128,128]{2,1,0:T(8,128)(2,1)S(1)}, u32[]{:S(2)}, u32[]{:S(2)}) collective-permute-start(bf16[4,128,128]{2,1,0:T(8,128)(2,1)S(1)} %add_convert_fusion), channel_id=1, source_target_pairs={{0,4},{2,0},{6,2},{4,6},{1,5},{3,1},{7,3},{5,7},{8,12},{10,8},{14,... | collective-permute-start | bytes 393224 | tf_op jit(solution)/shard_map/ppermute | solution.py:93
  46.2 1.5 %collective-permute-done.10.refs_2_ = bf16[4,128,128]{2,1,0:T(8,128)(2,1)S(1)} collective-permute-done((bf16[4,128,128]{2,1,0:T(8,128)(2,1)S(1)}, bf16[4,128,128]{2,1,0:T(8,128)(2,1)S(1)}, u32[]{:S(2)}, u32[]{:S(2)}) %collective-permute-start.10) | collective-permute-done | bytes 131104 | tf_op jit(solution)/shard_map/ppermute | solution.py:93
  47.7 0.0 collective-permute-done.11.refs_4_
  47.7 1.5 %collective-permute-done.9.refs_1_ = bf16[4,128,128]{2,1,0:T(8,128)(2,1)S(1)} collective-permute-done((bf16[4,128,128]{2,1,0:T(8,128)(2,1)S(1)}, bf16[4,128,128]{2,1,0:T(8,128)(2,1)S(1)}, u32[]{:S(2)}, u32[]{:S(2)}) %collective-permute-start.9) | collective-permute-done | bytes 131104 | tf_op jit(solution)/shard_map/ppermute | solution.py:93
  49.2 0.8 %lay_out.1 = (bf16[512,128]{1,0:T(8,128)(2,1)}, bf16[512,128]{1,0:T(8,128)(2,1)}) custom-call(bf16[4,128,128]{2,1,0:T(8,128)(2,1)S(1)} %get-tuple-element.60.refs_0_, bf16[4,128,128]{2,1,0:T(8,128)(2,1)S(1)} %collective-permute-done.9.refs_1_, bf16[4,128,128]{2,1,0:T(8,128)(2,1)S(1)} %collective-permute-done.10.refs_2_, ...), custom_call_target="tpu_custom_call" | custom-call | flops 1048576 | bytes 65536 | tf_op jit(solution)/shard_map/lay_out/pallas_call | solution.py:340
  50.0 0.3 collective-permute-done.13
  50.3 0.0 collective-permute-done.12
  50.3 1.2 %maximum_select_fusion = bf16[1,128,32,128]{3,2,1,0:T(8,128)(2,1)} fusion(bf16[1,128,16,128]{3,2,1,0:T(8,128)(2,1)S(1)} %bitcast.13, bf16[1,128,16,128]{3,2,1,0:T(8,128)(2,1)S(1)} %bitcast.12, pred[]{:T(512)S(6)} %eq.3), kind=kLoop, calls=%fused_computation | loop fusion | flops 2621440 | bytes 2097153 | tf_op jit(solution)/shard_map/jit(_where)/select_n | solution.py:464
  (5 shorter events, 0.1 us)
Async XLA Ops:
  1.8 8.0 %collective-permute-start = (bf16[4,128,128]{2,1,0:T(8,128)(2,1)S(1)}, bf16[4,128,128]{2,1,0:T(8,128)(2,1)S(1)}, u32[]{:S(2)}, u32[]{:S(2)}) collective-permute-start(bf16[4,128,128]{2,1,0:T(8,128)(2,1)S(1)} %get-tuple-element.37.refs_0_), channel_id=1, source_target_pairs={{0,4},{2,0},{6,2},{4,6},{1,5},{3,1},{7,3},{5,7},{8,12},{10,8},{14,... | collective-permute-start | bytes 393224 | tf_op jit(solution)/shard_map/ppermute | solution.py:93
  5.9 11.3 %collective-permute-start.2 = (bf16[4,128,128]{2,1,0:T(8,128)(2,1)S(1)}, bf16[4,128,128]{2,1,0:T(8,128)(2,1)S(1)}, u32[]{:S(2)}, u32[]{:S(2)}) collective-permute-start(bf16[4,128,128]{2,1,0:T(8,128)(2,1)S(1)} %get-tuple-element.37.refs_0_), channel_id=1, source_target_pairs={{0,2},{2,6},{6,4},{4,0},{1,3},{3,7},{7,5},{5,1},{8,10},{10,14},{14... | collective-permute-start | bytes 393224 | tf_op jit(solution)/shard_map/ppermute | solution.py:93
  7.9 9.3 %copy-start = (s32[8]{0:T(128)S(1)}, s32[8]{0:T(128)}, u32[]{:S(2)}) copy-start(s32[8]{0:T(128)} %order_ref.3) | copy-start | bytes 100
  9.8 7.4 %collective-permute-start.3 = (bf16[4,128,128]{2,1,0:T(8,128)(2,1)S(1)}, bf16[4,128,128]{2,1,0:T(8,128)(2,1)S(1)}, u32[]{:S(2)}, u32[]{:S(2)}) collective-permute-start(bf16[4,128,128]{2,1,0:T(8,128)(2,1)S(1)} %collective-permute-done.refs_1_), channel_id=1, source_target_pairs={{0,4},{2,0},{6,2},{4,6},{1,5},{3,1},{7,3},{5,7},{8,12},{10,8},{14,... | collective-permute-start | bytes 393224 | tf_op jit(solution)/shard_map/ppermute | solution.py:93
  15.1 5.5 %collective-permute-start.1 = (bf16[4,128,128]{2,1,0:T(8,128)(2,1)S(1)}, bf16[4,128,128]{2,1,0:T(8,128)(2,1)S(1)}, u32[]{:S(2)}, u32[]{:S(2)}) collective-permute-start(bf16[4,128,128]{2,1,0:T(8,128)(2,1)S(1)} %get-tuple-element.40.refs_4_), channel_id=1, source_target_pairs={{0,4},{2,0},{6,2},{4,6},{1,5},{3,1},{7,3},{5,7},{8,12},{10,8},{14,... | collective-permute-start | bytes 393224 | tf_op jit(solution)/shard_map/ppermute | solution.py:93
  15.2 12.9 %collective-permute-start.4 = (bf16[4,128,128]{2,1,0:T(8,128)(2,1)S(1)}, bf16[4,128,128]{2,1,0:T(8,128)(2,1)S(1)}, u32[]{:S(2)}, u32[]{:S(2)}) collective-permute-start(bf16[4,128,128]{2,1,0:T(8,128)(2,1)S(1)} %get-tuple-element.40.refs_4_), channel_id=1, source_target_pairs={{0,2},{2,6},{6,4},{4,0},{1,3},{3,7},{7,5},{5,1},{8,10},{10,14},{14... | collective-permute-start | bytes 393224 | tf_op jit(solution)/shard_map/ppermute | solution.py:93
  20.6 7.5 %collective-permute-start.5 = (bf16[4,128,128]{2,1,0:T(8,128)(2,1)S(1)}, bf16[4,128,128]{2,1,0:T(8,128)(2,1)S(1)}, u32[]{:S(2)}, u32[]{:S(2)}) collective-permute-start(bf16[4,128,128]{2,1,0:T(8,128)(2,1)S(1)} %collective-permute-done.1.refs_5_), channel_id=1, source_target_pairs={{0,4},{2,0},{6,2},{4,6},{1,5},{3,1},{7,3},{5,7},{8,12},{10,8},{14,... | collective-permute-start | bytes 393224 | tf_op jit(solution)/shard_map/ppermute | solution.py:93
  26.0 8.5 %collective-permute-start.6 = (bf16[4,128,128]{2,1,0:T(8,128)(2,1)S(1)}, bf16[4,128,128]{2,1,0:T(8,128)(2,1)S(1)}, u32[]{:S(2)}, u32[]{:S(2)}) collective-permute-start(bf16[4,128,128]{2,1,0:T(8,128)(2,1)S(1)} %pad_maximum_fusion), channel_id=1, source_target_pairs={{0,4},{2,0},{6,2},{4,6},{1,5},{3,1},{7,3},{5,7},{8,12},{10,8},{14,... | collective-permute-start | bytes 393224 | tf_op jit(solution)/shard_map/ppermute | solution.py:93
  26.1 8.4 %collective-permute-start.7 = (bf16[4,128,128]{2,1,0:T(8,128)(2,1)S(1)}, bf16[4,128,128]{2,1,0:T(8,128)(2,1)S(1)}, u32[]{:S(2)}, u32[]{:S(2)}) collective-permute-start(bf16[4,128,128]{2,1,0:T(8,128)(2,1)S(1)} %pad_maximum_fusion.1), channel_id=1, source_target_pairs={{0,2},{2,6},{6,4},{4,0},{1,3},{3,7},{7,5},{5,1},{8,10},{10,14},{14... | collective-permute-start | bytes 393224 | tf_op jit(solution)/shard_map/ppermute | solution.py:93
  29.8 20.6 %collective-permute-start.12 = (bf16[128,16,128]{2,1,0:T(8,128)(2,1)S(1)}, bf16[128,16,128]{2,1,0:T(8,128)(2,1)S(1)}, u32[]{:S(2)}, u32[]{:S(2)}) collective-permute-start(bf16[128,16,128]{2,1,0:T(8,128)(2,1)S(1)} %get-tuple-element.47), channel_id=1, source_target_pairs={{0,24},{8,0},{16,8},{24,16},{1,25},{9,1},{17,9},{25,17},{2,26},{10... | collective-permute-start | bytes 1572872 | tf_op jit(solution)/shard_map/ppermute | solution.py:110
  33.9 16.4 %collective-permute-start.13 = (bf16[128,16,128]{2,1,0:T(8,128)(2,1)S(1)}, bf16[128,16,128]{2,1,0:T(8,128)(2,1)S(1)}, u32[]{:S(2)}, u32[]{:S(2)}) collective-permute-start(bf16[128,16,128]{2,1,0:T(8,128)(2,1)S(1)} %get-tuple-element.68), channel_id=1, source_target_pairs={{0,24},{8,0},{16,8},{24,16},{1,25},{9,1},{17,9},{25,17},{2,26},{10... | collective-permute-start | bytes 1572872 | tf_op jit(solution)/shard_map/ppermute | solution.py:110
  37.3 6.8 %collective-permute-start.8 = (bf16[4,128,128]{2,1,0:T(8,128)(2,1)S(1)}, bf16[4,128,128]{2,1,0:T(8,128)(2,1)S(1)}, u32[]{:S(2)}, u32[]{:S(2)}) collective-permute-start(bf16[4,128,128]{2,1,0:T(8,128)(2,1)S(1)} %get-tuple-element.61), channel_id=1, source_target_pairs={{0,4},{2,0},{6,2},{4,6},{1,5},{3,1},{7,3},{5,7},{8,12},{10,8},{14,... | collective-permute-start | bytes 393224 | tf_op jit(solution)/shard_map/ppermute | solution.py:93
  39.7 8.0 %collective-permute-start.11 = (bf16[4,128,128]{2,1,0:T(8,128)(2,1)S(1)}, bf16[4,128,128]{2,1,0:T(8,128)(2,1)S(1)}, u32[]{:S(2)}, u32[]{:S(2)}) collective-permute-start(bf16[4,128,128]{2,1,0:T(8,128)(2,1)S(1)} %add_convert_fusion.1), channel_id=1, source_target_pairs={{0,4},{2,0},{6,2},{4,6},{1,5},{3,1},{7,3},{5,7},{8,12},{10,8},{14,... | collective-permute-start | bytes 393224 | tf_op jit(solution)/shard_map/ppermute | solution.py:93
  39.8 8.0 %collective-permute-start.10 = (bf16[4,128,128]{2,1,0:T(8,128)(2,1)S(1)}, bf16[4,128,128]{2,1,0:T(8,128)(2,1)S(1)}, u32[]{:S(2)}, u32[]{:S(2)}) collective-permute-start(bf16[4,128,128]{2,1,0:T(8,128)(2,1)S(1)} %get-tuple-element.63), channel_id=1, source_target_pairs={{0,2},{2,6},{6,4},{4,0},{1,3},{3,7},{7,5},{5,1},{8,10},{10,14},{14... | collective-permute-start | bytes 393224 | tf_op jit(solution)/shard_map/ppermute | solution.py:93
  44.2 5.0 %collective-permute-start.9 = (bf16[4,128,128]{2,1,0:T(8,128)(2,1)S(1)}, bf16[4,128,128]{2,1,0:T(8,128)(2,1)S(1)}, u32[]{:S(2)}, u32[]{:S(2)}) collective-permute-start(bf16[4,128,128]{2,1,0:T(8,128)(2,1)S(1)} %add_convert_fusion), channel_id=1, source_target_pairs={{0,4},{2,0},{6,2},{4,6},{1,5},{3,1},{7,3},{5,7},{8,12},{10,8},{14,... | collective-permute-start | bytes 393224 | tf_op jit(solution)/shard_map/ppermute | solution.py:93
